TPU v7x, 128 devices: a whole 4x4x4 slice. The times are simulated.
128 devices in a mesh: expert: 64 (over x, z, y), dp: 2 (over core).
Axes of the slice: x: 4, y: 4, z: 4, core: 2. Of those that a mesh axis runs over, the one named last changes fastest.
Arguments:
- tokens: bfloat16 [16384, 7168], P(('expert', 'dp')), may hold values from -6 to 6
- grad_out: bfloat16 [16384, 7168], P(('expert', 'dp')), may hold values from -6 to 6
- gates: float32 [16384, 8], P(('expert', 'dp')), may hold values from 0.1 to 0.6
- expert_ids: int32 [16384, 8], P(('expert', 'dp')), may hold values from 0 to 255, as said below
- expert_weights: bfloat16 [64, 192, 7168], P('expert', None, 'dp'), may hold values from -1 to 1
- moment_one: float32 [64, 192, 7168], P('expert', None, 'dp'), may hold values from -6 to 6
- moment_two: float32 [64, 192, 7168], P('expert', None, 'dp'), may hold values from 1 to 1000
Outputs:
- grad_tokens: bfloat16 [16384, 7168], P(('expert', 'dp'))
- new_moment_one: float32 [64, 192, 7168], P('expert', None, 'dp')
- new_moment_two: float32 [64, 192, 7168], P('expert', None, 'dp')
Inputs may be any that keep to these rules, and one draw needn't show every extreme that they name: `expert_ids`: each row names 8 different experts. In each device's aligned block of 128 rows no expert under 4 is named by more than 8 rows; in every draw some expert under 4 is named by exactly 8 rows in every block.
All inputs are finite; a program needn't handle non-finite values.
Results may differ from a plain program's by a relative error of at most 0.0095.
Values may be sent and summed in bfloat16 or wider, within the bound.
No kernel may reach another device: no remote copies, remote signals or barrier semaphores. Data moves between devices by JAX's collectives and lax.ppermute only.
A program may use at most 128 MiB of HBM per device.

v0:
```python
import jax
import jax.numpy as jnp
from jax import lax
from jax.sharding import PartitionSpec as P

GROUP = 16


beta_one = 0.9
beta_two = 0.95


def local_backward(pair_pre, d_hidden, w_pair):
    slab_width = d_hidden.shape[1]
    gate_pre = pair_pre[:, :slab_width]
    up_pre = pair_pre[:, slab_width:]
    sigmoid_gate = jax.nn.sigmoid(gate_pre)
    activated = gate_pre * sigmoid_gate
    hidden = (activated * up_pre).astype(jnp.bfloat16)
    d_gate = d_hidden * up_pre * sigmoid_gate * (1.0 + gate_pre * (1.0 - sigmoid_gate))
    d_up = d_hidden * activated
    d_pair = jnp.concatenate([d_gate, d_up], axis=1).astype(jnp.bfloat16)
    back_rows = jnp.dot(d_pair, w_pair, preferred_element_type=jnp.float32).astype(jnp.bfloat16)
    return (hidden, d_pair, back_rows)


def shards(tokens, grad_out, gates, expert_ids, expert_weights, moment_one, moment_two):
    tok_count, feature_width = tokens.shape
    top_count = expert_ids.shape[1]
    axis_count = lax.axis_size("expert")
    expert_count = axis_count // GROUP
    routed_count = 64 * expert_count
    rows_sent = tok_count * top_count
    slot_rows = 2 * rows_sent // routed_count
    window_slots = expert_count * slot_rows
    flat_ids = expert_ids.reshape(-1)
    in_window = flat_ids < expert_count
    onehot = (flat_ids[:, None] == jnp.arange(expert_count, dtype=jnp.int32)[None, :]).astype(
        jnp.int32
    )
    before = jnp.cumsum(onehot, axis=0, dtype=jnp.int32) - onehot
    position = jnp.sum(before * onehot, axis=1, dtype=jnp.int32)
    key_of_row = jnp.where(in_window, flat_ids * slot_rows + position, window_slots)
    table = (
        jnp.zeros((window_slots + 1,), jnp.int32)
        .at[key_of_row]
        .set(jnp.arange(rows_sent, dtype=jnp.int32) + 1)[:window_slots]
    )
    filler = jnp.broadcast_to(
        table.reshape(expert_count, 1, slot_rows), (expert_count, GROUP, slot_rows)
    ).reshape(-1)
    occupied = filler > 0
    source_row = jnp.maximum(filler - 1, 0)
    source_tok = source_row // top_count
    slot_gate = jnp.where(occupied, gates.reshape(-1)[source_row], 0.0)
    sent_inputs = jnp.where(occupied[:, None], tokens[source_tok], jnp.zeros((), tokens.dtype))
    sent_grads = (slot_gate[:, None] * grad_out[source_tok].astype(jnp.float32)).astype(
        jnp.bfloat16
    )
    got_inputs, got_grads = (
        lax.all_to_all(sent_inputs, "expert", split_axis=0, concat_axis=0, tiled=True),
        lax.all_to_all(sent_grads, "expert", split_axis=0, concat_axis=0, tiled=True),
    )
    weights = lax.all_gather(expert_weights[0], "dp", axis=1, tiled=True)
    slab_width = weights.shape[0] // 3
    w_pair = weights[: 2 * slab_width]
    w_down = weights[2 * slab_width :]
    pair_pre = lax.dot_general(
        got_inputs, w_pair, (((1,), (1,)), ((), ())), preferred_element_type=jnp.float32
    )
    d_hidden = lax.dot_general(
        got_grads, w_down, (((1,), (1,)), ((), ())), preferred_element_type=jnp.float32
    )
    hidden, d_pair, back_rows = local_backward(pair_pre, d_hidden, w_pair)
    returned = lax.all_to_all(back_rows, "expert", split_axis=0, concat_axis=0, tiled=True)
    in_terms = lax.dot_general(
        got_inputs, d_pair, (((0,), (0,)), ((), ())), preferred_element_type=jnp.float32
    )
    out_terms = lax.dot_general(
        got_grads, hidden, (((0,), (0,)), ((), ())), preferred_element_type=jnp.float32
    )
    weight_grad = jnp.transpose(
        lax.psum_scatter(
            jnp.concatenate([in_terms, out_terms], axis=1).astype(jnp.bfloat16),
            "dp",
            scatter_dimension=0,
            tiled=True,
        ).astype(jnp.float32)
    )
    summed = jnp.sum(
        returned.reshape(expert_count, GROUP, slot_rows, feature_width), axis=1, dtype=jnp.float32
    ).reshape(window_slots, feature_width)
    padded = jnp.concatenate([summed, jnp.zeros((1, feature_width), jnp.float32)], axis=0)
    picked = padded[key_of_row].reshape(tok_count, top_count, feature_width)
    grad_tokens = jnp.sum(picked, axis=1).astype(jnp.bfloat16)
    new_a = beta_one * moment_one[0] + (1.0 - beta_one) * weight_grad
    new_b = beta_two * moment_two[0] + (1.0 - beta_two) * weight_grad * weight_grad
    return (grad_tokens, new_a[None], new_b[None])


def solution(mesh):
    return jax.shard_map(
        shards,
        mesh=mesh,
        in_specs=(
            P(("expert", "dp"), None),
            P(("expert", "dp"), None),
            P(("expert", "dp"), None),
            P(("expert", "dp"), None),
            P("expert", None, "dp"),
            P("expert", None, "dp"),
            P("expert", None, "dp"),
        ),
        out_specs=(P(("expert", "dp"), None), P("expert", None, "dp"), P("expert", None, "dp")),
        check_vma=False,
    )
```

profile of v0, /device:TPU:103, one launch (start us, length us, event | category | flops | bytes accessed | tf_op | source)
XLA Modules:
  0.0 432.6 jit_solution(2463022901274647359)
XLA Ops:
  7.2 0.8 broadcast_compare_fusion
  8.0 0.7 broadcast_multiply_fusion
  8.7 0.8 copy.12
  9.5 0.1 eq.29
  9.6 0.1 eq.25
  9.7 0.1 copy.10
  9.8 0.1 lt.41
  9.9 0.1 copy.11
  10.0 0.1 mul.84
  10.1 1.1 reduce-window.6
  11.3 0.2 slice_reduce_fusion
  11.5 0.2 reduce-window.9
  11.8 4.3 scatter_custom_fusion
  16.1 0.1 max.22
  16.2 0.1 gt.18
  16.3 0.1 reshape.239
  16.4 0.1 reshape.234
  16.6 7.0 %gather_fusion.2 = bf16[512,7168]{1,0:T(8,128)(2,1)} fusion(bf16[128,7168]{1,0:T(8,128)(2,1)S(1)} %copy-done, s32[1024]{0:T(1024)S(1)} %pad_clamp_fusion), kind=kCustom, calls=%fused_computation.2 | custom fusion | bytes 14682112 | tf_op jit(solution)/shard_map/gather | solution.py:56
  23.6 6.7 %bitcast_select_fusion = bf16[64,8,7168]{2,1,0:T(8,128)(2,1)} fusion(bf16[512,7168]{1,0:T(8,128)(2,1)} %gather_fusion.2, pred[64,8]{1,0:T(8,128)(4,1)S(1)} %bitcast.75), kind=kLoop, calls=%fused_computation.16 | loop fusion | flops 3670016 | bytes 14680576 | tf_op jit(solution)/shard_map/jit(_where)/select_n | solution.py:56
  30.3 10.1 %all-to-all-start.1 = ((bf16[64,8,7168]{2,1,0:T(8,128)(2,1)}), bf16[64,8,7168]{2,1,0:T(8,128)(2,1)}, u32[]{:S(2)}, u32[]{:S(2)}) async-start(bf16[64,8,7168]{2,1,0:T(8,128)(2,1)} %bitcast_select_fusion), calls=%async_computation.1 | async-start | bytes 14680064 | tf_op jit(solution)/shard_map/all_to_all | solution.py:61
  40.4 0.1 reshape.188
  40.5 0.1 copy.14
  40.6 0.1 reshape.181
  40.7 2.3 gather_fusion
  43.0 0.1 gather.17
  43.1 7.0 %gather_fusion.1 = bf16[512,7168]{1,0:T(8,128)(2,1)} fusion(bf16[128,7168]{1,0:T(8,128)(2,1)S(1)} %copy-done.2, s32[1024]{0:T(1024)S(1)} %pad_clamp_fusion), kind=kCustom, calls=%fused_computation.1 | custom fusion | bytes 14682112 | tf_op jit(solution)/shard_map/gather | solution.py:57
  50.1 8.4 %fusion = bf16[64,8,7168]{2,1,0:T(8,128)(2,1)} fusion(bf16[512,7168]{1,0:T(8,128)(2,1)} %gather_fusion.1, f32[64,8]{1,0:T(8,128)S(1)} %broadcast_select_fusion), kind=kLoop, calls=%fused_computation.8 | loop fusion | flops 11010048 | bytes 14682112 | tf_op jit(solution)/shard_map/convert_element_type | solution.py:57
  58.5 89.7 %all-to-all-done.1 = bf16[64,8,7168]{2,1,0:T(8,128)(2,1)} async-done(((bf16[64,8,7168]{2,1,0:T(8,128)(2,1)}), bf16[64,8,7168]{2,1,0:T(8,128)(2,1)}, u32[]{:S(2)}, u32[]{:S(2)}) %all-to-all-start.1) | async-done | bytes 7340064 | tf_op jit(solution)/shard_map/all_to_all | solution.py:61
  148.3 7.1 %all-to-all-start = ((bf16[64,8,7168]{2,1,0:T(8,128)(2,1)}), bf16[64,8,7168]{2,1,0:T(8,128)(2,1)}, u32[]{:S(2)}, u32[]{:S(2)}) async-start(bf16[64,8,7168]{2,1,0:T(8,128)(2,1)} %fusion), calls=%async_computation | async-start | bytes 14680064 | tf_op jit(solution)/shard_map/all_to_all | solution.py:62
  155.4 0.2 all-gather.3.cloned.1.call-start
  155.6 0.5 all-gather.3.cloned.1.call-update
  156.1 18.1 %all-gather.3.cloned.1.call-done = bf16[1,192,7168]{2,1,0:T(8,128)(2,1)} async-done(((bf16[1,192,3584]{2,1,0:T(8,128)(2,1)}), bf16[1,192,7168]{2,1,0:T(8,128)(2,1)}) %all-gather.3.cloned.1.call-update) | async-done | bytes 2752528 | tf_op jit(solution)/shard_map/all_gather | solution.py:64
  174.2 6.2 %fusion.3 = f32[512,128]{0,1:T(8,128)S(1)} fusion(bf16[64,8,7168]{2,1,0:T(8,128)(2,1)} %all-to-all-done.1, bf16[1,192,7168]{2,1,0:T(8,128)(2,1)} %all-gather.3.cloned.1.call-done), kind=kOutput, calls=%fused_computation.14 | convolution fusion | flops 939524096 | bytes 9437184 | tf_op jit(solution)/shard_map/dot_general | solution.py:68
  180.4 84.7 %all-to-all-done = bf16[64,8,7168]{2,1,0:T(8,128)(2,1)} async-done(((bf16[64,8,7168]{2,1,0:T(8,128)(2,1)}), bf16[64,8,7168]{2,1,0:T(8,128)(2,1)}, u32[]{:S(2)}, u32[]{:S(2)}) %all-to-all-start) | async-done | bytes 7340064 | tf_op jit(solution)/shard_map/all_to_all | solution.py:62
  265.1 5.8 %multiply_convert_fusion.2 = (bf16[512,64]{0,1:T(8,128)(2,1)S(1)}, bf16[512,64]{0,1:T(8,128)(2,1)S(1)}) fusion(f32[512,128]{0,1:T(8,128)S(1)} %fusion.3, bf16[1,192,7168]{2,1,0:T(8,128)(2,1)} %all-gather.3.cloned.1.call-done, bf16[64,8,7168]{2,1,0:T(8,128)(2,1)} %all-to-all-done), kind=kOutput, calls=%fused_computation.32 | convolution fusion | flops 470188032 | bytes 8650752 | tf_op jit(solution)/shard_map/dot_general | solution.py:71
  270.9 5.1 %fusion.1 = bf16[64,8,7168]{2,1,0:T(8,128)(2,1)} fusion(bf16[1,192,7168]{2,1,0:T(8,128)(2,1)S(1)} %copy-done.3, bf16[512,64]{0,1:T(8,128)(2,1)S(1)} %get-tuple-element.6, bf16[512,64]{0,1:T(8,128)(2,1)S(1)} %get-tuple-element.5), kind=kOutput, calls=%fused_computation.10 | convolution fusion | flops 943456256 | bytes 9306112 | tf_op jit(solution)/shard_map/dot_general | solution.py:23
  276.0 7.1 %all-to-all-start.2 = ((bf16[64,8,7168]{2,1,0:T(8,128)(2,1)}), bf16[64,8,7168]{2,1,0:T(8,128)(2,1)}, u32[]{:S(2)}, u32[]{:S(2)}) async-start(bf16[64,8,7168]{2,1,0:T(8,128)(2,1)} %fusion.1), calls=%async_computation.2 | async-start | bytes 14680064 | tf_op jit(solution)/shard_map/all_to_all | solution.py:75
  283.1 0.3 reduce-scatter.2.cloned.1.call-start
  283.3 4.5 %convolution_convert_fusion.2 = bf16[7168,64]{0,1:T(8,128)(2,1)S(1)} fusion(bf16[64,8,7168]{2,1,0:T(8,128)(2,1)} %all-to-all-done, f32[512,128]{0,1:T(8,128)S(1)} %fusion.3), kind=kOutput, calls=%fused_computation.12 | convolution fusion | flops 470417408 | bytes 8519680 | tf_op jit(solution)/shard_map/dot_general | solution.py:79
  287.8 4.2 convolution_convert_fusion.1
  292.0 1.7 pad_maximum_fusion
  293.8 15.3 %reduce-scatter.2.cloned.1.call-done = bf16[3584,192]{0,1:T(8,128)(2,1)} async-done(((bf16[7168,192]{0,1:T(8,128)(2,1)}), bf16[3584,192]{0,1:T(8,128)(2,1)}) %reduce-scatter.2.cloned.1.call-update) | async-done | bytes 1376272 | tf_op jit(solution)/shard_map/reduce_scatter | solution.py:83
  309.1 6.4 %fusion.9 = (f32[1,192,3584]{2,1,0:T(8,128)}, f32[1,192,3584]{2,1,0:T(8,128)}) fusion(bf16[3584,192]{0,1:T(8,128)(2,1)} %reduce-scatter.2.cloned.1.call-done, f32[1,192,3584]{2,1,0:T(8,128)} %param.13, f32[1,192,3584]{2,1,0:T(8,128)} %param.12), kind=kLoop, calls=%fused_computation.22 | loop fusion | flops 5505024 | bytes 12386304 | tf_op jit(solution)/shard_map/broadcast_in_dim | solution.py:98
  315.4 77.4 %all-to-all-done.2 = bf16[64,8,7168]{2,1,0:T(8,128)(2,1)} async-done(((bf16[64,8,7168]{2,1,0:T(8,128)(2,1)}), bf16[64,8,7168]{2,1,0:T(8,128)(2,1)}, u32[]{:S(2)}, u32[]{:S(2)}) %all-to-all-start.2) | async-done | bytes 7340064 | tf_op jit(solution)/shard_map/all_to_all | solution.py:75
  392.8 4.4 %convert_reduce_fusion = f32[4,8,7168]{2,1,0:T(8,128)S(1)} fusion(bf16[64,8,7168]{2,1,0:T(8,128)(2,1)} %all-to-all-done.2), kind=kLoop, calls=%fused_computation.6 | loop fusion | flops 7110656 | bytes 8257536 | tf_op jit(solution)/shard_map/reduce_sum | solution.py:90
  397.2 0.1 concatenate.12
  397.3 13.7 %gather_fusion.3 = f32[1024,7168]{1,0:T(8,128)} fusion(f32[33,7168]{1,0:T(8,128)S(1)} %concatenate.12, s32[1024]{0:T(1024)S(1)} %broadcast_clamp_fusion), kind=kCustom, calls=%fused_computation.3 | custom fusion | bytes 58724352 | tf_op jit(solution)/shard_map/gather | solution.py:94
  411.0 14.7 %bitcast_reduce_fusion = bf16[128,7168]{1,0:T(8,128)(2,1)} fusion(f32[1024,7168]{1,0:T(8,128)} %gather_fusion.3), kind=kLoop, calls=%fused_computation.5 | loop fusion | flops 6422528 | bytes 31195136 | tf_op jit(solution)/shard_map/reduce_sum | solution.py:95
  (29 shorter events, 0.2 us)
Async XLA Ops:
  7.2 9.4 %copy-start = (bf16[128,7168]{1,0:T(8,128)(2,1)S(1)}, bf16[128,7168]{1,0:T(8,128)(2,1)}, u32[]{:S(2)}) copy-start(bf16[128,7168]{1,0:T(8,128)(2,1)} %param.7) | copy-start | bytes 5505028
  30.3 10.2 %copy-start.4 = (f32[128,8]{0,1:T(8,128)S(1)}, f32[128,8]{0,1:T(8,128)}, u32[]{:S(2)}) copy-start(f32[128,8]{0,1:T(8,128)} %param.9) | copy-start | bytes 12292
  30.3 118.0 %all-to-all-start.1 = ((bf16[64,8,7168]{2,1,0:T(8,128)(2,1)}), bf16[64,8,7168]{2,1,0:T(8,128)(2,1)}, u32[]{:S(2)}, u32[]{:S(2)}) async-start(bf16[64,8,7168]{2,1,0:T(8,128)(2,1)} %bitcast_select_fusion), calls=%async_computation.1 | async-start | bytes 14680064 | tf_op jit(solution)/shard_map/all_to_all | solution.py:61
  40.4 2.7 copy-start.2
  148.3 116.8 %all-to-all-start = ((bf16[64,8,7168]{2,1,0:T(8,128)(2,1)}), bf16[64,8,7168]{2,1,0:T(8,128)(2,1)}, u32[]{:S(2)}, u32[]{:S(2)}) async-start(bf16[64,8,7168]{2,1,0:T(8,128)(2,1)} %fusion), calls=%async_computation | async-start | bytes 14680064 | tf_op jit(solution)/shard_map/all_to_all | solution.py:62
  155.4 18.9 %all-gather.3.cloned.1.call-start = ((), (), s32[]{:S(2)}) async-start(), calls=%async_computation.5 | async-start | bytes 4128768 | tf_op jit(solution)/shard_map/all_gather | solution.py:64
  265.1 5.8 %copy-start.3 = (bf16[1,192,7168]{2,1,0:T(8,128)(2,1)S(1)}, bf16[1,192,7168]{2,1,0:T(8,128)(2,1)}, u32[]{:S(2)}) copy-start(bf16[1,192,7168]{2,1,0:T(8,128)(2,1)} %all-gather.3.cloned.1.call-done) | copy-start | bytes 8257540
  276.0 116.9 %all-to-all-start.2 = ((bf16[64,8,7168]{2,1,0:T(8,128)(2,1)}), bf16[64,8,7168]{2,1,0:T(8,128)(2,1)}, u32[]{:S(2)}, u32[]{:S(2)}) async-start(bf16[64,8,7168]{2,1,0:T(8,128)(2,1)} %fusion.1), calls=%async_computation.2 | async-start | bytes 14680064 | tf_op jit(solution)/shard_map/all_to_all | solution.py:75
  283.1 26.0 %reduce-scatter.2.cloned.1.call-start = ((), (), s32[]{:S(2)}) async-start(), calls=%async_computation.4 | async-start | bytes 4128768 | tf_op jit(solution)/shard_map/reduce_scatter | solution.py:83
  411.0 14.7 %copy-start.1 = (bf16[128,7168]{1,0:T(8,128)(2,1)S(1)}, bf16[128,7168]{1,0:T(8,128)(2,1)}, u32[]{:S(2)}) copy-start(bf16[128,7168]{1,0:T(8,128)(2,1)} %param.7) | copy-start | bytes 5505028
Sparse Core Ops, SparseCore 0:
  157.9 16.3 all-gather.2
  293.9 15.1 reduce-scatter.1
where the time goes:
time: 433 us
  waiting for transfers between devices  286 us (66%)
  other arithmetic  45.3 us (10%)
  local copies, waits for them, and re-layouts  36.8 us (8%)
  matrix products  25.7 us (6%)
  starting transfers between devices  24.7 us (6%)
  between operations  14.3 us (3%)
    all_to_all x1, waiting for transfers between devices, shards(): lax.all_to_all(sent_inputs, 'expert', split_axis=0, concat_axis=0, tiled=...  89.7 us
    all_to_all x1, waiting for transfers between devices, shards(): lax.all_to_all(sent_grads, 'expert', split_axis=0, concat_axis=0, tiled=T...  84.7 us
    all_to_all x1, waiting for transfers between devices, shards(): lax.all_to_all(back_rows, 'expert', split_axis=0, concat_axis=0, tiled=True)  77.4 us
    all_gather x1, waiting for transfers between devices, shards(): weights = lax.all_gather(expert_weights[0], 'dp', axis=1, tiled=True)  18.1 us
    reduce_scatter x1, waiting for transfers between devices, shards(): lax.psum_scatter(jnp.concatenate([in_terms, out_terms], axis=1).astype(jn...  15.3 us
    reduce_sum x1, other arithmetic, shards(): grad_tokens = jnp.sum(picked, axis=1).astype(jnp.bfloat16)  14.7 us
    gather x1, local copies, waits for them, and re-layouts, shards(): picked = padded[key_of_row].reshape(tok_count, top_count, feature_width)  13.7 us
    all_to_all x1, starting transfers between devices, shards(): lax.all_to_all(sent_inputs, 'expert', split_axis=0, concat_axis=0, tiled=...  10.1 us
  transfers between devices with their start and end apart: 5, of which 5 were waited for; matrix products, arithmetic and copies ran while one was open for 9% of the time, Pallas kernels for 0%

commit v1 on v0

v1 whole, which is shorter than its diff:
```python
import functools

import jax
import jax.numpy as jnp
from jax import lax
from jax.experimental import pallas as pl
from jax.experimental.pallas import tpu as pltpu
from jax.sharding import PartitionSpec as P

N = 4
SLOT = 8
HID = 64
D = 7168
HALF = D // 2
EIGHTH = HALF // N
QUARTER = 2 * EIGHTH
ROWS = N * SLOT
GROUPED = N * ROWS
BF = jnp.bfloat16
F32 = jnp.float32
beta_one = 0.9
beta_two = 0.95


def rotation(axis, step):
    pairs = []
    for x in range(N):
        for z in range(N):
            for y in range(N):
                for c in range(2):
                    to = {"x": x, "z": z, "y": y, "c": c}
                    to[axis] = (to[axis] + step) % (2 if axis == "c" else N)
                    source = ((x * N + z) * N + y) * 2 + c
                    target = ((to["x"] * N + to["z"]) * N + to["y"]) * 2 + to["c"]
                    pairs.append((source, target))
    return pairs


def turn(value, axis, step):
    return lax.ppermute(value, ("expert", "dp"), rotation(axis, step))


def call(kernel, name, outs, place, *ins, flops=0, scratch=()):
    outs = [jax.ShapeDtypeStruct(s, t) for s, t in outs]
    size = sum(v.size * v.dtype.itemsize for v in (*ins, *outs))
    return pl.pallas_call(
        kernel,
        name=name,
        out_shape=outs,
        in_specs=[pl.BlockSpec(memory_space=pltpu.SMEM)]
        + [pl.BlockSpec(memory_space=pltpu.VMEM)] * len(ins),
        out_specs=[pl.BlockSpec(memory_space=pltpu.VMEM)] * len(outs),
        scratch_shapes=list(scratch),
        cost_estimate=pl.CostEstimate(flops=flops, bytes_accessed=size, transcendentals=0),
        compiler_params=pltpu.CompilerParams(vmem_limit_bytes=32 * 1024 * 1024),
    )(place, *ins)


def wrap(v):
    return lax.rem(v + 2 * N, N)


def aligned(v):
    return pl.multiple_of(v, 128)


def mm(a, b, dims):
    return lax.dot_general(a, b, (dims, ((), ())), preferred_element_type=F32)


NN = ((1,), (0,))
NT = ((1,), (1,))
TN = ((0,), (0,))


def route_kernel(place, ids, gates, tokens, o0, o1, o2, o3, pick_out, pick_t_out, gate_out):
    tok = ids.shape[0]
    x = place[0]
    idv = ids[...]
    gv = gates[...]
    lane = lax.broadcasted_iota(jnp.int32, (tok, 128), 1)
    masks = jnp.zeros((tok, 128), F32)
    columns = []
    for k in range(N):
        hit = idv == wrap(x + k)
        member = jnp.sum(hit.astype(F32), axis=1, keepdims=True)
        gate = jnp.sum(jnp.where(hit, gv, 0.0), axis=1, keepdims=True)
        masks = jnp.where(lane == k, member, masks)
        columns.append((member, gate))
    row_i = lax.broadcasted_iota(jnp.int32, (tok, tok), 0)
    col_i = lax.broadcasted_iota(jnp.int32, (tok, tok), 1)
    earlier = (col_i < row_i).astype(BF)
    before = mm(earlier, masks.astype(BF), NN)
    pick = jnp.zeros((tok, 128), F32)
    weighted = jnp.zeros((tok, 128), F32)
    for k in range(N):
        member, gate = columns[k]
        spot = before[:, k : k + 1].astype(jnp.int32) + k * SLOT
        on = (lane == spot) & (member > 0.0)
        pick = jnp.where(on, 1.0, pick)
        weighted = jnp.where(on, gate, weighted)
    pick_t = jnp.transpose(pick)[:ROWS]
    gate_out[...] = jnp.sum(jnp.transpose(weighted)[:ROWS], axis=1, keepdims=True)
    pick_out[...] = pick[:, :ROWS].astype(BF)
    pick_t = pick_t.astype(BF)
    pick_t_out[...] = pick_t
    for q in range(N):
        cols = slice(q * QUARTER, (q + 1) * QUARTER)
        got = mm(pick_t, tokens[:, cols], NN)
        for k, o in enumerate((o0, o1, o2, o3)):
            o[:, cols] = got[k * SLOT : (k + 1) * SLOT].astype(BF)


def grads_kernel(place, pick_t, gate, grad_out, o0, o1, o2, o3):
    for q in range(N):
        cols = slice(q * QUARTER, (q + 1) * QUARTER)
        got = mm(pick_t[...], grad_out[:, cols], NN) * gate[...]
        for k, o in enumerate((o0, o1, o2, o3)):
            o[:, cols] = got[k * SLOT : (k + 1) * SLOT].astype(BF)


def split_kernel(place, i0, i1, i2, i3, o0, o1, o2, o3):
    y = place[2]
    for k, o in enumerate((o0, o1, o2, o3)):
        q = wrap(y + k)
        for c in range(2):
            cols = pl.ds(aligned(c * HALF + q * EIGHTH), EIGHTH)
            rows = jnp.concatenate([r[:, cols].astype(F32) for r in (i0, i1, i2, i3)], axis=0)
            o[:, c * EIGHTH : (c + 1) * EIGHTH] = rows.astype(BF)


def pair_kernel(place, i0, i1, i2, i3, a, b):
    a[:ROWS] = i0[...]
    a[ROWS:] = i1[...]
    b[:ROWS] = i2[...]
    b[ROWS:] = i3[...]


def stack_weights_kernel(place, w0, w1, w2, w3, out):
    y = place[2]
    for k, w in enumerate((w0, w1, w2, w3)):
        block = wrap(y - k)
        for part in range(3):
            rows = pl.ds(pl.multiple_of(part * N * HID + block * HID, HID), HID)
            out[rows, :] = w[part * HID : (part + 1) * HID]


def split_columns_kernel(place, w, o0, o1, o2, o3):
    y = place[2]
    for k, o in enumerate((o0, o1, o2, o3)):
        o[...] = w[0, :, pl.ds(aligned(wrap(y + k) * EIGHTH), EIGHTH)]


def forward_kernel(lo, hi, place, a0, b0, a1, b1, a2, b2, a3, b3, own, other, o0, o1, o2, o3):
    c = place[3]
    mine = pl.ds(aligned(c * EIGHTH), EIGHTH)
    theirs = pl.ds(aligned((1 - c) * EIGHTH), EIGHTH)
    w_own = own[lo:hi]
    w_other = other[lo:hi]
    for n, (a, b) in enumerate(((a0, b0), (a1, b1), (a2, b2), (a3, b3))):
        for h, v in enumerate((a, b)):
            part = mm(v[:, mine], w_own, NT) + mm(v[:, theirs], w_other, NT)
            for s in range(2):
                o = (o0, o1, o2, o3)[2 * h + s]
                o[n * ROWS : (n + 1) * ROWS] = part[s * ROWS : (s + 1) * ROWS].astype(o.dtype)


def middle_kernel(place, p0, p1, p2, p3, d0, d1, d2, d3, out):
    width = N * HID
    pair = p0[...] + p1[...].astype(F32) + p2[...].astype(F32) + p3[...].astype(F32)
    d_hidden = d0[...] + d1[...].astype(F32) + d2[...].astype(F32) + d3[...].astype(F32)
    gate = pair[:, :width]
    up = pair[:, width:]
    sig = jax.nn.sigmoid(gate)
    act = gate * sig
    out[:, :width] = (d_hidden * up * sig * (1.0 + gate * (1.0 - sig))).astype(BF)
    out[:, width : 2 * width] = (d_hidden * act).astype(BF)
    out[:, 2 * width :] = (act * up).astype(BF)


def back_kernel(place, h0, h1, h2, h3, own, other, o0, o1, o2, o3):
    c = place[3]
    width = 2 * N * HID
    for n, o in enumerate((o0, o1, o2, o3)):
        rows = slice(n * ROWS, (n + 1) * ROWS)
        h = jnp.concatenate([r[rows, :width] for r in (h0, h1, h2, h3)], axis=0)
        o[:, pl.ds(aligned(c * EIGHTH), EIGHTH)] = mm(h, own[:width], NN).astype(BF)
        o[:, pl.ds(aligned((1 - c) * EIGHTH), EIGHTH)] = mm(h, other[:width], NN).astype(BF)


def weight_grad_kernel(place, h0, h1, h2, h3, *refs):
    xs, gs, (mine, theirs) = refs[:8], refs[8:16], refs[16:]
    c = place[3]
    width = 2 * N * HID
    hs = jnp.concatenate(
        [r[n * ROWS : (n + 1) * ROWS] for n in range(N) for r in (h0, h1, h2, h3)], axis=0
    )
    for o, half in ((theirs, 1 - c), (mine, c)):
        cols = pl.ds(aligned(half * EIGHTH), EIGHTH)
        x = jnp.concatenate([v[:, cols] for v in xs], axis=0)
        o[:width] = mm(hs[:, :width], x, TN).astype(o.dtype)
        g = jnp.concatenate([v[:, cols] for v in gs], axis=0)
        o[width:] = mm(hs[:, width:], g, TN).astype(o.dtype)


def grad_blocks_kernel(place, mine, got, o0, o1, o2, o3):
    y = place[2]
    for k, o in enumerate((o0, o1, o2, o3)):
        block = wrap(y - k)
        for part in range(3):
            rows = pl.ds(pl.multiple_of(part * N * HID + block * HID, HID), HID)
            total = mine[rows, :] + got[rows, :].astype(F32)
            o[part * HID : (part + 1) * HID] = total.astype(o.dtype)


def sum_back_kernel(place, r0, r1, r2, r3, o0, o1, o2, o3):
    for m, o in enumerate((o0, o1, o2, o3)):
        rows = slice(m * ROWS, (m + 1) * ROWS)
        total = (r0[rows].astype(F32) + r1[rows].astype(F32)) + (
            r2[rows].astype(F32) + r3[rows].astype(F32)
        )
        o[...] = total.astype(BF)


def join_kernel(place, i0, i1, i2, i3, o0, o1, o2, o3):
    y = place[2]
    for m, v in enumerate((i0, i1, i2, i3)):
        q = wrap(y + m)
        for c in range(2):
            cols = pl.ds(aligned(c * HALF + q * EIGHTH), EIGHTH)
            value = v[:, c * EIGHTH : (c + 1) * EIGHTH].astype(F32)
            for p, o in enumerate((o0, o1, o2, o3)):
                o[:, cols] = value[p * SLOT : (p + 1) * SLOT].astype(BF)


def combine_kernel(place, pick, r0, r1, r2, r3, out):
    for q in range(N):
        cols = slice(q * QUARTER, (q + 1) * QUARTER)
        rows = jnp.concatenate([r[:, cols].astype(F32) for r in (r0, r1, r2, r3)], axis=0)
        out[:, cols] = mm(pick[...], rows.astype(BF), NN).astype(BF)


def moments_kernel(place, g0, g1, g2, g3, one, two, new_one, new_two):
    step = pl.program_id(0)
    for k, g in enumerate((g0, g1, g2, g3)):

        @pl.when(step == k)
        def _():
            grad = g[...].astype(F32)
            new_one[0] = beta_one * one[0] + (1.0 - beta_one) * grad
            new_two[0] = beta_two * two[0] + (1.0 - beta_two) * grad * grad


def moments(place, grads, one, two):
    rows = one.shape[1]
    piece = pl.BlockSpec((rows, EIGHTH), lambda k, place: (0, 0))
    block = pl.BlockSpec((1, rows, EIGHTH), lambda k, place: (0, 0, lax.rem(place[2] + k, N)))
    return pl.pallas_call(
        moments_kernel,
        name="moments",
        grid_spec=pltpu.PrefetchScalarGridSpec(
            num_scalar_prefetch=1,
            grid=(N,),
            in_specs=[piece] * N + [block] * 2,
            out_specs=[block] * 2,
        ),
        out_shape=[jax.ShapeDtypeStruct(v.shape, v.dtype) for v in (one, two)],
        cost_estimate=pl.CostEstimate(
            flops=6 * one.size, bytes_accessed=17 * one.size, transcendentals=0
        ),
        compiler_params=pltpu.CompilerParams(vmem_limit_bytes=32 * 1024 * 1024),
    )(place, *grads, one, two)


def spread(parts, axis, sign=1):
    return [parts[0]] + [turn(parts[k], axis, sign * k) for k in range(1, N)]


def ring_gather(place, parts):
    a0, b0 = call(pair_kernel, "pair", [((2 * ROWS, QUARTER), BF)] * 2, place, *parts)
    a1, b1 = turn(a0, "z", 1), turn(b0, "z", 1)
    a3, b3 = turn(a0, "z", -1), turn(b0, "z", -1)
    a2 = turn(a1, "z", 1)
    b2 = turn(b3, "z", -1)
    return [a0, b0, a1, b1, a2, b2, a3, b3]


def shards(tokens, grad_out, gates, expert_ids, expert_weights, moment_one, moment_two):
    expert = lax.axis_index("expert")
    core = lax.axis_index("dp")
    place = jnp.stack([expert // (N * N), expert // N % N, expert % N, core]).astype(jnp.int32)
    tok = tokens.shape[0]
    width = N * HID
    slot_out = [((SLOT, D), BF)] * N
    row_out = [((ROWS, QUARTER), BF)] * N
    block_rows = expert_weights.shape[1]

    *inputs, pick, pick_t, gate = call(
        route_kernel,
        "route",
        slot_out + [((tok, ROWS), BF), ((ROWS, tok), BF), ((ROWS, 1), F32)],
        place,
        expert_ids,
        gates,
        tokens,
        flops=2 * ROWS * tok * D,
    )
    inputs = spread(inputs, "x")
    grads = call(
        grads_kernel, "grads", slot_out, place, pick_t, gate, grad_out, flops=2 * ROWS * tok * D
    )
    grads = spread(grads, "x")
    w_parts = call(
        split_columns_kernel,
        "split_columns",
        [((block_rows, EIGHTH), BF)] * N,
        place,
        expert_weights,
    )
    inputs = spread(call(split_kernel, "split", row_out, place, *inputs), "y")
    grads = spread(call(split_kernel, "split", row_out, place, *grads), "y")
    w_parts = spread(w_parts, "y")
    (w_own,) = call(
        stack_weights_kernel, "stack_weights", [((N * block_rows, EIGHTH), BF)], place, *w_parts
    )
    w_other = turn(w_own, "c", 1)
    inputs = ring_gather(place, inputs)
    grads = ring_gather(place, grads)

    pair = call(
        functools.partial(forward_kernel, 0, 2 * width),
        "pair_part",
        [((GROUPED, 2 * width), F32)] + [((GROUPED, 2 * width), BF)] * 3,
        place,
        *inputs,
        w_own,
        w_other,
        flops=2 * N * GROUPED * QUARTER * 2 * width,
    )
    pair = spread(pair, "y", -1)
    d_hidden = call(
        functools.partial(forward_kernel, 2 * width, 3 * width),
        "d_hidden_part",
        [((GROUPED, width), F32)] + [((GROUPED, width), BF)] * 3,
        place,
        *grads,
        w_own,
        w_other,
        flops=2 * N * GROUPED * QUARTER * width,
    )
    d_hidden = spread(d_hidden, "y", -1)
    (held,) = call(
        middle_kernel, "middle", [((GROUPED, 3 * width), BF)], place, *pair, *d_hidden
    )
    held = [held] + [turn(held, "y", k) for k in range(1, N)]

    back = call(
        back_kernel,
        "back",
        [((GROUPED, QUARTER), BF)] * N,
        place,
        *held,
        w_own,
        w_other,
        flops=2 * N * GROUPED * QUARTER * 2 * width,
    )
    back = spread(back, "z", -1)
    grad_mine, grad_theirs = call(
        weight_grad_kernel,
        "weight_grad",
        [((3 * width, EIGHTH), F32), ((3 * width, EIGHTH), BF)],
        place,
        *held,
        *inputs,
        *grads,
        flops=2 * N * GROUPED * QUARTER * 3 * width,
    )
    grad_got = turn(grad_theirs, "c", 1)
    blocks = call(
        grad_blocks_kernel,
        "grad_blocks",
        [((block_rows, EIGHTH), F32)] + [((block_rows, EIGHTH), BF)] * 3,
        place,
        grad_mine,
        grad_got,
    )
    back = spread(call(sum_back_kernel, "sum_back", row_out, place, *back), "y", -1)
    blocks = spread(blocks, "y", -1)
    back = spread(call(join_kernel, "join", slot_out, place, *back), "x", -1)
    new_one, new_two = moments(place, blocks, moment_one, moment_two)
    (grad_tokens,) = call(
        combine_kernel,
        "combine",
        [((tok, D), BF)],
        place,
        pick,
        *back,
        flops=2 * ROWS * tok * D,
    )
    return grad_tokens, new_one, new_two


def solution(mesh):
    return jax.shard_map(
        shards,
        mesh=mesh,
        in_specs=(
            P(("expert", "dp"), None),
            P(("expert", "dp"), None),
            P(("expert", "dp"), None),
            P(("expert", "dp"), None),
            P("expert", None, "dp"),
            P("expert", None, "dp"),
            P("expert", None, "dp"),
        ),
        out_specs=(P(("expert", "dp"), None), P("expert", None, "dp"), P("expert", None, "dp")),
        check_vma=False,
    )
```

time: 433 us -> 177 us (0.41)
  the two profiles are of different devices: /device:TPU:103 before, /device:TPU:0 now
where the time goes in v1:
time: 177 us
  waiting for transfers between devices  72.6 us (41%)
  starting transfers between devices  72.4 us (41%)
  Pallas kernels  27.4 us (15%)
  local copies, waits for them, and re-layouts  3.06 us (2%)
    ppermute x50, waiting for transfers between devices, turn(): return lax.ppermute(value, ('expert', 'dp'), rotation(axis, step))  72.6 us
    ppermute x50, starting transfers between devices, turn(): return lax.ppermute(value, ('expert', 'dp'), rotation(axis, step))  72.4 us
    pallas_call x17, Pallas kernels, call(): pl.pallas_call(kernel, name=name, out_shape=outs, in_specs=[pl.BlockSpec(...  23.4 us
    pallas_call x1, Pallas kernels, moments(): pl.pallas_call(moments_kernel, name='moments', grid_spec=pltpu.PrefetchSc...  4.01 us
  transfers between devices with their start and end apart: 50, of which 21 were waited for; matrix products, arithmetic and copies ran while one was open for 0% of the time, Pallas kernels for 11%

profile of v1, /device:TPU:0, one launch (start us, length us, event | category | flops | bytes accessed | tf_op | source)
XLA Modules:
  0.0 176.5 jit_solution(18116913035411626629)
XLA Ops:
  0.8 1.3 copy-done.4
  2.8 1.7 collective-permute-start.12
  4.5 2.9 %collective-permute-start.13 = (bf16[192,896]{1,0:T(8,128)(2,1)S(1)}, bf16[192,896]{1,0:T(8,128)(2,1)S(1)}, u32[]{:S(2)}, u32[]{:S(2)}) collective-permute-start(bf16[192,896]{1,0:T(8,128)(2,1)S(1)} %get-tuple-element.71), channel_id=1, source_target_pairs={{0,4},{1,5},{2,6},{3,7},{4,0},{5,1},{6,2},{7,3},{8,12},{9,13},{10,... | collective-permute-start | bytes 1032200 | tf_op jit(solution)/shard_map/ppermute | solution.py:40
  7.4 1.3 collective-permute-start.14
  8.7 5.2 %collective-permute-done.12.w1 = bf16[192,896]{1,0:T(8,128)(2,1)S(1)} collective-permute-done((bf16[192,896]{1,0:T(8,128)(2,1)S(1)}, bf16[192,896]{1,0:T(8,128)(2,1)S(1)}, u32[]{:S(2)}, u32[]{:S(2)}) %collective-permute-start.12) | collective-permute-done | bytes 344096 | tf_op jit(solution)/shard_map/ppermute | solution.py:40
  14.0 8.5 %collective-permute-done.13.w2 = bf16[192,896]{1,0:T(8,128)(2,1)S(1)} collective-permute-done((bf16[192,896]{1,0:T(8,128)(2,1)S(1)}, bf16[192,896]{1,0:T(8,128)(2,1)S(1)}, u32[]{:S(2)}, u32[]{:S(2)}) %collective-permute-start.13) | collective-permute-done | bytes 344096 | tf_op jit(solution)/shard_map/ppermute | solution.py:40
  23.5 1.5 copy-done.2
  25.0 1.4 route.1
  26.4 1.6 collective-permute-start
  28.0 2.7 %collective-permute-start.1 = (bf16[8,7168]{1,0:T(8,128)(2,1)S(1)}, bf16[8,7168]{1,0:T(8,128)(2,1)S(1)}, u32[]{:S(2)}, u32[]{:S(2)}) collective-permute-start(bf16[8,7168]{1,0:T(8,128)(2,1)S(1)} %get-tuple-element.61), channel_id=1, source_target_pairs={{0,64},{1,65},{2,66},{3,67},{4,68},{5,69},{6,70},{7,71},{8,72},{9,... | collective-permute-start | bytes 344072 | tf_op jit(solution)/shard_map/ppermute | solution.py:40
  30.7 1.4 collective-permute-start.2
  33.7 1.3 collective-permute-start.20
  35.1 2.0 %collective-permute-done.1.i2 = bf16[8,7168]{1,0:T(8,128)(2,1)S(1)} collective-permute-done((bf16[8,7168]{1,0:T(8,128)(2,1)S(1)}, bf16[8,7168]{1,0:T(8,128)(2,1)S(1)}, u32[]{:S(2)}, u32[]{:S(2)}) %collective-permute-start.1) | collective-permute-done | bytes 114720 | tf_op jit(solution)/shard_map/ppermute | solution.py:40
  37.7 1.3 collective-permute-start.3
  39.0 2.8 %collective-permute-done.19.i1 = bf16[8,7168]{1,0:T(8,128)(2,1)S(1)} collective-permute-done((bf16[8,7168]{1,0:T(8,128)(2,1)S(1)}, bf16[8,7168]{1,0:T(8,128)(2,1)S(1)}, u32[]{:S(2)}, u32[]{:S(2)}) %collective-permute-start.19) | collective-permute-done | bytes 114720 | tf_op jit(solution)/shard_map/ppermute | solution.py:40
  41.7 2.6 %collective-permute-start.4 = (bf16[32,1792]{1,0:T(8,128)(2,1)S(1)}, bf16[32,1792]{1,0:T(8,128)(2,1)S(1)}, u32[]{:S(2)}, u32[]{:S(2)}) collective-permute-start(bf16[32,1792]{1,0:T(8,128)(2,1)S(1)} %get-tuple-element.65), channel_id=1, source_target_pairs={{0,4},{1,5},{2,6},{3,7},{4,0},{5,1},{6,2},{7,3},{8,12},{9,13},{10,... | collective-permute-start | bytes 344072 | tf_op jit(solution)/shard_map/ppermute | solution.py:40
  44.3 1.3 collective-permute-start.5
  50.8 2.0 %collective-permute-start.6 = (bf16[64,1792]{1,0:T(8,128)(2,1)S(1)}, bf16[64,1792]{1,0:T(8,128)(2,1)S(1)}, u32[]{:S(2)}, u32[]{:S(2)}) collective-permute-start(bf16[64,1792]{1,0:T(8,128)(2,1)S(1)} %get-tuple-element.67.a0.refs_0_), channel_id=1, source_target_pairs={{0,8},{1,9},{2,10},{3,11},{4,12},{5,13},{6,14},{7,15},{8,16},{9,17... | collective-permute-start | bytes 688136 | tf_op jit(solution)/shard_map/ppermute | solution.py:40
  53.7 4.0 %collective-permute-start.9 = (bf16[64,1792]{1,0:T(8,128)(2,1)S(1)}, bf16[64,1792]{1,0:T(8,128)(2,1)S(1)}, u32[]{:S(2)}, u32[]{:S(2)}) collective-permute-start(bf16[64,1792]{1,0:T(8,128)(2,1)S(1)} %get-tuple-element.68.b0.refs_1_), channel_id=1, source_target_pairs={{0,24},{1,25},{2,26},{3,27},{4,28},{5,29},{6,30},{7,31},{8,0},{9,1... | collective-permute-start | bytes 688136 | tf_op jit(solution)/shard_map/ppermute | solution.py:40
  58.4 3.2 %collective-permute-start.28 = (bf16[64,1792]{1,0:T(8,128)(2,1)S(1)}, bf16[64,1792]{1,0:T(8,128)(2,1)S(1)}, u32[]{:S(2)}, u32[]{:S(2)}) collective-permute-start(bf16[64,1792]{1,0:T(8,128)(2,1)S(1)} %get-tuple-element.88.b0.refs_9_), channel_id=1, source_target_pairs={{0,24},{1,25},{2,26},{3,27},{4,28},{5,29},{6,30},{7,31},{8,0},{9,1... | collective-permute-start | bytes 688136 | tf_op jit(solution)/shard_map/ppermute | solution.py:40
  61.6 2.1 %collective-permute-done.9.b3.refs_7_ = bf16[64,1792]{1,0:T(8,128)(2,1)S(1)} collective-permute-done((bf16[64,1792]{1,0:T(8,128)(2,1)S(1)}, bf16[64,1792]{1,0:T(8,128)(2,1)S(1)}, u32[]{:S(2)}, u32[]{:S(2)}) %collective-permute-start.9) | collective-permute-done | bytes 229408 | tf_op jit(solution)/shard_map/ppermute | solution.py:40
  63.8 3.7 %collective-permute-start.30 = (bf16[64,1792]{1,0:T(8,128)(2,1)S(1)}, bf16[64,1792]{1,0:T(8,128)(2,1)S(1)}, u32[]{:S(2)}, u32[]{:S(2)}) collective-permute-start(bf16[64,1792]{1,0:T(8,128)(2,1)S(1)} %get-tuple-element.87.a0.refs_8_), channel_id=1, source_target_pairs={{0,24},{1,25},{2,26},{3,27},{4,28},{5,29},{6,30},{7,31},{8,0},{9,1... | collective-permute-start | bytes 688136 | tf_op jit(solution)/shard_map/ppermute | solution.py:40
  68.7 3.7 %collective-permute-start.29 = (bf16[64,1792]{1,0:T(8,128)(2,1)S(1)}, bf16[64,1792]{1,0:T(8,128)(2,1)S(1)}, u32[]{:S(2)}, u32[]{:S(2)}) collective-permute-start(bf16[64,1792]{1,0:T(8,128)(2,1)S(1)} %collective-permute-done.28.b3.refs_15_), channel_id=1, source_target_pairs={{0,24},{1,25},{2,26},{3,27},{4,28},{5,29},{6,30},{7,31},{8,0},{9,1... | collective-permute-start | bytes 688136 | tf_op jit(solution)/shard_map/ppermute | solution.py:40
  73.6 3.7 %collective-permute-start.11 = (bf16[64,1792]{1,0:T(8,128)(2,1)S(1)}, bf16[64,1792]{1,0:T(8,128)(2,1)S(1)}, u32[]{:S(2)}, u32[]{:S(2)}) collective-permute-start(bf16[64,1792]{1,0:T(8,128)(2,1)S(1)} %get-tuple-element.67.a0.refs_0_), channel_id=1, source_target_pairs={{0,24},{1,25},{2,26},{3,27},{4,28},{5,29},{6,30},{7,31},{8,0},{9,1... | collective-permute-start | bytes 688136 | tf_op jit(solution)/shard_map/ppermute | solution.py:40
  78.5 3.7 %collective-permute-start.10 = (bf16[64,1792]{1,0:T(8,128)(2,1)S(1)}, bf16[64,1792]{1,0:T(8,128)(2,1)S(1)}, u32[]{:S(2)}, u32[]{:S(2)}) collective-permute-start(bf16[64,1792]{1,0:T(8,128)(2,1)S(1)} %collective-permute-done.9.b3.refs_7_), channel_id=1, source_target_pairs={{0,24},{1,25},{2,26},{3,27},{4,28},{5,29},{6,30},{7,31},{8,0},{9,1... | collective-permute-start | bytes 688136 | tf_op jit(solution)/shard_map/ppermute | solution.py:40
  82.2 2.9 %d_hidden_part.1 = (f32[128,256]{1,0:T(8,128)S(1)}, bf16[128,256]{1,0:T(8,128)(2,1)S(1)}, bf16[128,256]{1,0:T(8,128)(2,1)S(1)}, bf16[128,256]{1,0:T(8,128)(2,1)S(1)}) custom-call(s32[4]{0:T(128)S(1)} %pad_add_fusion.place, bf16[64,1792]{1,0:T(8,128)(2,1)S(1)} %get-tuple-element.87.a0.refs_8_, bf16[64,1792]{1,0:T(8,128)(2,1)S(1)} %get-tuple-element.88.b0.refs_9_, ...), custom_call_target="tpu_custom_call" | custom-call | flops 469762048 | bytes 4915200 | tf_op jit(solution)/shard_map/d_hidden_part/pallas_call | solution.py:46
  85.9 5.1 %pair_part.1 = (f32[128,512]{1,0:T(8,128)S(1)}, bf16[128,512]{1,0:T(8,128)(2,1)S(1)}, bf16[128,512]{1,0:T(8,128)(2,1)S(1)}, bf16[128,512]{1,0:T(8,128)(2,1)S(1)}) custom-call(s32[4]{0:T(128)S(1)} %pad_add_fusion.place, bf16[64,1792]{1,0:T(8,128)(2,1)S(1)} %get-tuple-element.67.a0.refs_0_, bf16[64,1792]{1,0:T(8,128)(2,1)S(1)} %get-tuple-element.68.b0.refs_1_, ...), custom_call_target="tpu_custom_call" | custom-call | flops 939524096 | bytes 5242880 | tf_op jit(solution)/shard_map/pair_part/pallas_call | solution.py:46
  91.9 2.6 %collective-permute-start.17 = (bf16[128,512]{1,0:T(8,128)(2,1)S(1)}, bf16[128,512]{1,0:T(8,128)(2,1)S(1)}, u32[]{:S(2)}, u32[]{:S(2)}) collective-permute-start(bf16[128,512]{1,0:T(8,128)(2,1)S(1)} %get-tuple-element.75), channel_id=1, source_target_pairs={{0,4},{1,5},{2,6},{3,7},{4,0},{5,1},{6,2},{7,3},{8,12},{9,13},{10,... | collective-permute-start | bytes 393224 | tf_op jit(solution)/shard_map/ppermute | solution.py:40
  94.5 2.7 %collective-permute-start.32 = (bf16[128,256]{1,0:T(8,128)(2,1)S(1)}, bf16[128,256]{1,0:T(8,128)(2,1)S(1)}, u32[]{:S(2)}, u32[]{:S(2)}) collective-permute-start(bf16[128,256]{1,0:T(8,128)(2,1)S(1)} %get-tuple-element.91), channel_id=1, source_target_pairs={{0,4},{1,5},{2,6},{3,7},{4,0},{5,1},{6,2},{7,3},{8,12},{9,13},{10,... | collective-permute-start | bytes 196616 | tf_op jit(solution)/shard_map/ppermute | solution.py:40
  97.2 1.4 collective-permute-start.33
  98.6 2.4 %collective-permute-done.32.d2 = bf16[128,256]{1,0:T(8,128)(2,1)S(1)} collective-permute-done((bf16[128,256]{1,0:T(8,128)(2,1)S(1)}, bf16[128,256]{1,0:T(8,128)(2,1)S(1)}, u32[]{:S(2)}, u32[]{:S(2)}) %collective-permute-start.32) | collective-permute-done | bytes 65568 | tf_op jit(solution)/shard_map/ppermute | solution.py:40
  101.0 2.4 %collective-permute-done.33.d3 = bf16[128,256]{1,0:T(8,128)(2,1)S(1)} collective-permute-done((bf16[128,256]{1,0:T(8,128)(2,1)S(1)}, bf16[128,256]{1,0:T(8,128)(2,1)S(1)}, u32[]{:S(2)}, u32[]{:S(2)}) %collective-permute-start.33) | collective-permute-done | bytes 65568 | tf_op jit(solution)/shard_map/ppermute | solution.py:40
  105.7 1.9 %collective-permute-start.36 = (bf16[128,768]{1,0:T(8,128)(2,1)S(1)}, bf16[128,768]{1,0:T(8,128)(2,1)S(1)}, u32[]{:S(2)}, u32[]{:S(2)}) collective-permute-start(bf16[128,768]{1,0:T(8,128)(2,1)S(1)} %middle.1.h0), channel_id=1, source_target_pairs={{0,6},{1,7},{2,0},{3,1},{4,2},{5,3},{6,4},{7,5},{8,14},{9,15},{10,... | collective-permute-start | bytes 589832 | tf_op jit(solution)/shard_map/ppermute | solution.py:40
  107.6 5.5 %collective-permute-done.34.h1 = bf16[128,768]{1,0:T(8,128)(2,1)S(1)} collective-permute-done((bf16[128,768]{1,0:T(8,128)(2,1)S(1)}, bf16[128,768]{1,0:T(8,128)(2,1)S(1)}, u32[]{:S(2)}, u32[]{:S(2)}) %collective-permute-start.34) | collective-permute-done | bytes 196640 | tf_op jit(solution)/shard_map/ppermute | solution.py:40
  114.0 2.4 %weight_grad.1 = (f32[768,896]{1,0:T(8,128)S(1)}, bf16[768,896]{1,0:T(8,128)(2,1)S(1)}) custom-call(s32[4]{0:T(128)S(1)} %pad_add_fusion.place, bf16[128,768]{1,0:T(8,128)(2,1)S(1)} %middle.1.h0, bf16[128,768]{1,0:T(8,128)(2,1)S(1)} %collective-permute-done.34.h1, bf16[128,768]{1,0:T(8,128)(2,1)S(1)} %collective-permute-done.35.h2, ...), custom_call_target="tpu_custom_call" | custom-call | flops 1409286144 | bytes 8585216 | tf_op jit(solution)/shard_map/weight_grad/pallas_call | solution.py:46
  116.5 1.9 %back.1 = (bf16[128,1792]{1,0:T(8,128)(2,1)S(1)}, bf16[128,1792]{1,0:T(8,128)(2,1)S(1)}, bf16[128,1792]{1,0:T(8,128)(2,1)S(1)}, bf16[128,1792]{1,0:T(8,128)(2,1)S(1)}) custom-call(s32[4]{0:T(128)S(1)} %pad_add_fusion.place, bf16[128,768]{1,0:T(8,128)(2,1)S(1)} %middle.1.h0, bf16[128,768]{1,0:T(8,128)(2,1)S(1)} %collective-permute-done.34.h1, ...), custom_call_target="tpu_custom_call" | custom-call | flops 939524096 | bytes 5373952 | tf_op jit(solution)/shard_map/back/pallas_call | solution.py:46
  118.4 3.7 %collective-permute-start.37 = (bf16[128,1792]{1,0:T(8,128)(2,1)S(1)}, bf16[128,1792]{1,0:T(8,128)(2,1)S(1)}, u32[]{:S(2)}, u32[]{:S(2)}) collective-permute-start(bf16[128,1792]{1,0:T(8,128)(2,1)S(1)} %get-tuple-element.94), channel_id=1, source_target_pairs={{0,24},{1,25},{2,26},{3,27},{4,28},{5,29},{6,30},{7,31},{8,0},{9,1... | collective-permute-start | bytes 1376264 | tf_op jit(solution)/shard_map/ppermute | solution.py:40
  123.1 19.3 %collective-permute-done.37.r1 = bf16[128,1792]{1,0:T(8,128)(2,1)S(1)} collective-permute-done((bf16[128,1792]{1,0:T(8,128)(2,1)S(1)}, bf16[128,1792]{1,0:T(8,128)(2,1)S(1)}, u32[]{:S(2)}, u32[]{:S(2)}) %collective-permute-start.37) | collective-permute-done | bytes 458784 | tf_op jit(solution)/shard_map/ppermute | solution.py:40
  142.4 3.4 %collective-permute-done.39.r3 = bf16[128,1792]{1,0:T(8,128)(2,1)S(1)} collective-permute-done((bf16[128,1792]{1,0:T(8,128)(2,1)S(1)}, bf16[128,1792]{1,0:T(8,128)(2,1)S(1)}, u32[]{:S(2)}, u32[]{:S(2)}) %collective-permute-start.39) | collective-permute-done | bytes 458784 | tf_op jit(solution)/shard_map/ppermute | solution.py:40
  146.6 2.4 %collective-permute-start.40 = (bf16[32,1792]{1,0:T(8,128)(2,1)S(1)}, bf16[32,1792]{1,0:T(8,128)(2,1)S(1)}, u32[]{:S(2)}, u32[]{:S(2)}) collective-permute-start(bf16[32,1792]{1,0:T(8,128)(2,1)S(1)} %get-tuple-element.98), channel_id=1, source_target_pairs={{0,6},{1,7},{2,0},{3,1},{4,2},{5,3},{6,4},{7,5},{8,14},{9,15},{10,... | collective-permute-start | bytes 344072 | tf_op jit(solution)/shard_map/ppermute | solution.py:40
  150.7 2.6 %collective-permute-start.47 = (bf16[192,896]{1,0:T(8,128)(2,1)S(1)}, bf16[192,896]{1,0:T(8,128)(2,1)S(1)}, u32[]{:S(2)}, u32[]{:S(2)}) collective-permute-start(bf16[192,896]{1,0:T(8,128)(2,1)S(1)} %get-tuple-element.108), channel_id=1, source_target_pairs={{0,6},{1,7},{2,0},{3,1},{4,2},{5,3},{6,4},{7,5},{8,14},{9,15},{10,... | collective-permute-start | bytes 1032200 | tf_op jit(solution)/shard_map/ppermute | solution.py:40
  153.3 2.3 %collective-permute-start.48 = (bf16[192,896]{1,0:T(8,128)(2,1)S(1)}, bf16[192,896]{1,0:T(8,128)(2,1)S(1)}, u32[]{:S(2)}, u32[]{:S(2)}) collective-permute-start(bf16[192,896]{1,0:T(8,128)(2,1)S(1)} %get-tuple-element.109), channel_id=1, source_target_pairs={{0,4},{1,5},{2,6},{3,7},{4,0},{5,1},{6,2},{7,3},{8,12},{9,13},{10,... | collective-permute-start | bytes 1032200 | tf_op jit(solution)/shard_map/ppermute | solution.py:40
  156.3 1.7 collective-permute-done.42.i3
  158.7 1.6 collective-permute-start.44
  160.3 3.8 %collective-permute-done.43.r1 = bf16[8,7168]{1,0:T(8,128)(2,1)S(1)} collective-permute-done((bf16[8,7168]{1,0:T(8,128)(2,1)S(1)}, bf16[8,7168]{1,0:T(8,128)(2,1)S(1)}, u32[]{:S(2)}, u32[]{:S(2)}) %collective-permute-start.43) | collective-permute-done | bytes 114720 | tf_op jit(solution)/shard_map/ppermute | solution.py:40
  165.0 5.1 %collective-permute-done.45.r3 = bf16[8,7168]{1,0:T(8,128)(2,1)S(1)} collective-permute-done((bf16[8,7168]{1,0:T(8,128)(2,1)S(1)}, bf16[8,7168]{1,0:T(8,128)(2,1)S(1)}, u32[]{:S(2)}, u32[]{:S(2)}) %collective-permute-start.45) | collective-permute-done | bytes 114720 | tf_op jit(solution)/shard_map/ppermute | solution.py:40
  170.1 2.4 %combine.1 = bf16[128,7168]{1,0:T(8,128)(2,1)} custom-call(s32[4]{0:T(128)S(1)} %pad_add_fusion.place, bf16[128,32]{1,0:T(8,128)(2,1)S(1)} %get-tuple-element.58.pick, bf16[8,7168]{1,0:T(8,128)(2,1)S(1)} %get-tuple-element.101.r0, bf16[8,7168]{1,0:T(8,128)(2,1)S(1)} %collective-permute-done.43.r1, bf16[8,7168]{1,0:T(8,128)(2,1)S(1)} %collective-permute-done.44.r2, ...), custom_call_target="tpu_custom_call" | custom-call | flops 58720256 | bytes 2301952 | tf_op jit(solution)/shard_map/combine/pallas_call | solution.py:46
  172.5 4.0 %moments.1 = (f32[1,192,3584]{2,1,0:T(8,128)}, f32[1,192,3584]{2,1,0:T(8,128)}) custom-call(s32[4]{0:T(128)S(1)} %pad_add_fusion.place, f32[192,896]{1,0:T(8,128)S(1)} %get-tuple-element.107.g0, bf16[192,896]{1,0:T(8,128)(2,1)S(1)} %collective-permute-done.47.g1, bf16[192,896]{1,0:T(8,128)(2,1)S(1)} %collective-permute-done.48.g2, ...), custom_call_target="tpu_custom_call" | custom-call | flops 4128768 | bytes 11698176 | tf_op jit(solution)/shard_map/moments/pallas_call | solution.py:258
  (87 shorter events, 25.0 us)
Async XLA Ops:
  2.8 11.2 %collective-permute-start.12 = (bf16[192,896]{1,0:T(8,128)(2,1)S(1)}, bf16[192,896]{1,0:T(8,128)(2,1)S(1)}, u32[]{:S(2)}, u32[]{:S(2)}) collective-permute-start(bf16[192,896]{1,0:T(8,128)(2,1)S(1)} %get-tuple-element.70), channel_id=1, source_target_pairs={{0,2},{1,3},{2,4},{3,5},{4,6},{5,7},{6,0},{7,1},{8,10},{9,11},{10,... | collective-permute-start | bytes 1032200 | tf_op jit(solution)/shard_map/ppermute | solution.py:40
  4.5 18.0 %collective-permute-start.13 = (bf16[192,896]{1,0:T(8,128)(2,1)S(1)}, bf16[192,896]{1,0:T(8,128)(2,1)S(1)}, u32[]{:S(2)}, u32[]{:S(2)}) collective-permute-start(bf16[192,896]{1,0:T(8,128)(2,1)S(1)} %get-tuple-element.71), channel_id=1, source_target_pairs={{0,4},{1,5},{2,6},{3,7},{4,0},{5,1},{6,2},{7,3},{8,12},{9,13},{10,... | collective-permute-start | bytes 1032200 | tf_op jit(solution)/shard_map/ppermute | solution.py:40
  7.4 15.2 %collective-permute-start.14 = (bf16[192,896]{1,0:T(8,128)(2,1)S(1)}, bf16[192,896]{1,0:T(8,128)(2,1)S(1)}, u32[]{:S(2)}, u32[]{:S(2)}) collective-permute-start(bf16[192,896]{1,0:T(8,128)(2,1)S(1)} %get-tuple-element.72), channel_id=1, source_target_pairs={{0,6},{1,7},{2,0},{3,1},{4,2},{5,3},{6,4},{7,5},{8,14},{9,15},{10,... | collective-permute-start | bytes 1032200 | tf_op jit(solution)/shard_map/ppermute | solution.py:40
  23.2 59.0 %collective-permute-start.15 = (bf16[768,896]{1,0:T(8,128)(2,1)S(1)}, bf16[768,896]{1,0:T(8,128)(2,1)S(1)}, u32[]{:S(2)}, u32[]{:S(2)}) collective-permute-start(bf16[768,896]{1,0:T(8,128)(2,1)S(1)} %stack_weights.1.own), channel_id=1, source_target_pairs={{0,1},{1,0},{2,3},{3,2},{4,5},{5,4},{6,7},{7,6},{8,9},{9,8},{10,11... | collective-permute-start | bytes 4128776 | tf_op jit(solution)/shard_map/ppermute | solution.py:40
  26.4 7.3 %collective-permute-start = (bf16[8,7168]{1,0:T(8,128)(2,1)S(1)}, bf16[8,7168]{1,0:T(8,128)(2,1)S(1)}, u32[]{:S(2)}, u32[]{:S(2)}) collective-permute-start(bf16[8,7168]{1,0:T(8,128)(2,1)S(1)} %get-tuple-element.60), channel_id=1, source_target_pairs={{0,32},{1,33},{2,34},{3,35},{4,36},{5,37},{6,38},{7,39},{8,40},{9,... | collective-permute-start | bytes 344072 | tf_op jit(solution)/shard_map/ppermute | solution.py:40
  28.0 9.1 %collective-permute-start.1 = (bf16[8,7168]{1,0:T(8,128)(2,1)S(1)}, bf16[8,7168]{1,0:T(8,128)(2,1)S(1)}, u32[]{:S(2)}, u32[]{:S(2)}) collective-permute-start(bf16[8,7168]{1,0:T(8,128)(2,1)S(1)} %get-tuple-element.61), channel_id=1, source_target_pairs={{0,64},{1,65},{2,66},{3,67},{4,68},{5,69},{6,70},{7,71},{8,72},{9,... | collective-permute-start | bytes 344072 | tf_op jit(solution)/shard_map/ppermute | solution.py:40
  30.7 6.4 %collective-permute-start.2 = (bf16[8,7168]{1,0:T(8,128)(2,1)S(1)}, bf16[8,7168]{1,0:T(8,128)(2,1)S(1)}, u32[]{:S(2)}, u32[]{:S(2)}) collective-permute-start(bf16[8,7168]{1,0:T(8,128)(2,1)S(1)} %get-tuple-element.62), channel_id=1, source_target_pairs={{0,96},{1,97},{2,98},{3,99},{4,100},{5,101},{6,102},{7,103},{8,104... | collective-permute-start | bytes 344072 | tf_op jit(solution)/shard_map/ppermute | solution.py:40
  33.1 8.7 %collective-permute-start.19 = (bf16[8,7168]{1,0:T(8,128)(2,1)S(1)}, bf16[8,7168]{1,0:T(8,128)(2,1)S(1)}, u32[]{:S(2)}, u32[]{:S(2)}) collective-permute-start(bf16[8,7168]{1,0:T(8,128)(2,1)S(1)} %get-tuple-element.80), channel_id=1, source_target_pairs={{0,32},{1,33},{2,34},{3,35},{4,36},{5,37},{6,38},{7,39},{8,40},{9,... | collective-permute-start | bytes 344072 | tf_op jit(solution)/shard_map/ppermute | solution.py:40
  33.7 10.6 %collective-permute-start.20 = (bf16[8,7168]{1,0:T(8,128)(2,1)S(1)}, bf16[8,7168]{1,0:T(8,128)(2,1)S(1)}, u32[]{:S(2)}, u32[]{:S(2)}) collective-permute-start(bf16[8,7168]{1,0:T(8,128)(2,1)S(1)} %get-tuple-element.81), channel_id=1, source_target_pairs={{0,64},{1,65},{2,66},{3,67},{4,68},{5,69},{6,70},{7,71},{8,72},{9,... | collective-permute-start | bytes 344072 | tf_op jit(solution)/shard_map/ppermute | solution.py:40
  37.1 8.6 %collective-permute-start.21 = (bf16[8,7168]{1,0:T(8,128)(2,1)S(1)}, bf16[8,7168]{1,0:T(8,128)(2,1)S(1)}, u32[]{:S(2)}, u32[]{:S(2)}) collective-permute-start(bf16[8,7168]{1,0:T(8,128)(2,1)S(1)} %get-tuple-element.82), channel_id=1, source_target_pairs={{0,96},{1,97},{2,98},{3,99},{4,100},{5,101},{6,102},{7,103},{8,104... | collective-permute-start | bytes 344072 | tf_op jit(solution)/shard_map/ppermute | solution.py:40
  37.7 9.3 %collective-permute-start.3 = (bf16[32,1792]{1,0:T(8,128)(2,1)S(1)}, bf16[32,1792]{1,0:T(8,128)(2,1)S(1)}, u32[]{:S(2)}, u32[]{:S(2)}) collective-permute-start(bf16[32,1792]{1,0:T(8,128)(2,1)S(1)} %get-tuple-element.64), channel_id=1, source_target_pairs={{0,2},{1,3},{2,4},{3,5},{4,6},{5,7},{6,0},{7,1},{8,10},{9,11},{10,... | collective-permute-start | bytes 344072 | tf_op jit(solution)/shard_map/ppermute | solution.py:40
  41.7 7.4 %collective-permute-start.4 = (bf16[32,1792]{1,0:T(8,128)(2,1)S(1)}, bf16[32,1792]{1,0:T(8,128)(2,1)S(1)}, u32[]{:S(2)}, u32[]{:S(2)}) collective-permute-start(bf16[32,1792]{1,0:T(8,128)(2,1)S(1)} %get-tuple-element.65), channel_id=1, source_target_pairs={{0,4},{1,5},{2,6},{3,7},{4,0},{5,1},{6,2},{7,3},{8,12},{9,13},{10,... | collective-permute-start | bytes 344072 | tf_op jit(solution)/shard_map/ppermute | solution.py:40
  46.2 7.5 %collective-permute-start.22 = (bf16[32,1792]{1,0:T(8,128)(2,1)S(1)}, bf16[32,1792]{1,0:T(8,128)(2,1)S(1)}, u32[]{:S(2)}, u32[]{:S(2)}) collective-permute-start(bf16[32,1792]{1,0:T(8,128)(2,1)S(1)} %get-tuple-element.84), channel_id=1, source_target_pairs={{0,2},{1,3},{2,4},{3,5},{4,6},{5,7},{6,0},{7,1},{8,10},{9,11},{10,... | collective-permute-start | bytes 344072 | tf_op jit(solution)/shard_map/ppermute | solution.py:40
  47.0 10.7 %collective-permute-start.23 = (bf16[32,1792]{1,0:T(8,128)(2,1)S(1)}, bf16[32,1792]{1,0:T(8,128)(2,1)S(1)}, u32[]{:S(2)}, u32[]{:S(2)}) collective-permute-start(bf16[32,1792]{1,0:T(8,128)(2,1)S(1)} %get-tuple-element.85), channel_id=1, source_target_pairs={{0,4},{1,5},{2,6},{3,7},{4,0},{5,1},{6,2},{7,3},{8,12},{9,13},{10,... | collective-permute-start | bytes 344072 | tf_op jit(solution)/shard_map/ppermute | solution.py:40
  49.2 8.6 %collective-permute-start.24 = (bf16[32,1792]{1,0:T(8,128)(2,1)S(1)}, bf16[32,1792]{1,0:T(8,128)(2,1)S(1)}, u32[]{:S(2)}, u32[]{:S(2)}) collective-permute-start(bf16[32,1792]{1,0:T(8,128)(2,1)S(1)} %get-tuple-element.86), channel_id=1, source_target_pairs={{0,6},{1,7},{2,0},{3,1},{4,2},{5,3},{6,4},{7,5},{8,14},{9,15},{10,... | collective-permute-start | bytes 344072 | tf_op jit(solution)/shard_map/ppermute | solution.py:40
  50.8 10.9 %collective-permute-start.6 = (bf16[64,1792]{1,0:T(8,128)(2,1)S(1)}, bf16[64,1792]{1,0:T(8,128)(2,1)S(1)}, u32[]{:S(2)}, u32[]{:S(2)}) collective-permute-start(bf16[64,1792]{1,0:T(8,128)(2,1)S(1)} %get-tuple-element.67.a0.refs_0_), channel_id=1, source_target_pairs={{0,8},{1,9},{2,10},{3,11},{4,12},{5,13},{6,14},{7,15},{8,16},{9,17... | collective-permute-start | bytes 688136 | tf_op jit(solution)/shard_map/ppermute | solution.py:40
  53.7 10.1 %collective-permute-start.9 = (bf16[64,1792]{1,0:T(8,128)(2,1)S(1)}, bf16[64,1792]{1,0:T(8,128)(2,1)S(1)}, u32[]{:S(2)}, u32[]{:S(2)}) collective-permute-start(bf16[64,1792]{1,0:T(8,128)(2,1)S(1)} %get-tuple-element.68.b0.refs_1_), channel_id=1, source_target_pairs={{0,24},{1,25},{2,26},{3,27},{4,28},{5,29},{6,30},{7,31},{8,0},{9,1... | collective-permute-start | bytes 688136 | tf_op jit(solution)/shard_map/ppermute | solution.py:40
  58.3 9.1 %collective-permute-start.25 = (bf16[64,1792]{1,0:T(8,128)(2,1)S(1)}, bf16[64,1792]{1,0:T(8,128)(2,1)S(1)}, u32[]{:S(2)}, u32[]{:S(2)}) collective-permute-start(bf16[64,1792]{1,0:T(8,128)(2,1)S(1)} %get-tuple-element.87.a0.refs_8_), channel_id=1, source_target_pairs={{0,8},{1,9},{2,10},{3,11},{4,12},{5,13},{6,14},{7,15},{8,16},{9,17... | collective-permute-start | bytes 688136 | tf_op jit(solution)/shard_map/ppermute | solution.py:40
  58.4 10.3 %collective-permute-start.28 = (bf16[64,1792]{1,0:T(8,128)(2,1)S(1)}, bf16[64,1792]{1,0:T(8,128)(2,1)S(1)}, u32[]{:S(2)}, u32[]{:S(2)}) collective-permute-start(bf16[64,1792]{1,0:T(8,128)(2,1)S(1)} %get-tuple-element.88.b0.refs_9_), channel_id=1, source_target_pairs={{0,24},{1,25},{2,26},{3,27},{4,28},{5,29},{6,30},{7,31},{8,0},{9,1... | collective-permute-start | bytes 688136 | tf_op jit(solution)/shard_map/ppermute | solution.py:40
  61.6 10.8 %collective-permute-start.26 = (bf16[64,1792]{1,0:T(8,128)(2,1)S(1)}, bf16[64,1792]{1,0:T(8,128)(2,1)S(1)}, u32[]{:S(2)}, u32[]{:S(2)}) collective-permute-start(bf16[64,1792]{1,0:T(8,128)(2,1)S(1)} %get-tuple-element.88.b0.refs_9_), channel_id=1, source_target_pairs={{0,8},{1,9},{2,10},{3,11},{4,12},{5,13},{6,14},{7,15},{8,16},{9,17... | collective-permute-start | bytes 688136 | tf_op jit(solution)/shard_map/ppermute | solution.py:40
  63.8 9.8 %collective-permute-start.30 = (bf16[64,1792]{1,0:T(8,128)(2,1)S(1)}, bf16[64,1792]{1,0:T(8,128)(2,1)S(1)}, u32[]{:S(2)}, u32[]{:S(2)}) collective-permute-start(bf16[64,1792]{1,0:T(8,128)(2,1)S(1)} %get-tuple-element.87.a0.refs_8_), channel_id=1, source_target_pairs={{0,24},{1,25},{2,26},{3,27},{4,28},{5,29},{6,30},{7,31},{8,0},{9,1... | collective-permute-start | bytes 688136 | tf_op jit(solution)/shard_map/ppermute | solution.py:40
  67.5 9.8 %collective-permute-start.27 = (bf16[64,1792]{1,0:T(8,128)(2,1)S(1)}, bf16[64,1792]{1,0:T(8,128)(2,1)S(1)}, u32[]{:S(2)}, u32[]{:S(2)}) collective-permute-start(bf16[64,1792]{1,0:T(8,128)(2,1)S(1)} %collective-permute-done.25.a1.refs_10_), channel_id=1, source_target_pairs={{0,8},{1,9},{2,10},{3,11},{4,12},{5,13},{6,14},{7,15},{8,16},{9,17... | collective-permute-start | bytes 688136 | tf_op jit(solution)/shard_map/ppermute | solution.py:40
  68.7 9.8 %collective-permute-start.29 = (bf16[64,1792]{1,0:T(8,128)(2,1)S(1)}, bf16[64,1792]{1,0:T(8,128)(2,1)S(1)}, u32[]{:S(2)}, u32[]{:S(2)}) collective-permute-start(bf16[64,1792]{1,0:T(8,128)(2,1)S(1)} %collective-permute-done.28.b3.refs_15_), channel_id=1, source_target_pairs={{0,24},{1,25},{2,26},{3,27},{4,28},{5,29},{6,30},{7,31},{8,0},{9,1... | collective-permute-start | bytes 688136 | tf_op jit(solution)/shard_map/ppermute | solution.py:40
  72.4 13.4 %collective-permute-start.7 = (bf16[64,1792]{1,0:T(8,128)(2,1)S(1)}, bf16[64,1792]{1,0:T(8,128)(2,1)S(1)}, u32[]{:S(2)}, u32[]{:S(2)}) collective-permute-start(bf16[64,1792]{1,0:T(8,128)(2,1)S(1)} %get-tuple-element.68.b0.refs_1_), channel_id=1, source_target_pairs={{0,8},{1,9},{2,10},{3,11},{4,12},{5,13},{6,14},{7,15},{8,16},{9,17... | collective-permute-start | bytes 688136 | tf_op jit(solution)/shard_map/ppermute | solution.py:40
  73.6 12.2 %collective-permute-start.11 = (bf16[64,1792]{1,0:T(8,128)(2,1)S(1)}, bf16[64,1792]{1,0:T(8,128)(2,1)S(1)}, u32[]{:S(2)}, u32[]{:S(2)}) collective-permute-start(bf16[64,1792]{1,0:T(8,128)(2,1)S(1)} %get-tuple-element.67.a0.refs_0_), channel_id=1, source_target_pairs={{0,24},{1,25},{2,26},{3,27},{4,28},{5,29},{6,30},{7,31},{8,0},{9,1... | collective-permute-start | bytes 688136 | tf_op jit(solution)/shard_map/ppermute | solution.py:40
  77.3 8.5 %collective-permute-start.8 = (bf16[64,1792]{1,0:T(8,128)(2,1)S(1)}, bf16[64,1792]{1,0:T(8,128)(2,1)S(1)}, u32[]{:S(2)}, u32[]{:S(2)}) collective-permute-start(bf16[64,1792]{1,0:T(8,128)(2,1)S(1)} %collective-permute-done.6.a1.refs_2_), channel_id=1, source_target_pairs={{0,8},{1,9},{2,10},{3,11},{4,12},{5,13},{6,14},{7,15},{8,16},{9,17... | collective-permute-start | bytes 688136 | tf_op jit(solution)/shard_map/ppermute | solution.py:40
  78.5 7.3 %collective-permute-start.10 = (bf16[64,1792]{1,0:T(8,128)(2,1)S(1)}, bf16[64,1792]{1,0:T(8,128)(2,1)S(1)}, u32[]{:S(2)}, u32[]{:S(2)}) collective-permute-start(bf16[64,1792]{1,0:T(8,128)(2,1)S(1)} %collective-permute-done.9.b3.refs_7_), channel_id=1, source_target_pairs={{0,24},{1,25},{2,26},{3,27},{4,28},{5,29},{6,30},{7,31},{8,0},{9,1... | collective-permute-start | bytes 688136 | tf_op jit(solution)/shard_map/ppermute | solution.py:40
  85.1 12.1 %collective-permute-start.31 = (bf16[128,256]{1,0:T(8,128)(2,1)S(1)}, bf16[128,256]{1,0:T(8,128)(2,1)S(1)}, u32[]{:S(2)}, u32[]{:S(2)}) collective-permute-start(bf16[128,256]{1,0:T(8,128)(2,1)S(1)} %get-tuple-element.90), channel_id=1, source_target_pairs={{0,6},{1,7},{2,0},{3,1},{4,2},{5,3},{6,4},{7,5},{8,14},{9,15},{10,... | collective-permute-start | bytes 196616 | tf_op jit(solution)/shard_map/ppermute | solution.py:40
  91.0 12.4 %collective-permute-start.16 = (bf16[128,512]{1,0:T(8,128)(2,1)S(1)}, bf16[128,512]{1,0:T(8,128)(2,1)S(1)}, u32[]{:S(2)}, u32[]{:S(2)}) collective-permute-start(bf16[128,512]{1,0:T(8,128)(2,1)S(1)} %get-tuple-element.74), channel_id=1, source_target_pairs={{0,6},{1,7},{2,0},{3,1},{4,2},{5,3},{6,4},{7,5},{8,14},{9,15},{10,... | collective-permute-start | bytes 393224 | tf_op jit(solution)/shard_map/ppermute | solution.py:40
  91.9 11.5 %collective-permute-start.17 = (bf16[128,512]{1,0:T(8,128)(2,1)S(1)}, bf16[128,512]{1,0:T(8,128)(2,1)S(1)}, u32[]{:S(2)}, u32[]{:S(2)}) collective-permute-start(bf16[128,512]{1,0:T(8,128)(2,1)S(1)} %get-tuple-element.75), channel_id=1, source_target_pairs={{0,4},{1,5},{2,6},{3,7},{4,0},{5,1},{6,2},{7,3},{8,12},{9,13},{10,... | collective-permute-start | bytes 393224 | tf_op jit(solution)/shard_map/ppermute | solution.py:40
  94.5 8.9 %collective-permute-start.18 = (bf16[128,512]{1,0:T(8,128)(2,1)S(1)}, bf16[128,512]{1,0:T(8,128)(2,1)S(1)}, u32[]{:S(2)}, u32[]{:S(2)}) collective-permute-start(bf16[128,512]{1,0:T(8,128)(2,1)S(1)} %get-tuple-element.76), channel_id=1, source_target_pairs={{0,2},{1,3},{2,4},{3,5},{4,6},{5,7},{6,0},{7,1},{8,10},{9,11},{10,... | collective-permute-start | bytes 393224 | tf_op jit(solution)/shard_map/ppermute | solution.py:40
  94.5 6.5 %collective-permute-start.32 = (bf16[128,256]{1,0:T(8,128)(2,1)S(1)}, bf16[128,256]{1,0:T(8,128)(2,1)S(1)}, u32[]{:S(2)}, u32[]{:S(2)}) collective-permute-start(bf16[128,256]{1,0:T(8,128)(2,1)S(1)} %get-tuple-element.91), channel_id=1, source_target_pairs={{0,4},{1,5},{2,6},{3,7},{4,0},{5,1},{6,2},{7,3},{8,12},{9,13},{10,... | collective-permute-start | bytes 196616 | tf_op jit(solution)/shard_map/ppermute | solution.py:40
  97.2 6.1 %collective-permute-start.33 = (bf16[128,256]{1,0:T(8,128)(2,1)S(1)}, bf16[128,256]{1,0:T(8,128)(2,1)S(1)}, u32[]{:S(2)}, u32[]{:S(2)}) collective-permute-start(bf16[128,256]{1,0:T(8,128)(2,1)S(1)} %get-tuple-element.92), channel_id=1, source_target_pairs={{0,2},{1,3},{2,4},{3,5},{4,6},{5,7},{6,0},{7,1},{8,10},{9,11},{10,... | collective-permute-start | bytes 196616 | tf_op jit(solution)/shard_map/ppermute | solution.py:40
  104.1 9.1 %collective-permute-start.34 = (bf16[128,768]{1,0:T(8,128)(2,1)S(1)}, bf16[128,768]{1,0:T(8,128)(2,1)S(1)}, u32[]{:S(2)}, u32[]{:S(2)}) collective-permute-start(bf16[128,768]{1,0:T(8,128)(2,1)S(1)} %middle.1.h0), channel_id=1, source_target_pairs={{0,2},{1,3},{2,4},{3,5},{4,6},{5,7},{6,0},{7,1},{8,10},{9,11},{10,... | collective-permute-start | bytes 589832 | tf_op jit(solution)/shard_map/ppermute | solution.py:40
  104.7 8.4 %collective-permute-start.35 = (bf16[128,768]{1,0:T(8,128)(2,1)S(1)}, bf16[128,768]{1,0:T(8,128)(2,1)S(1)}, u32[]{:S(2)}, u32[]{:S(2)}) collective-permute-start(bf16[128,768]{1,0:T(8,128)(2,1)S(1)} %middle.1.h0), channel_id=1, source_target_pairs={{0,4},{1,5},{2,6},{3,7},{4,0},{5,1},{6,2},{7,3},{8,12},{9,13},{10,... | collective-permute-start | bytes 589832 | tf_op jit(solution)/shard_map/ppermute | solution.py:40
  105.7 8.3 %collective-permute-start.36 = (bf16[128,768]{1,0:T(8,128)(2,1)S(1)}, bf16[128,768]{1,0:T(8,128)(2,1)S(1)}, u32[]{:S(2)}, u32[]{:S(2)}) collective-permute-start(bf16[128,768]{1,0:T(8,128)(2,1)S(1)} %middle.1.h0), channel_id=1, source_target_pairs={{0,6},{1,7},{2,0},{3,1},{4,2},{5,3},{6,4},{7,5},{8,14},{9,15},{10,... | collective-permute-start | bytes 589832 | tf_op jit(solution)/shard_map/ppermute | solution.py:40
  116.4 33.5 %collective-permute-start.46 = (bf16[768,896]{1,0:T(8,128)(2,1)S(1)}, bf16[768,896]{1,0:T(8,128)(2,1)S(1)}, u32[]{:S(2)}, u32[]{:S(2)}) collective-permute-start(bf16[768,896]{1,0:T(8,128)(2,1)S(1)} %get-tuple-element.106), channel_id=1, source_target_pairs={{0,1},{1,0},{2,3},{3,2},{4,5},{5,4},{6,7},{7,6},{8,9},{9,8},{10,11... | collective-permute-start | bytes 4128776 | tf_op jit(solution)/shard_map/ppermute | solution.py:40
  118.4 24.0 %collective-permute-start.37 = (bf16[128,1792]{1,0:T(8,128)(2,1)S(1)}, bf16[128,1792]{1,0:T(8,128)(2,1)S(1)}, u32[]{:S(2)}, u32[]{:S(2)}) collective-permute-start(bf16[128,1792]{1,0:T(8,128)(2,1)S(1)} %get-tuple-element.94), channel_id=1, source_target_pairs={{0,24},{1,25},{2,26},{3,27},{4,28},{5,29},{6,30},{7,31},{8,0},{9,1... | collective-permute-start | bytes 1376264 | tf_op jit(solution)/shard_map/ppermute | solution.py:40
  122.1 20.3 %collective-permute-start.38 = (bf16[128,1792]{1,0:T(8,128)(2,1)S(1)}, bf16[128,1792]{1,0:T(8,128)(2,1)S(1)}, u32[]{:S(2)}, u32[]{:S(2)}) collective-permute-start(bf16[128,1792]{1,0:T(8,128)(2,1)S(1)} %get-tuple-element.95), channel_id=1, source_target_pairs={{0,16},{1,17},{2,18},{3,19},{4,20},{5,21},{6,22},{7,23},{8,24},{9,... | collective-permute-start | bytes 1376264 | tf_op jit(solution)/shard_map/ppermute | solution.py:40
  122.1 23.7 %collective-permute-start.39 = (bf16[128,1792]{1,0:T(8,128)(2,1)S(1)}, bf16[128,1792]{1,0:T(8,128)(2,1)S(1)}, u32[]{:S(2)}, u32[]{:S(2)}) collective-permute-start(bf16[128,1792]{1,0:T(8,128)(2,1)S(1)} %get-tuple-element.96), channel_id=1, source_target_pairs={{0,8},{1,9},{2,10},{3,11},{4,12},{5,13},{6,14},{7,15},{8,16},{9,17... | collective-permute-start | bytes 1376264 | tf_op jit(solution)/shard_map/ppermute | solution.py:40
  146.6 9.1 %collective-permute-start.40 = (bf16[32,1792]{1,0:T(8,128)(2,1)S(1)}, bf16[32,1792]{1,0:T(8,128)(2,1)S(1)}, u32[]{:S(2)}, u32[]{:S(2)}) collective-permute-start(bf16[32,1792]{1,0:T(8,128)(2,1)S(1)} %get-tuple-element.98), channel_id=1, source_target_pairs={{0,6},{1,7},{2,0},{3,1},{4,2},{5,3},{6,4},{7,5},{8,14},{9,15},{10,... | collective-permute-start | bytes 344072 | tf_op jit(solution)/shard_map/ppermute | solution.py:40
  149.0 7.3 %collective-permute-start.41 = (bf16[32,1792]{1,0:T(8,128)(2,1)S(1)}, bf16[32,1792]{1,0:T(8,128)(2,1)S(1)}, u32[]{:S(2)}, u32[]{:S(2)}) collective-permute-start(bf16[32,1792]{1,0:T(8,128)(2,1)S(1)} %get-tuple-element.99), channel_id=1, source_target_pairs={{0,4},{1,5},{2,6},{3,7},{4,0},{5,1},{6,2},{7,3},{8,12},{9,13},{10,... | collective-permute-start | bytes 344072 | tf_op jit(solution)/shard_map/ppermute | solution.py:40
  149.0 9.0 %collective-permute-start.42 = (bf16[32,1792]{1,0:T(8,128)(2,1)S(1)}, bf16[32,1792]{1,0:T(8,128)(2,1)S(1)}, u32[]{:S(2)}, u32[]{:S(2)}) collective-permute-start(bf16[32,1792]{1,0:T(8,128)(2,1)S(1)} %get-tuple-element.100), channel_id=1, source_target_pairs={{0,2},{1,3},{2,4},{3,5},{4,6},{5,7},{6,0},{7,1},{8,10},{9,11},{10,... | collective-permute-start | bytes 344072 | tf_op jit(solution)/shard_map/ppermute | solution.py:40
  150.7 21.8 %collective-permute-start.47 = (bf16[192,896]{1,0:T(8,128)(2,1)S(1)}, bf16[192,896]{1,0:T(8,128)(2,1)S(1)}, u32[]{:S(2)}, u32[]{:S(2)}) collective-permute-start(bf16[192,896]{1,0:T(8,128)(2,1)S(1)} %get-tuple-element.108), channel_id=1, source_target_pairs={{0,6},{1,7},{2,0},{3,1},{4,2},{5,3},{6,4},{7,5},{8,14},{9,15},{10,... | collective-permute-start | bytes 1032200 | tf_op jit(solution)/shard_map/ppermute | solution.py:40
  153.3 19.2 %collective-permute-start.48 = (bf16[192,896]{1,0:T(8,128)(2,1)S(1)}, bf16[192,896]{1,0:T(8,128)(2,1)S(1)}, u32[]{:S(2)}, u32[]{:S(2)}) collective-permute-start(bf16[192,896]{1,0:T(8,128)(2,1)S(1)} %get-tuple-element.109), channel_id=1, source_target_pairs={{0,4},{1,5},{2,6},{3,7},{4,0},{5,1},{6,2},{7,3},{8,12},{9,13},{10,... | collective-permute-start | bytes 1032200 | tf_op jit(solution)/shard_map/ppermute | solution.py:40
  155.6 16.9 %collective-permute-start.49 = (bf16[192,896]{1,0:T(8,128)(2,1)S(1)}, bf16[192,896]{1,0:T(8,128)(2,1)S(1)}, u32[]{:S(2)}, u32[]{:S(2)}) collective-permute-start(bf16[192,896]{1,0:T(8,128)(2,1)S(1)} %get-tuple-element.110), channel_id=1, source_target_pairs={{0,2},{1,3},{2,4},{3,5},{4,6},{5,7},{6,0},{7,1},{8,10},{9,11},{10,... | collective-permute-start | bytes 1032200 | tf_op jit(solution)/shard_map/ppermute | solution.py:40
  158.7 6.4 %collective-permute-start.44 = (bf16[8,7168]{1,0:T(8,128)(2,1)S(1)}, bf16[8,7168]{1,0:T(8,128)(2,1)S(1)}, u32[]{:S(2)}, u32[]{:S(2)}) collective-permute-start(bf16[8,7168]{1,0:T(8,128)(2,1)S(1)} %get-tuple-element.103), channel_id=1, source_target_pairs={{0,64},{1,65},{2,66},{3,67},{4,68},{5,69},{6,70},{7,71},{8,72},{9,... | collective-permute-start | bytes 344072 | tf_op jit(solution)/shard_map/ppermute | solution.py:40
  164.1 6.0 %collective-permute-start.45 = (bf16[8,7168]{1,0:T(8,128)(2,1)S(1)}, bf16[8,7168]{1,0:T(8,128)(2,1)S(1)}, u32[]{:S(2)}, u32[]{:S(2)}) collective-permute-start(bf16[8,7168]{1,0:T(8,128)(2,1)S(1)} %get-tuple-element.104), channel_id=1, source_target_pairs={{0,32},{1,33},{2,34},{3,35},{4,36},{5,37},{6,38},{7,39},{8,40},{9,... | collective-permute-start | bytes 344072 | tf_op jit(solution)/shard_map/ppermute | solution.py:40
  (9 other events, 108.3 us)

commit v2 on v1

v2 whole, which is shorter than its diff:
```python
import functools

import jax
import jax.numpy as jnp
from jax import lax
from jax.experimental import pallas as pl
from jax.experimental.pallas import tpu as pltpu
from jax.sharding import PartitionSpec as P

N = 4
SLOT = 8
HID = 64
D = 7168
HALF = D // 2
EIGHTH = HALF // N
QUARTER = 2 * EIGHTH
ROWS = N * SLOT
GROUPED = N * ROWS
HELD = 2 * ROWS
CHUNK = N * HELD
BF = jnp.bfloat16
F32 = jnp.float32
VMEM_LIMIT = 16 * 1024 * 1024
VMEM_MOST = 56 * 1024 * 1024
beta_one = 0.9
beta_two = 0.95


def rotation(axis, step):
    pairs = []
    for x in range(N):
        for z in range(N):
            for y in range(N):
                for c in range(2):
                    to = {"x": x, "z": z, "y": y, "c": c}
                    to[axis] = (to[axis] + step) % (2 if axis == "c" else N)
                    source = ((x * N + z) * N + y) * 2 + c
                    target = ((to["x"] * N + to["z"]) * N + to["y"]) * 2 + to["c"]
                    pairs.append((source, target))
    return pairs


def turn(value, axis, step):
    return lax.ppermute(value, ("expert", "dp"), rotation(axis, step))


def call(kernel, name, outs, place, *ins, flops=0, scratch=()):
    outs = [jax.ShapeDtypeStruct(s, t) for s, t in outs]
    size = sum(v.size * v.dtype.itemsize for v in (*ins, *outs))
    return pl.pallas_call(
        kernel,
        name=name,
        out_shape=outs,
        in_specs=[pl.BlockSpec(memory_space=pltpu.SMEM)]
        + [pl.BlockSpec(memory_space=pltpu.VMEM)] * len(ins),
        out_specs=[pl.BlockSpec(memory_space=pltpu.VMEM)] * len(outs),
        scratch_shapes=list(scratch),
        cost_estimate=pl.CostEstimate(flops=flops, bytes_accessed=size, transcendentals=0),
        compiler_params=pltpu.CompilerParams(vmem_limit_bytes=VMEM_LIMIT),
    )(place, *ins)


def wrap(v):
    return lax.rem(v + 2 * N, N)


def aligned(v):
    return pl.multiple_of(v, 128)


def mm(a, b, dims):
    return lax.dot_general(a, b, (dims, ((), ())), preferred_element_type=F32)


NN = ((1,), (0,))
NT = ((1,), (1,))
TN = ((0,), (0,))


def route_kernel(
    ids_in, gates_in, tokens, grads, out, pick_out, ids, gates, tok_buf, grad_buf, sems
):
    tok = ids.shape[1]
    small = [
        pltpu.make_async_copy(ids_in, ids, sems.at[4 * N]),
        pltpu.make_async_copy(gates_in, gates, sems.at[4 * N + 1]),
    ]
    for copy in small:
        copy.start()
    copies = []
    for q in range(N):
        for i, (source, buf) in enumerate(((tokens, tok_buf), (grads, grad_buf))):
            for c in range(2):
                cols = pl.ds(c * HALF + q * EIGHTH, EIGHTH)
                copy = pltpu.make_async_copy(
                    source.at[:, cols], buf.at[:, cols], sems.at[q * 4 + i * 2 + c]
                )
                copy.start()
                copies.append(copy)
    row_i = lax.broadcasted_iota(jnp.int32, (tok, tok), 0)
    col_i = lax.broadcasted_iota(jnp.int32, (tok, tok), 1)
    slot = lax.broadcasted_iota(jnp.int32, (ROWS, tok), 0)
    for copy in small:
        copy.wait()
    idv = ids[...]
    gv = gates[...]
    hits = [idv == e for e in range(N)]
    members = [jnp.sum(h.astype(F32), axis=0, keepdims=True) for h in hits]
    chosen = [jnp.sum(jnp.where(h, gv, 0.0), axis=0, keepdims=True) for h in hits]
    mask = jnp.concatenate(members + [jnp.zeros((8 - N, tok), F32)], axis=0)
    before = mm(mask, (row_i < col_i).astype(F32), NN).astype(jnp.int32)
    place_of = jnp.zeros((ROWS, tok), jnp.int32)
    weight = jnp.zeros((ROWS, tok), F32)
    for e in range(N):
        spot = jnp.where(members[e] > 0.0, before[e : e + 1] + e * SLOT, -1)
        mine = slot // SLOT == e
        place_of = jnp.where(mine, spot, place_of)
        weight = jnp.where(mine, chosen[e], weight)
    on = place_of == slot
    pick = jnp.where(on, 1.0, 0.0).astype(BF)
    pick_out[...] = pick
    gate = jnp.sum(jnp.where(on, weight, 0.0), axis=1, keepdims=True)
    for q in range(N):
        for copy in copies[q * 4 : q * 4 + 4]:
            copy.wait()
        for c in range(2):
            cols = slice(c * HALF + q * EIGHTH, c * HALF + (q + 1) * EIGHTH)
            rows = mm(pick, tok_buf[:, cols], NN)
            scaled = mm(pick, grad_buf[:, cols], NN) * gate
            for e in range(N):
                at = slice(e * SLOT, (e + 1) * SLOT)
                both = jnp.concatenate([rows[at], scaled[at]], axis=0).astype(BF)
                out[e * N + q, :, c * EIGHTH : (c + 1) * EIGHTH] = both


def route(ids, gates, tokens, grad_out):
    tok = tokens.shape[0]
    vmem = pl.BlockSpec(memory_space=pltpu.VMEM)
    hbm = pl.BlockSpec(memory_space=pltpu.HBM)
    return pl.pallas_call(
        route_kernel,
        name="route",
        in_specs=[hbm] * 4,
        out_specs=[vmem, vmem],
        out_shape=[
            jax.ShapeDtypeStruct((N * N, 2 * SLOT, QUARTER), BF),
            jax.ShapeDtypeStruct((ROWS, tok), BF),
        ],
        scratch_shapes=[
            pltpu.VMEM(ids.shape, jnp.int32),
            pltpu.VMEM(gates.shape, F32),
            pltpu.VMEM((tok, D), BF),
            pltpu.VMEM((tok, D), BF),
            pltpu.SemaphoreType.DMA((4 * N + 2,)),
        ],
        cost_estimate=pl.CostEstimate(
            flops=4 * ROWS * tok * D, bytes_accessed=6 * tok * D, transcendentals=0
        ),
        compiler_params=pltpu.CompilerParams(vmem_limit_bytes=VMEM_MOST),
    )(ids, gates, tokens, grad_out)


def pair_kernel(place, got, a, b):
    for g in range(N):
        pieces = [got[x * N + g].astype(F32) for x in range(N)]
        for part in range(2):
            rows = [v[part * SLOT : (part + 1) * SLOT] for v in pieces]
            at = (part * 2 + g % 2) * ROWS
            (a, b)[g // 2][at : at + ROWS] = jnp.concatenate(rows, axis=0).astype(BF)


def stack_kernel(place, a0, b0, a1, b3, plus, minus):
    plus[:GROUPED] = a1[...]
    plus[GROUPED:] = b0[...]
    minus[:GROUPED] = b3[...]
    minus[GROUPED:] = a0[...]


def pieces_of(refs):
    if len(refs) == 4:
        a, b, c, d = refs
        return a, b, c, d
    plus, minus = refs
    low, high = pl.ds(0, GROUPED), pl.ds(GROUPED, GROUPED)
    return plus.at[low], minus.at[low], minus.at[high], plus.at[high]


def stack_weights_kernel(place, *refs):
    *pieces, own, other = refs
    y = place[2]
    for out, parts in ((own, pieces[:N]), (other, pieces[N:])):
        for k, w in enumerate(parts):
            block = wrap(y - k)
            for part in range(3):
                rows = pl.ds(pl.multiple_of(part * N * HID + block * HID, HID), HID)
                out[rows, :] = w[part * HID : (part + 1) * HID]


def split_columns_kernel(place, w, o0, o1, o2, o3):
    y = place[2]
    for k, o in enumerate((o0, o1, o2, o3)):
        o[...] = w[0, :, pl.ds(aligned(wrap(y + k) * EIGHTH), EIGHTH)]


def forward_kernel(place, *refs):
    *chunk, own, other, o0, o1, o2, o3, part = refs
    pieces = pieces_of(chunk)
    y, c = place[2], place[3]
    width = N * HID
    mine = pl.ds(aligned(c * EIGHTH), EIGHTH)
    theirs = pl.ds(aligned((1 - c) * EIGHTH), EIGHTH)
    for rows, span in (
        (slice(0, HELD), slice(0, 2 * width)),
        (slice(HELD, 2 * HELD), slice(2 * width, 3 * width)),
    ):
        v_mine = jnp.concatenate([v[rows, mine] for v in pieces], axis=0)
        v_theirs = jnp.concatenate([v[rows, theirs] for v in pieces], axis=0)
        part[:, span] = mm(v_mine, own[span], NT) + mm(v_theirs, other[span], NT)
    for k, o in enumerate((o0, o1, o2, o3)):
        at = wrap(y - k) * ROWS
        for s in range(2):
            rows = pl.ds(pl.multiple_of(s * GROUPED + at, ROWS), ROWS)
            o[s * ROWS : (s + 1) * ROWS] = part[rows, :].astype(o.dtype)


def middle_kernel(place, p0, p1, p2, p3, out):
    width = N * HID
    total = p0[...] + p1[...].astype(F32) + p2[...].astype(F32) + p3[...].astype(F32)
    pair = total[:, : 2 * width]
    d_hidden = total[:, 2 * width :]
    gate = pair[:, :width]
    up = pair[:, width:]
    sig = jax.nn.sigmoid(gate)
    act = gate * sig
    out[:, :width] = (d_hidden * up * sig * (1.0 + gate * (1.0 - sig))).astype(BF)
    out[:, width : 2 * width] = (d_hidden * act).astype(BF)
    out[:, 2 * width :] = (act * up).astype(BF)


def back_kernel(place, h0, h1, h2, h3, own, other, held, *outs):
    y, c = place[2], place[3]
    width = 2 * N * HID
    for k, h in enumerate((h0, h1, h2, h3)):
        at = wrap(y - k) * ROWS
        for s in range(2):
            rows = pl.ds(pl.multiple_of(s * GROUPED + at, ROWS), ROWS)
            held[rows, :] = h[s * ROWS : (s + 1) * ROWS]
    h = held[:, :width]
    for w, half in ((own, c), (other, 1 - c)):
        cols = pl.ds(aligned(half * EIGHTH), EIGHTH)
        part = mm(h, w[:width], NN)
        for i, o in enumerate(outs):
            o[:, cols] = part[i * HELD : (i + 1) * HELD].astype(BF)


def pass_on_kernel(place, own_a, own_b, got_a, got_b, out_a, out_b):
    out_a[...] = (own_a[...].astype(F32) + got_a[...].astype(F32)).astype(BF)
    out_b[...] = (own_b[...].astype(F32) + got_b[...].astype(F32)).astype(BF)


def weight_grad(half, h1, h2, chunks, out):
    pieces = (*pieces_of(chunks[:4]), *pieces_of(chunks[4:]))
    width = 2 * N * HID
    cols = pl.ds(aligned(half * EIGHTH), EIGHTH)
    hs = jnp.concatenate([h1[...], h2[...]], axis=0)
    x = jnp.concatenate([v[:HELD, cols] for v in pieces], axis=0)
    out[:width] = mm(hs[:, :width], x, TN).astype(out.dtype)
    g = jnp.concatenate([v[HELD : 2 * HELD, cols] for v in pieces], axis=0)
    out[width:] = mm(hs[:, width:], g, TN).astype(out.dtype)


def their_grad_kernel(place, h1, h2, *refs):
    *chunks, out = refs
    weight_grad(1 - place[3], h1, h2, chunks, out)


def my_grad_kernel(place, got, h1, h2, *refs):
    *chunks, o0, o1, o2, o3, mine = refs
    y = place[2]
    weight_grad(place[3], h1, h2, chunks, mine)
    for k, o in enumerate((o0, o1, o2, o3)):
        block = wrap(y - k)
        for part in range(3):
            rows = pl.ds(pl.multiple_of(part * N * HID + block * HID, HID), HID)
            total = mine[rows, :] + got[rows, :].astype(F32)
            o[part * HID : (part + 1) * HID] = total.astype(o.dtype)


def sum_back_kernel(place, own_a, own_b, got_a, got_b, out):
    for h, (own, got) in enumerate(((own_a, got_a), (own_b, got_b))):
        total = own[...].astype(F32) + got[...].astype(F32)
        for s in range(2):
            for x in range(N):
                at = s * ROWS + x * SLOT
                out[x * N + 2 * h + s] = total[at : at + SLOT].astype(BF)


def combine_kernel(place, pick, got, out):
    for q in range(N):
        rows = jnp.concatenate([got[e * N + q].astype(F32) for e in range(N)], axis=0)
        total = mm(pick[...], rows.astype(BF), TN).astype(BF)
        for c in range(2):
            at = c * HALF + q * EIGHTH
            out[:, at : at + EIGHTH] = total[:, c * EIGHTH : (c + 1) * EIGHTH]


def moments_kernel(place, g0, g1, g2, g3, one, two, new_one, new_two):
    step = pl.program_id(0)
    for k, g in enumerate((g0, g1, g2, g3)):

        @pl.when(step == k)
        def _():
            grad = g[...].astype(F32)
            new_one[0] = beta_one * one[0] + (1.0 - beta_one) * grad
            new_two[0] = beta_two * two[0] + (1.0 - beta_two) * grad * grad


def moments(place, grads, one, two):
    rows = one.shape[1]
    piece = pl.BlockSpec((rows, EIGHTH), lambda k, place: (0, 0))
    block = pl.BlockSpec((1, rows, EIGHTH), lambda k, place: (0, 0, lax.rem(place[2] + k, N)))
    return pl.pallas_call(
        moments_kernel,
        name="moments",
        grid_spec=pltpu.PrefetchScalarGridSpec(
            num_scalar_prefetch=1,
            grid=(N,),
            in_specs=[piece] * N + [block] * 2,
            out_specs=[block] * 2,
        ),
        out_shape=[jax.ShapeDtypeStruct(v.shape, v.dtype) for v in (one, two)],
        cost_estimate=pl.CostEstimate(
            flops=6 * one.size, bytes_accessed=17 * one.size, transcendentals=0
        ),
        compiler_params=pltpu.CompilerParams(vmem_limit_bytes=VMEM_MOST),
    )(place, *grads, one, two)


def exchange(value, axes):
    groups = {}
    for index in range(N * N * N):
        at = {"x": index // (N * N), "z": index // N % N, "y": index % N}
        groups.setdefault(tuple(at[a] for a in at if a not in axes), []).append(index)
    return lax.all_to_all(
        value, "expert", 0, 0, axis_index_groups=list(groups.values()), tiled=True
    )


def spread(parts, axis, sign=1):
    moved = {k: turn(parts[k], axis, sign * k) for k in (2, 1, 3)}
    return [parts[0]] + [moved[k] for k in range(1, N)]


def after(values, *earlier):
    return lax.optimization_barrier((values, earlier))[0]


def add(place, own_a, own_b, got_a, got_b):
    half = ((HELD, QUARTER), BF)
    return call(pass_on_kernel, "pass_on", [half] * 2, place, own_a, own_b, got_a, got_b)


def middle_part(place, chunk, w_own, w_other, *earlier):
    width = 3 * N * HID
    part = call(
        forward_kernel,
        "forward",
        [((HELD, width), F32)] + [((HELD, width), BF)] * 3,
        place,
        *chunk,
        w_own,
        w_other,
        flops=2 * CHUNK * QUARTER * width,
        scratch=[pltpu.VMEM((CHUNK, width), F32)],
    )
    part = after(spread(part, "y", -1), *earlier)
    (held,) = call(middle_kernel, "middle", [((HELD, width), BF)], place, *part)
    return held


def back_part(place, held, w_own, w_other):
    return call(
        back_kernel,
        "back",
        [((CHUNK, 3 * N * HID), BF)] + [((HELD, QUARTER), BF)] * 4,
        place,
        *held,
        w_own,
        w_other,
        flops=4 * CHUNK * QUARTER * N * HID,
    )


def shards(tokens, grad_out, gates, expert_ids, expert_weights, moment_one, moment_two):
    expert = lax.axis_index("expert")
    core = lax.axis_index("dp")
    place = jnp.stack([expert // (N * N), expert // N % N, expert % N, core]).astype(jnp.int32)
    tok = tokens.shape[0]
    width = N * HID
    slots = ((N * N, SLOT, QUARTER), BF)
    block_rows = expert_weights.shape[1]

    sent, pick = route(expert_ids.T, gates.T, tokens, grad_out)
    got = exchange(sent, "xy")
    w_columns = call(
        split_columns_kernel,
        "split_columns",
        [((block_rows, EIGHTH), BF)] * N,
        place,
        expert_weights,
    )
    w_parts = spread(after(w_columns, got), "y")
    got = after(got, w_columns[1])
    a0, b0 = call(pair_kernel, "pair", [((GROUPED, QUARTER), BF)] * 2, place, got)
    a1, b3 = turn(a0, "z", 1), turn(b0, "z", -1)
    first = a0, b0, a1, b3
    plus, minus = call(
        stack_kernel, "stack", [((2 * GROUPED, QUARTER), BF)] * 2, place, *first
    )
    w_parts = after(w_parts, plus)
    second = turn(plus, "z", 1), turn(minus, "z", -1)
    w_others = [turn(w, "c", 1) for w in w_parts]
    w_own, w_other = call(
        stack_weights_kernel,
        "stack_weights",
        [((N * block_rows, EIGHTH), BF)] * 2,
        place,
        *w_parts,
        *w_others,
    )

    mid_one = middle_part(place, first, w_own, w_other)
    held_one = spread([mid_one] * N, "y")
    held_one, r_a0, r_b0, r_a1, r_b3 = back_part(place, held_one, w_own, w_other)
    got_a, got_b = turn(r_a1, "z", 1), turn(r_b3, "z", -1)
    second = after(second, mid_one)
    held_two = middle_part(place, second, w_own, w_other, r_a1)
    held_two = after(spread([held_two] * N, "y"), got_a, got_b)
    held_two, r_a2, r_b2, r_a3, r_b1 = back_part(place, held_two, w_own, w_other)
    got_a, got_b = add(place, r_a2, r_b2, got_a, got_b)
    held = after((held_one, held_two), got_a)
    got_a, got_b = turn(got_a, "z", 1), turn(got_b, "z", -1)
    flops = N * GROUPED * QUARTER * 3 * width
    (grad_theirs,) = call(
        their_grad_kernel,
        "their_grad",
        [((3 * width, EIGHTH), BF)],
        place,
        *held,
        *first,
        *second,
        flops=flops,
    )
    grad_got = turn(grad_theirs, "c", 1)
    blocks = call(
        my_grad_kernel,
        "my_grad",
        [((block_rows, EIGHTH), F32)] + [((block_rows, EIGHTH), BF)] * 3,
        place,
        grad_got,
        *held,
        *first,
        *second,
        flops=flops,
        scratch=[pltpu.VMEM((3 * width, EIGHTH), F32)],
    )
    got_a, got_b = after((got_a, got_b), blocks[0])
    got_a, got_b = add(place, r_a3, r_b1, got_a, got_b)
    got_a, got_b = turn(got_a, "z", 1), turn(got_b, "z", -1)
    blocks = spread(blocks, "y", -1)
    got_a, got_b = after((got_a, got_b), *blocks)
    (back,) = call(sum_back_kernel, "sum_back", [slots], place, r_a0, r_b0, got_a, got_b)
    back = exchange(back, "xy")
    new_one, new_two = moments(place, blocks, moment_one, moment_two)
    back = after(back, new_one)
    (grad_tokens,) = call(
        combine_kernel,
        "combine",
        [((tok, D), BF)],
        place,
        pick,
        back,
        flops=2 * ROWS * tok * D,
    )
    return grad_tokens, new_one, new_two


def solution(mesh):
    return jax.shard_map(
        shards,
        mesh=mesh,
        in_specs=(
            P(("expert", "dp"), None),
            P(("expert", "dp"), None),
            P(("expert", "dp"), None),
            P(("expert", "dp"), None),
            P("expert", None, "dp"),
            P("expert", None, "dp"),
            P("expert", None, "dp"),
        ),
        out_specs=(P(("expert", "dp"), None), P("expert", None, "dp"), P("expert", None, "dp")),
        check_vma=False,
    )
```

time: 177 us -> 147 us (0.83)
  starting transfers between devices: 72.4 us -> 43.5 us
    ppermute x50 -> x33, starting transfers between devices: 72.4 us -> 32.7 us  [turn(): return lax.ppermute(value, ('expert', 'dp'), rotation(axis, step))]
    ppermute x50 -> x33, waiting for transfers between devices: 72.6 us -> 53.4 us  [turn(): return lax.ppermute(value, ('expert', 'dp'), rotation(axis, step))]
    all_to_all x0 -> x2, waiting for transfers between devices: none -> 18.8 us  [exchange(): lax.all_to_all(value, 'expert', 0, 0, axis_index_groups=list(groups.value...]
    all_to_all x0 -> x2, starting transfers between devices: none -> 10.8 us  [exchange(): lax.all_to_all(value, 'expert', 0, 0, axis_index_groups=list(groups.value...]
    pallas_call x17 -> x16, Pallas kernels: 23.4 us -> 18.2 us  [call(): pl.pallas_call(kernel, name=name, out_shape=outs, in_specs=[pl.BlockSpec(...]
    pallas_call x0 -> x1, Pallas kernels: none -> 3.5 us  [route(): pl.pallas_call(route_kernel, name='route', in_specs=[hbm] * 4, out_specs=...]
    pallas_call x1, Pallas kernels: 4.01 us -> 6.9 us  [moments(): pl.pallas_call(moments_kernel, name='moments', grid_spec=pltpu.PrefetchSc...]
  transfers between devices with their start and end apart: 50 -> 35, of which waited for: 21 -> 25; matrix products, arithmetic and copies ran while one was open for 0% -> 0% of each run, Pallas kernels for 11% -> 12%
where the time goes in v2:
time: 147 us
  waiting for transfers between devices  72.1 us (49%)
  starting transfers between devices  43.5 us (30%)
  Pallas kernels  28.6 us (19%)
  local copies, waits for them, and re-layouts  1.6 us (1%)
    ppermute x33, waiting for transfers between devices, turn(): return lax.ppermute(value, ('expert', 'dp'), rotation(axis, step))  53.4 us
    ppermute x33, starting transfers between devices, turn(): return lax.ppermute(value, ('expert', 'dp'), rotation(axis, step))  32.7 us
    all_to_all x2, waiting for transfers between devices, exchange(): lax.all_to_all(value, 'expert', 0, 0, axis_index_groups=list(groups.value...  18.8 us
    pallas_call x16, Pallas kernels, call(): pl.pallas_call(kernel, name=name, out_shape=outs, in_specs=[pl.BlockSpec(...  18.2 us
    all_to_all x2, starting transfers between devices, exchange(): lax.all_to_all(value, 'expert', 0, 0, axis_index_groups=list(groups.value...  10.8 us
    pallas_call x1, Pallas kernels, moments(): pl.pallas_call(moments_kernel, name='moments', grid_spec=pltpu.PrefetchSc...  6.9 us
    pallas_call x1, Pallas kernels, route(): pl.pallas_call(route_kernel, name='route', in_specs=[hbm] * 4, out_specs=...  3.5 us
  transfers between devices with their start and end apart: 35, of which 25 were waited for; matrix products, arithmetic and copies ran while one was open for 0% of the time, Pallas kernels for 12%

profile of v2, /device:TPU:0, one launch (start us, length us, event | category | flops | bytes accessed | tf_op | source)
XLA Modules:
  0.0 146.9 jit_solution(4621113211918458792)
XLA Ops:
  0.6 3.5 %route.1 = (bf16[16,16,1792]{2,1,0:T(8,128)(2,1)}, bf16[32,128]{1,0:T(8,128)(2,1)}) custom-call(s32[8,128]{1,0:T(8,128)} %bitcast.6, f32[8,128]{1,0:T(8,128)} %bitcast.7, bf16[128,7168]{1,0:T(8,128)(2,1)} %tokens.1, bf16[128,7168]{1,0:T(8,128)(2,1)} %grads.1), custom_call_target="tpu_custom_call" | custom-call | flops 117440512 | bytes 5505024 | tf_op jit(solution)/shard_map/route/pallas_call | solution.py:140
  4.2 7.3 %all-to-all-start = ((bf16[16,16,1792]{2,1,0:T(8,128)(2,1)}), bf16[16,16,1792]{2,1,0:T(8,128)(2,1)S(1)}, u32[]{:S(2)}, u32[]{:S(2)}) async-start(bf16[16,16,1792]{2,1,0:T(8,128)(2,1)} %get-tuple-element.74), calls=%async_computation | async-start | bytes 1835008 | tf_op jit(solution)/shard_map/all_to_all | solution.py:344
  12.9 14.5 %all-to-all-done.got = bf16[16,16,1792]{2,1,0:T(8,128)(2,1)S(1)} async-done(((bf16[16,16,1792]{2,1,0:T(8,128)(2,1)}), bf16[16,16,1792]{2,1,0:T(8,128)(2,1)S(1)}, u32[]{:S(2)}, u32[]{:S(2)}) %all-to-all-start) | async-done | bytes 917536 | tf_op jit(solution)/shard_map/all_to_all | solution.py:344
  28.1 2.0 %collective-permute-start = (bf16[128,1792]{1,0:T(8,128)(2,1)S(1)}, bf16[128,1792]{1,0:T(8,128)(2,1)S(1)}, u32[]{:S(2)}, u32[]{:S(2)}) collective-permute-start(bf16[128,1792]{1,0:T(8,128)(2,1)S(1)} %get-tuple-element.77.a0.refs_0_), channel_id=1, source_target_pairs={{0,8},{1,9},{2,10},{3,11},{4,12},{5,13},{6,14},{7,15},{8,16},{9,17... | collective-permute-start | bytes 1376264 | tf_op jit(solution)/shard_map/ppermute | solution.py:44
  30.0 2.2 %collective-permute-start.1 = (bf16[128,1792]{1,0:T(8,128)(2,1)S(1)}, bf16[128,1792]{1,0:T(8,128)(2,1)S(1)}, u32[]{:S(2)}, u32[]{:S(2)}) collective-permute-start(bf16[128,1792]{1,0:T(8,128)(2,1)S(1)} %get-tuple-element.78.b0.refs_1_), channel_id=1, source_target_pairs={{0,24},{1,25},{2,26},{3,27},{4,28},{5,29},{6,30},{7,31},{8,0},{9,1... | collective-permute-start | bytes 1376264 | tf_op jit(solution)/shard_map/ppermute | solution.py:44
  32.8 1.1 collective-permute-start.3
  34.0 1.8 %collective-permute-start.4 = (bf16[192,896]{1,0:T(8,128)(2,1)S(1)}, bf16[192,896]{1,0:T(8,128)(2,1)S(1)}, u32[]{:S(2)}, u32[]{:S(2)}) collective-permute-start(bf16[192,896]{1,0:T(8,128)(2,1)S(1)} %get-tuple-element.85), channel_id=1, source_target_pairs={{0,6},{1,7},{2,0},{3,1},{4,2},{5,3},{6,4},{7,5},{8,14},{9,15},{10,... | collective-permute-start | bytes 1032200 | tf_op jit(solution)/shard_map/ppermute | solution.py:44
  35.7 4.7 %collective-permute-done.a1.refs_2_ = bf16[128,1792]{1,0:T(8,128)(2,1)S(1)} collective-permute-done((bf16[128,1792]{1,0:T(8,128)(2,1)S(1)}, bf16[128,1792]{1,0:T(8,128)(2,1)S(1)}, u32[]{:S(2)}, u32[]{:S(2)}) %collective-permute-start) | collective-permute-done | bytes 458784 | tf_op jit(solution)/shard_map/ppermute | solution.py:44
  41.1 1.9 %collective-permute-done.2.refs_1_ = bf16[192,896]{1,0:T(8,128)(2,1)S(1)} collective-permute-done((bf16[192,896]{1,0:T(8,128)(2,1)}, bf16[192,896]{1,0:T(8,128)(2,1)S(1)}, u32[]{:S(2)}, u32[]{:S(2)}) %collective-permute-start.2) | collective-permute-done | bytes 344096 | tf_op jit(solution)/shard_map/ppermute | solution.py:44
  43.0 5.3 %collective-permute-done.3.refs_2_ = bf16[192,896]{1,0:T(8,128)(2,1)S(1)} collective-permute-done((bf16[192,896]{1,0:T(8,128)(2,1)S(1)}, bf16[192,896]{1,0:T(8,128)(2,1)S(1)}, u32[]{:S(2)}, u32[]{:S(2)}) %collective-permute-start.3) | collective-permute-done | bytes 344096 | tf_op jit(solution)/shard_map/ppermute | solution.py:44
  48.7 1.7 %collective-permute-start.16 = (bf16[256,1792]{1,0:T(8,128)(2,1)S(1)}, bf16[256,1792]{1,0:T(8,128)(2,1)S(1)}, u32[]{:S(2)}, u32[]{:S(2)}) collective-permute-start(bf16[256,1792]{1,0:T(8,128)(2,1)S(1)} %get-tuple-element.103), channel_id=1, source_target_pairs={{0,24},{1,25},{2,26},{3,27},{4,28},{5,29},{6,30},{7,31},{8,0},{9,1... | collective-permute-start | bytes 2752520 | tf_op jit(solution)/shard_map/ppermute | solution.py:44
  51.3 1.1 collective-permute-done.6.refs_5_
  54.1 1.6 %forward.2 = (f32[64,768]{1,0:T(8,128)S(1)}, bf16[64,768]{1,0:T(8,128)(2,1)S(1)}, bf16[64,768]{1,0:T(8,128)(2,1)S(1)}, bf16[64,768]{1,0:T(8,128)(2,1)S(1)}) custom-call(s32[4]{0:T(128)S(1)} %pad_add_fusion.place, bf16[128,1792]{1,0:T(8,128)(2,1)S(1)} %get-tuple-element.77.a0.refs_0_, bf16[128,1792]{1,0:T(8,128)(2,1)S(1)} %get-tuple-element.78.b0.refs_1_, ...), custom_call_target="tpu_custom_call" | custom-call | flops 704643072 | bytes 5079040 | tf_op jit(solution)/shard_map/forward/pallas_call | solution.py:50
  55.7 2.7 %collective-permute-start.9 = (bf16[64,768]{1,0:T(8,128)(2,1)S(1)}, bf16[64,768]{1,0:T(8,128)(2,1)S(1)}, u32[]{:S(2)}, u32[]{:S(2)}) collective-permute-start(bf16[64,768]{1,0:T(8,128)(2,1)S(1)} %get-tuple-element.94), channel_id=1, source_target_pairs={{0,6},{1,7},{2,0},{3,1},{4,2},{5,3},{6,4},{7,5},{8,14},{9,15},{10,... | collective-permute-start | bytes 294920 | tf_op jit(solution)/shard_map/ppermute | solution.py:44
  59.4 3.5 %collective-permute-done.9.p1 = bf16[64,768]{1,0:T(8,128)(2,1)S(1)} collective-permute-done((bf16[64,768]{1,0:T(8,128)(2,1)S(1)}, bf16[64,768]{1,0:T(8,128)(2,1)S(1)}, u32[]{:S(2)}, u32[]{:S(2)}) %collective-permute-start.9) | collective-permute-done | bytes 98336 | tf_op jit(solution)/shard_map/ppermute | solution.py:44
  62.9 2.6 %collective-permute-done.10.p2 = bf16[64,768]{1,0:T(8,128)(2,1)S(1)} collective-permute-done((bf16[64,768]{1,0:T(8,128)(2,1)S(1)}, bf16[64,768]{1,0:T(8,128)(2,1)S(1)}, u32[]{:S(2)}, u32[]{:S(2)}) %collective-permute-start.10) | collective-permute-done | bytes 98336 | tf_op jit(solution)/shard_map/ppermute | solution.py:44
  65.5 1.0 collective-permute-done.11.p3
  68.5 0.9 collective-permute-start.12
  69.4 3.5 %collective-permute-done.14.h3 = bf16[64,768]{1,0:T(8,128)(2,1)S(1)} collective-permute-done((bf16[64,768]{1,0:T(8,128)(2,1)S(1)}, bf16[64,768]{1,0:T(8,128)(2,1)S(1)}, u32[]{:S(2)}, u32[]{:S(2)}) %collective-permute-start.14) | collective-permute-done | bytes 98336 | tf_op jit(solution)/shard_map/ppermute | solution.py:44
  72.9 1.8 %collective-permute-done.13.h2 = bf16[64,768]{1,0:T(8,128)(2,1)S(1)} collective-permute-done((bf16[64,768]{1,0:T(8,128)(2,1)S(1)}, bf16[64,768]{1,0:T(8,128)(2,1)S(1)}, u32[]{:S(2)}, u32[]{:S(2)}) %collective-permute-start.13) | collective-permute-done | bytes 98336 | tf_op jit(solution)/shard_map/ppermute | solution.py:44
  75.5 1.2 back.2
  76.8 2.9 %collective-permute-start.24 = (bf16[64,1792]{1,0:T(8,128)(2,1)S(1)}, bf16[64,1792]{1,0:T(8,128)(2,1)S(1)}, u32[]{:S(2)}, u32[]{:S(2)}) collective-permute-start(bf16[64,1792]{1,0:T(8,128)(2,1)S(1)} %get-tuple-element.115), channel_id=1, source_target_pairs={{0,24},{1,25},{2,26},{3,27},{4,28},{5,29},{6,30},{7,31},{8,0},{9,1... | collective-permute-start | bytes 688136 | tf_op jit(solution)/shard_map/ppermute | solution.py:44
  79.7 1.6 %forward.3 = (f32[64,768]{1,0:T(8,128)S(1)}, bf16[64,768]{1,0:T(8,128)(2,1)S(1)}, bf16[64,768]{1,0:T(8,128)(2,1)S(1)}, bf16[64,768]{1,0:T(8,128)(2,1)S(1)}) custom-call(s32[4]{0:T(128)S(1)} %pad_add_fusion.place, bf16[256,1792]{1,0:T(8,128)(2,1)S(1)} %collective-permute-done.15.refs_0_.refs_4_, ...), custom_call_target="tpu_custom_call" | custom-call | flops 704643072 | bytes 5079040 | tf_op jit(solution)/shard_map/forward/pallas_call | solution.py:50
  81.3 1.2 collective-permute-start.17
  82.5 0.9 collective-permute-start.18
  83.5 2.7 %collective-permute-done.17.p1 = bf16[64,768]{1,0:T(8,128)(2,1)S(1)} collective-permute-done((bf16[64,768]{1,0:T(8,128)(2,1)S(1)}, bf16[64,768]{1,0:T(8,128)(2,1)S(1)}, u32[]{:S(2)}, u32[]{:S(2)}) %collective-permute-start.17) | collective-permute-done | bytes 98336 | tf_op jit(solution)/shard_map/ppermute | solution.py:44
  86.2 2.6 %collective-permute-done.18.p2 = bf16[64,768]{1,0:T(8,128)(2,1)S(1)} collective-permute-done((bf16[64,768]{1,0:T(8,128)(2,1)S(1)}, bf16[64,768]{1,0:T(8,128)(2,1)S(1)}, u32[]{:S(2)}, u32[]{:S(2)}) %collective-permute-start.18) | collective-permute-done | bytes 98336 | tf_op jit(solution)/shard_map/ppermute | solution.py:44
  88.8 1.0 collective-permute-done.19.p3
  90.4 1.2 collective-permute-start.22
  91.6 0.9 collective-permute-start.21
  92.9 2.4 %collective-permute-done.22.h3 = bf16[64,768]{1,0:T(8,128)(2,1)S(1)} collective-permute-done((bf16[64,768]{1,0:T(8,128)(2,1)S(1)}, bf16[64,768]{1,0:T(8,128)(2,1)S(1)}, u32[]{:S(2)}, u32[]{:S(2)}) %collective-permute-start.22) | collective-permute-done | bytes 98336 | tf_op jit(solution)/shard_map/ppermute | solution.py:44
  95.3 2.4 %collective-permute-done.21.h2 = bf16[64,768]{1,0:T(8,128)(2,1)S(1)} collective-permute-done((bf16[64,768]{1,0:T(8,128)(2,1)S(1)}, bf16[64,768]{1,0:T(8,128)(2,1)S(1)}, u32[]{:S(2)}, u32[]{:S(2)}) %collective-permute-start.21) | collective-permute-done | bytes 98336 | tf_op jit(solution)/shard_map/ppermute | solution.py:44
  97.7 1.0 collective-permute-done.20.h1
  98.8 1.2 back.3
  100.7 1.6 %their_grad.1 = bf16[768,896]{1,0:T(8,128)(2,1)S(1)} custom-call(s32[4]{0:T(128)S(1)} %pad_add_fusion.place, bf16[256,768]{1,0:T(8,128)(2,1)S(1)} %get-tuple-element.128.h1, bf16[256,768]{1,0:T(8,128)(2,1)S(1)} %get-tuple-element.129.h2, bf16[128,1792]{1,0:T(8,128)(2,1)S(1)} %get-tuple-element.77.a0.refs_0_, ...), custom_call_target="tpu_custom_call" | custom-call | flops 704643072 | bytes 5832704 | tf_op jit(solution)/shard_map/their_grad/pallas_call | solution.py:50
  102.3 3.3 %collective-permute-start.26 = (bf16[64,1792]{1,0:T(8,128)(2,1)S(1)}, bf16[64,1792]{1,0:T(8,128)(2,1)S(1)}, u32[]{:S(2)}, u32[]{:S(2)}) collective-permute-start(bf16[64,1792]{1,0:T(8,128)(2,1)S(1)} %get-tuple-element.125), channel_id=1, source_target_pairs={{0,24},{1,25},{2,26},{3,27},{4,28},{5,29},{6,30},{7,31},{8,0},{9,1... | collective-permute-start | bytes 688136 | tf_op jit(solution)/shard_map/ppermute | solution.py:44
  105.6 1.9 %my_grad.1 = (f32[192,896]{1,0:T(8,128)S(1)}, bf16[192,896]{1,0:T(8,128)(2,1)S(1)}, bf16[192,896]{1,0:T(8,128)(2,1)S(1)}, bf16[192,896]{1,0:T(8,128)(2,1)S(1)}) custom-call(s32[4]{0:T(128)S(1)} %pad_add_fusion.place, bf16[768,896]{1,0:T(8,128)(2,1)S(1)} %collective-permute-done.27.got, bf16[256,768]{1,0:T(8,128)(2,1)S(1)} %get-tuple-element.128.h1, ...), custom_call_target="tpu_custom_call" | custom-call | flops 704643072 | bytes 7553024 | tf_op jit(solution)/shard_map/my_grad/pallas_call | solution.py:50
  108.4 1.1 collective-permute-start.30
  109.5 0.9 collective-permute-start.31
  111.1 3.4 %collective-permute-done.25.got_a = bf16[64,1792]{1,0:T(8,128)(2,1)S(1)} collective-permute-done((bf16[64,1792]{1,0:T(8,128)(2,1)S(1)}, bf16[64,1792]{1,0:T(8,128)(2,1)S(1)}, u32[]{:S(2)}, u32[]{:S(2)}) %collective-permute-start.25) | collective-permute-done | bytes 229408 | tf_op jit(solution)/shard_map/ppermute | solution.py:44
  115.2 3.2 %collective-permute-start.29 = (bf16[64,1792]{1,0:T(8,128)(2,1)S(1)}, bf16[64,1792]{1,0:T(8,128)(2,1)S(1)}, u32[]{:S(2)}, u32[]{:S(2)}) collective-permute-start(bf16[64,1792]{1,0:T(8,128)(2,1)S(1)} %get-tuple-element.134), channel_id=1, source_target_pairs={{0,24},{1,25},{2,26},{3,27},{4,28},{5,29},{6,30},{7,31},{8,0},{9,1... | collective-permute-start | bytes 688136 | tf_op jit(solution)/shard_map/ppermute | solution.py:44
  118.5 4.8 %collective-permute-done.28.got_a = bf16[64,1792]{1,0:T(8,128)(2,1)S(1)} collective-permute-done((bf16[64,1792]{1,0:T(8,128)(2,1)S(1)}, bf16[64,1792]{1,0:T(8,128)(2,1)S(1)}, u32[]{:S(2)}, u32[]{:S(2)}) %collective-permute-start.28) | collective-permute-done | bytes 229408 | tf_op jit(solution)/shard_map/ppermute | solution.py:44
  123.3 5.0 %collective-permute-done.32.g3 = bf16[192,896]{1,0:T(8,128)(2,1)S(1)} collective-permute-done((bf16[192,896]{1,0:T(8,128)(2,1)S(1)}, bf16[192,896]{1,0:T(8,128)(2,1)S(1)}, u32[]{:S(2)}, u32[]{:S(2)}) %collective-permute-start.32) | collective-permute-done | bytes 344096 | tf_op jit(solution)/shard_map/ppermute | solution.py:44
  128.3 1.4 sum_back.1
  129.7 3.6 %all-to-all-start.1 = ((bf16[16,8,1792]{2,1,0:T(8,128)(2,1)}), bf16[16,8,1792]{2,1,0:T(8,128)(2,1)S(1)}, u32[]{:S(2)}, u32[]{:S(2)}) async-start(bf16[16,8,1792]{2,1,0:T(8,128)(2,1)} %sum_back.1), calls=%async_computation.1 | async-start | bytes 917504 | tf_op jit(solution)/shard_map/all_to_all | solution.py:344
  133.3 6.9 %moments.1 = (f32[1,192,3584]{2,1,0:T(8,128)}, f32[1,192,3584]{2,1,0:T(8,128)}) custom-call(s32[4]{0:T(128)} %copy-done.2, f32[192,896]{1,0:T(8,128)} %copy-done.1, bf16[192,896]{1,0:T(8,128)(2,1)} %copy-done.6, bf16[192,896]{1,0:T(8,128)(2,1)} %copy-done.7, bf16[192,896]{1,0:T(8,128)(2,1)} %copy-done.8, f32[1,192,3584]{2,1,0:T(8,128)} %one.1, ...), custom_call_target="tpu_custom_call" | custom-call | flops 4128768 | bytes 11698176 | tf_op jit(solution)/shard_map/moments/pallas_call | solution.py:322
  140.2 4.3 %all-to-all-done.1.got = bf16[16,8,1792]{2,1,0:T(8,128)(2,1)S(1)} async-done(((bf16[16,8,1792]{2,1,0:T(8,128)(2,1)}), bf16[16,8,1792]{2,1,0:T(8,128)(2,1)S(1)}, u32[]{:S(2)}, u32[]{:S(2)}) %all-to-all-start.1) | async-done | bytes 458784 | tf_op jit(solution)/shard_map/all_to_all | solution.py:344
  144.5 2.4 %combine.1 = bf16[128,7168]{1,0:T(8,128)(2,1)} custom-call(s32[4]{0:T(128)S(1)} %copy-done.3, bf16[32,128]{1,0:T(8,128)(2,1)S(1)} %copy-done.4, bf16[16,8,1792]{2,1,0:T(8,128)(2,1)S(1)} %all-to-all-done.1.got), custom_call_target="tpu_custom_call" | custom-call | flops 58720256 | bytes 2301952 | tf_op jit(solution)/shard_map/combine/pallas_call | solution.py:50
  (59 shorter events, 14.1 us)
Async XLA Ops:
  4.1 7.4 %copy-start = (bf16[1,192,3584]{2,1,0:T(8,128)(2,1)S(1)}, bf16[1,192,3584]{2,1,0:T(8,128)(2,1)}, u32[]{:S(2)}) copy-start(bf16[1,192,3584]{2,1,0:T(8,128)(2,1)} %w.1) | copy-start | bytes 4128772
  4.2 23.3 %all-to-all-start = ((bf16[16,16,1792]{2,1,0:T(8,128)(2,1)}), bf16[16,16,1792]{2,1,0:T(8,128)(2,1)S(1)}, u32[]{:S(2)}, u32[]{:S(2)}) async-start(bf16[16,16,1792]{2,1,0:T(8,128)(2,1)} %get-tuple-element.74), calls=%async_computation | async-start | bytes 1835008 | tf_op jit(solution)/shard_map/all_to_all | solution.py:344
  11.5 116.7 %copy-start.2 = (s32[4]{0:T(128)}, s32[4]{0:T(128)S(1)}, u32[]{:S(2)}) copy-start(s32[4]{0:T(128)S(1)} %pad_add_fusion.place) | copy-start | bytes 52
  12.2 0.7 copy-start.5
  28.1 12.4 %collective-permute-start = (bf16[128,1792]{1,0:T(8,128)(2,1)S(1)}, bf16[128,1792]{1,0:T(8,128)(2,1)S(1)}, u32[]{:S(2)}, u32[]{:S(2)}) collective-permute-start(bf16[128,1792]{1,0:T(8,128)(2,1)S(1)} %get-tuple-element.77.a0.refs_0_), channel_id=1, source_target_pairs={{0,8},{1,9},{2,10},{3,11},{4,12},{5,13},{6,14},{7,15},{8,16},{9,17... | collective-permute-start | bytes 1376264 | tf_op jit(solution)/shard_map/ppermute | solution.py:44
  30.0 10.4 %collective-permute-start.1 = (bf16[128,1792]{1,0:T(8,128)(2,1)S(1)}, bf16[128,1792]{1,0:T(8,128)(2,1)S(1)}, u32[]{:S(2)}, u32[]{:S(2)}) collective-permute-start(bf16[128,1792]{1,0:T(8,128)(2,1)S(1)} %get-tuple-element.78.b0.refs_1_), channel_id=1, source_target_pairs={{0,24},{1,25},{2,26},{3,27},{4,28},{5,29},{6,30},{7,31},{8,0},{9,1... | collective-permute-start | bytes 1376264 | tf_op jit(solution)/shard_map/ppermute | solution.py:44
  32.2 10.8 %collective-permute-start.2 = (bf16[192,896]{1,0:T(8,128)(2,1)}, bf16[192,896]{1,0:T(8,128)(2,1)S(1)}, u32[]{:S(2)}, u32[]{:S(2)}) collective-permute-start(bf16[192,896]{1,0:T(8,128)(2,1)} %copy-done.5), channel_id=1, source_target_pairs={{0,2},{1,3},{2,4},{3,5},{4,6},{5,7},{6,0},{7,1},{8,10},{9,11},{10,... | collective-permute-start | bytes 1032200 | tf_op jit(solution)/shard_map/ppermute | solution.py:44
  32.8 15.5 %collective-permute-start.3 = (bf16[192,896]{1,0:T(8,128)(2,1)S(1)}, bf16[192,896]{1,0:T(8,128)(2,1)S(1)}, u32[]{:S(2)}, u32[]{:S(2)}) collective-permute-start(bf16[192,896]{1,0:T(8,128)(2,1)S(1)} %get-tuple-element.84), channel_id=1, source_target_pairs={{0,4},{1,5},{2,6},{3,7},{4,0},{5,1},{6,2},{7,3},{8,12},{9,13},{10,... | collective-permute-start | bytes 1032200 | tf_op jit(solution)/shard_map/ppermute | solution.py:44
  34.0 14.8 %collective-permute-start.4 = (bf16[192,896]{1,0:T(8,128)(2,1)S(1)}, bf16[192,896]{1,0:T(8,128)(2,1)S(1)}, u32[]{:S(2)}, u32[]{:S(2)}) collective-permute-start(bf16[192,896]{1,0:T(8,128)(2,1)S(1)} %get-tuple-element.85), channel_id=1, source_target_pairs={{0,6},{1,7},{2,0},{3,1},{4,2},{5,3},{6,4},{7,5},{8,14},{9,15},{10,... | collective-permute-start | bytes 1032200 | tf_op jit(solution)/shard_map/ppermute | solution.py:44
  48.7 2.5 %collective-permute-start.5 = (bf16[192,896]{1,0:T(8,128)(2,1)S(1)}, bf16[192,896]{1,0:T(8,128)(2,1)S(1)}, u32[]{:S(2)}, u32[]{:S(2)}) collective-permute-start(bf16[192,896]{1,0:T(8,128)(2,1)S(1)} %get-tuple-element.87.refs_0_), channel_id=1, source_target_pairs={{0,1},{1,0},{2,3},{3,2},{4,5},{5,4},{6,7},{7,6},{8,9},{9,8},{10,11... | collective-permute-start | bytes 1032200 | tf_op jit(solution)/shard_map/ppermute | solution.py:44
  48.7 31.0 %collective-permute-start.16 = (bf16[256,1792]{1,0:T(8,128)(2,1)S(1)}, bf16[256,1792]{1,0:T(8,128)(2,1)S(1)}, u32[]{:S(2)}, u32[]{:S(2)}) collective-permute-start(bf16[256,1792]{1,0:T(8,128)(2,1)S(1)} %get-tuple-element.103), channel_id=1, source_target_pairs={{0,24},{1,25},{2,26},{3,27},{4,28},{5,29},{6,30},{7,31},{8,0},{9,1... | collective-permute-start | bytes 2752520 | tf_op jit(solution)/shard_map/ppermute | solution.py:44
  50.4 29.3 %collective-permute-start.15 = (bf16[256,1792]{1,0:T(8,128)(2,1)S(1)}, bf16[256,1792]{1,0:T(8,128)(2,1)S(1)}, u32[]{:S(2)}, u32[]{:S(2)}) collective-permute-start(bf16[256,1792]{1,0:T(8,128)(2,1)S(1)} %get-tuple-element.86), channel_id=1, source_target_pairs={{0,8},{1,9},{2,10},{3,11},{4,12},{5,13},{6,14},{7,15},{8,16},{9,17... | collective-permute-start | bytes 2752520 | tf_op jit(solution)/shard_map/ppermute | solution.py:44
  50.8 1.7 %collective-permute-start.6 = (bf16[192,896]{1,0:T(8,128)(2,1)S(1)}, bf16[192,896]{1,0:T(8,128)(2,1)S(1)}, u32[]{:S(2)}, u32[]{:S(2)}) collective-permute-start(bf16[192,896]{1,0:T(8,128)(2,1)S(1)} %collective-permute-done.2.refs_1_), channel_id=1, source_target_pairs={{0,1},{1,0},{2,3},{3,2},{4,5},{5,4},{6,7},{7,6},{8,9},{9,8},{10,11... | collective-permute-start | bytes 1032200 | tf_op jit(solution)/shard_map/ppermute | solution.py:44
  50.8 2.1 %collective-permute-start.7 = (bf16[192,896]{1,0:T(8,128)(2,1)S(1)}, bf16[192,896]{1,0:T(8,128)(2,1)S(1)}, u32[]{:S(2)}, u32[]{:S(2)}) collective-permute-start(bf16[192,896]{1,0:T(8,128)(2,1)S(1)} %collective-permute-done.3.refs_2_), channel_id=1, source_target_pairs={{0,1},{1,0},{2,3},{3,2},{4,5},{5,4},{6,7},{7,6},{8,9},{9,8},{10,11... | collective-permute-start | bytes 1032200 | tf_op jit(solution)/shard_map/ppermute | solution.py:44
  51.3 2.1 %collective-permute-start.8 = (bf16[192,896]{1,0:T(8,128)(2,1)S(1)}, bf16[192,896]{1,0:T(8,128)(2,1)S(1)}, u32[]{:S(2)}, u32[]{:S(2)}) collective-permute-start(bf16[192,896]{1,0:T(8,128)(2,1)S(1)} %collective-permute-done.4.refs_3_), channel_id=1, source_target_pairs={{0,1},{1,0},{2,3},{3,2},{4,5},{5,4},{6,7},{7,6},{8,9},{9,8},{10,11... | collective-permute-start | bytes 1032200 | tf_op jit(solution)/shard_map/ppermute | solution.py:44
  55.7 7.2 %collective-permute-start.9 = (bf16[64,768]{1,0:T(8,128)(2,1)S(1)}, bf16[64,768]{1,0:T(8,128)(2,1)S(1)}, u32[]{:S(2)}, u32[]{:S(2)}) collective-permute-start(bf16[64,768]{1,0:T(8,128)(2,1)S(1)} %get-tuple-element.94), channel_id=1, source_target_pairs={{0,6},{1,7},{2,0},{3,1},{4,2},{5,3},{6,4},{7,5},{8,14},{9,15},{10,... | collective-permute-start | bytes 294920 | tf_op jit(solution)/shard_map/ppermute | solution.py:44
  58.4 7.1 %collective-permute-start.10 = (bf16[64,768]{1,0:T(8,128)(2,1)S(1)}, bf16[64,768]{1,0:T(8,128)(2,1)S(1)}, u32[]{:S(2)}, u32[]{:S(2)}) collective-permute-start(bf16[64,768]{1,0:T(8,128)(2,1)S(1)} %get-tuple-element.95), channel_id=1, source_target_pairs={{0,4},{1,5},{2,6},{3,7},{4,0},{5,1},{6,2},{7,3},{8,12},{9,13},{10,... | collective-permute-start | bytes 294920 | tf_op jit(solution)/shard_map/ppermute | solution.py:44
  59.1 7.5 %collective-permute-start.11 = (bf16[64,768]{1,0:T(8,128)(2,1)S(1)}, bf16[64,768]{1,0:T(8,128)(2,1)S(1)}, u32[]{:S(2)}, u32[]{:S(2)}) collective-permute-start(bf16[64,768]{1,0:T(8,128)(2,1)S(1)} %get-tuple-element.96), channel_id=1, source_target_pairs={{0,2},{1,3},{2,4},{3,5},{4,6},{5,7},{6,0},{7,1},{8,10},{9,11},{10,... | collective-permute-start | bytes 294920 | tf_op jit(solution)/shard_map/ppermute | solution.py:44
  67.2 5.7 %collective-permute-start.14 = (bf16[64,768]{1,0:T(8,128)(2,1)S(1)}, bf16[64,768]{1,0:T(8,128)(2,1)S(1)}, u32[]{:S(2)}, u32[]{:S(2)}) collective-permute-start(bf16[64,768]{1,0:T(8,128)(2,1)S(1)} %middle.2.h0), channel_id=1, source_target_pairs={{0,6},{1,7},{2,0},{3,1},{4,2},{5,3},{6,4},{7,5},{8,14},{9,15},{10,... | collective-permute-start | bytes 294920 | tf_op jit(solution)/shard_map/ppermute | solution.py:44
  67.8 6.9 %collective-permute-start.13 = (bf16[64,768]{1,0:T(8,128)(2,1)S(1)}, bf16[64,768]{1,0:T(8,128)(2,1)S(1)}, u32[]{:S(2)}, u32[]{:S(2)}) collective-permute-start(bf16[64,768]{1,0:T(8,128)(2,1)S(1)} %middle.2.h0), channel_id=1, source_target_pairs={{0,4},{1,5},{2,6},{3,7},{4,0},{5,1},{6,2},{7,3},{8,12},{9,13},{10,... | collective-permute-start | bytes 294920 | tf_op jit(solution)/shard_map/ppermute | solution.py:44
  68.5 7.1 %collective-permute-start.12 = (bf16[64,768]{1,0:T(8,128)(2,1)S(1)}, bf16[64,768]{1,0:T(8,128)(2,1)S(1)}, u32[]{:S(2)}, u32[]{:S(2)}) collective-permute-start(bf16[64,768]{1,0:T(8,128)(2,1)S(1)} %middle.2.h0), channel_id=1, source_target_pairs={{0,2},{1,3},{2,4},{3,5},{4,6},{5,7},{6,0},{7,1},{8,10},{9,11},{10,... | collective-permute-start | bytes 294920 | tf_op jit(solution)/shard_map/ppermute | solution.py:44
  76.8 16.1 %collective-permute-start.24 = (bf16[64,1792]{1,0:T(8,128)(2,1)S(1)}, bf16[64,1792]{1,0:T(8,128)(2,1)S(1)}, u32[]{:S(2)}, u32[]{:S(2)}) collective-permute-start(bf16[64,1792]{1,0:T(8,128)(2,1)S(1)} %get-tuple-element.115), channel_id=1, source_target_pairs={{0,24},{1,25},{2,26},{3,27},{4,28},{5,29},{6,30},{7,31},{8,0},{9,1... | collective-permute-start | bytes 688136 | tf_op jit(solution)/shard_map/ppermute | solution.py:44
  79.7 13.2 %collective-permute-start.23 = (bf16[64,1792]{1,0:T(8,128)(2,1)S(1)}, bf16[64,1792]{1,0:T(8,128)(2,1)S(1)}, u32[]{:S(2)}, u32[]{:S(2)}) collective-permute-start(bf16[64,1792]{1,0:T(8,128)(2,1)S(1)} %get-tuple-element.110), channel_id=1, source_target_pairs={{0,8},{1,9},{2,10},{3,11},{4,12},{5,13},{6,14},{7,15},{8,16},{9,17... | collective-permute-start | bytes 688136 | tf_op jit(solution)/shard_map/ppermute | solution.py:44
  81.3 4.9 %collective-permute-start.17 = (bf16[64,768]{1,0:T(8,128)(2,1)S(1)}, bf16[64,768]{1,0:T(8,128)(2,1)S(1)}, u32[]{:S(2)}, u32[]{:S(2)}) collective-permute-start(bf16[64,768]{1,0:T(8,128)(2,1)S(1)} %get-tuple-element.107), channel_id=1, source_target_pairs={{0,6},{1,7},{2,0},{3,1},{4,2},{5,3},{6,4},{7,5},{8,14},{9,15},{10,... | collective-permute-start | bytes 294920 | tf_op jit(solution)/shard_map/ppermute | solution.py:44
  82.5 6.3 %collective-permute-start.18 = (bf16[64,768]{1,0:T(8,128)(2,1)S(1)}, bf16[64,768]{1,0:T(8,128)(2,1)S(1)}, u32[]{:S(2)}, u32[]{:S(2)}) collective-permute-start(bf16[64,768]{1,0:T(8,128)(2,1)S(1)} %get-tuple-element.108), channel_id=1, source_target_pairs={{0,4},{1,5},{2,6},{3,7},{4,0},{5,1},{6,2},{7,3},{8,12},{9,13},{10,... | collective-permute-start | bytes 294920 | tf_op jit(solution)/shard_map/ppermute | solution.py:44
  83.4 6.5 %collective-permute-start.19 = (bf16[64,768]{1,0:T(8,128)(2,1)S(1)}, bf16[64,768]{1,0:T(8,128)(2,1)S(1)}, u32[]{:S(2)}, u32[]{:S(2)}) collective-permute-start(bf16[64,768]{1,0:T(8,128)(2,1)S(1)} %get-tuple-element.109), channel_id=1, source_target_pairs={{0,2},{1,3},{2,4},{3,5},{4,6},{5,7},{6,0},{7,1},{8,10},{9,11},{10,... | collective-permute-start | bytes 294920 | tf_op jit(solution)/shard_map/ppermute | solution.py:44
  90.4 4.9 %collective-permute-start.22 = (bf16[64,768]{1,0:T(8,128)(2,1)S(1)}, bf16[64,768]{1,0:T(8,128)(2,1)S(1)}, u32[]{:S(2)}, u32[]{:S(2)}) collective-permute-start(bf16[64,768]{1,0:T(8,128)(2,1)S(1)} %middle.3.h0), channel_id=1, source_target_pairs={{0,6},{1,7},{2,0},{3,1},{4,2},{5,3},{6,4},{7,5},{8,14},{9,15},{10,... | collective-permute-start | bytes 294920 | tf_op jit(solution)/shard_map/ppermute | solution.py:44
  91.6 6.2 %collective-permute-start.21 = (bf16[64,768]{1,0:T(8,128)(2,1)S(1)}, bf16[64,768]{1,0:T(8,128)(2,1)S(1)}, u32[]{:S(2)}, u32[]{:S(2)}) collective-permute-start(bf16[64,768]{1,0:T(8,128)(2,1)S(1)} %middle.3.h0), channel_id=1, source_target_pairs={{0,4},{1,5},{2,6},{3,7},{4,0},{5,1},{6,2},{7,3},{8,12},{9,13},{10,... | collective-permute-start | bytes 294920 | tf_op jit(solution)/shard_map/ppermute | solution.py:44
  92.5 6.3 %collective-permute-start.20 = (bf16[64,768]{1,0:T(8,128)(2,1)S(1)}, bf16[64,768]{1,0:T(8,128)(2,1)S(1)}, u32[]{:S(2)}, u32[]{:S(2)}) collective-permute-start(bf16[64,768]{1,0:T(8,128)(2,1)S(1)} %middle.3.h0), channel_id=1, source_target_pairs={{0,2},{1,3},{2,4},{3,5},{4,6},{5,7},{6,0},{7,1},{8,10},{9,11},{10,... | collective-permute-start | bytes 294920 | tf_op jit(solution)/shard_map/ppermute | solution.py:44
  102.2 3.4 %collective-permute-start.27 = (bf16[768,896]{1,0:T(8,128)(2,1)S(1)}, bf16[768,896]{1,0:T(8,128)(2,1)S(1)}, u32[]{:S(2)}, u32[]{:S(2)}) collective-permute-start(bf16[768,896]{1,0:T(8,128)(2,1)S(1)} %their_grad.1), channel_id=1, source_target_pairs={{0,1},{1,0},{2,3},{3,2},{4,5},{5,4},{6,7},{7,6},{8,9},{9,8},{10,11... | collective-permute-start | bytes 4128776 | tf_op jit(solution)/shard_map/ppermute | solution.py:44
  102.3 8.8 %collective-permute-start.26 = (bf16[64,1792]{1,0:T(8,128)(2,1)S(1)}, bf16[64,1792]{1,0:T(8,128)(2,1)S(1)}, u32[]{:S(2)}, u32[]{:S(2)}) collective-permute-start(bf16[64,1792]{1,0:T(8,128)(2,1)S(1)} %get-tuple-element.125), channel_id=1, source_target_pairs={{0,24},{1,25},{2,26},{3,27},{4,28},{5,29},{6,30},{7,31},{8,0},{9,1... | collective-permute-start | bytes 688136 | tf_op jit(solution)/shard_map/ppermute | solution.py:44
  105.6 8.9 %collective-permute-start.25 = (bf16[64,1792]{1,0:T(8,128)(2,1)S(1)}, bf16[64,1792]{1,0:T(8,128)(2,1)S(1)}, u32[]{:S(2)}, u32[]{:S(2)}) collective-permute-start(bf16[64,1792]{1,0:T(8,128)(2,1)S(1)} %get-tuple-element.124), channel_id=1, source_target_pairs={{0,8},{1,9},{2,10},{3,11},{4,12},{5,13},{6,14},{7,15},{8,16},{9,17... | collective-permute-start | bytes 688136 | tf_op jit(solution)/shard_map/ppermute | solution.py:44
  107.6 0.8 copy-start.1
  108.4 14.9 %collective-permute-start.30 = (bf16[192,896]{1,0:T(8,128)(2,1)S(1)}, bf16[192,896]{1,0:T(8,128)(2,1)S(1)}, u32[]{:S(2)}, u32[]{:S(2)}) collective-permute-start(bf16[192,896]{1,0:T(8,128)(2,1)S(1)} %get-tuple-element.135), channel_id=1, source_target_pairs={{0,6},{1,7},{2,0},{3,1},{4,2},{5,3},{6,4},{7,5},{8,14},{9,15},{10,... | collective-permute-start | bytes 1032200 | tf_op jit(solution)/shard_map/ppermute | solution.py:44
  109.5 13.8 %collective-permute-start.31 = (bf16[192,896]{1,0:T(8,128)(2,1)S(1)}, bf16[192,896]{1,0:T(8,128)(2,1)S(1)}, u32[]{:S(2)}, u32[]{:S(2)}) collective-permute-start(bf16[192,896]{1,0:T(8,128)(2,1)S(1)} %get-tuple-element.136), channel_id=1, source_target_pairs={{0,4},{1,5},{2,6},{3,7},{4,0},{5,1},{6,2},{7,3},{8,12},{9,13},{10,... | collective-permute-start | bytes 1032200 | tf_op jit(solution)/shard_map/ppermute | solution.py:44
  110.4 17.8 %collective-permute-start.32 = (bf16[192,896]{1,0:T(8,128)(2,1)S(1)}, bf16[192,896]{1,0:T(8,128)(2,1)S(1)}, u32[]{:S(2)}, u32[]{:S(2)}) collective-permute-start(bf16[192,896]{1,0:T(8,128)(2,1)S(1)} %get-tuple-element.137), channel_id=1, source_target_pairs={{0,2},{1,3},{2,4},{3,5},{4,6},{5,7},{6,0},{7,1},{8,10},{9,11},{10,... | collective-permute-start | bytes 1032200 | tf_op jit(solution)/shard_map/ppermute | solution.py:44
  115.1 8.1 %collective-permute-start.28 = (bf16[64,1792]{1,0:T(8,128)(2,1)S(1)}, bf16[64,1792]{1,0:T(8,128)(2,1)S(1)}, u32[]{:S(2)}, u32[]{:S(2)}) collective-permute-start(bf16[64,1792]{1,0:T(8,128)(2,1)S(1)} %get-tuple-element.133), channel_id=1, source_target_pairs={{0,8},{1,9},{2,10},{3,11},{4,12},{5,13},{6,14},{7,15},{8,16},{9,17... | collective-permute-start | bytes 688136 | tf_op jit(solution)/shard_map/ppermute | solution.py:44
  115.2 8.0 %collective-permute-start.29 = (bf16[64,1792]{1,0:T(8,128)(2,1)S(1)}, bf16[64,1792]{1,0:T(8,128)(2,1)S(1)}, u32[]{:S(2)}, u32[]{:S(2)}) collective-permute-start(bf16[64,1792]{1,0:T(8,128)(2,1)S(1)} %get-tuple-element.134), channel_id=1, source_target_pairs={{0,24},{1,25},{2,26},{3,27},{4,28},{5,29},{6,30},{7,31},{8,0},{9,1... | collective-permute-start | bytes 688136 | tf_op jit(solution)/shard_map/ppermute | solution.py:44
  123.3 10.0 %copy-start.6 = (bf16[192,896]{1,0:T(8,128)(2,1)}, bf16[192,896]{1,0:T(8,128)(2,1)S(1)}, u32[]{:S(2)}) copy-start(bf16[192,896]{1,0:T(8,128)(2,1)S(1)} %collective-permute-done.30.g1) | copy-start | bytes 1032196
  123.3 10.0 %copy-start.7 = (bf16[192,896]{1,0:T(8,128)(2,1)}, bf16[192,896]{1,0:T(8,128)(2,1)S(1)}, u32[]{:S(2)}) copy-start(bf16[192,896]{1,0:T(8,128)(2,1)S(1)} %collective-permute-done.31.g2) | copy-start | bytes 1032196
  128.3 5.0 %copy-start.8 = (bf16[192,896]{1,0:T(8,128)(2,1)}, bf16[192,896]{1,0:T(8,128)(2,1)S(1)}, u32[]{:S(2)}) copy-start(bf16[192,896]{1,0:T(8,128)(2,1)S(1)} %collective-permute-done.32.g3) | copy-start | bytes 1032196
  129.7 14.8 %all-to-all-start.1 = ((bf16[16,8,1792]{2,1,0:T(8,128)(2,1)}), bf16[16,8,1792]{2,1,0:T(8,128)(2,1)S(1)}, u32[]{:S(2)}, u32[]{:S(2)}) async-start(bf16[16,8,1792]{2,1,0:T(8,128)(2,1)} %sum_back.1), calls=%async_computation.1 | async-start | bytes 917504 | tf_op jit(solution)/shard_map/all_to_all | solution.py:344
  133.3 11.2 %copy-start.3 = (s32[4]{0:T(128)S(1)}, s32[4]{0:T(128)}, u32[]{:S(2)}) copy-start(s32[4]{0:T(128)} %copy-done.2) | copy-start | bytes 52
  133.3 11.2 %copy-start.4 = (bf16[32,128]{1,0:T(8,128)(2,1)S(1)}, bf16[32,128]{1,0:T(8,128)(2,1)}, u32[]{:S(2)}) copy-start(bf16[32,128]{1,0:T(8,128)(2,1)} %get-tuple-element.73.pick) | copy-start | bytes 24580

commit v3 on v2

--- a/solution.py
+++ b/solution.py
@@ -44,7 +44,7 @@
     return lax.ppermute(value, ("expert", "dp"), rotation(axis, step))
 
 
-def call(kernel, name, outs, place, *ins, flops=0, scratch=()):
+def call(kernel, name, outs, place, *ins, flops=0, scratch=(), own_copies=()):
     outs = [jax.ShapeDtypeStruct(s, t) for s, t in outs]
     size = sum(v.size * v.dtype.itemsize for v in (*ins, *outs))
     return pl.pallas_call(
@@ -53,7 +53,10 @@
         out_shape=outs,
         in_specs=[pl.BlockSpec(memory_space=pltpu.SMEM)]
         + [pl.BlockSpec(memory_space=pltpu.VMEM)] * len(ins),
-        out_specs=[pl.BlockSpec(memory_space=pltpu.VMEM)] * len(outs),
+        out_specs=[
+            pl.BlockSpec(memory_space=pl.ANY if i in own_copies else pltpu.VMEM)
+            for i in range(len(outs))
+        ],
         scratch_shapes=list(scratch),
         cost_estimate=pl.CostEstimate(flops=flops, bytes_accessed=size, transcendentals=0),
         compiler_params=pltpu.CompilerParams(vmem_limit_bytes=VMEM_LIMIT),
@@ -237,71 +240,86 @@
     out[:, 2 * width :] = (act * up).astype(BF)
 
 
-def back_kernel(place, h0, h1, h2, h3, own, other, held, *outs):
-    y, c = place[2], place[3]
+def back_kernel(place, held, own, other, a0, b0, a1, b3, minus, plus):
+    c = place[3]
     width = 2 * N * HID
-    for k, h in enumerate((h0, h1, h2, h3)):
-        at = wrap(y - k) * ROWS
-        for s in range(2):
-            rows = pl.ds(pl.multiple_of(s * GROUPED + at, ROWS), ROWS)
-            held[rows, :] = h[s * ROWS : (s + 1) * ROWS]
     h = held[:, :width]
+    low, high = slice(0, HELD), slice(HELD, 2 * HELD)
+    targets = ((a0, low), (b0, low), (a1, low), (b3, low))
+    targets += ((minus, low), (plus, low), (plus, high), (minus, high))
     for w, half in ((own, c), (other, 1 - c)):
         cols = pl.ds(aligned(half * EIGHTH), EIGHTH)
         part = mm(h, w[:width], NN)
-        for i, o in enumerate(outs):
-            o[:, cols] = part[i * HELD : (i + 1) * HELD].astype(BF)
+        for i, (o, rows) in enumerate(targets):
+            o[rows, cols] = part[i * HELD : (i + 1) * HELD].astype(BF)
 
 
 def pass_on_kernel(place, own_a, own_b, got_a, got_b, out_a, out_b):
-    out_a[...] = (own_a[...].astype(F32) + got_a[...].astype(F32)).astype(BF)
-    out_b[...] = (own_b[...].astype(F32) + got_b[...].astype(F32)).astype(BF)
-
-
-def weight_grad(half, h1, h2, chunks, out):
+    out_a[...] = (own_a[...].astype(F32) + got_a[:HELD].astype(F32)).astype(BF)
+    out_b[...] = (own_b[...].astype(F32) + got_b[:HELD].astype(F32)).astype(BF)
+
+
+def weight_grad(half, held, chunks, out):
     pieces = (*pieces_of(chunks[:4]), *pieces_of(chunks[4:]))
     width = 2 * N * HID
     cols = pl.ds(aligned(half * EIGHTH), EIGHTH)
-    hs = jnp.concatenate([h1[...], h2[...]], axis=0)
     x = jnp.concatenate([v[:HELD, cols] for v in pieces], axis=0)
-    out[:width] = mm(hs[:, :width], x, TN).astype(out.dtype)
+    out[:width] = mm(held[:, :width], x, TN).astype(out.dtype)
     g = jnp.concatenate([v[HELD : 2 * HELD, cols] for v in pieces], axis=0)
-    out[width:] = mm(hs[:, width:], g, TN).astype(out.dtype)
-
-
-def their_grad_kernel(place, h1, h2, *refs):
-    *chunks, out = refs
-    weight_grad(1 - place[3], h1, h2, chunks, out)
-
-
-def my_grad_kernel(place, got, h1, h2, *refs):
+    out[width:] = mm(held[:, width:], g, TN).astype(out.dtype)
+
+
+def their_grad_kernel(place, *refs):
+    parts = refs[:N], refs[N : 2 * N]
+    *chunks, held, o0, o1, o2, theirs = refs[2 * N :]
+    y = place[2]
+    for i, chunk in enumerate(parts):
+        for k, h in enumerate(chunk):
+            at = wrap(y - k) * ROWS
+            for s in range(2):
+                rows = pl.ds(pl.multiple_of(i * CHUNK + s * GROUPED + at, ROWS), ROWS)
+                held[rows, :] = h[s * ROWS : (s + 1) * ROWS]
+    weight_grad(1 - place[3], held, chunks, theirs)
+    for i, o in enumerate((o0, o1, o2)):
+        o[...] = theirs[i * N * HID : (i + 1) * N * HID]
+
+
+def my_grad_kernel(place, got0, got1, got2, held, *refs):
     *chunks, o0, o1, o2, o3, mine = refs
     y = place[2]
-    weight_grad(place[3], h1, h2, chunks, mine)
+    weight_grad(place[3], held, chunks, mine)
     for k, o in enumerate((o0, o1, o2, o3)):
-        block = wrap(y - k)
-        for part in range(3):
-            rows = pl.ds(pl.multiple_of(part * N * HID + block * HID, HID), HID)
-            total = mine[rows, :] + got[rows, :].astype(F32)
+        block = pl.multiple_of(wrap(y - k) * HID, HID)
+        for part, got in enumerate((got0, got1, got2)):
+            own = mine[pl.ds(pl.multiple_of(part * N * HID + block, HID), HID), :]
+            total = own + got[pl.ds(block, HID), :].astype(F32)
             o[part * HID : (part + 1) * HID] = total.astype(o.dtype)
 
 
-def sum_back_kernel(place, own_a, own_b, got_a, got_b, out):
-    for h, (own, got) in enumerate(((own_a, got_a), (own_b, got_b))):
-        total = own[...].astype(F32) + got[...].astype(F32)
+def sum_back_kernel(place, a0, b0, a1, b3, got_minus, got_plus, out):
+    for h, (i, j, k) in enumerate(((a0, a1, got_plus), (b0, b3, got_minus))):
+        total = i[...].astype(F32) + (j[...].astype(F32) + k[HELD:].astype(F32))
         for s in range(2):
             for x in range(N):
                 at = s * ROWS + x * SLOT
                 out[x * N + 2 * h + s] = total[at : at + SLOT].astype(BF)
 
 
-def combine_kernel(place, pick, got, out):
+def combine_kernel(place, pick, got, out, sums, sems):
+    copies = []
     for q in range(N):
         rows = jnp.concatenate([got[e * N + q].astype(F32) for e in range(N)], axis=0)
-        total = mm(pick[...], rows.astype(BF), TN).astype(BF)
+        sums[q] = mm(pick[...], rows.astype(BF), TN).astype(BF)
         for c in range(2):
-            at = c * HALF + q * EIGHTH
-            out[:, at : at + EIGHTH] = total[:, c * EIGHTH : (c + 1) * EIGHTH]
+            copy = pltpu.make_async_copy(
+                sums.at[q, :, pl.ds(c * EIGHTH, EIGHTH)],
+                out.at[:, pl.ds(c * HALF + q * EIGHTH, EIGHTH)],
+                sems.at[q * 2 + c],
+            )
+            copy.start()
+            copies.append(copy)
+    for copy in copies:
+        copy.wait()
 
 
 def moments_kernel(place, g0, g1, g2, g3, one, two, new_one, new_two):
@@ -355,14 +373,14 @@
     return lax.optimization_barrier((values, earlier))[0]
 
 
-def add(place, own_a, own_b, got_a, got_b):
+def pass_on(place, *parts):
     half = ((HELD, QUARTER), BF)
-    return call(pass_on_kernel, "pass_on", [half] * 2, place, own_a, own_b, got_a, got_b)
-
-
-def middle_part(place, chunk, w_own, w_other, *earlier):
+    return call(pass_on_kernel, "pass_on", [half] * 2, place, *parts)
+
+
+def forward_part(place, chunk, w_own, w_other):
     width = 3 * N * HID
-    part = call(
+    return call(
         forward_kernel,
         "forward",
         [((HELD, width), F32)] + [((HELD, width), BF)] * 3,
@@ -373,21 +391,22 @@
         flops=2 * CHUNK * QUARTER * width,
         scratch=[pltpu.VMEM((CHUNK, width), F32)],
     )
-    part = after(spread(part, "y", -1), *earlier)
-    (held,) = call(middle_kernel, "middle", [((HELD, width), BF)], place, *part)
-    return held
+
+
+def middle_part(place, part):
+    return call(middle_kernel, "middle", [((HELD, 3 * N * HID), BF)], place, *part)[0]
 
 
 def back_part(place, held, w_own, w_other):
     return call(
         back_kernel,
         "back",
-        [((CHUNK, 3 * N * HID), BF)] + [((HELD, QUARTER), BF)] * 4,
-        place,
-        *held,
+        [((HELD, QUARTER), BF)] * 4 + [((2 * HELD, QUARTER), BF)] * 2,
+        place,
+        held,
         w_own,
         w_other,
-        flops=4 * CHUNK * QUARTER * N * HID,
+        flops=8 * CHUNK * QUARTER * N * HID,
     )
 
 
@@ -409,7 +428,7 @@
         place,
         expert_weights,
     )
-    w_parts = spread(after(w_columns, got), "y")
+    w_parts = spread(w_columns, "y")
     got = after(got, w_columns[1])
     a0, b0 = call(pair_kernel, "pair", [((GROUPED, QUARTER), BF)] * 2, place, got)
     a1, b3 = turn(a0, "z", 1), turn(b0, "z", -1)
@@ -429,47 +448,48 @@
         *w_others,
     )
 
-    mid_one = middle_part(place, first, w_own, w_other)
+    part_one = forward_part(place, first, w_own, w_other)
+    part_one = spread(part_one, "y", -1)
+    part_two = forward_part(place, second, w_own, w_other)
+    part_one = after(part_one, part_two[1])
+    part_two = spread(part_two, "y", -1)
+    mid_one = middle_part(place, part_one)
     held_one = spread([mid_one] * N, "y")
-    held_one, r_a0, r_b0, r_a1, r_b3 = back_part(place, held_one, w_own, w_other)
-    got_a, got_b = turn(r_a1, "z", 1), turn(r_b3, "z", -1)
-    second = after(second, mid_one)
-    held_two = middle_part(place, second, w_own, w_other, r_a1)
-    held_two = after(spread([held_two] * N, "y"), got_a, got_b)
-    held_two, r_a2, r_b2, r_a3, r_b1 = back_part(place, held_two, w_own, w_other)
-    got_a, got_b = add(place, r_a2, r_b2, got_a, got_b)
-    held = after((held_one, held_two), got_a)
-    got_a, got_b = turn(got_a, "z", 1), turn(got_b, "z", -1)
+    mid_two = middle_part(place, part_two)
+    held_two = spread([mid_two] * N, "y")
     flops = N * GROUPED * QUARTER * 3 * width
-    (grad_theirs,) = call(
+    held, *theirs = call(
         their_grad_kernel,
         "their_grad",
-        [((3 * width, EIGHTH), BF)],
-        place,
-        *held,
+        [((2 * CHUNK, 3 * width), BF)] + [((width, EIGHTH), BF)] * 3,
+        place,
+        *held_one,
+        *held_two,
         *first,
         *second,
         flops=flops,
-    )
-    grad_got = turn(grad_theirs, "c", 1)
+        scratch=[pltpu.VMEM((3 * width, EIGHTH), BF)],
+    )
+    a0, b0, a1, b3, minus, plus = back_part(place, held, w_own, w_other)
+    got_minus, got_plus = turn(minus, "z", -1), turn(plus, "z", 1)
+    got = [turn(v, "c", 1) for v in theirs]
     blocks = call(
         my_grad_kernel,
         "my_grad",
         [((block_rows, EIGHTH), F32)] + [((block_rows, EIGHTH), BF)] * 3,
         place,
-        grad_got,
-        *held,
+        *got,
+        after(held, a1),
         *first,
         *second,
         flops=flops,
         scratch=[pltpu.VMEM((3 * width, EIGHTH), F32)],
     )
-    got_a, got_b = after((got_a, got_b), blocks[0])
-    got_a, got_b = add(place, r_a3, r_b1, got_a, got_b)
-    got_a, got_b = turn(got_a, "z", 1), turn(got_b, "z", -1)
+    a1, b3 = pass_on(place, *after((a1, b3, got_minus, got_plus), blocks[0]))
+    a1, b3 = turn(a1, "z", -1), turn(b3, "z", 1)
     blocks = spread(blocks, "y", -1)
-    got_a, got_b = after((got_a, got_b), *blocks)
-    (back,) = call(sum_back_kernel, "sum_back", [slots], place, r_a0, r_b0, got_a, got_b)
+    parts = after((a0, b0, a1, b3, got_minus, got_plus), *blocks)
+    (back,) = call(sum_back_kernel, "sum_back", [slots], place, *parts)
     back = exchange(back, "xy")
     new_one, new_two = moments(place, blocks, moment_one, moment_two)
     back = after(back, new_one)
@@ -481,6 +501,8 @@
         pick,
         back,
         flops=2 * ROWS * tok * D,
+        scratch=[pltpu.VMEM((N, tok, QUARTER), BF), pltpu.SemaphoreType.DMA((2 * N,))],
+        own_copies=(0,),
     )
     return grad_tokens, new_one, new_two
 

time: 147 us -> 135 us (0.918)
  waiting for transfers between devices: 72.1 us -> 59.2 us
  Pallas kernels: 28.6 us -> 27.1 us
  starting transfers between devices: 43.5 us -> 45 us
    ppermute x33, waiting for transfers between devices: 53.4 us -> 40.5 us  [turn(): return lax.ppermute(value, ('expert', 'dp'), rotation(axis, step))]
    pallas_call x16 -> x14, Pallas kernels: 18.2 us -> 16.7 us  [call(): pl.pallas_call(kernel, name=name, out_shape=outs, in_specs=[pl.BlockSpec(...]
  transfers between devices with their start and end apart: 35 -> 35, of which waited for: 25 -> 23; matrix products, arithmetic and copies ran while one was open for 0% -> 0% of each run, Pallas kernels for 12% -> 13%
where the time goes in v3:
time: 135 us; the launch traced here: 134 us
  waiting for transfers between devices  59.2 us (44%)
  starting transfers between devices  45 us (33%)
  Pallas kernels  27.1 us (20%)
  local copies, waits for them, and re-layouts  1.6 us (1%)
    ppermute x33, waiting for transfers between devices, turn(): return lax.ppermute(value, ('expert', 'dp'), rotation(axis, step))  40.5 us
    ppermute x33, starting transfers between devices, turn(): return lax.ppermute(value, ('expert', 'dp'), rotation(axis, step))  34.2 us
    all_to_all x2, waiting for transfers between devices, exchange(): lax.all_to_all(value, 'expert', 0, 0, axis_index_groups=list(groups.value...  18.8 us
    pallas_call x14, Pallas kernels, call(): pl.pallas_call(kernel, name=name, out_shape=outs, in_specs=[pl.BlockSpec(...  16.7 us
    all_to_all x2, starting transfers between devices, exchange(): lax.all_to_all(value, 'expert', 0, 0, axis_index_groups=list(groups.value...  10.8 us
    pallas_call x1, Pallas kernels, moments(): pl.pallas_call(moments_kernel, name='moments', grid_spec=pltpu.PrefetchSc...  6.9 us
    pallas_call x1, Pallas kernels, route(): pl.pallas_call(route_kernel, name='route', in_specs=[hbm] * 4, out_specs=...  3.5 us
  transfers between devices with their start and end apart: 35, of which 23 were waited for; matrix products, arithmetic and copies ran while one was open for 0% of the time, Pallas kernels for 13%

profile of v3, /device:TPU:0, one launch (start us, length us, event | category | flops | bytes accessed | tf_op | source)
XLA Modules:
  0.0 134.1 jit_solution(7769934239548048033)
XLA Ops:
  0.6 3.5 %route.1 = (bf16[16,16,1792]{2,1,0:T(8,128)(2,1)}, bf16[32,128]{1,0:T(8,128)(2,1)}) custom-call(s32[8,128]{1,0:T(8,128)} %bitcast.6, f32[8,128]{1,0:T(8,128)} %bitcast.7, bf16[128,7168]{1,0:T(8,128)(2,1)} %tokens.1, bf16[128,7168]{1,0:T(8,128)(2,1)} %grads.1), custom_call_target="tpu_custom_call" | custom-call | flops 117440512 | bytes 5505024 | tf_op jit(solution)/shard_map/route/pallas_call | solution.py:143
  4.2 7.3 %all-to-all-start = ((bf16[16,16,1792]{2,1,0:T(8,128)(2,1)}), bf16[16,16,1792]{2,1,0:T(8,128)(2,1)S(1)}, u32[]{:S(2)}, u32[]{:S(2)}) async-start(bf16[16,16,1792]{2,1,0:T(8,128)(2,1)} %get-tuple-element.63), calls=%async_computation | async-start | bytes 1835008 | tf_op jit(solution)/shard_map/all_to_all | solution.py:362
  12.9 14.5 %all-to-all-done.got = bf16[16,16,1792]{2,1,0:T(8,128)(2,1)S(1)} async-done(((bf16[16,16,1792]{2,1,0:T(8,128)(2,1)}), bf16[16,16,1792]{2,1,0:T(8,128)(2,1)S(1)}, u32[]{:S(2)}, u32[]{:S(2)}) %all-to-all-start) | async-done | bytes 917536 | tf_op jit(solution)/shard_map/all_to_all | solution.py:362
  28.1 2.0 %collective-permute-start = (bf16[128,1792]{1,0:T(8,128)(2,1)S(1)}, bf16[128,1792]{1,0:T(8,128)(2,1)S(1)}, u32[]{:S(2)}, u32[]{:S(2)}) collective-permute-start(bf16[128,1792]{1,0:T(8,128)(2,1)S(1)} %get-tuple-element.66.a0.refs_0_.refs_8_), channel_id=1, source_target_pairs={{0,8},{1,9},{2,10},{3,11},{4,12},{5,13},{6,14},{7,15},{8,16},{9,17... | collective-permute-start | bytes 1376264 | tf_op jit(solution)/shard_map/ppermute | solution.py:44
  30.0 2.2 %collective-permute-start.1 = (bf16[128,1792]{1,0:T(8,128)(2,1)S(1)}, bf16[128,1792]{1,0:T(8,128)(2,1)S(1)}, u32[]{:S(2)}, u32[]{:S(2)}) collective-permute-start(bf16[128,1792]{1,0:T(8,128)(2,1)S(1)} %get-tuple-element.67.b0.refs_1_.refs_9_), channel_id=1, source_target_pairs={{0,24},{1,25},{2,26},{3,27},{4,28},{5,29},{6,30},{7,31},{8,0},{9,1... | collective-permute-start | bytes 1376264 | tf_op jit(solution)/shard_map/ppermute | solution.py:44
  32.2 0.9 collective-permute-start.3
  33.1 2.4 %collective-permute-start.4 = (bf16[192,896]{1,0:T(8,128)(2,1)S(1)}, bf16[192,896]{1,0:T(8,128)(2,1)S(1)}, u32[]{:S(2)}, u32[]{:S(2)}) collective-permute-start(bf16[192,896]{1,0:T(8,128)(2,1)S(1)} %get-tuple-element.70), channel_id=1, source_target_pairs={{0,6},{1,7},{2,0},{3,1},{4,2},{5,3},{6,4},{7,5},{8,14},{9,15},{10,... | collective-permute-start | bytes 1032200 | tf_op jit(solution)/shard_map/ppermute | solution.py:44
  35.5 4.9 %collective-permute-done.a1.refs_2_.refs_10_ = bf16[128,1792]{1,0:T(8,128)(2,1)S(1)} collective-permute-done((bf16[128,1792]{1,0:T(8,128)(2,1)S(1)}, bf16[128,1792]{1,0:T(8,128)(2,1)S(1)}, u32[]{:S(2)}, u32[]{:S(2)}) %collective-permute-start) | collective-permute-done | bytes 458784 | tf_op jit(solution)/shard_map/ppermute | solution.py:44
  41.1 3.1 %collective-permute-start.13 = (bf16[256,1792]{1,0:T(8,128)(2,1)S(1)}, bf16[256,1792]{1,0:T(8,128)(2,1)S(1)}, u32[]{:S(2)}, u32[]{:S(2)}) collective-permute-start(bf16[256,1792]{1,0:T(8,128)(2,1)S(1)} %get-tuple-element.82), channel_id=1, source_target_pairs={{0,24},{1,25},{2,26},{3,27},{4,28},{5,29},{6,30},{7,31},{8,0},{9,1... | collective-permute-start | bytes 2752520 | tf_op jit(solution)/shard_map/ppermute | solution.py:44
  44.9 2.9 %collective-permute-done.4.refs_3_ = bf16[192,896]{1,0:T(8,128)(2,1)S(1)} collective-permute-done((bf16[192,896]{1,0:T(8,128)(2,1)S(1)}, bf16[192,896]{1,0:T(8,128)(2,1)S(1)}, u32[]{:S(2)}, u32[]{:S(2)}) %collective-permute-start.4) | collective-permute-done | bytes 344096 | tf_op jit(solution)/shard_map/ppermute | solution.py:44
  47.8 0.8 collective-permute-done.2.refs_1_
  49.1 1.1 collective-permute-done.5.refs_4_
  51.9 0.8 stack_weights.1
  52.7 1.6 %forward.2 = (f32[64,768]{1,0:T(8,128)S(1)}, bf16[64,768]{1,0:T(8,128)(2,1)S(1)}, bf16[64,768]{1,0:T(8,128)(2,1)S(1)}, bf16[64,768]{1,0:T(8,128)(2,1)S(1)}) custom-call(s32[4]{0:T(128)S(1)} %pad_add_fusion.place, bf16[128,1792]{1,0:T(8,128)(2,1)S(1)} %get-tuple-element.66.a0.refs_0_.refs_8_, bf16[128,1792]{1,0:T(8,128)(2,1)S(1)} %get-tuple-element.67.b0.refs_1_.refs_9_, ...), custom_call_target="tpu_custom_call" | custom-call | flops 704643072 | bytes 5079040 | tf_op jit(solution)/shard_map/forward/pallas_call | solution.py:50
  54.3 1.9 %collective-permute-start.9 = (bf16[64,768]{1,0:T(8,128)(2,1)S(1)}, bf16[64,768]{1,0:T(8,128)(2,1)S(1)}, u32[]{:S(2)}, u32[]{:S(2)}) collective-permute-start(bf16[64,768]{1,0:T(8,128)(2,1)S(1)} %get-tuple-element.79), channel_id=1, source_target_pairs={{0,6},{1,7},{2,0},{3,1},{4,2},{5,3},{6,4},{7,5},{8,14},{9,15},{10,... | collective-permute-start | bytes 294920 | tf_op jit(solution)/shard_map/ppermute | solution.py:44
  56.2 0.8 collective-permute-start.10
  57.6 3.0 %collective-permute-done.13.refs_1_.refs_13_.refs_5_ = bf16[256,1792]{1,0:T(8,128)(2,1)S(1)} collective-permute-done((bf16[256,1792]{1,0:T(8,128)(2,1)S(1)}, bf16[256,1792]{1,0:T(8,128)(2,1)S(1)}, u32[]{:S(2)}, u32[]{:S(2)}) %collective-permute-start.13) | collective-permute-done | bytes 917536 | tf_op jit(solution)/shard_map/ppermute | solution.py:44
  60.6 3.4 %collective-permute-done.12.refs_0_.refs_12_.refs_4_ = bf16[256,1792]{1,0:T(8,128)(2,1)S(1)} collective-permute-done((bf16[256,1792]{1,0:T(8,128)(2,1)S(1)}, bf16[256,1792]{1,0:T(8,128)(2,1)S(1)}, u32[]{:S(2)}, u32[]{:S(2)}) %collective-permute-start.12) | collective-permute-done | bytes 917536 | tf_op jit(solution)/shard_map/ppermute | solution.py:44
  64.0 1.6 %forward.3 = (f32[64,768]{1,0:T(8,128)S(1)}, bf16[64,768]{1,0:T(8,128)(2,1)S(1)}, bf16[64,768]{1,0:T(8,128)(2,1)S(1)}, bf16[64,768]{1,0:T(8,128)(2,1)S(1)}) custom-call(s32[4]{0:T(128)S(1)} %pad_add_fusion.place, bf16[256,1792]{1,0:T(8,128)(2,1)S(1)} %collective-permute-done.12.refs_0_.refs_12_.refs_4_, ...), custom_call_target="tpu_custom_call" | custom-call | flops 704643072 | bytes 5079040 | tf_op jit(solution)/shard_map/forward/pallas_call | solution.py:50
  65.6 3.5 %collective-permute-start.17 = (bf16[64,768]{1,0:T(8,128)(2,1)S(1)}, bf16[64,768]{1,0:T(8,128)(2,1)S(1)}, u32[]{:S(2)}, u32[]{:S(2)}) collective-permute-start(bf16[64,768]{1,0:T(8,128)(2,1)S(1)} %get-tuple-element.83), channel_id=1, source_target_pairs={{0,6},{1,7},{2,0},{3,1},{4,2},{5,3},{6,4},{7,5},{8,14},{9,15},{10,... | collective-permute-start | bytes 294920 | tf_op jit(solution)/shard_map/ppermute | solution.py:44
  69.2 0.9 collective-permute-start.19
  70.7 2.5 %collective-permute-start.16 = (bf16[64,768]{1,0:T(8,128)(2,1)S(1)}, bf16[64,768]{1,0:T(8,128)(2,1)S(1)}, u32[]{:S(2)}, u32[]{:S(2)}) collective-permute-start(bf16[64,768]{1,0:T(8,128)(2,1)S(1)} %middle.2.refs_0_), channel_id=1, source_target_pairs={{0,6},{1,7},{2,0},{3,1},{4,2},{5,3},{6,4},{7,5},{8,14},{9,15},{10,... | collective-permute-start | bytes 294920 | tf_op jit(solution)/shard_map/ppermute | solution.py:44
  73.2 2.2 %collective-permute-start.15 = (bf16[64,768]{1,0:T(8,128)(2,1)S(1)}, bf16[64,768]{1,0:T(8,128)(2,1)S(1)}, u32[]{:S(2)}, u32[]{:S(2)}) collective-permute-start(bf16[64,768]{1,0:T(8,128)(2,1)S(1)} %middle.2.refs_0_), channel_id=1, source_target_pairs={{0,4},{1,5},{2,6},{3,7},{4,0},{5,1},{6,2},{7,3},{8,12},{9,13},{10,... | collective-permute-start | bytes 294920 | tf_op jit(solution)/shard_map/ppermute | solution.py:44
  75.4 0.9 collective-permute-done.18.p2
  76.3 1.3 collective-permute-done.19.p3
  78.2 2.0 %collective-permute-start.22 = (bf16[64,768]{1,0:T(8,128)(2,1)S(1)}, bf16[64,768]{1,0:T(8,128)(2,1)S(1)}, u32[]{:S(2)}, u32[]{:S(2)}) collective-permute-start(bf16[64,768]{1,0:T(8,128)(2,1)S(1)} %middle.3.refs_4_), channel_id=1, source_target_pairs={{0,6},{1,7},{2,0},{3,1},{4,2},{5,3},{6,4},{7,5},{8,14},{9,15},{10,... | collective-permute-start | bytes 294920 | tf_op jit(solution)/shard_map/ppermute | solution.py:44
  80.3 0.9 collective-permute-start.20
  81.2 1.3 collective-permute-done.14.refs_1_
  82.5 1.0 collective-permute-done.22.refs_7_
  83.5 3.0 %collective-permute-done.21.refs_6_ = bf16[64,768]{1,0:T(8,128)(2,1)S(1)} collective-permute-done((bf16[64,768]{1,0:T(8,128)(2,1)S(1)}, bf16[64,768]{1,0:T(8,128)(2,1)S(1)}, u32[]{:S(2)}, u32[]{:S(2)}) %collective-permute-start.21) | collective-permute-done | bytes 98336 | tf_op jit(solution)/shard_map/ppermute | solution.py:44
  87.1 1.7 %their_grad.1 = (bf16[512,768]{1,0:T(8,128)(2,1)S(1)}, bf16[256,896]{1,0:T(8,128)(2,1)S(1)}, bf16[256,896]{1,0:T(8,128)(2,1)S(1)}, bf16[256,896]{1,0:T(8,128)(2,1)S(1)}) custom-call(s32[4]{0:T(128)S(1)} %pad_add_fusion.place, bf16[64,768]{1,0:T(8,128)(2,1)S(1)} %middle.2.refs_0_, bf16[64,768]{1,0:T(8,128)(2,1)S(1)} %collective-permute-done.14.refs_1_, ...), custom_call_target="tpu_custom_call" | custom-call | flops 704643072 | bytes 6619136 | tf_op jit(solution)/shard_map/their_grad/pallas_call | solution.py:50
  89.5 1.8 %back.1 = (bf16[64,1792]{1,0:T(8,128)(2,1)S(1)}, bf16[64,1792]{1,0:T(8,128)(2,1)S(1)}, bf16[64,1792]{1,0:T(8,128)(2,1)S(1)}, bf16[64,1792]{1,0:T(8,128)(2,1)S(1)...) custom-call(s32[4]{0:T(128)S(1)} %pad_add_fusion.place, bf16[512,768]{1,0:T(8,128)(2,1)S(1)} %get-tuple-element.101.held, ...), custom_call_target="tpu_custom_call" | custom-call | flops 939524096 | bytes 5373952 | tf_op jit(solution)/shard_map/back/pallas_call | solution.py:50
  91.6 1.8 %collective-permute-start.24 = (bf16[128,1792]{1,0:T(8,128)(2,1)S(1)}, bf16[128,1792]{1,0:T(8,128)(2,1)S(1)}, u32[]{:S(2)}, u32[]{:S(2)}) collective-permute-start(bf16[128,1792]{1,0:T(8,128)(2,1)S(1)} %get-tuple-element.97), channel_id=1, source_target_pairs={{0,8},{1,9},{2,10},{3,11},{4,12},{5,13},{6,14},{7,15},{8,16},{9,17... | collective-permute-start | bytes 1376264 | tf_op jit(solution)/shard_map/ppermute | solution.py:44
  93.4 2.0 %my_grad.1 = (f32[192,896]{1,0:T(8,128)S(1)}, bf16[192,896]{1,0:T(8,128)(2,1)S(1)}, bf16[192,896]{1,0:T(8,128)(2,1)S(1)}, bf16[192,896]{1,0:T(8,128)(2,1)S(1)}) custom-call(s32[4]{0:T(128)S(1)} %pad_add_fusion.place, bf16[256,896]{1,0:T(8,128)(2,1)S(1)} %collective-permute-done.25.got0, bf16[256,896]{1,0:T(8,128)(2,1)S(1)} %collective-permute-done.26.got1, ...), custom_call_target="tpu_custom_call" | custom-call | flops 704643072 | bytes 7553024 | tf_op jit(solution)/shard_map/my_grad/pallas_call | solution.py:50
  95.4 0.8 copy-done.1
  96.2 0.9 collective-permute-start.30
  97.6 1.3 collective-permute-start.32
  98.9 5.3 %collective-permute-done.23.got_a.got_minus = bf16[128,1792]{1,0:T(8,128)(2,1)S(1)} collective-permute-done((bf16[128,1792]{1,0:T(8,128)(2,1)S(1)}, bf16[128,1792]{1,0:T(8,128)(2,1)S(1)}, u32[]{:S(2)}, u32[]{:S(2)}) %collective-permute-start.23) | collective-permute-done | bytes 458784 | tf_op jit(solution)/shard_map/ppermute | solution.py:44
  104.2 1.3 collective-permute-done.24.got_b.got_plus
  106.5 1.8 %collective-permute-start.29 = (bf16[64,1792]{1,0:T(8,128)(2,1)S(1)}, bf16[64,1792]{1,0:T(8,128)(2,1)S(1)}, u32[]{:S(2)}, u32[]{:S(2)}) collective-permute-start(bf16[64,1792]{1,0:T(8,128)(2,1)S(1)} %get-tuple-element.108), channel_id=1, source_target_pairs={{0,8},{1,9},{2,10},{3,11},{4,12},{5,13},{6,14},{7,15},{8,16},{9,17... | collective-permute-start | bytes 688136 | tf_op jit(solution)/shard_map/ppermute | solution.py:44
  108.3 4.9 %collective-permute-done.28.a1 = bf16[64,1792]{1,0:T(8,128)(2,1)S(1)} collective-permute-done((bf16[64,1792]{1,0:T(8,128)(2,1)S(1)}, bf16[64,1792]{1,0:T(8,128)(2,1)S(1)}, u32[]{:S(2)}, u32[]{:S(2)}) %collective-permute-start.28) | collective-permute-done | bytes 229408 | tf_op jit(solution)/shard_map/ppermute | solution.py:44
  113.2 1.4 %collective-permute-done.29.b3 = bf16[64,1792]{1,0:T(8,128)(2,1)S(1)} collective-permute-done((bf16[64,1792]{1,0:T(8,128)(2,1)S(1)}, bf16[64,1792]{1,0:T(8,128)(2,1)S(1)}, u32[]{:S(2)}, u32[]{:S(2)}) %collective-permute-start.29) | collective-permute-done | bytes 229408 | tf_op jit(solution)/shard_map/ppermute | solution.py:44
  114.6 1.0 collective-permute-done.32.g3
  115.6 1.5 %sum_back.1 = bf16[16,8,1792]{2,1,0:T(8,128)(2,1)} custom-call(s32[4]{0:T(128)S(1)} %pad_add_fusion.place, bf16[64,1792]{1,0:T(8,128)(2,1)S(1)} %get-tuple-element.112.a0, bf16[64,1792]{1,0:T(8,128)(2,1)S(1)} %get-tuple-element.113.b0, bf16[64,1792]{1,0:T(8,128)(2,1)S(1)} %collective-permute-done.28.a1, bf16[64,1792]{1,0:T(8,128)(2,1)S(1)} %collective-permute-done.29.b3, ...), custom_call_target="tpu_custom_call" | custom-call | bytes 2293760 | tf_op jit(solution)/shard_map/sum_back/pallas_call | solution.py:50
  117.0 3.6 %all-to-all-start.1 = ((bf16[16,8,1792]{2,1,0:T(8,128)(2,1)}), bf16[16,8,1792]{2,1,0:T(8,128)(2,1)S(1)}, u32[]{:S(2)}, u32[]{:S(2)}) async-start(bf16[16,8,1792]{2,1,0:T(8,128)(2,1)} %sum_back.1), calls=%async_computation.1 | async-start | bytes 917504 | tf_op jit(solution)/shard_map/all_to_all | solution.py:362
  120.7 6.9 %moments.1 = (f32[1,192,3584]{2,1,0:T(8,128)}, f32[1,192,3584]{2,1,0:T(8,128)}) custom-call(s32[4]{0:T(128)} %copy-done.2, f32[192,896]{1,0:T(8,128)} %copy-done.1, bf16[192,896]{1,0:T(8,128)(2,1)} %copy-done.6, bf16[192,896]{1,0:T(8,128)(2,1)} %copy-done.7, bf16[192,896]{1,0:T(8,128)(2,1)} %copy-done.8, f32[1,192,3584]{2,1,0:T(8,128)} %one.1, ...), custom_call_target="tpu_custom_call" | custom-call | flops 4128768 | bytes 11698176 | tf_op jit(solution)/shard_map/moments/pallas_call | solution.py:340
  127.6 4.3 %all-to-all-done.1.got = bf16[16,8,1792]{2,1,0:T(8,128)(2,1)S(1)} async-done(((bf16[16,8,1792]{2,1,0:T(8,128)(2,1)}), bf16[16,8,1792]{2,1,0:T(8,128)(2,1)S(1)}, u32[]{:S(2)}, u32[]{:S(2)}) %all-to-all-start.1) | async-done | bytes 458784 | tf_op jit(solution)/shard_map/all_to_all | solution.py:362
  131.8 2.1 %combine.1 = bf16[128,7168]{1,0:T(8,128)(2,1)} custom-call(s32[4]{0:T(128)S(1)} %copy-done.3, bf16[32,128]{1,0:T(8,128)(2,1)S(1)} %copy-done.4, bf16[16,8,1792]{2,1,0:T(8,128)(2,1)S(1)} %all-to-all-done.1.got), custom_call_target="tpu_custom_call" | custom-call | flops 58720256 | bytes 2301952 | tf_op jit(solution)/shard_map/combine/pallas_call | solution.py:50
  (57 shorter events, 10.7 us)
Async XLA Ops:
  4.1 7.4 %copy-start = (bf16[1,192,3584]{2,1,0:T(8,128)(2,1)S(1)}, bf16[1,192,3584]{2,1,0:T(8,128)(2,1)}, u32[]{:S(2)}) copy-start(bf16[1,192,3584]{2,1,0:T(8,128)(2,1)} %w.1) | copy-start | bytes 4128772
  4.2 23.3 %all-to-all-start = ((bf16[16,16,1792]{2,1,0:T(8,128)(2,1)}), bf16[16,16,1792]{2,1,0:T(8,128)(2,1)S(1)}, u32[]{:S(2)}, u32[]{:S(2)}) async-start(bf16[16,16,1792]{2,1,0:T(8,128)(2,1)} %get-tuple-element.63), calls=%async_computation | async-start | bytes 1835008 | tf_op jit(solution)/shard_map/all_to_all | solution.py:362
  11.5 104.0 %copy-start.2 = (s32[4]{0:T(128)}, s32[4]{0:T(128)S(1)}, u32[]{:S(2)}) copy-start(s32[4]{0:T(128)S(1)} %pad_add_fusion.place) | copy-start | bytes 52
  12.2 0.7 copy-start.5
  28.1 12.4 %collective-permute-start = (bf16[128,1792]{1,0:T(8,128)(2,1)S(1)}, bf16[128,1792]{1,0:T(8,128)(2,1)S(1)}, u32[]{:S(2)}, u32[]{:S(2)}) collective-permute-start(bf16[128,1792]{1,0:T(8,128)(2,1)S(1)} %get-tuple-element.66.a0.refs_0_.refs_8_), channel_id=1, source_target_pairs={{0,8},{1,9},{2,10},{3,11},{4,12},{5,13},{6,14},{7,15},{8,16},{9,17... | collective-permute-start | bytes 1376264 | tf_op jit(solution)/shard_map/ppermute | solution.py:44
  30.0 10.4 %collective-permute-start.1 = (bf16[128,1792]{1,0:T(8,128)(2,1)S(1)}, bf16[128,1792]{1,0:T(8,128)(2,1)S(1)}, u32[]{:S(2)}, u32[]{:S(2)}) collective-permute-start(bf16[128,1792]{1,0:T(8,128)(2,1)S(1)} %get-tuple-element.67.b0.refs_1_.refs_9_), channel_id=1, source_target_pairs={{0,24},{1,25},{2,26},{3,27},{4,28},{5,29},{6,30},{7,31},{8,0},{9,1... | collective-permute-start | bytes 1376264 | tf_op jit(solution)/shard_map/ppermute | solution.py:44
  32.2 12.7 %collective-permute-start.3 = (bf16[192,896]{1,0:T(8,128)(2,1)}, bf16[192,896]{1,0:T(8,128)(2,1)S(1)}, u32[]{:S(2)}, u32[]{:S(2)}) collective-permute-start(bf16[192,896]{1,0:T(8,128)(2,1)} %copy-done.5), channel_id=1, source_target_pairs={{0,4},{1,5},{2,6},{3,7},{4,0},{5,1},{6,2},{7,3},{8,12},{9,13},{10,... | collective-permute-start | bytes 1032200 | tf_op jit(solution)/shard_map/ppermute | solution.py:44
  33.1 14.7 %collective-permute-start.4 = (bf16[192,896]{1,0:T(8,128)(2,1)S(1)}, bf16[192,896]{1,0:T(8,128)(2,1)S(1)}, u32[]{:S(2)}, u32[]{:S(2)}) collective-permute-start(bf16[192,896]{1,0:T(8,128)(2,1)S(1)} %get-tuple-element.70), channel_id=1, source_target_pairs={{0,6},{1,7},{2,0},{3,1},{4,2},{5,3},{6,4},{7,5},{8,14},{9,15},{10,... | collective-permute-start | bytes 1032200 | tf_op jit(solution)/shard_map/ppermute | solution.py:44
  35.5 13.1 %collective-permute-start.2 = (bf16[192,896]{1,0:T(8,128)(2,1)S(1)}, bf16[192,896]{1,0:T(8,128)(2,1)S(1)}, u32[]{:S(2)}, u32[]{:S(2)}) collective-permute-start(bf16[192,896]{1,0:T(8,128)(2,1)S(1)} %get-tuple-element.64), channel_id=1, source_target_pairs={{0,2},{1,3},{2,4},{3,5},{4,6},{5,7},{6,0},{7,1},{8,10},{9,11},{10,... | collective-permute-start | bytes 1032200 | tf_op jit(solution)/shard_map/ppermute | solution.py:44
  41.1 19.5 %collective-permute-start.13 = (bf16[256,1792]{1,0:T(8,128)(2,1)S(1)}, bf16[256,1792]{1,0:T(8,128)(2,1)S(1)}, u32[]{:S(2)}, u32[]{:S(2)}) collective-permute-start(bf16[256,1792]{1,0:T(8,128)(2,1)S(1)} %get-tuple-element.82), channel_id=1, source_target_pairs={{0,24},{1,25},{2,26},{3,27},{4,28},{5,29},{6,30},{7,31},{8,0},{9,1... | collective-permute-start | bytes 2752520 | tf_op jit(solution)/shard_map/ppermute | solution.py:44
  44.2 19.8 %collective-permute-start.12 = (bf16[256,1792]{1,0:T(8,128)(2,1)S(1)}, bf16[256,1792]{1,0:T(8,128)(2,1)S(1)}, u32[]{:S(2)}, u32[]{:S(2)}) collective-permute-start(bf16[256,1792]{1,0:T(8,128)(2,1)S(1)} %get-tuple-element.71), channel_id=1, source_target_pairs={{0,8},{1,9},{2,10},{3,11},{4,12},{5,13},{6,14},{7,15},{8,16},{9,17... | collective-permute-start | bytes 2752520 | tf_op jit(solution)/shard_map/ppermute | solution.py:44
  48.6 1.7 %collective-permute-start.5 = (bf16[192,896]{1,0:T(8,128)(2,1)S(1)}, bf16[192,896]{1,0:T(8,128)(2,1)S(1)}, u32[]{:S(2)}, u32[]{:S(2)}) collective-permute-start(bf16[192,896]{1,0:T(8,128)(2,1)S(1)} %get-tuple-element.72.refs_0_), channel_id=1, source_target_pairs={{0,1},{1,0},{2,3},{3,2},{4,5},{5,4},{6,7},{7,6},{8,9},{9,8},{10,11... | collective-permute-start | bytes 1032200 | tf_op jit(solution)/shard_map/ppermute | solution.py:44
  48.6 2.1 %collective-permute-start.6 = (bf16[192,896]{1,0:T(8,128)(2,1)S(1)}, bf16[192,896]{1,0:T(8,128)(2,1)S(1)}, u32[]{:S(2)}, u32[]{:S(2)}) collective-permute-start(bf16[192,896]{1,0:T(8,128)(2,1)S(1)} %collective-permute-done.2.refs_1_), channel_id=1, source_target_pairs={{0,1},{1,0},{2,3},{3,2},{4,5},{5,4},{6,7},{7,6},{8,9},{9,8},{10,11... | collective-permute-start | bytes 1032200 | tf_op jit(solution)/shard_map/ppermute | solution.py:44
  49.1 2.1 %collective-permute-start.7 = (bf16[192,896]{1,0:T(8,128)(2,1)S(1)}, bf16[192,896]{1,0:T(8,128)(2,1)S(1)}, u32[]{:S(2)}, u32[]{:S(2)}) collective-permute-start(bf16[192,896]{1,0:T(8,128)(2,1)S(1)} %collective-permute-done.3.refs_2_), channel_id=1, source_target_pairs={{0,1},{1,0},{2,3},{3,2},{4,5},{5,4},{6,7},{7,6},{8,9},{9,8},{10,11... | collective-permute-start | bytes 1032200 | tf_op jit(solution)/shard_map/ppermute | solution.py:44
  50.3 1.7 %collective-permute-start.8 = (bf16[192,896]{1,0:T(8,128)(2,1)S(1)}, bf16[192,896]{1,0:T(8,128)(2,1)S(1)}, u32[]{:S(2)}, u32[]{:S(2)}) collective-permute-start(bf16[192,896]{1,0:T(8,128)(2,1)S(1)} %collective-permute-done.4.refs_3_), channel_id=1, source_target_pairs={{0,1},{1,0},{2,3},{3,2},{4,5},{5,4},{6,7},{7,6},{8,9},{9,8},{10,11... | collective-permute-start | bytes 1032200 | tf_op jit(solution)/shard_map/ppermute | solution.py:44
  54.3 14.8 %collective-permute-start.9 = (bf16[64,768]{1,0:T(8,128)(2,1)S(1)}, bf16[64,768]{1,0:T(8,128)(2,1)S(1)}, u32[]{:S(2)}, u32[]{:S(2)}) collective-permute-start(bf16[64,768]{1,0:T(8,128)(2,1)S(1)} %get-tuple-element.79), channel_id=1, source_target_pairs={{0,6},{1,7},{2,0},{3,1},{4,2},{5,3},{6,4},{7,5},{8,14},{9,15},{10,... | collective-permute-start | bytes 294920 | tf_op jit(solution)/shard_map/ppermute | solution.py:44
  56.2 12.9 %collective-permute-start.10 = (bf16[64,768]{1,0:T(8,128)(2,1)S(1)}, bf16[64,768]{1,0:T(8,128)(2,1)S(1)}, u32[]{:S(2)}, u32[]{:S(2)}) collective-permute-start(bf16[64,768]{1,0:T(8,128)(2,1)S(1)} %get-tuple-element.80), channel_id=1, source_target_pairs={{0,4},{1,5},{2,6},{3,7},{4,0},{5,1},{6,2},{7,3},{8,12},{9,13},{10,... | collective-permute-start | bytes 294920 | tf_op jit(solution)/shard_map/ppermute | solution.py:44
  56.9 12.2 %collective-permute-start.11 = (bf16[64,768]{1,0:T(8,128)(2,1)S(1)}, bf16[64,768]{1,0:T(8,128)(2,1)S(1)}, u32[]{:S(2)}, u32[]{:S(2)}) collective-permute-start(bf16[64,768]{1,0:T(8,128)(2,1)S(1)} %get-tuple-element.81), channel_id=1, source_target_pairs={{0,2},{1,3},{2,4},{3,5},{4,6},{5,7},{6,0},{7,1},{8,10},{9,11},{10,... | collective-permute-start | bytes 294920 | tf_op jit(solution)/shard_map/ppermute | solution.py:44
  65.6 12.0 %collective-permute-start.17 = (bf16[64,768]{1,0:T(8,128)(2,1)S(1)}, bf16[64,768]{1,0:T(8,128)(2,1)S(1)}, u32[]{:S(2)}, u32[]{:S(2)}) collective-permute-start(bf16[64,768]{1,0:T(8,128)(2,1)S(1)} %get-tuple-element.83), channel_id=1, source_target_pairs={{0,6},{1,7},{2,0},{3,1},{4,2},{5,3},{6,4},{7,5},{8,14},{9,15},{10,... | collective-permute-start | bytes 294920 | tf_op jit(solution)/shard_map/ppermute | solution.py:44
  69.1 7.2 %collective-permute-start.18 = (bf16[64,768]{1,0:T(8,128)(2,1)S(1)}, bf16[64,768]{1,0:T(8,128)(2,1)S(1)}, u32[]{:S(2)}, u32[]{:S(2)}) collective-permute-start(bf16[64,768]{1,0:T(8,128)(2,1)S(1)} %get-tuple-element.89), channel_id=1, source_target_pairs={{0,4},{1,5},{2,6},{3,7},{4,0},{5,1},{6,2},{7,3},{8,12},{9,13},{10,... | collective-permute-start | bytes 294920 | tf_op jit(solution)/shard_map/ppermute | solution.py:44
  69.2 8.4 %collective-permute-start.19 = (bf16[64,768]{1,0:T(8,128)(2,1)S(1)}, bf16[64,768]{1,0:T(8,128)(2,1)S(1)}, u32[]{:S(2)}, u32[]{:S(2)}) collective-permute-start(bf16[64,768]{1,0:T(8,128)(2,1)S(1)} %get-tuple-element.90), channel_id=1, source_target_pairs={{0,2},{1,3},{2,4},{3,5},{4,6},{5,7},{6,0},{7,1},{8,10},{9,11},{10,... | collective-permute-start | bytes 294920 | tf_op jit(solution)/shard_map/ppermute | solution.py:44
  70.7 9.6 %collective-permute-start.16 = (bf16[64,768]{1,0:T(8,128)(2,1)S(1)}, bf16[64,768]{1,0:T(8,128)(2,1)S(1)}, u32[]{:S(2)}, u32[]{:S(2)}) collective-permute-start(bf16[64,768]{1,0:T(8,128)(2,1)S(1)} %middle.2.refs_0_), channel_id=1, source_target_pairs={{0,6},{1,7},{2,0},{3,1},{4,2},{5,3},{6,4},{7,5},{8,14},{9,15},{10,... | collective-permute-start | bytes 294920 | tf_op jit(solution)/shard_map/ppermute | solution.py:44
  73.2 8.0 %collective-permute-start.15 = (bf16[64,768]{1,0:T(8,128)(2,1)S(1)}, bf16[64,768]{1,0:T(8,128)(2,1)S(1)}, u32[]{:S(2)}, u32[]{:S(2)}) collective-permute-start(bf16[64,768]{1,0:T(8,128)(2,1)S(1)} %middle.2.refs_0_), channel_id=1, source_target_pairs={{0,4},{1,5},{2,6},{3,7},{4,0},{5,1},{6,2},{7,3},{8,12},{9,13},{10,... | collective-permute-start | bytes 294920 | tf_op jit(solution)/shard_map/ppermute | solution.py:44
  76.3 6.1 %collective-permute-start.14 = (bf16[64,768]{1,0:T(8,128)(2,1)S(1)}, bf16[64,768]{1,0:T(8,128)(2,1)S(1)}, u32[]{:S(2)}, u32[]{:S(2)}) collective-permute-start(bf16[64,768]{1,0:T(8,128)(2,1)S(1)} %middle.2.refs_0_), channel_id=1, source_target_pairs={{0,2},{1,3},{2,4},{3,5},{4,6},{5,7},{6,0},{7,1},{8,10},{9,11},{10,... | collective-permute-start | bytes 294920 | tf_op jit(solution)/shard_map/ppermute | solution.py:44
  78.2 5.2 %collective-permute-start.22 = (bf16[64,768]{1,0:T(8,128)(2,1)S(1)}, bf16[64,768]{1,0:T(8,128)(2,1)S(1)}, u32[]{:S(2)}, u32[]{:S(2)}) collective-permute-start(bf16[64,768]{1,0:T(8,128)(2,1)S(1)} %middle.3.refs_4_), channel_id=1, source_target_pairs={{0,6},{1,7},{2,0},{3,1},{4,2},{5,3},{6,4},{7,5},{8,14},{9,15},{10,... | collective-permute-start | bytes 294920 | tf_op jit(solution)/shard_map/ppermute | solution.py:44
  80.2 6.2 %collective-permute-start.21 = (bf16[64,768]{1,0:T(8,128)(2,1)S(1)}, bf16[64,768]{1,0:T(8,128)(2,1)S(1)}, u32[]{:S(2)}, u32[]{:S(2)}) collective-permute-start(bf16[64,768]{1,0:T(8,128)(2,1)S(1)} %middle.3.refs_4_), channel_id=1, source_target_pairs={{0,4},{1,5},{2,6},{3,7},{4,0},{5,1},{6,2},{7,3},{8,12},{9,13},{10,... | collective-permute-start | bytes 294920 | tf_op jit(solution)/shard_map/ppermute | solution.py:44
  80.3 6.9 %collective-permute-start.20 = (bf16[64,768]{1,0:T(8,128)(2,1)S(1)}, bf16[64,768]{1,0:T(8,128)(2,1)S(1)}, u32[]{:S(2)}, u32[]{:S(2)}) collective-permute-start(bf16[64,768]{1,0:T(8,128)(2,1)S(1)} %middle.3.refs_4_), channel_id=1, source_target_pairs={{0,2},{1,3},{2,4},{3,5},{4,6},{5,7},{6,0},{7,1},{8,10},{9,11},{10,... | collective-permute-start | bytes 294920 | tf_op jit(solution)/shard_map/ppermute | solution.py:44
  88.8 4.6 %collective-permute-start.25 = (bf16[256,896]{1,0:T(8,128)(2,1)S(1)}, bf16[256,896]{1,0:T(8,128)(2,1)S(1)}, u32[]{:S(2)}, u32[]{:S(2)}) collective-permute-start(bf16[256,896]{1,0:T(8,128)(2,1)S(1)} %get-tuple-element.98), channel_id=1, source_target_pairs={{0,1},{1,0},{2,3},{3,2},{4,5},{5,4},{6,7},{7,6},{8,9},{9,8},{10,11... | collective-permute-start | bytes 1376264 | tf_op jit(solution)/shard_map/ppermute | solution.py:44
  88.9 4.5 %collective-permute-start.26 = (bf16[256,896]{1,0:T(8,128)(2,1)S(1)}, bf16[256,896]{1,0:T(8,128)(2,1)S(1)}, u32[]{:S(2)}, u32[]{:S(2)}) collective-permute-start(bf16[256,896]{1,0:T(8,128)(2,1)S(1)} %get-tuple-element.99), channel_id=1, source_target_pairs={{0,1},{1,0},{2,3},{3,2},{4,5},{5,4},{6,7},{7,6},{8,9},{9,8},{10,11... | collective-permute-start | bytes 1376264 | tf_op jit(solution)/shard_map/ppermute | solution.py:44
  89.4 4.0 %collective-permute-start.27 = (bf16[256,896]{1,0:T(8,128)(2,1)S(1)}, bf16[256,896]{1,0:T(8,128)(2,1)S(1)}, u32[]{:S(2)}, u32[]{:S(2)}) collective-permute-start(bf16[256,896]{1,0:T(8,128)(2,1)S(1)} %get-tuple-element.100), channel_id=1, source_target_pairs={{0,1},{1,0},{2,3},{3,2},{4,5},{5,4},{6,7},{7,6},{8,9},{9,8},{10,11... | collective-permute-start | bytes 1376264 | tf_op jit(solution)/shard_map/ppermute | solution.py:44
  91.3 12.9 %collective-permute-start.23 = (bf16[128,1792]{1,0:T(8,128)(2,1)S(1)}, bf16[128,1792]{1,0:T(8,128)(2,1)S(1)}, u32[]{:S(2)}, u32[]{:S(2)}) collective-permute-start(bf16[128,1792]{1,0:T(8,128)(2,1)S(1)} %get-tuple-element.96), channel_id=1, source_target_pairs={{0,24},{1,25},{2,26},{3,27},{4,28},{5,29},{6,30},{7,31},{8,0},{9,1... | collective-permute-start | bytes 1376264 | tf_op jit(solution)/shard_map/ppermute | solution.py:44
  91.6 13.9 %collective-permute-start.24 = (bf16[128,1792]{1,0:T(8,128)(2,1)S(1)}, bf16[128,1792]{1,0:T(8,128)(2,1)S(1)}, u32[]{:S(2)}, u32[]{:S(2)}) collective-permute-start(bf16[128,1792]{1,0:T(8,128)(2,1)S(1)} %get-tuple-element.97), channel_id=1, source_target_pairs={{0,8},{1,9},{2,10},{3,11},{4,12},{5,13},{6,14},{7,15},{8,16},{9,17... | collective-permute-start | bytes 1376264 | tf_op jit(solution)/shard_map/ppermute | solution.py:44
  95.4 0.8 copy-start.1
  96.2 18.3 %collective-permute-start.30 = (bf16[192,896]{1,0:T(8,128)(2,1)S(1)}, bf16[192,896]{1,0:T(8,128)(2,1)S(1)}, u32[]{:S(2)}, u32[]{:S(2)}) collective-permute-start(bf16[192,896]{1,0:T(8,128)(2,1)S(1)} %get-tuple-element.109), channel_id=1, source_target_pairs={{0,6},{1,7},{2,0},{3,1},{4,2},{5,3},{6,4},{7,5},{8,14},{9,15},{10,... | collective-permute-start | bytes 1032200 | tf_op jit(solution)/shard_map/ppermute | solution.py:44
  97.1 17.4 %collective-permute-start.31 = (bf16[192,896]{1,0:T(8,128)(2,1)S(1)}, bf16[192,896]{1,0:T(8,128)(2,1)S(1)}, u32[]{:S(2)}, u32[]{:S(2)}) collective-permute-start(bf16[192,896]{1,0:T(8,128)(2,1)S(1)} %get-tuple-element.110), channel_id=1, source_target_pairs={{0,4},{1,5},{2,6},{3,7},{4,0},{5,1},{6,2},{7,3},{8,12},{9,13},{10,... | collective-permute-start | bytes 1032200 | tf_op jit(solution)/shard_map/ppermute | solution.py:44
  97.6 18.0 %collective-permute-start.32 = (bf16[192,896]{1,0:T(8,128)(2,1)S(1)}, bf16[192,896]{1,0:T(8,128)(2,1)S(1)}, u32[]{:S(2)}, u32[]{:S(2)}) collective-permute-start(bf16[192,896]{1,0:T(8,128)(2,1)S(1)} %get-tuple-element.111), channel_id=1, source_target_pairs={{0,2},{1,3},{2,4},{3,5},{4,6},{5,7},{6,0},{7,1},{8,10},{9,11},{10,... | collective-permute-start | bytes 1032200 | tf_op jit(solution)/shard_map/ppermute | solution.py:44
  106.2 7.0 %collective-permute-start.28 = (bf16[64,1792]{1,0:T(8,128)(2,1)S(1)}, bf16[64,1792]{1,0:T(8,128)(2,1)S(1)}, u32[]{:S(2)}, u32[]{:S(2)}) collective-permute-start(bf16[64,1792]{1,0:T(8,128)(2,1)S(1)} %get-tuple-element.107), channel_id=1, source_target_pairs={{0,24},{1,25},{2,26},{3,27},{4,28},{5,29},{6,30},{7,31},{8,0},{9,1... | collective-permute-start | bytes 688136 | tf_op jit(solution)/shard_map/ppermute | solution.py:44
  106.5 8.1 %collective-permute-start.29 = (bf16[64,1792]{1,0:T(8,128)(2,1)S(1)}, bf16[64,1792]{1,0:T(8,128)(2,1)S(1)}, u32[]{:S(2)}, u32[]{:S(2)}) collective-permute-start(bf16[64,1792]{1,0:T(8,128)(2,1)S(1)} %get-tuple-element.108), channel_id=1, source_target_pairs={{0,8},{1,9},{2,10},{3,11},{4,12},{5,13},{6,14},{7,15},{8,16},{9,17... | collective-permute-start | bytes 688136 | tf_op jit(solution)/shard_map/ppermute | solution.py:44
  114.6 6.0 %copy-start.6 = (bf16[192,896]{1,0:T(8,128)(2,1)}, bf16[192,896]{1,0:T(8,128)(2,1)S(1)}, u32[]{:S(2)}) copy-start(bf16[192,896]{1,0:T(8,128)(2,1)S(1)} %collective-permute-done.30.g1) | copy-start | bytes 1032196
  114.6 6.1 %copy-start.7 = (bf16[192,896]{1,0:T(8,128)(2,1)}, bf16[192,896]{1,0:T(8,128)(2,1)S(1)}, u32[]{:S(2)}) copy-start(bf16[192,896]{1,0:T(8,128)(2,1)S(1)} %collective-permute-done.31.g2) | copy-start | bytes 1032196
  115.6 5.1 %copy-start.8 = (bf16[192,896]{1,0:T(8,128)(2,1)}, bf16[192,896]{1,0:T(8,128)(2,1)S(1)}, u32[]{:S(2)}) copy-start(bf16[192,896]{1,0:T(8,128)(2,1)S(1)} %collective-permute-done.32.g3) | copy-start | bytes 1032196
  117.0 14.8 %all-to-all-start.1 = ((bf16[16,8,1792]{2,1,0:T(8,128)(2,1)}), bf16[16,8,1792]{2,1,0:T(8,128)(2,1)S(1)}, u32[]{:S(2)}, u32[]{:S(2)}) async-start(bf16[16,8,1792]{2,1,0:T(8,128)(2,1)} %sum_back.1), calls=%async_computation.1 | async-start | bytes 917504 | tf_op jit(solution)/shard_map/all_to_all | solution.py:362
  120.6 11.2 %copy-start.3 = (s32[4]{0:T(128)S(1)}, s32[4]{0:T(128)}, u32[]{:S(2)}) copy-start(s32[4]{0:T(128)} %copy-done.2) | copy-start | bytes 52
  120.7 11.2 %copy-start.4 = (bf16[32,128]{1,0:T(8,128)(2,1)S(1)}, bf16[32,128]{1,0:T(8,128)(2,1)}, u32[]{:S(2)}) copy-start(bf16[32,128]{1,0:T(8,128)(2,1)} %get-tuple-element.62.pick) | copy-start | bytes 24580

commit v4 on v3

--- a/solution.py
+++ b/solution.py
@@ -240,18 +240,20 @@
     out[:, 2 * width :] = (act * up).astype(BF)
 
 
-def back_kernel(place, held, own, other, a0, b0, a1, b3, minus, plus):
+def back_kernel(first, place, held, own, other, *outs):
     c = place[3]
     width = 2 * N * HID
-    h = held[:, :width]
-    low, high = slice(0, HELD), slice(HELD, 2 * HELD)
-    targets = ((a0, low), (b0, low), (a1, low), (b3, low))
-    targets += ((minus, low), (plus, low), (plus, high), (minus, high))
+    h = held[first : first + CHUNK, :width]
+    if len(outs) == 2:
+        minus, plus = outs
+        targets = (minus, 0), (plus, 0), (plus, HELD), (minus, HELD)
+    else:
+        targets = [(o, 0) for o in outs]
     for w, half in ((own, c), (other, 1 - c)):
         cols = pl.ds(aligned(half * EIGHTH), EIGHTH)
         part = mm(h, w[:width], NN)
-        for i, (o, rows) in enumerate(targets):
-            o[rows, cols] = part[i * HELD : (i + 1) * HELD].astype(BF)
+        for i, (o, at) in enumerate(targets):
+            o[at : at + HELD, cols] = part[i * HELD : (i + 1) * HELD].astype(BF)
 
 
 def pass_on_kernel(place, own_a, own_b, got_a, got_b, out_a, out_b):
@@ -397,16 +399,17 @@
     return call(middle_kernel, "middle", [((HELD, 3 * N * HID), BF)], place, *part)[0]
 
 
-def back_part(place, held, w_own, w_other):
+def back_part(place, held, w_own, w_other, chunk):
+    shape = (HELD, QUARTER) if chunk == 0 else (2 * HELD, QUARTER)
     return call(
-        back_kernel,
+        functools.partial(back_kernel, chunk * CHUNK),
         "back",
-        [((HELD, QUARTER), BF)] * 4 + [((2 * HELD, QUARTER), BF)] * 2,
+        [(shape, BF)] * (CHUNK // shape[0]),
         place,
         held,
         w_own,
         w_other,
-        flops=8 * CHUNK * QUARTER * N * HID,
+        flops=4 * CHUNK * QUARTER * N * HID,
     )
 
 
@@ -470,7 +473,7 @@
         flops=flops,
         scratch=[pltpu.VMEM((3 * width, EIGHTH), BF)],
     )
-    a0, b0, a1, b3, minus, plus = back_part(place, held, w_own, w_other)
+    minus, plus = back_part(place, held, w_own, w_other, 1)
     got_minus, got_plus = turn(minus, "z", -1), turn(plus, "z", 1)
     got = [turn(v, "c", 1) for v in theirs]
     blocks = call(
@@ -479,12 +482,13 @@
         [((block_rows, EIGHTH), F32)] + [((block_rows, EIGHTH), BF)] * 3,
         place,
         *got,
-        after(held, a1),
+        after(held, minus),
         *first,
         *second,
         flops=flops,
         scratch=[pltpu.VMEM((3 * width, EIGHTH), F32)],
     )
+    a0, b0, a1, b3 = back_part(place, after(held, blocks[0]), w_own, w_other, 0)
     a1, b3 = pass_on(place, *after((a1, b3, got_minus, got_plus), blocks[0]))
     a1, b3 = turn(a1, "z", -1), turn(b3, "z", 1)
     blocks = spread(blocks, "y", -1)

time: 135 us -> 135 us (level)
  waiting for transfers between devices: 59.2 us -> 56.9 us
  starting transfers between devices: 45 us -> 47.3 us
    ppermute x33, starting transfers between devices: 34.2 us -> 36.4 us  [turn(): return lax.ppermute(value, ('expert', 'dp'), rotation(axis, step))]
    pallas_call x14 -> x15, Pallas kernels: 16.7 us -> 17.5 us  [call(): pl.pallas_call(kernel, name=name, out_shape=outs, in_specs=[pl.BlockSpec(...]
  transfers between devices with their start and end apart: 35 -> 35, of which waited for: 23 -> 21; matrix products, arithmetic and copies ran while one was open for 0% -> 0% of each run, Pallas kernels for 13% -> 14%
where the time goes in v4:
time: 135 us; the launch traced here: 134 us
  waiting for transfers between devices  56.9 us (42%)
  starting transfers between devices  47.3 us (35%)
  Pallas kernels  27.9 us (21%)
    ppermute x33, waiting for transfers between devices, turn(): return lax.ppermute(value, ('expert', 'dp'), rotation(axis, step))  39.2 us
    ppermute x33, starting transfers between devices, turn(): return lax.ppermute(value, ('expert', 'dp'), rotation(axis, step))  36.4 us
    all_to_all x2, waiting for transfers between devices, exchange(): lax.all_to_all(value, 'expert', 0, 0, axis_index_groups=list(groups.value...  17.7 us
    pallas_call x15, Pallas kernels, call(): pl.pallas_call(kernel, name=name, out_shape=outs, in_specs=[pl.BlockSpec(...  17.5 us
    all_to_all x2, starting transfers between devices, exchange(): lax.all_to_all(value, 'expert', 0, 0, axis_index_groups=list(groups.value...  11 us
    pallas_call x1, Pallas kernels, moments(): pl.pallas_call(moments_kernel, name='moments', grid_spec=pltpu.PrefetchSc...  6.9 us
    pallas_call x1, Pallas kernels, route(): pl.pallas_call(route_kernel, name='route', in_specs=[hbm] * 4, out_specs=...  3.5 us
  transfers between devices with their start and end apart: 35, of which 21 were waited for; matrix products, arithmetic and copies ran while one was open for 0% of the time, Pallas kernels for 14%

profile of v4, /device:TPU:0, one launch (start us, length us, event | category | flops | bytes accessed | tf_op | source)
XLA Modules:
  0.0 134.1 jit_solution(11253880767126948217)
XLA Ops:
  0.6 3.5 %route.1 = (bf16[16,16,1792]{2,1,0:T(8,128)(2,1)}, bf16[32,128]{1,0:T(8,128)(2,1)}) custom-call(s32[8,128]{1,0:T(8,128)} %bitcast.6, f32[8,128]{1,0:T(8,128)} %bitcast.7, bf16[128,7168]{1,0:T(8,128)(2,1)} %tokens.1, bf16[128,7168]{1,0:T(8,128)(2,1)} %grads.1), custom_call_target="tpu_custom_call" | custom-call | flops 117440512 | bytes 5505024 | tf_op jit(solution)/shard_map/route/pallas_call | solution.py:143
  4.2 7.3 %all-to-all-start = ((bf16[16,16,1792]{2,1,0:T(8,128)(2,1)}), bf16[16,16,1792]{2,1,0:T(8,128)(2,1)S(1)}, u32[]{:S(2)}, u32[]{:S(2)}) async-start(bf16[16,16,1792]{2,1,0:T(8,128)(2,1)} %get-tuple-element.64), calls=%async_computation | async-start | bytes 1835008 | tf_op jit(solution)/shard_map/all_to_all | solution.py:364
  12.2 0.7 copy-done.5
  12.9 14.5 %all-to-all-done.got = bf16[16,16,1792]{2,1,0:T(8,128)(2,1)S(1)} async-done(((bf16[16,16,1792]{2,1,0:T(8,128)(2,1)}), bf16[16,16,1792]{2,1,0:T(8,128)(2,1)S(1)}, u32[]{:S(2)}, u32[]{:S(2)}) %all-to-all-start) | async-done | bytes 917536 | tf_op jit(solution)/shard_map/all_to_all | solution.py:364
  28.1 2.0 %collective-permute-start = (bf16[128,1792]{1,0:T(8,128)(2,1)S(1)}, bf16[128,1792]{1,0:T(8,128)(2,1)S(1)}, u32[]{:S(2)}, u32[]{:S(2)}) collective-permute-start(bf16[128,1792]{1,0:T(8,128)(2,1)S(1)} %get-tuple-element.67.a0.refs_0_.refs_8_), channel_id=1, source_target_pairs={{0,8},{1,9},{2,10},{3,11},{4,12},{5,13},{6,14},{7,15},{8,16},{9,17... | collective-permute-start | bytes 1376264 | tf_op jit(solution)/shard_map/ppermute | solution.py:44
  30.0 2.2 %collective-permute-start.1 = (bf16[128,1792]{1,0:T(8,128)(2,1)S(1)}, bf16[128,1792]{1,0:T(8,128)(2,1)S(1)}, u32[]{:S(2)}, u32[]{:S(2)}) collective-permute-start(bf16[128,1792]{1,0:T(8,128)(2,1)S(1)} %get-tuple-element.68.b0.refs_1_.refs_9_), channel_id=1, source_target_pairs={{0,24},{1,25},{2,26},{3,27},{4,28},{5,29},{6,30},{7,31},{8,0},{9,1... | collective-permute-start | bytes 1376264 | tf_op jit(solution)/shard_map/ppermute | solution.py:44
  32.2 0.9 collective-permute-start.3
  33.1 2.4 %collective-permute-start.4 = (bf16[192,896]{1,0:T(8,128)(2,1)S(1)}, bf16[192,896]{1,0:T(8,128)(2,1)S(1)}, u32[]{:S(2)}, u32[]{:S(2)}) collective-permute-start(bf16[192,896]{1,0:T(8,128)(2,1)S(1)} %get-tuple-element.71), channel_id=1, source_target_pairs={{0,6},{1,7},{2,0},{3,1},{4,2},{5,3},{6,4},{7,5},{8,14},{9,15},{10,... | collective-permute-start | bytes 1032200 | tf_op jit(solution)/shard_map/ppermute | solution.py:44
  35.5 4.9 %collective-permute-done.a1.refs_2_.refs_10_ = bf16[128,1792]{1,0:T(8,128)(2,1)S(1)} collective-permute-done((bf16[128,1792]{1,0:T(8,128)(2,1)S(1)}, bf16[128,1792]{1,0:T(8,128)(2,1)S(1)}, u32[]{:S(2)}, u32[]{:S(2)}) %collective-permute-start) | collective-permute-done | bytes 458784 | tf_op jit(solution)/shard_map/ppermute | solution.py:44
  41.1 3.1 %collective-permute-start.13 = (bf16[256,1792]{1,0:T(8,128)(2,1)S(1)}, bf16[256,1792]{1,0:T(8,128)(2,1)S(1)}, u32[]{:S(2)}, u32[]{:S(2)}) collective-permute-start(bf16[256,1792]{1,0:T(8,128)(2,1)S(1)} %get-tuple-element.83), channel_id=1, source_target_pairs={{0,24},{1,25},{2,26},{3,27},{4,28},{5,29},{6,30},{7,31},{8,0},{9,1... | collective-permute-start | bytes 2752520 | tf_op jit(solution)/shard_map/ppermute | solution.py:44
  44.2 0.7 collective-permute-done.3.refs_2_
  44.9 2.9 %collective-permute-done.4.refs_3_ = bf16[192,896]{1,0:T(8,128)(2,1)S(1)} collective-permute-done((bf16[192,896]{1,0:T(8,128)(2,1)S(1)}, bf16[192,896]{1,0:T(8,128)(2,1)S(1)}, u32[]{:S(2)}, u32[]{:S(2)}) %collective-permute-start.4) | collective-permute-done | bytes 344096 | tf_op jit(solution)/shard_map/ppermute | solution.py:44
  47.8 0.8 collective-permute-done.2.refs_1_
  49.1 1.1 collective-permute-done.5.refs_4_
  51.9 0.8 stack_weights.1
  52.7 1.6 %forward.2 = (f32[64,768]{1,0:T(8,128)S(1)}, bf16[64,768]{1,0:T(8,128)(2,1)S(1)}, bf16[64,768]{1,0:T(8,128)(2,1)S(1)}, bf16[64,768]{1,0:T(8,128)(2,1)S(1)}) custom-call(s32[4]{0:T(128)S(1)} %pad_add_fusion.place, bf16[128,1792]{1,0:T(8,128)(2,1)S(1)} %get-tuple-element.67.a0.refs_0_.refs_8_, bf16[128,1792]{1,0:T(8,128)(2,1)S(1)} %get-tuple-element.68.b0.refs_1_.refs_9_, ...), custom_call_target="tpu_custom_call" | custom-call | flops 704643072 | bytes 5079040 | tf_op jit(solution)/shard_map/forward/pallas_call | solution.py:50
  54.3 1.9 %collective-permute-start.9 = (bf16[64,768]{1,0:T(8,128)(2,1)S(1)}, bf16[64,768]{1,0:T(8,128)(2,1)S(1)}, u32[]{:S(2)}, u32[]{:S(2)}) collective-permute-start(bf16[64,768]{1,0:T(8,128)(2,1)S(1)} %get-tuple-element.80), channel_id=1, source_target_pairs={{0,6},{1,7},{2,0},{3,1},{4,2},{5,3},{6,4},{7,5},{8,14},{9,15},{10,... | collective-permute-start | bytes 294920 | tf_op jit(solution)/shard_map/ppermute | solution.py:44
  56.2 0.8 collective-permute-start.10
  57.6 3.0 %collective-permute-done.13.refs_1_.refs_13_.refs_5_ = bf16[256,1792]{1,0:T(8,128)(2,1)S(1)} collective-permute-done((bf16[256,1792]{1,0:T(8,128)(2,1)S(1)}, bf16[256,1792]{1,0:T(8,128)(2,1)S(1)}, u32[]{:S(2)}, u32[]{:S(2)}) %collective-permute-start.13) | collective-permute-done | bytes 917536 | tf_op jit(solution)/shard_map/ppermute | solution.py:44
  60.6 3.4 %collective-permute-done.12.refs_0_.refs_12_.refs_4_ = bf16[256,1792]{1,0:T(8,128)(2,1)S(1)} collective-permute-done((bf16[256,1792]{1,0:T(8,128)(2,1)S(1)}, bf16[256,1792]{1,0:T(8,128)(2,1)S(1)}, u32[]{:S(2)}, u32[]{:S(2)}) %collective-permute-start.12) | collective-permute-done | bytes 917536 | tf_op jit(solution)/shard_map/ppermute | solution.py:44
  64.0 1.6 %forward.3 = (f32[64,768]{1,0:T(8,128)S(1)}, bf16[64,768]{1,0:T(8,128)(2,1)S(1)}, bf16[64,768]{1,0:T(8,128)(2,1)S(1)}, bf16[64,768]{1,0:T(8,128)(2,1)S(1)}) custom-call(s32[4]{0:T(128)S(1)} %pad_add_fusion.place, bf16[256,1792]{1,0:T(8,128)(2,1)S(1)} %collective-permute-done.12.refs_0_.refs_12_.refs_4_, ...), custom_call_target="tpu_custom_call" | custom-call | flops 704643072 | bytes 5079040 | tf_op jit(solution)/shard_map/forward/pallas_call | solution.py:50
  65.6 3.5 %collective-permute-start.17 = (bf16[64,768]{1,0:T(8,128)(2,1)S(1)}, bf16[64,768]{1,0:T(8,128)(2,1)S(1)}, u32[]{:S(2)}, u32[]{:S(2)}) collective-permute-start(bf16[64,768]{1,0:T(8,128)(2,1)S(1)} %get-tuple-element.84), channel_id=1, source_target_pairs={{0,6},{1,7},{2,0},{3,1},{4,2},{5,3},{6,4},{7,5},{8,14},{9,15},{10,... | collective-permute-start | bytes 294920 | tf_op jit(solution)/shard_map/ppermute | solution.py:44
  69.2 0.9 collective-permute-start.19
  70.7 2.5 %collective-permute-start.16 = (bf16[64,768]{1,0:T(8,128)(2,1)S(1)}, bf16[64,768]{1,0:T(8,128)(2,1)S(1)}, u32[]{:S(2)}, u32[]{:S(2)}) collective-permute-start(bf16[64,768]{1,0:T(8,128)(2,1)S(1)} %middle.2.refs_0_), channel_id=1, source_target_pairs={{0,6},{1,7},{2,0},{3,1},{4,2},{5,3},{6,4},{7,5},{8,14},{9,15},{10,... | collective-permute-start | bytes 294920 | tf_op jit(solution)/shard_map/ppermute | solution.py:44
  73.2 2.2 %collective-permute-start.15 = (bf16[64,768]{1,0:T(8,128)(2,1)S(1)}, bf16[64,768]{1,0:T(8,128)(2,1)S(1)}, u32[]{:S(2)}, u32[]{:S(2)}) collective-permute-start(bf16[64,768]{1,0:T(8,128)(2,1)S(1)} %middle.2.refs_0_), channel_id=1, source_target_pairs={{0,4},{1,5},{2,6},{3,7},{4,0},{5,1},{6,2},{7,3},{8,12},{9,13},{10,... | collective-permute-start | bytes 294920 | tf_op jit(solution)/shard_map/ppermute | solution.py:44
  75.4 0.9 collective-permute-done.18.p2
  76.3 1.3 collective-permute-done.19.p3
  78.2 2.0 %collective-permute-start.22 = (bf16[64,768]{1,0:T(8,128)(2,1)S(1)}, bf16[64,768]{1,0:T(8,128)(2,1)S(1)}, u32[]{:S(2)}, u32[]{:S(2)}) collective-permute-start(bf16[64,768]{1,0:T(8,128)(2,1)S(1)} %middle.3.refs_4_), channel_id=1, source_target_pairs={{0,6},{1,7},{2,0},{3,1},{4,2},{5,3},{6,4},{7,5},{8,14},{9,15},{10,... | collective-permute-start | bytes 294920 | tf_op jit(solution)/shard_map/ppermute | solution.py:44
  80.3 0.9 collective-permute-start.20
  81.2 1.3 collective-permute-done.14.refs_1_
  82.5 1.0 collective-permute-done.22.refs_7_
  83.5 3.0 %collective-permute-done.21.refs_6_ = bf16[64,768]{1,0:T(8,128)(2,1)S(1)} collective-permute-done((bf16[64,768]{1,0:T(8,128)(2,1)S(1)}, bf16[64,768]{1,0:T(8,128)(2,1)S(1)}, u32[]{:S(2)}, u32[]{:S(2)}) %collective-permute-start.21) | collective-permute-done | bytes 98336 | tf_op jit(solution)/shard_map/ppermute | solution.py:44
  87.1 1.7 %their_grad.1 = (bf16[512,768]{1,0:T(8,128)(2,1)S(1)}, bf16[256,896]{1,0:T(8,128)(2,1)S(1)}, bf16[256,896]{1,0:T(8,128)(2,1)S(1)}, bf16[256,896]{1,0:T(8,128)(2,1)S(1)}) custom-call(s32[4]{0:T(128)S(1)} %pad_add_fusion.place, bf16[64,768]{1,0:T(8,128)(2,1)S(1)} %middle.2.refs_0_, bf16[64,768]{1,0:T(8,128)(2,1)S(1)} %collective-permute-done.14.refs_1_, ...), custom_call_target="tpu_custom_call" | custom-call | flops 704643072 | bytes 6619136 | tf_op jit(solution)/shard_map/their_grad/pallas_call | solution.py:50
  89.5 1.2 back.2
  90.9 3.2 %collective-permute-start.26 = (bf16[128,1792]{1,0:T(8,128)(2,1)S(1)}, bf16[128,1792]{1,0:T(8,128)(2,1)S(1)}, u32[]{:S(2)}, u32[]{:S(2)}) collective-permute-start(bf16[128,1792]{1,0:T(8,128)(2,1)S(1)} %get-tuple-element.96), channel_id=1, source_target_pairs={{0,24},{1,25},{2,26},{3,27},{4,28},{5,29},{6,30},{7,31},{8,0},{9,1... | collective-permute-start | bytes 1376264 | tf_op jit(solution)/shard_map/ppermute | solution.py:44
  94.1 2.0 %my_grad.1 = (f32[192,896]{1,0:T(8,128)S(1)}, bf16[192,896]{1,0:T(8,128)(2,1)S(1)}, bf16[192,896]{1,0:T(8,128)(2,1)S(1)}, bf16[192,896]{1,0:T(8,128)(2,1)S(1)}) custom-call(s32[4]{0:T(128)S(1)} %pad_add_fusion.place, bf16[256,896]{1,0:T(8,128)(2,1)S(1)} %collective-permute-done.23.got0, bf16[256,896]{1,0:T(8,128)(2,1)S(1)} %collective-permute-done.24.got1, ...), custom_call_target="tpu_custom_call" | custom-call | flops 704643072 | bytes 7553024 | tf_op jit(solution)/shard_map/my_grad/pallas_call | solution.py:50
  96.1 1.0 collective-permute-start.30
  97.5 1.3 collective-permute-start.32
  98.8 1.2 back.3
  100.1 4.8 %collective-permute-done.27.got_b.got_plus = bf16[128,1792]{1,0:T(8,128)(2,1)S(1)} collective-permute-done((bf16[128,1792]{1,0:T(8,128)(2,1)S(1)}, bf16[128,1792]{1,0:T(8,128)(2,1)S(1)}, u32[]{:S(2)}, u32[]{:S(2)}) %collective-permute-start.27) | collective-permute-done | bytes 458784 | tf_op jit(solution)/shard_map/ppermute | solution.py:44
  105.6 3.0 %collective-permute-start.28 = (bf16[64,1792]{1,0:T(8,128)(2,1)S(1)}, bf16[64,1792]{1,0:T(8,128)(2,1)S(1)}, u32[]{:S(2)}, u32[]{:S(2)}) collective-permute-start(bf16[64,1792]{1,0:T(8,128)(2,1)S(1)} %get-tuple-element.109), channel_id=1, source_target_pairs={{0,24},{1,25},{2,26},{3,27},{4,28},{5,29},{6,30},{7,31},{8,0},{9,1... | collective-permute-start | bytes 688136 | tf_op jit(solution)/shard_map/ppermute | solution.py:44
  108.6 4.3 %collective-permute-done.28.a1 = bf16[64,1792]{1,0:T(8,128)(2,1)S(1)} collective-permute-done((bf16[64,1792]{1,0:T(8,128)(2,1)S(1)}, bf16[64,1792]{1,0:T(8,128)(2,1)S(1)}, u32[]{:S(2)}, u32[]{:S(2)}) %collective-permute-start.28) | collective-permute-done | bytes 229408 | tf_op jit(solution)/shard_map/ppermute | solution.py:44
  112.9 3.4 %collective-permute-done.29.b3 = bf16[64,1792]{1,0:T(8,128)(2,1)S(1)} collective-permute-done((bf16[64,1792]{1,0:T(8,128)(2,1)S(1)}, bf16[64,1792]{1,0:T(8,128)(2,1)S(1)}, u32[]{:S(2)}, u32[]{:S(2)}) %collective-permute-start.29) | collective-permute-done | bytes 229408 | tf_op jit(solution)/shard_map/ppermute | solution.py:44
  116.4 1.5 %sum_back.1 = bf16[16,8,1792]{2,1,0:T(8,128)(2,1)} custom-call(s32[4]{0:T(128)S(1)} %pad_add_fusion.place, bf16[64,1792]{1,0:T(8,128)(2,1)S(1)} %get-tuple-element.114.a0, bf16[64,1792]{1,0:T(8,128)(2,1)S(1)} %get-tuple-element.115.b0, bf16[64,1792]{1,0:T(8,128)(2,1)S(1)} %collective-permute-done.28.a1, bf16[64,1792]{1,0:T(8,128)(2,1)S(1)} %collective-permute-done.29.b3, ...), custom_call_target="tpu_custom_call" | custom-call | bytes 2293760 | tf_op jit(solution)/shard_map/sum_back/pallas_call | solution.py:50
  117.9 3.7 %all-to-all-start.1 = ((bf16[16,8,1792]{2,1,0:T(8,128)(2,1)}), bf16[16,8,1792]{2,1,0:T(8,128)(2,1)S(1)}, u32[]{:S(2)}, u32[]{:S(2)}) async-start(bf16[16,8,1792]{2,1,0:T(8,128)(2,1)} %sum_back.1), calls=%async_computation.1 | async-start | bytes 917504 | tf_op jit(solution)/shard_map/all_to_all | solution.py:364
  121.6 6.9 %moments.1 = (f32[1,192,3584]{2,1,0:T(8,128)}, f32[1,192,3584]{2,1,0:T(8,128)}) custom-call(s32[4]{0:T(128)} %copy-done.2, f32[192,896]{1,0:T(8,128)} %copy-done.1, bf16[192,896]{1,0:T(8,128)(2,1)} %copy-done.6, bf16[192,896]{1,0:T(8,128)(2,1)} %copy-done.7, bf16[192,896]{1,0:T(8,128)(2,1)} %copy-done.8, f32[1,192,3584]{2,1,0:T(8,128)} %one.1, ...), custom_call_target="tpu_custom_call" | custom-call | flops 4128768 | bytes 11698176 | tf_op jit(solution)/shard_map/moments/pallas_call | solution.py:342
  128.6 3.2 %all-to-all-done.1.got = bf16[16,8,1792]{2,1,0:T(8,128)(2,1)S(1)} async-done(((bf16[16,8,1792]{2,1,0:T(8,128)(2,1)}), bf16[16,8,1792]{2,1,0:T(8,128)(2,1)S(1)}, u32[]{:S(2)}, u32[]{:S(2)}) %all-to-all-start.1) | async-done | bytes 458784 | tf_op jit(solution)/shard_map/all_to_all | solution.py:364
  131.7 2.2 %combine.1 = bf16[128,7168]{1,0:T(8,128)(2,1)} custom-call(s32[4]{0:T(128)S(1)} %copy-done.3, bf16[32,128]{1,0:T(8,128)(2,1)S(1)} %copy-done.4, bf16[16,8,1792]{2,1,0:T(8,128)(2,1)S(1)} %all-to-all-done.1.got), custom_call_target="tpu_custom_call" | custom-call | flops 58720256 | bytes 2301952 | tf_op jit(solution)/shard_map/combine/pallas_call | solution.py:50
  (58 shorter events, 8.7 us)
Async XLA Ops:
  4.1 7.4 %copy-start = (bf16[1,192,3584]{2,1,0:T(8,128)(2,1)S(1)}, bf16[1,192,3584]{2,1,0:T(8,128)(2,1)}, u32[]{:S(2)}) copy-start(bf16[1,192,3584]{2,1,0:T(8,128)(2,1)} %w.1) | copy-start | bytes 4128772
  4.2 23.3 %all-to-all-start = ((bf16[16,16,1792]{2,1,0:T(8,128)(2,1)}), bf16[16,16,1792]{2,1,0:T(8,128)(2,1)S(1)}, u32[]{:S(2)}, u32[]{:S(2)}) async-start(bf16[16,16,1792]{2,1,0:T(8,128)(2,1)} %get-tuple-element.64), calls=%async_computation | async-start | bytes 1835008 | tf_op jit(solution)/shard_map/all_to_all | solution.py:364
  11.5 104.9 %copy-start.2 = (s32[4]{0:T(128)}, s32[4]{0:T(128)S(1)}, u32[]{:S(2)}) copy-start(s32[4]{0:T(128)S(1)} %pad_add_fusion.place) | copy-start | bytes 52
  12.2 0.7 copy-start.5
  28.1 12.4 %collective-permute-start = (bf16[128,1792]{1,0:T(8,128)(2,1)S(1)}, bf16[128,1792]{1,0:T(8,128)(2,1)S(1)}, u32[]{:S(2)}, u32[]{:S(2)}) collective-permute-start(bf16[128,1792]{1,0:T(8,128)(2,1)S(1)} %get-tuple-element.67.a0.refs_0_.refs_8_), channel_id=1, source_target_pairs={{0,8},{1,9},{2,10},{3,11},{4,12},{5,13},{6,14},{7,15},{8,16},{9,17... | collective-permute-start | bytes 1376264 | tf_op jit(solution)/shard_map/ppermute | solution.py:44
  30.0 10.4 %collective-permute-start.1 = (bf16[128,1792]{1,0:T(8,128)(2,1)S(1)}, bf16[128,1792]{1,0:T(8,128)(2,1)S(1)}, u32[]{:S(2)}, u32[]{:S(2)}) collective-permute-start(bf16[128,1792]{1,0:T(8,128)(2,1)S(1)} %get-tuple-element.68.b0.refs_1_.refs_9_), channel_id=1, source_target_pairs={{0,24},{1,25},{2,26},{3,27},{4,28},{5,29},{6,30},{7,31},{8,0},{9,1... | collective-permute-start | bytes 1376264 | tf_op jit(solution)/shard_map/ppermute | solution.py:44
  32.2 12.7 %collective-permute-start.3 = (bf16[192,896]{1,0:T(8,128)(2,1)}, bf16[192,896]{1,0:T(8,128)(2,1)S(1)}, u32[]{:S(2)}, u32[]{:S(2)}) collective-permute-start(bf16[192,896]{1,0:T(8,128)(2,1)} %copy-done.5), channel_id=1, source_target_pairs={{0,4},{1,5},{2,6},{3,7},{4,0},{5,1},{6,2},{7,3},{8,12},{9,13},{10,... | collective-permute-start | bytes 1032200 | tf_op jit(solution)/shard_map/ppermute | solution.py:44
  33.1 14.7 %collective-permute-start.4 = (bf16[192,896]{1,0:T(8,128)(2,1)S(1)}, bf16[192,896]{1,0:T(8,128)(2,1)S(1)}, u32[]{:S(2)}, u32[]{:S(2)}) collective-permute-start(bf16[192,896]{1,0:T(8,128)(2,1)S(1)} %get-tuple-element.71), channel_id=1, source_target_pairs={{0,6},{1,7},{2,0},{3,1},{4,2},{5,3},{6,4},{7,5},{8,14},{9,15},{10,... | collective-permute-start | bytes 1032200 | tf_op jit(solution)/shard_map/ppermute | solution.py:44
  35.5 13.1 %collective-permute-start.2 = (bf16[192,896]{1,0:T(8,128)(2,1)S(1)}, bf16[192,896]{1,0:T(8,128)(2,1)S(1)}, u32[]{:S(2)}, u32[]{:S(2)}) collective-permute-start(bf16[192,896]{1,0:T(8,128)(2,1)S(1)} %get-tuple-element.65), channel_id=1, source_target_pairs={{0,2},{1,3},{2,4},{3,5},{4,6},{5,7},{6,0},{7,1},{8,10},{9,11},{10,... | collective-permute-start | bytes 1032200 | tf_op jit(solution)/shard_map/ppermute | solution.py:44
  41.1 19.5 %collective-permute-start.13 = (bf16[256,1792]{1,0:T(8,128)(2,1)S(1)}, bf16[256,1792]{1,0:T(8,128)(2,1)S(1)}, u32[]{:S(2)}, u32[]{:S(2)}) collective-permute-start(bf16[256,1792]{1,0:T(8,128)(2,1)S(1)} %get-tuple-element.83), channel_id=1, source_target_pairs={{0,24},{1,25},{2,26},{3,27},{4,28},{5,29},{6,30},{7,31},{8,0},{9,1... | collective-permute-start | bytes 2752520 | tf_op jit(solution)/shard_map/ppermute | solution.py:44
  44.2 19.8 %collective-permute-start.12 = (bf16[256,1792]{1,0:T(8,128)(2,1)S(1)}, bf16[256,1792]{1,0:T(8,128)(2,1)S(1)}, u32[]{:S(2)}, u32[]{:S(2)}) collective-permute-start(bf16[256,1792]{1,0:T(8,128)(2,1)S(1)} %get-tuple-element.72), channel_id=1, source_target_pairs={{0,8},{1,9},{2,10},{3,11},{4,12},{5,13},{6,14},{7,15},{8,16},{9,17... | collective-permute-start | bytes 2752520 | tf_op jit(solution)/shard_map/ppermute | solution.py:44
  48.6 1.7 %collective-permute-start.5 = (bf16[192,896]{1,0:T(8,128)(2,1)S(1)}, bf16[192,896]{1,0:T(8,128)(2,1)S(1)}, u32[]{:S(2)}, u32[]{:S(2)}) collective-permute-start(bf16[192,896]{1,0:T(8,128)(2,1)S(1)} %get-tuple-element.73.refs_0_), channel_id=1, source_target_pairs={{0,1},{1,0},{2,3},{3,2},{4,5},{5,4},{6,7},{7,6},{8,9},{9,8},{10,11... | collective-permute-start | bytes 1032200 | tf_op jit(solution)/shard_map/ppermute | solution.py:44
  48.6 2.1 %collective-permute-start.6 = (bf16[192,896]{1,0:T(8,128)(2,1)S(1)}, bf16[192,896]{1,0:T(8,128)(2,1)S(1)}, u32[]{:S(2)}, u32[]{:S(2)}) collective-permute-start(bf16[192,896]{1,0:T(8,128)(2,1)S(1)} %collective-permute-done.2.refs_1_), channel_id=1, source_target_pairs={{0,1},{1,0},{2,3},{3,2},{4,5},{5,4},{6,7},{7,6},{8,9},{9,8},{10,11... | collective-permute-start | bytes 1032200 | tf_op jit(solution)/shard_map/ppermute | solution.py:44
  49.1 2.1 %collective-permute-start.7 = (bf16[192,896]{1,0:T(8,128)(2,1)S(1)}, bf16[192,896]{1,0:T(8,128)(2,1)S(1)}, u32[]{:S(2)}, u32[]{:S(2)}) collective-permute-start(bf16[192,896]{1,0:T(8,128)(2,1)S(1)} %collective-permute-done.3.refs_2_), channel_id=1, source_target_pairs={{0,1},{1,0},{2,3},{3,2},{4,5},{5,4},{6,7},{7,6},{8,9},{9,8},{10,11... | collective-permute-start | bytes 1032200 | tf_op jit(solution)/shard_map/ppermute | solution.py:44
  50.3 1.7 %collective-permute-start.8 = (bf16[192,896]{1,0:T(8,128)(2,1)S(1)}, bf16[192,896]{1,0:T(8,128)(2,1)S(1)}, u32[]{:S(2)}, u32[]{:S(2)}) collective-permute-start(bf16[192,896]{1,0:T(8,128)(2,1)S(1)} %collective-permute-done.4.refs_3_), channel_id=1, source_target_pairs={{0,1},{1,0},{2,3},{3,2},{4,5},{5,4},{6,7},{7,6},{8,9},{9,8},{10,11... | collective-permute-start | bytes 1032200 | tf_op jit(solution)/shard_map/ppermute | solution.py:44
  54.3 14.8 %collective-permute-start.9 = (bf16[64,768]{1,0:T(8,128)(2,1)S(1)}, bf16[64,768]{1,0:T(8,128)(2,1)S(1)}, u32[]{:S(2)}, u32[]{:S(2)}) collective-permute-start(bf16[64,768]{1,0:T(8,128)(2,1)S(1)} %get-tuple-element.80), channel_id=1, source_target_pairs={{0,6},{1,7},{2,0},{3,1},{4,2},{5,3},{6,4},{7,5},{8,14},{9,15},{10,... | collective-permute-start | bytes 294920 | tf_op jit(solution)/shard_map/ppermute | solution.py:44
  56.2 12.9 %collective-permute-start.10 = (bf16[64,768]{1,0:T(8,128)(2,1)S(1)}, bf16[64,768]{1,0:T(8,128)(2,1)S(1)}, u32[]{:S(2)}, u32[]{:S(2)}) collective-permute-start(bf16[64,768]{1,0:T(8,128)(2,1)S(1)} %get-tuple-element.81), channel_id=1, source_target_pairs={{0,4},{1,5},{2,6},{3,7},{4,0},{5,1},{6,2},{7,3},{8,12},{9,13},{10,... | collective-permute-start | bytes 294920 | tf_op jit(solution)/shard_map/ppermute | solution.py:44
  56.9 12.2 %collective-permute-start.11 = (bf16[64,768]{1,0:T(8,128)(2,1)S(1)}, bf16[64,768]{1,0:T(8,128)(2,1)S(1)}, u32[]{:S(2)}, u32[]{:S(2)}) collective-permute-start(bf16[64,768]{1,0:T(8,128)(2,1)S(1)} %get-tuple-element.82), channel_id=1, source_target_pairs={{0,2},{1,3},{2,4},{3,5},{4,6},{5,7},{6,0},{7,1},{8,10},{9,11},{10,... | collective-permute-start | bytes 294920 | tf_op jit(solution)/shard_map/ppermute | solution.py:44
  65.6 12.0 %collective-permute-start.17 = (bf16[64,768]{1,0:T(8,128)(2,1)S(1)}, bf16[64,768]{1,0:T(8,128)(2,1)S(1)}, u32[]{:S(2)}, u32[]{:S(2)}) collective-permute-start(bf16[64,768]{1,0:T(8,128)(2,1)S(1)} %get-tuple-element.84), channel_id=1, source_target_pairs={{0,6},{1,7},{2,0},{3,1},{4,2},{5,3},{6,4},{7,5},{8,14},{9,15},{10,... | collective-permute-start | bytes 294920 | tf_op jit(solution)/shard_map/ppermute | solution.py:44
  69.1 7.2 %collective-permute-start.18 = (bf16[64,768]{1,0:T(8,128)(2,1)S(1)}, bf16[64,768]{1,0:T(8,128)(2,1)S(1)}, u32[]{:S(2)}, u32[]{:S(2)}) collective-permute-start(bf16[64,768]{1,0:T(8,128)(2,1)S(1)} %get-tuple-element.90), channel_id=1, source_target_pairs={{0,4},{1,5},{2,6},{3,7},{4,0},{5,1},{6,2},{7,3},{8,12},{9,13},{10,... | collective-permute-start | bytes 294920 | tf_op jit(solution)/shard_map/ppermute | solution.py:44
  69.2 8.4 %collective-permute-start.19 = (bf16[64,768]{1,0:T(8,128)(2,1)S(1)}, bf16[64,768]{1,0:T(8,128)(2,1)S(1)}, u32[]{:S(2)}, u32[]{:S(2)}) collective-permute-start(bf16[64,768]{1,0:T(8,128)(2,1)S(1)} %get-tuple-element.91), channel_id=1, source_target_pairs={{0,2},{1,3},{2,4},{3,5},{4,6},{5,7},{6,0},{7,1},{8,10},{9,11},{10,... | collective-permute-start | bytes 294920 | tf_op jit(solution)/shard_map/ppermute | solution.py:44
  70.7 9.6 %collective-permute-start.16 = (bf16[64,768]{1,0:T(8,128)(2,1)S(1)}, bf16[64,768]{1,0:T(8,128)(2,1)S(1)}, u32[]{:S(2)}, u32[]{:S(2)}) collective-permute-start(bf16[64,768]{1,0:T(8,128)(2,1)S(1)} %middle.2.refs_0_), channel_id=1, source_target_pairs={{0,6},{1,7},{2,0},{3,1},{4,2},{5,3},{6,4},{7,5},{8,14},{9,15},{10,... | collective-permute-start | bytes 294920 | tf_op jit(solution)/shard_map/ppermute | solution.py:44
  73.2 8.0 %collective-permute-start.15 = (bf16[64,768]{1,0:T(8,128)(2,1)S(1)}, bf16[64,768]{1,0:T(8,128)(2,1)S(1)}, u32[]{:S(2)}, u32[]{:S(2)}) collective-permute-start(bf16[64,768]{1,0:T(8,128)(2,1)S(1)} %middle.2.refs_0_), channel_id=1, source_target_pairs={{0,4},{1,5},{2,6},{3,7},{4,0},{5,1},{6,2},{7,3},{8,12},{9,13},{10,... | collective-permute-start | bytes 294920 | tf_op jit(solution)/shard_map/ppermute | solution.py:44
  76.3 6.1 %collective-permute-start.14 = (bf16[64,768]{1,0:T(8,128)(2,1)S(1)}, bf16[64,768]{1,0:T(8,128)(2,1)S(1)}, u32[]{:S(2)}, u32[]{:S(2)}) collective-permute-start(bf16[64,768]{1,0:T(8,128)(2,1)S(1)} %middle.2.refs_0_), channel_id=1, source_target_pairs={{0,2},{1,3},{2,4},{3,5},{4,6},{5,7},{6,0},{7,1},{8,10},{9,11},{10,... | collective-permute-start | bytes 294920 | tf_op jit(solution)/shard_map/ppermute | solution.py:44
  78.2 5.2 %collective-permute-start.22 = (bf16[64,768]{1,0:T(8,128)(2,1)S(1)}, bf16[64,768]{1,0:T(8,128)(2,1)S(1)}, u32[]{:S(2)}, u32[]{:S(2)}) collective-permute-start(bf16[64,768]{1,0:T(8,128)(2,1)S(1)} %middle.3.refs_4_), channel_id=1, source_target_pairs={{0,6},{1,7},{2,0},{3,1},{4,2},{5,3},{6,4},{7,5},{8,14},{9,15},{10,... | collective-permute-start | bytes 294920 | tf_op jit(solution)/shard_map/ppermute | solution.py:44
  80.2 6.2 %collective-permute-start.21 = (bf16[64,768]{1,0:T(8,128)(2,1)S(1)}, bf16[64,768]{1,0:T(8,128)(2,1)S(1)}, u32[]{:S(2)}, u32[]{:S(2)}) collective-permute-start(bf16[64,768]{1,0:T(8,128)(2,1)S(1)} %middle.3.refs_4_), channel_id=1, source_target_pairs={{0,4},{1,5},{2,6},{3,7},{4,0},{5,1},{6,2},{7,3},{8,12},{9,13},{10,... | collective-permute-start | bytes 294920 | tf_op jit(solution)/shard_map/ppermute | solution.py:44
  80.3 6.9 %collective-permute-start.20 = (bf16[64,768]{1,0:T(8,128)(2,1)S(1)}, bf16[64,768]{1,0:T(8,128)(2,1)S(1)}, u32[]{:S(2)}, u32[]{:S(2)}) collective-permute-start(bf16[64,768]{1,0:T(8,128)(2,1)S(1)} %middle.3.refs_4_), channel_id=1, source_target_pairs={{0,2},{1,3},{2,4},{3,5},{4,6},{5,7},{6,0},{7,1},{8,10},{9,11},{10,... | collective-permute-start | bytes 294920 | tf_op jit(solution)/shard_map/ppermute | solution.py:44
  88.8 5.2 %collective-permute-start.23 = (bf16[256,896]{1,0:T(8,128)(2,1)S(1)}, bf16[256,896]{1,0:T(8,128)(2,1)S(1)}, u32[]{:S(2)}, u32[]{:S(2)}) collective-permute-start(bf16[256,896]{1,0:T(8,128)(2,1)S(1)} %get-tuple-element.93), channel_id=1, source_target_pairs={{0,1},{1,0},{2,3},{3,2},{4,5},{5,4},{6,7},{7,6},{8,9},{9,8},{10,11... | collective-permute-start | bytes 1376264 | tf_op jit(solution)/shard_map/ppermute | solution.py:44
  88.9 5.2 %collective-permute-start.24 = (bf16[256,896]{1,0:T(8,128)(2,1)S(1)}, bf16[256,896]{1,0:T(8,128)(2,1)S(1)}, u32[]{:S(2)}, u32[]{:S(2)}) collective-permute-start(bf16[256,896]{1,0:T(8,128)(2,1)S(1)} %get-tuple-element.94), channel_id=1, source_target_pairs={{0,1},{1,0},{2,3},{3,2},{4,5},{5,4},{6,7},{7,6},{8,9},{9,8},{10,11... | collective-permute-start | bytes 1376264 | tf_op jit(solution)/shard_map/ppermute | solution.py:44
  89.4 4.7 %collective-permute-start.25 = (bf16[256,896]{1,0:T(8,128)(2,1)S(1)}, bf16[256,896]{1,0:T(8,128)(2,1)S(1)}, u32[]{:S(2)}, u32[]{:S(2)}) collective-permute-start(bf16[256,896]{1,0:T(8,128)(2,1)S(1)} %get-tuple-element.95), channel_id=1, source_target_pairs={{0,1},{1,0},{2,3},{3,2},{4,5},{5,4},{6,7},{7,6},{8,9},{9,8},{10,11... | collective-permute-start | bytes 1376264 | tf_op jit(solution)/shard_map/ppermute | solution.py:44
  90.8 14.1 %collective-permute-start.27 = (bf16[128,1792]{1,0:T(8,128)(2,1)S(1)}, bf16[128,1792]{1,0:T(8,128)(2,1)S(1)}, u32[]{:S(2)}, u32[]{:S(2)}) collective-permute-start(bf16[128,1792]{1,0:T(8,128)(2,1)S(1)} %get-tuple-element.104), channel_id=1, source_target_pairs={{0,8},{1,9},{2,10},{3,11},{4,12},{5,13},{6,14},{7,15},{8,16},{9,17... | collective-permute-start | bytes 1376264 | tf_op jit(solution)/shard_map/ppermute | solution.py:44
  90.9 14.1 %collective-permute-start.26 = (bf16[128,1792]{1,0:T(8,128)(2,1)S(1)}, bf16[128,1792]{1,0:T(8,128)(2,1)S(1)}, u32[]{:S(2)}, u32[]{:S(2)}) collective-permute-start(bf16[128,1792]{1,0:T(8,128)(2,1)S(1)} %get-tuple-element.96), channel_id=1, source_target_pairs={{0,24},{1,25},{2,26},{3,27},{4,28},{5,29},{6,30},{7,31},{8,0},{9,1... | collective-permute-start | bytes 1376264 | tf_op jit(solution)/shard_map/ppermute | solution.py:44
  96.1 9.5 %copy-start.1 = (f32[192,896]{1,0:T(8,128)}, f32[192,896]{1,0:T(8,128)S(1)}, u32[]{:S(2)}) copy-start(f32[192,896]{1,0:T(8,128)S(1)} %get-tuple-element.98.g0) | copy-start | bytes 2064388
  96.1 20.3 %collective-permute-start.30 = (bf16[192,896]{1,0:T(8,128)(2,1)S(1)}, bf16[192,896]{1,0:T(8,128)(2,1)S(1)}, u32[]{:S(2)}, u32[]{:S(2)}) collective-permute-start(bf16[192,896]{1,0:T(8,128)(2,1)S(1)} %get-tuple-element.111), channel_id=1, source_target_pairs={{0,6},{1,7},{2,0},{3,1},{4,2},{5,3},{6,4},{7,5},{8,14},{9,15},{10,... | collective-permute-start | bytes 1032200 | tf_op jit(solution)/shard_map/ppermute | solution.py:44
  97.0 19.3 %collective-permute-start.31 = (bf16[192,896]{1,0:T(8,128)(2,1)S(1)}, bf16[192,896]{1,0:T(8,128)(2,1)S(1)}, u32[]{:S(2)}, u32[]{:S(2)}) collective-permute-start(bf16[192,896]{1,0:T(8,128)(2,1)S(1)} %get-tuple-element.112), channel_id=1, source_target_pairs={{0,4},{1,5},{2,6},{3,7},{4,0},{5,1},{6,2},{7,3},{8,12},{9,13},{10,... | collective-permute-start | bytes 1032200 | tf_op jit(solution)/shard_map/ppermute | solution.py:44
  97.5 18.9 %collective-permute-start.32 = (bf16[192,896]{1,0:T(8,128)(2,1)S(1)}, bf16[192,896]{1,0:T(8,128)(2,1)S(1)}, u32[]{:S(2)}, u32[]{:S(2)}) collective-permute-start(bf16[192,896]{1,0:T(8,128)(2,1)S(1)} %get-tuple-element.113), channel_id=1, source_target_pairs={{0,2},{1,3},{2,4},{3,5},{4,6},{5,7},{6,0},{7,1},{8,10},{9,11},{10,... | collective-permute-start | bytes 1032200 | tf_op jit(solution)/shard_map/ppermute | solution.py:44
  105.6 7.4 %collective-permute-start.28 = (bf16[64,1792]{1,0:T(8,128)(2,1)S(1)}, bf16[64,1792]{1,0:T(8,128)(2,1)S(1)}, u32[]{:S(2)}, u32[]{:S(2)}) collective-permute-start(bf16[64,1792]{1,0:T(8,128)(2,1)S(1)} %get-tuple-element.109), channel_id=1, source_target_pairs={{0,24},{1,25},{2,26},{3,27},{4,28},{5,29},{6,30},{7,31},{8,0},{9,1... | collective-permute-start | bytes 688136 | tf_op jit(solution)/shard_map/ppermute | solution.py:44
  108.6 7.8 %collective-permute-start.29 = (bf16[64,1792]{1,0:T(8,128)(2,1)S(1)}, bf16[64,1792]{1,0:T(8,128)(2,1)S(1)}, u32[]{:S(2)}, u32[]{:S(2)}) collective-permute-start(bf16[64,1792]{1,0:T(8,128)(2,1)S(1)} %get-tuple-element.110), channel_id=1, source_target_pairs={{0,8},{1,9},{2,10},{3,11},{4,12},{5,13},{6,14},{7,15},{8,16},{9,17... | collective-permute-start | bytes 688136 | tf_op jit(solution)/shard_map/ppermute | solution.py:44
  116.4 5.2 %copy-start.6 = (bf16[192,896]{1,0:T(8,128)(2,1)}, bf16[192,896]{1,0:T(8,128)(2,1)S(1)}, u32[]{:S(2)}) copy-start(bf16[192,896]{1,0:T(8,128)(2,1)S(1)} %collective-permute-done.30.g1) | copy-start | bytes 1032196
  116.4 5.2 %copy-start.7 = (bf16[192,896]{1,0:T(8,128)(2,1)}, bf16[192,896]{1,0:T(8,128)(2,1)S(1)}, u32[]{:S(2)}) copy-start(bf16[192,896]{1,0:T(8,128)(2,1)S(1)} %collective-permute-done.31.g2) | copy-start | bytes 1032196
  116.4 5.2 %copy-start.8 = (bf16[192,896]{1,0:T(8,128)(2,1)}, bf16[192,896]{1,0:T(8,128)(2,1)S(1)}, u32[]{:S(2)}) copy-start(bf16[192,896]{1,0:T(8,128)(2,1)S(1)} %collective-permute-done.32.g3) | copy-start | bytes 1032196
  117.9 13.8 %all-to-all-start.1 = ((bf16[16,8,1792]{2,1,0:T(8,128)(2,1)}), bf16[16,8,1792]{2,1,0:T(8,128)(2,1)S(1)}, u32[]{:S(2)}, u32[]{:S(2)}) async-start(bf16[16,8,1792]{2,1,0:T(8,128)(2,1)} %sum_back.1), calls=%async_computation.1 | async-start | bytes 917504 | tf_op jit(solution)/shard_map/all_to_all | solution.py:364
  121.6 10.1 %copy-start.3 = (s32[4]{0:T(128)S(1)}, s32[4]{0:T(128)}, u32[]{:S(2)}) copy-start(s32[4]{0:T(128)} %copy-done.2) | copy-start | bytes 52
  121.6 10.1 %copy-start.4 = (bf16[32,128]{1,0:T(8,128)(2,1)S(1)}, bf16[32,128]{1,0:T(8,128)(2,1)}, u32[]{:S(2)}) copy-start(bf16[32,128]{1,0:T(8,128)(2,1)} %get-tuple-element.63.pick) | copy-start | bytes 24580

commit v5 on v4

--- a/solution.py
+++ b/solution.py
@@ -240,10 +240,10 @@
     out[:, 2 * width :] = (act * up).astype(BF)
 
 
-def back_kernel(first, place, held, own, other, *outs):
+def back_kernel(place, held, own, other, *outs):
     c = place[3]
     width = 2 * N * HID
-    h = held[first : first + CHUNK, :width]
+    h = held[:, :width]
     if len(outs) == 2:
         minus, plus = outs
         targets = (minus, 0), (plus, 0), (plus, HELD), (minus, HELD)
@@ -261,35 +261,56 @@
     out_b[...] = (own_b[...].astype(F32) + got_b[:HELD].astype(F32)).astype(BF)
 
 
-def weight_grad(half, held, chunks, out):
-    pieces = (*pieces_of(chunks[:4]), *pieces_of(chunks[4:]))
+def weight_grad(half, held, chunk, add):
+    pieces = pieces_of(chunk)
     width = 2 * N * HID
     cols = pl.ds(aligned(half * EIGHTH), EIGHTH)
     x = jnp.concatenate([v[:HELD, cols] for v in pieces], axis=0)
-    out[:width] = mm(held[:, :width], x, TN).astype(out.dtype)
+    add(slice(0, width), mm(held[:, :width], x, TN))
     g = jnp.concatenate([v[HELD : 2 * HELD, cols] for v in pieces], axis=0)
-    out[width:] = mm(held[:, width:], g, TN).astype(out.dtype)
+    add(slice(width, 3 * N * HID), mm(held[:, width:], g, TN))
+
+
+def assemble(y, parts, held):
+    for k, h in enumerate(parts):
+        at = wrap(y - k) * ROWS
+        for s in range(2):
+            rows = pl.ds(pl.multiple_of(s * GROUPED + at, ROWS), ROWS)
+            held[rows, :] = h[s * ROWS : (s + 1) * ROWS]
+
+
+def first_grad_kernel(place, *refs):
+    *chunk, held, theirs, mine = refs[N:]
+    assemble(place[2], refs[:N], held)
+    for out, half in ((theirs, 1 - place[3]), (mine, place[3])):
+
+        def add(rows, value, out=out):
+            out[rows] = value
+
+        weight_grad(half, held, chunk, add)
 
 
 def their_grad_kernel(place, *refs):
-    parts = refs[:N], refs[N : 2 * N]
-    *chunks, held, o0, o1, o2, theirs = refs[2 * N :]
+    before, plus, minus, held, o0, o1, o2 = refs[N:]
+    assemble(place[2], refs[:N], held)
+
+    def add(rows, value):
+        total = (value + before[rows]).astype(BF)
+        for i, o in enumerate((o0, o1, o2)):
+            at = i * N * HID - rows.start
+            if 0 <= at < total.shape[0]:
+                o[...] = total[at : at + N * HID]
+
+    weight_grad(1 - place[3], held, (plus, minus), add)
+
+
+def my_grad_kernel(place, got0, got1, got2, held, before, plus, minus, o0, o1, o2, o3, mine):
     y = place[2]
-    for i, chunk in enumerate(parts):
-        for k, h in enumerate(chunk):
-            at = wrap(y - k) * ROWS
-            for s in range(2):
-                rows = pl.ds(pl.multiple_of(i * CHUNK + s * GROUPED + at, ROWS), ROWS)
-                held[rows, :] = h[s * ROWS : (s + 1) * ROWS]
-    weight_grad(1 - place[3], held, chunks, theirs)
-    for i, o in enumerate((o0, o1, o2)):
-        o[...] = theirs[i * N * HID : (i + 1) * N * HID]
-
-
-def my_grad_kernel(place, got0, got1, got2, held, *refs):
-    *chunks, o0, o1, o2, o3, mine = refs
-    y = place[2]
-    weight_grad(place[3], held, chunks, mine)
+
+    def add(rows, value):
+        mine[rows] = value + before[rows]
+
+    weight_grad(place[3], held, (plus, minus), add)
     for k, o in enumerate((o0, o1, o2, o3)):
         block = pl.multiple_of(wrap(y - k) * HID, HID)
         for part, got in enumerate((got0, got1, got2)):
@@ -402,7 +423,7 @@
 def back_part(place, held, w_own, w_other, chunk):
     shape = (HELD, QUARTER) if chunk == 0 else (2 * HELD, QUARTER)
     return call(
-        functools.partial(back_kernel, chunk * CHUNK),
+        back_kernel,
         "back",
         [(shape, BF)] * (CHUNK // shape[0]),
         place,
@@ -461,19 +482,26 @@
     mid_two = middle_part(place, part_two)
     held_two = spread([mid_two] * N, "y")
     flops = N * GROUPED * QUARTER * 3 * width
-    held, *theirs = call(
+    held_one, first_theirs, first_mine = call(
+        first_grad_kernel,
+        "first_grad",
+        [((CHUNK, 3 * width), BF)] + [((3 * width, EIGHTH), F32)] * 2,
+        place,
+        *held_one,
+        *first,
+        flops=flops,
+    )
+    held_two, *theirs = call(
         their_grad_kernel,
         "their_grad",
-        [((2 * CHUNK, 3 * width), BF)] + [((width, EIGHTH), BF)] * 3,
-        place,
-        *held_one,
+        [((CHUNK, 3 * width), BF)] + [((width, EIGHTH), BF)] * 3,
+        place,
         *held_two,
-        *first,
+        first_theirs,
         *second,
-        flops=flops,
-        scratch=[pltpu.VMEM((3 * width, EIGHTH), BF)],
-    )
-    minus, plus = back_part(place, held, w_own, w_other, 1)
+        flops=flops // 2,
+    )
+    minus, plus = back_part(place, held_two, w_own, w_other, 1)
     got_minus, got_plus = turn(minus, "z", -1), turn(plus, "z", 1)
     got = [turn(v, "c", 1) for v in theirs]
     blocks = call(
@@ -482,13 +510,13 @@
         [((block_rows, EIGHTH), F32)] + [((block_rows, EIGHTH), BF)] * 3,
         place,
         *got,
-        after(held, minus),
-        *first,
+        after(held_two, minus),
+        first_mine,
         *second,
-        flops=flops,
+        flops=flops // 2,
         scratch=[pltpu.VMEM((3 * width, EIGHTH), F32)],
     )
-    a0, b0, a1, b3 = back_part(place, after(held, blocks[0]), w_own, w_other, 0)
+    a0, b0, a1, b3 = back_part(place, after(held_one, blocks[0]), w_own, w_other, 0)
     a1, b3 = pass_on(place, *after((a1, b3, got_minus, got_plus), blocks[0]))
     a1, b3 = turn(a1, "z", -1), turn(b3, "z", 1)
     blocks = spread(blocks, "y", -1)

time: 135 us -> 132 us (0.978)
  waiting for transfers between devices: 56.9 us -> 55.2 us
    pallas_call x15 -> x16, Pallas kernels: 17.5 us -> 18 us  [call(): pl.pallas_call(kernel, name=name, out_shape=outs, in_specs=[pl.BlockSpec(...]
  transfers between devices with their start and end apart: 35 -> 35, of which waited for: 21 -> 20; matrix products, arithmetic and copies ran while one was open for 0% -> 0% of each run, Pallas kernels for 14% -> 15%
where the time goes in v5:
time: 132 us
  waiting for transfers between devices  55.2 us (42%)
  starting transfers between devices  46 us (35%)
  Pallas kernels  28.5 us (22%)
    ppermute x33, waiting for transfers between devices, turn(): return lax.ppermute(value, ('expert', 'dp'), rotation(axis, step))  38 us
    ppermute x33, starting transfers between devices, turn(): return lax.ppermute(value, ('expert', 'dp'), rotation(axis, step))  35.3 us
    pallas_call x16, Pallas kernels, call(): pl.pallas_call(kernel, name=name, out_shape=outs, in_specs=[pl.BlockSpec(...  18 us
    all_to_all x2, waiting for transfers between devices, exchange(): lax.all_to_all(value, 'expert', 0, 0, axis_index_groups=list(groups.value...  17.3 us
    all_to_all x2, starting transfers between devices, exchange(): lax.all_to_all(value, 'expert', 0, 0, axis_index_groups=list(groups.value...  10.7 us
    pallas_call x1, Pallas kernels, moments(): pl.pallas_call(moments_kernel, name='moments', grid_spec=pltpu.PrefetchSc...  6.9 us
    pallas_call x1, Pallas kernels, route(): pl.pallas_call(route_kernel, name='route', in_specs=[hbm] * 4, out_specs=...  3.6 us
  transfers between devices with their start and end apart: 35, of which 20 were waited for; matrix products, arithmetic and copies ran while one was open for 0% of the time, Pallas kernels for 15%

profile of v5, /device:TPU:0, one launch (start us, length us, event | category | flops | bytes accessed | tf_op | source)
XLA Modules:
  0.0 131.8 jit_solution(2385603863565782754)
XLA Ops:
  0.6 3.6 %route.1 = (bf16[16,16,1792]{2,1,0:T(8,128)(2,1)}, bf16[32,128]{1,0:T(8,128)(2,1)}) custom-call(s32[8,128]{1,0:T(8,128)} %bitcast.6, f32[8,128]{1,0:T(8,128)} %bitcast.7, bf16[128,7168]{1,0:T(8,128)(2,1)} %tokens.1, bf16[128,7168]{1,0:T(8,128)(2,1)} %grads.1), custom_call_target="tpu_custom_call" | custom-call | flops 117440512 | bytes 5505024 | tf_op jit(solution)/shard_map/route/pallas_call | solution.py:143
  4.3 7.1 %all-to-all-start = ((bf16[16,16,1792]{2,1,0:T(8,128)(2,1)}), bf16[16,16,1792]{2,1,0:T(8,128)(2,1)S(1)}, u32[]{:S(2)}, u32[]{:S(2)}) async-start(bf16[16,16,1792]{2,1,0:T(8,128)(2,1)} %get-tuple-element.67), calls=%async_computation | async-start | bytes 1835008 | tf_op jit(solution)/shard_map/all_to_all | solution.py:385
  12.2 0.7 copy-done.5
  12.9 14.5 %all-to-all-done.got = bf16[16,16,1792]{2,1,0:T(8,128)(2,1)S(1)} async-done(((bf16[16,16,1792]{2,1,0:T(8,128)(2,1)}), bf16[16,16,1792]{2,1,0:T(8,128)(2,1)S(1)}, u32[]{:S(2)}, u32[]{:S(2)}) %all-to-all-start) | async-done | bytes 917536 | tf_op jit(solution)/shard_map/all_to_all | solution.py:385
  28.0 2.0 %collective-permute-start = (bf16[128,1792]{1,0:T(8,128)(2,1)S(1)}, bf16[128,1792]{1,0:T(8,128)(2,1)S(1)}, u32[]{:S(2)}, u32[]{:S(2)}) collective-permute-start(bf16[128,1792]{1,0:T(8,128)(2,1)S(1)} %get-tuple-element.70.a0.refs_0_.refs_4_), channel_id=1, source_target_pairs={{0,8},{1,9},{2,10},{3,11},{4,12},{5,13},{6,14},{7,15},{8,16},{9,17... | collective-permute-start | bytes 1376264 | tf_op jit(solution)/shard_map/ppermute | solution.py:44
  30.0 2.2 %collective-permute-start.1 = (bf16[128,1792]{1,0:T(8,128)(2,1)S(1)}, bf16[128,1792]{1,0:T(8,128)(2,1)S(1)}, u32[]{:S(2)}, u32[]{:S(2)}) collective-permute-start(bf16[128,1792]{1,0:T(8,128)(2,1)S(1)} %get-tuple-element.71.b0.refs_1_.refs_5_), channel_id=1, source_target_pairs={{0,24},{1,25},{2,26},{3,27},{4,28},{5,29},{6,30},{7,31},{8,0},{9,1... | collective-permute-start | bytes 1376264 | tf_op jit(solution)/shard_map/ppermute | solution.py:44
  32.2 0.9 collective-permute-start.3
  33.1 2.4 %collective-permute-start.4 = (bf16[192,896]{1,0:T(8,128)(2,1)S(1)}, bf16[192,896]{1,0:T(8,128)(2,1)S(1)}, u32[]{:S(2)}, u32[]{:S(2)}) collective-permute-start(bf16[192,896]{1,0:T(8,128)(2,1)S(1)} %get-tuple-element.74), channel_id=1, source_target_pairs={{0,6},{1,7},{2,0},{3,1},{4,2},{5,3},{6,4},{7,5},{8,14},{9,15},{10,... | collective-permute-start | bytes 1032200 | tf_op jit(solution)/shard_map/ppermute | solution.py:44
  35.5 4.9 %collective-permute-done.a1.refs_2_.refs_6_ = bf16[128,1792]{1,0:T(8,128)(2,1)S(1)} collective-permute-done((bf16[128,1792]{1,0:T(8,128)(2,1)S(1)}, bf16[128,1792]{1,0:T(8,128)(2,1)S(1)}, u32[]{:S(2)}, u32[]{:S(2)}) %collective-permute-start) | collective-permute-done | bytes 458784 | tf_op jit(solution)/shard_map/ppermute | solution.py:44
  41.1 3.1 %collective-permute-start.13 = (bf16[256,1792]{1,0:T(8,128)(2,1)S(1)}, bf16[256,1792]{1,0:T(8,128)(2,1)S(1)}, u32[]{:S(2)}, u32[]{:S(2)}) collective-permute-start(bf16[256,1792]{1,0:T(8,128)(2,1)S(1)} %get-tuple-element.86), channel_id=1, source_target_pairs={{0,24},{1,25},{2,26},{3,27},{4,28},{5,29},{6,30},{7,31},{8,0},{9,1... | collective-permute-start | bytes 2752520 | tf_op jit(solution)/shard_map/ppermute | solution.py:44
  44.2 0.7 collective-permute-done.3.refs_2_
  44.9 2.9 %collective-permute-done.4.refs_3_ = bf16[192,896]{1,0:T(8,128)(2,1)S(1)} collective-permute-done((bf16[192,896]{1,0:T(8,128)(2,1)S(1)}, bf16[192,896]{1,0:T(8,128)(2,1)S(1)}, u32[]{:S(2)}, u32[]{:S(2)}) %collective-permute-start.4) | collective-permute-done | bytes 344096 | tf_op jit(solution)/shard_map/ppermute | solution.py:44
  47.8 0.8 collective-permute-done.2.refs_1_
  49.1 1.1 collective-permute-done.5.refs_4_
  51.9 0.8 stack_weights.1
  52.6 1.6 %forward.2 = (f32[64,768]{1,0:T(8,128)S(1)}, bf16[64,768]{1,0:T(8,128)(2,1)S(1)}, bf16[64,768]{1,0:T(8,128)(2,1)S(1)}, bf16[64,768]{1,0:T(8,128)(2,1)S(1)}) custom-call(s32[4]{0:T(128)S(1)} %pad_add_fusion.place, bf16[128,1792]{1,0:T(8,128)(2,1)S(1)} %get-tuple-element.70.a0.refs_0_.refs_4_, bf16[128,1792]{1,0:T(8,128)(2,1)S(1)} %get-tuple-element.71.b0.refs_1_.refs_5_, ...), custom_call_target="tpu_custom_call" | custom-call | flops 704643072 | bytes 5079040 | tf_op jit(solution)/shard_map/forward/pallas_call | solution.py:50
  54.2 1.9 %collective-permute-start.9 = (bf16[64,768]{1,0:T(8,128)(2,1)S(1)}, bf16[64,768]{1,0:T(8,128)(2,1)S(1)}, u32[]{:S(2)}, u32[]{:S(2)}) collective-permute-start(bf16[64,768]{1,0:T(8,128)(2,1)S(1)} %get-tuple-element.83), channel_id=1, source_target_pairs={{0,6},{1,7},{2,0},{3,1},{4,2},{5,3},{6,4},{7,5},{8,14},{9,15},{10,... | collective-permute-start | bytes 294920 | tf_op jit(solution)/shard_map/ppermute | solution.py:44
  56.1 0.8 collective-permute-start.10
  57.6 3.0 %collective-permute-done.13.refs_1_.refs_6_.minus = bf16[256,1792]{1,0:T(8,128)(2,1)S(1)} collective-permute-done((bf16[256,1792]{1,0:T(8,128)(2,1)S(1)}, bf16[256,1792]{1,0:T(8,128)(2,1)S(1)}, u32[]{:S(2)}, u32[]{:S(2)}) %collective-permute-start.13) | collective-permute-done | bytes 917536 | tf_op jit(solution)/shard_map/ppermute | solution.py:44
  60.6 3.4 %collective-permute-done.12.refs_0_.refs_5_.plus = bf16[256,1792]{1,0:T(8,128)(2,1)S(1)} collective-permute-done((bf16[256,1792]{1,0:T(8,128)(2,1)S(1)}, bf16[256,1792]{1,0:T(8,128)(2,1)S(1)}, u32[]{:S(2)}, u32[]{:S(2)}) %collective-permute-start.12) | collective-permute-done | bytes 917536 | tf_op jit(solution)/shard_map/ppermute | solution.py:44
  64.0 1.6 %forward.3 = (f32[64,768]{1,0:T(8,128)S(1)}, bf16[64,768]{1,0:T(8,128)(2,1)S(1)}, bf16[64,768]{1,0:T(8,128)(2,1)S(1)}, bf16[64,768]{1,0:T(8,128)(2,1)S(1)}) custom-call(s32[4]{0:T(128)S(1)} %pad_add_fusion.place, bf16[256,1792]{1,0:T(8,128)(2,1)S(1)} %collective-permute-done.12.refs_0_.refs_5_.plus, ...), custom_call_target="tpu_custom_call" | custom-call | flops 704643072 | bytes 5079040 | tf_op jit(solution)/shard_map/forward/pallas_call | solution.py:50
  65.6 2.9 %collective-permute-start.18 = (bf16[64,768]{1,0:T(8,128)(2,1)S(1)}, bf16[64,768]{1,0:T(8,128)(2,1)S(1)}, u32[]{:S(2)}, u32[]{:S(2)}) collective-permute-start(bf16[64,768]{1,0:T(8,128)(2,1)S(1)} %get-tuple-element.94), channel_id=1, source_target_pairs={{0,4},{1,5},{2,6},{3,7},{4,0},{5,1},{6,2},{7,3},{8,12},{9,13},{10,... | collective-permute-start | bytes 294920 | tf_op jit(solution)/shard_map/ppermute | solution.py:44
  69.2 1.5 %collective-permute-start.19 = (bf16[64,768]{1,0:T(8,128)(2,1)S(1)}, bf16[64,768]{1,0:T(8,128)(2,1)S(1)}, u32[]{:S(2)}, u32[]{:S(2)}) collective-permute-start(bf16[64,768]{1,0:T(8,128)(2,1)S(1)} %get-tuple-element.95), channel_id=1, source_target_pairs={{0,2},{1,3},{2,4},{3,5},{4,6},{5,7},{6,0},{7,1},{8,10},{9,11},{10,... | collective-permute-start | bytes 294920 | tf_op jit(solution)/shard_map/ppermute | solution.py:44
  71.2 1.9 %collective-permute-start.16 = (bf16[64,768]{1,0:T(8,128)(2,1)S(1)}, bf16[64,768]{1,0:T(8,128)(2,1)S(1)}, u32[]{:S(2)}, u32[]{:S(2)}) collective-permute-start(bf16[64,768]{1,0:T(8,128)(2,1)S(1)} %middle.2.refs_0_), channel_id=1, source_target_pairs={{0,6},{1,7},{2,0},{3,1},{4,2},{5,3},{6,4},{7,5},{8,14},{9,15},{10,... | collective-permute-start | bytes 294920 | tf_op jit(solution)/shard_map/ppermute | solution.py:44
  73.1 1.6 %collective-permute-start.15 = (bf16[64,768]{1,0:T(8,128)(2,1)S(1)}, bf16[64,768]{1,0:T(8,128)(2,1)S(1)}, u32[]{:S(2)}, u32[]{:S(2)}) collective-permute-start(bf16[64,768]{1,0:T(8,128)(2,1)S(1)} %middle.2.refs_0_), channel_id=1, source_target_pairs={{0,4},{1,5},{2,6},{3,7},{4,0},{5,1},{6,2},{7,3},{8,12},{9,13},{10,... | collective-permute-start | bytes 294920 | tf_op jit(solution)/shard_map/ppermute | solution.py:44
  74.8 1.9 %collective-permute-done.19.p3 = bf16[64,768]{1,0:T(8,128)(2,1)S(1)} collective-permute-done((bf16[64,768]{1,0:T(8,128)(2,1)S(1)}, bf16[64,768]{1,0:T(8,128)(2,1)S(1)}, u32[]{:S(2)}, u32[]{:S(2)}) %collective-permute-start.19) | collective-permute-done | bytes 98336 | tf_op jit(solution)/shard_map/ppermute | solution.py:44
  77.3 1.4 %collective-permute-start.22 = (bf16[64,768]{1,0:T(8,128)(2,1)S(1)}, bf16[64,768]{1,0:T(8,128)(2,1)S(1)}, u32[]{:S(2)}, u32[]{:S(2)}) collective-permute-start(bf16[64,768]{1,0:T(8,128)(2,1)S(1)} %middle.3.refs_0_), channel_id=1, source_target_pairs={{0,6},{1,7},{2,0},{3,1},{4,2},{5,3},{6,4},{7,5},{8,14},{9,15},{10,... | collective-permute-start | bytes 294920 | tf_op jit(solution)/shard_map/ppermute | solution.py:44
  78.7 0.7 collective-permute-start.21
  80.3 1.8 %collective-permute-done.14.refs_1_ = bf16[64,768]{1,0:T(8,128)(2,1)S(1)} collective-permute-done((bf16[64,768]{1,0:T(8,128)(2,1)S(1)}, bf16[64,768]{1,0:T(8,128)(2,1)S(1)}, u32[]{:S(2)}, u32[]{:S(2)}) %collective-permute-start.14) | collective-permute-done | bytes 98336 | tf_op jit(solution)/shard_map/ppermute | solution.py:44
  82.1 1.6 %first_grad.1 = (bf16[256,768]{1,0:T(8,128)(2,1)S(1)}, f32[768,896]{1,0:T(8,128)S(1)}, f32[768,896]{1,0:T(8,128)S(1)}) custom-call(s32[4]{0:T(128)S(1)} %pad_add_fusion.place, bf16[64,768]{1,0:T(8,128)(2,1)S(1)} %middle.2.refs_0_, bf16[64,768]{1,0:T(8,128)(2,1)S(1)} %collective-permute-done.14.refs_1_, bf16[64,768]{1,0:T(8,128)(2,1)S(1)} %collective-permute-done.15.refs_2_, ...), custom_call_target="tpu_custom_call" | custom-call | flops 704643072 | bytes 8126464 | tf_op jit(solution)/shard_map/first_grad/pallas_call | solution.py:50
  83.7 1.2 collective-permute-done.21.refs_2_
  84.9 1.0 collective-permute-done.20.refs_1_
  85.9 1.2 their_grad.1
  87.8 1.2 back.2
  89.1 3.2 %collective-permute-start.26 = (bf16[128,1792]{1,0:T(8,128)(2,1)S(1)}, bf16[128,1792]{1,0:T(8,128)(2,1)S(1)}, u32[]{:S(2)}, u32[]{:S(2)}) collective-permute-start(bf16[128,1792]{1,0:T(8,128)(2,1)S(1)} %get-tuple-element.101), channel_id=1, source_target_pairs={{0,24},{1,25},{2,26},{3,27},{4,28},{5,29},{6,30},{7,31},{8,0},{9,1... | collective-permute-start | bytes 1376264 | tf_op jit(solution)/shard_map/ppermute | solution.py:44
  92.3 1.5 %my_grad.1 = (f32[192,896]{1,0:T(8,128)S(1)}, bf16[192,896]{1,0:T(8,128)(2,1)S(1)}, bf16[192,896]{1,0:T(8,128)(2,1)S(1)}, bf16[192,896]{1,0:T(8,128)(2,1)S(1)}) custom-call(s32[4]{0:T(128)S(1)} %pad_add_fusion.place, bf16[256,896]{1,0:T(8,128)(2,1)S(1)} %collective-permute-done.23.got0, bf16[256,896]{1,0:T(8,128)(2,1)S(1)} %collective-permute-done.24.got1, ...), custom_call_target="tpu_custom_call" | custom-call | flops 352321536 | bytes 8077312 | tf_op jit(solution)/shard_map/my_grad/pallas_call | solution.py:50
  93.8 0.9 collective-permute-start.30
  94.7 0.9 collective-permute-start.31
  96.3 1.2 back.3
  97.6 5.6 %collective-permute-done.27.got_b.got_plus = bf16[128,1792]{1,0:T(8,128)(2,1)S(1)} collective-permute-done((bf16[128,1792]{1,0:T(8,128)(2,1)S(1)}, bf16[128,1792]{1,0:T(8,128)(2,1)S(1)}, u32[]{:S(2)}, u32[]{:S(2)}) %collective-permute-start.27) | collective-permute-done | bytes 458784 | tf_op jit(solution)/shard_map/ppermute | solution.py:44
  103.8 3.0 %collective-permute-start.28 = (bf16[64,1792]{1,0:T(8,128)(2,1)S(1)}, bf16[64,1792]{1,0:T(8,128)(2,1)S(1)}, u32[]{:S(2)}, u32[]{:S(2)}) collective-permute-start(bf16[64,1792]{1,0:T(8,128)(2,1)S(1)} %get-tuple-element.115), channel_id=1, source_target_pairs={{0,24},{1,25},{2,26},{3,27},{4,28},{5,29},{6,30},{7,31},{8,0},{9,1... | collective-permute-start | bytes 688136 | tf_op jit(solution)/shard_map/ppermute | solution.py:44
  106.8 4.3 %collective-permute-done.28.a1 = bf16[64,1792]{1,0:T(8,128)(2,1)S(1)} collective-permute-done((bf16[64,1792]{1,0:T(8,128)(2,1)S(1)}, bf16[64,1792]{1,0:T(8,128)(2,1)S(1)}, u32[]{:S(2)}, u32[]{:S(2)}) %collective-permute-start.28) | collective-permute-done | bytes 229408 | tf_op jit(solution)/shard_map/ppermute | solution.py:44
  111.2 3.4 %collective-permute-done.29.b3 = bf16[64,1792]{1,0:T(8,128)(2,1)S(1)} collective-permute-done((bf16[64,1792]{1,0:T(8,128)(2,1)S(1)}, bf16[64,1792]{1,0:T(8,128)(2,1)S(1)}, u32[]{:S(2)}, u32[]{:S(2)}) %collective-permute-start.29) | collective-permute-done | bytes 229408 | tf_op jit(solution)/shard_map/ppermute | solution.py:44
  114.7 1.5 %sum_back.1 = bf16[16,8,1792]{2,1,0:T(8,128)(2,1)} custom-call(s32[4]{0:T(128)S(1)} %pad_add_fusion.place, bf16[64,1792]{1,0:T(8,128)(2,1)S(1)} %get-tuple-element.120.a0, bf16[64,1792]{1,0:T(8,128)(2,1)S(1)} %get-tuple-element.121.b0, bf16[64,1792]{1,0:T(8,128)(2,1)S(1)} %collective-permute-done.28.a1, bf16[64,1792]{1,0:T(8,128)(2,1)S(1)} %collective-permute-done.29.b3, ...), custom_call_target="tpu_custom_call" | custom-call | bytes 2293760 | tf_op jit(solution)/shard_map/sum_back/pallas_call | solution.py:50
  116.1 3.6 %all-to-all-start.1 = ((bf16[16,8,1792]{2,1,0:T(8,128)(2,1)}), bf16[16,8,1792]{2,1,0:T(8,128)(2,1)S(1)}, u32[]{:S(2)}, u32[]{:S(2)}) async-start(bf16[16,8,1792]{2,1,0:T(8,128)(2,1)} %sum_back.1), calls=%async_computation.1 | async-start | bytes 917504 | tf_op jit(solution)/shard_map/all_to_all | solution.py:385
  119.8 6.9 %moments.1 = (f32[1,192,3584]{2,1,0:T(8,128)}, f32[1,192,3584]{2,1,0:T(8,128)}) custom-call(s32[4]{0:T(128)} %copy-done.2, f32[192,896]{1,0:T(8,128)} %copy-done.1, bf16[192,896]{1,0:T(8,128)(2,1)} %copy-done.6, bf16[192,896]{1,0:T(8,128)(2,1)} %copy-done.7, bf16[192,896]{1,0:T(8,128)(2,1)} %copy-done.8, f32[1,192,3584]{2,1,0:T(8,128)} %one.1, ...), custom_call_target="tpu_custom_call" | custom-call | flops 4128768 | bytes 11698176 | tf_op jit(solution)/shard_map/moments/pallas_call | solution.py:363
  126.7 2.8 %all-to-all-done.1.got = bf16[16,8,1792]{2,1,0:T(8,128)(2,1)S(1)} async-done(((bf16[16,8,1792]{2,1,0:T(8,128)(2,1)}), bf16[16,8,1792]{2,1,0:T(8,128)(2,1)S(1)}, u32[]{:S(2)}, u32[]{:S(2)}) %all-to-all-start.1) | async-done | bytes 458784 | tf_op jit(solution)/shard_map/all_to_all | solution.py:385
  129.4 2.1 %combine.1 = bf16[128,7168]{1,0:T(8,128)(2,1)} custom-call(s32[4]{0:T(128)S(1)} %copy-done.3, bf16[32,128]{1,0:T(8,128)(2,1)S(1)} %copy-done.4, bf16[16,8,1792]{2,1,0:T(8,128)(2,1)S(1)} %all-to-all-done.1.got), custom_call_target="tpu_custom_call" | custom-call | flops 58720256 | bytes 2301952 | tf_op jit(solution)/shard_map/combine/pallas_call | solution.py:50
  (59 shorter events, 9.8 us)
Async XLA Ops:
  0.6 10.9 %copy-start = (bf16[1,192,3584]{2,1,0:T(8,128)(2,1)S(1)}, bf16[1,192,3584]{2,1,0:T(8,128)(2,1)}, u32[]{:S(2)}) copy-start(bf16[1,192,3584]{2,1,0:T(8,128)(2,1)} %w.1) | copy-start | bytes 4128772
  4.3 23.2 %all-to-all-start = ((bf16[16,16,1792]{2,1,0:T(8,128)(2,1)}), bf16[16,16,1792]{2,1,0:T(8,128)(2,1)S(1)}, u32[]{:S(2)}, u32[]{:S(2)}) async-start(bf16[16,16,1792]{2,1,0:T(8,128)(2,1)} %get-tuple-element.67), calls=%async_computation | async-start | bytes 1835008 | tf_op jit(solution)/shard_map/all_to_all | solution.py:385
  11.5 103.1 %copy-start.2 = (s32[4]{0:T(128)}, s32[4]{0:T(128)S(1)}, u32[]{:S(2)}) copy-start(s32[4]{0:T(128)S(1)} %pad_add_fusion.place) | copy-start | bytes 52
  12.2 0.7 copy-start.5
  28.0 12.4 %collective-permute-start = (bf16[128,1792]{1,0:T(8,128)(2,1)S(1)}, bf16[128,1792]{1,0:T(8,128)(2,1)S(1)}, u32[]{:S(2)}, u32[]{:S(2)}) collective-permute-start(bf16[128,1792]{1,0:T(8,128)(2,1)S(1)} %get-tuple-element.70.a0.refs_0_.refs_4_), channel_id=1, source_target_pairs={{0,8},{1,9},{2,10},{3,11},{4,12},{5,13},{6,14},{7,15},{8,16},{9,17... | collective-permute-start | bytes 1376264 | tf_op jit(solution)/shard_map/ppermute | solution.py:44
  30.0 10.4 %collective-permute-start.1 = (bf16[128,1792]{1,0:T(8,128)(2,1)S(1)}, bf16[128,1792]{1,0:T(8,128)(2,1)S(1)}, u32[]{:S(2)}, u32[]{:S(2)}) collective-permute-start(bf16[128,1792]{1,0:T(8,128)(2,1)S(1)} %get-tuple-element.71.b0.refs_1_.refs_5_), channel_id=1, source_target_pairs={{0,24},{1,25},{2,26},{3,27},{4,28},{5,29},{6,30},{7,31},{8,0},{9,1... | collective-permute-start | bytes 1376264 | tf_op jit(solution)/shard_map/ppermute | solution.py:44
  32.2 12.7 %collective-permute-start.3 = (bf16[192,896]{1,0:T(8,128)(2,1)}, bf16[192,896]{1,0:T(8,128)(2,1)S(1)}, u32[]{:S(2)}, u32[]{:S(2)}) collective-permute-start(bf16[192,896]{1,0:T(8,128)(2,1)} %copy-done.5), channel_id=1, source_target_pairs={{0,4},{1,5},{2,6},{3,7},{4,0},{5,1},{6,2},{7,3},{8,12},{9,13},{10,... | collective-permute-start | bytes 1032200 | tf_op jit(solution)/shard_map/ppermute | solution.py:44
  33.1 14.7 %collective-permute-start.4 = (bf16[192,896]{1,0:T(8,128)(2,1)S(1)}, bf16[192,896]{1,0:T(8,128)(2,1)S(1)}, u32[]{:S(2)}, u32[]{:S(2)}) collective-permute-start(bf16[192,896]{1,0:T(8,128)(2,1)S(1)} %get-tuple-element.74), channel_id=1, source_target_pairs={{0,6},{1,7},{2,0},{3,1},{4,2},{5,3},{6,4},{7,5},{8,14},{9,15},{10,... | collective-permute-start | bytes 1032200 | tf_op jit(solution)/shard_map/ppermute | solution.py:44
  35.5 13.1 %collective-permute-start.2 = (bf16[192,896]{1,0:T(8,128)(2,1)S(1)}, bf16[192,896]{1,0:T(8,128)(2,1)S(1)}, u32[]{:S(2)}, u32[]{:S(2)}) collective-permute-start(bf16[192,896]{1,0:T(8,128)(2,1)S(1)} %get-tuple-element.68), channel_id=1, source_target_pairs={{0,2},{1,3},{2,4},{3,5},{4,6},{5,7},{6,0},{7,1},{8,10},{9,11},{10,... | collective-permute-start | bytes 1032200 | tf_op jit(solution)/shard_map/ppermute | solution.py:44
  41.1 19.5 %collective-permute-start.13 = (bf16[256,1792]{1,0:T(8,128)(2,1)S(1)}, bf16[256,1792]{1,0:T(8,128)(2,1)S(1)}, u32[]{:S(2)}, u32[]{:S(2)}) collective-permute-start(bf16[256,1792]{1,0:T(8,128)(2,1)S(1)} %get-tuple-element.86), channel_id=1, source_target_pairs={{0,24},{1,25},{2,26},{3,27},{4,28},{5,29},{6,30},{7,31},{8,0},{9,1... | collective-permute-start | bytes 2752520 | tf_op jit(solution)/shard_map/ppermute | solution.py:44
  44.2 19.8 %collective-permute-start.12 = (bf16[256,1792]{1,0:T(8,128)(2,1)S(1)}, bf16[256,1792]{1,0:T(8,128)(2,1)S(1)}, u32[]{:S(2)}, u32[]{:S(2)}) collective-permute-start(bf16[256,1792]{1,0:T(8,128)(2,1)S(1)} %get-tuple-element.75), channel_id=1, source_target_pairs={{0,8},{1,9},{2,10},{3,11},{4,12},{5,13},{6,14},{7,15},{8,16},{9,17... | collective-permute-start | bytes 2752520 | tf_op jit(solution)/shard_map/ppermute | solution.py:44
  48.6 1.7 %collective-permute-start.5 = (bf16[192,896]{1,0:T(8,128)(2,1)S(1)}, bf16[192,896]{1,0:T(8,128)(2,1)S(1)}, u32[]{:S(2)}, u32[]{:S(2)}) collective-permute-start(bf16[192,896]{1,0:T(8,128)(2,1)S(1)} %get-tuple-element.76.refs_0_), channel_id=1, source_target_pairs={{0,1},{1,0},{2,3},{3,2},{4,5},{5,4},{6,7},{7,6},{8,9},{9,8},{10,11... | collective-permute-start | bytes 1032200 | tf_op jit(solution)/shard_map/ppermute | solution.py:44
  48.6 2.1 %collective-permute-start.6 = (bf16[192,896]{1,0:T(8,128)(2,1)S(1)}, bf16[192,896]{1,0:T(8,128)(2,1)S(1)}, u32[]{:S(2)}, u32[]{:S(2)}) collective-permute-start(bf16[192,896]{1,0:T(8,128)(2,1)S(1)} %collective-permute-done.2.refs_1_), channel_id=1, source_target_pairs={{0,1},{1,0},{2,3},{3,2},{4,5},{5,4},{6,7},{7,6},{8,9},{9,8},{10,11... | collective-permute-start | bytes 1032200 | tf_op jit(solution)/shard_map/ppermute | solution.py:44
  49.1 2.1 %collective-permute-start.7 = (bf16[192,896]{1,0:T(8,128)(2,1)S(1)}, bf16[192,896]{1,0:T(8,128)(2,1)S(1)}, u32[]{:S(2)}, u32[]{:S(2)}) collective-permute-start(bf16[192,896]{1,0:T(8,128)(2,1)S(1)} %collective-permute-done.3.refs_2_), channel_id=1, source_target_pairs={{0,1},{1,0},{2,3},{3,2},{4,5},{5,4},{6,7},{7,6},{8,9},{9,8},{10,11... | collective-permute-start | bytes 1032200 | tf_op jit(solution)/shard_map/ppermute | solution.py:44
  50.2 1.7 %collective-permute-start.8 = (bf16[192,896]{1,0:T(8,128)(2,1)S(1)}, bf16[192,896]{1,0:T(8,128)(2,1)S(1)}, u32[]{:S(2)}, u32[]{:S(2)}) collective-permute-start(bf16[192,896]{1,0:T(8,128)(2,1)S(1)} %collective-permute-done.4.refs_3_), channel_id=1, source_target_pairs={{0,1},{1,0},{2,3},{3,2},{4,5},{5,4},{6,7},{7,6},{8,9},{9,8},{10,11... | collective-permute-start | bytes 1032200 | tf_op jit(solution)/shard_map/ppermute | solution.py:44
  54.2 14.9 %collective-permute-start.9 = (bf16[64,768]{1,0:T(8,128)(2,1)S(1)}, bf16[64,768]{1,0:T(8,128)(2,1)S(1)}, u32[]{:S(2)}, u32[]{:S(2)}) collective-permute-start(bf16[64,768]{1,0:T(8,128)(2,1)S(1)} %get-tuple-element.83), channel_id=1, source_target_pairs={{0,6},{1,7},{2,0},{3,1},{4,2},{5,3},{6,4},{7,5},{8,14},{9,15},{10,... | collective-permute-start | bytes 294920 | tf_op jit(solution)/shard_map/ppermute | solution.py:44
  56.1 13.0 %collective-permute-start.10 = (bf16[64,768]{1,0:T(8,128)(2,1)S(1)}, bf16[64,768]{1,0:T(8,128)(2,1)S(1)}, u32[]{:S(2)}, u32[]{:S(2)}) collective-permute-start(bf16[64,768]{1,0:T(8,128)(2,1)S(1)} %get-tuple-element.84), channel_id=1, source_target_pairs={{0,4},{1,5},{2,6},{3,7},{4,0},{5,1},{6,2},{7,3},{8,12},{9,13},{10,... | collective-permute-start | bytes 294920 | tf_op jit(solution)/shard_map/ppermute | solution.py:44
  56.9 12.3 %collective-permute-start.11 = (bf16[64,768]{1,0:T(8,128)(2,1)S(1)}, bf16[64,768]{1,0:T(8,128)(2,1)S(1)}, u32[]{:S(2)}, u32[]{:S(2)}) collective-permute-start(bf16[64,768]{1,0:T(8,128)(2,1)S(1)} %get-tuple-element.85), channel_id=1, source_target_pairs={{0,2},{1,3},{2,4},{3,5},{4,6},{5,7},{6,0},{7,1},{8,10},{9,11},{10,... | collective-permute-start | bytes 294920 | tf_op jit(solution)/shard_map/ppermute | solution.py:44
  65.6 9.2 %collective-permute-start.18 = (bf16[64,768]{1,0:T(8,128)(2,1)S(1)}, bf16[64,768]{1,0:T(8,128)(2,1)S(1)}, u32[]{:S(2)}, u32[]{:S(2)}) collective-permute-start(bf16[64,768]{1,0:T(8,128)(2,1)S(1)} %get-tuple-element.94), channel_id=1, source_target_pairs={{0,4},{1,5},{2,6},{3,7},{4,0},{5,1},{6,2},{7,3},{8,12},{9,13},{10,... | collective-permute-start | bytes 294920 | tf_op jit(solution)/shard_map/ppermute | solution.py:44
  68.5 8.2 %collective-permute-start.17 = (bf16[64,768]{1,0:T(8,128)(2,1)S(1)}, bf16[64,768]{1,0:T(8,128)(2,1)S(1)}, u32[]{:S(2)}, u32[]{:S(2)}) collective-permute-start(bf16[64,768]{1,0:T(8,128)(2,1)S(1)} %get-tuple-element.87), channel_id=1, source_target_pairs={{0,6},{1,7},{2,0},{3,1},{4,2},{5,3},{6,4},{7,5},{8,14},{9,15},{10,... | collective-permute-start | bytes 294920 | tf_op jit(solution)/shard_map/ppermute | solution.py:44
  69.2 7.5 %collective-permute-start.19 = (bf16[64,768]{1,0:T(8,128)(2,1)S(1)}, bf16[64,768]{1,0:T(8,128)(2,1)S(1)}, u32[]{:S(2)}, u32[]{:S(2)}) collective-permute-start(bf16[64,768]{1,0:T(8,128)(2,1)S(1)} %get-tuple-element.95), channel_id=1, source_target_pairs={{0,2},{1,3},{2,4},{3,5},{4,6},{5,7},{6,0},{7,1},{8,10},{9,11},{10,... | collective-permute-start | bytes 294920 | tf_op jit(solution)/shard_map/ppermute | solution.py:44
  71.2 8.2 %collective-permute-start.16 = (bf16[64,768]{1,0:T(8,128)(2,1)S(1)}, bf16[64,768]{1,0:T(8,128)(2,1)S(1)}, u32[]{:S(2)}, u32[]{:S(2)}) collective-permute-start(bf16[64,768]{1,0:T(8,128)(2,1)S(1)} %middle.2.refs_0_), channel_id=1, source_target_pairs={{0,6},{1,7},{2,0},{3,1},{4,2},{5,3},{6,4},{7,5},{8,14},{9,15},{10,... | collective-permute-start | bytes 294920 | tf_op jit(solution)/shard_map/ppermute | solution.py:44
  73.1 7.2 %collective-permute-start.15 = (bf16[64,768]{1,0:T(8,128)(2,1)S(1)}, bf16[64,768]{1,0:T(8,128)(2,1)S(1)}, u32[]{:S(2)}, u32[]{:S(2)}) collective-permute-start(bf16[64,768]{1,0:T(8,128)(2,1)S(1)} %middle.2.refs_0_), channel_id=1, source_target_pairs={{0,4},{1,5},{2,6},{3,7},{4,0},{5,1},{6,2},{7,3},{8,12},{9,13},{10,... | collective-permute-start | bytes 294920 | tf_op jit(solution)/shard_map/ppermute | solution.py:44
  74.8 7.3 %collective-permute-start.14 = (bf16[64,768]{1,0:T(8,128)(2,1)S(1)}, bf16[64,768]{1,0:T(8,128)(2,1)S(1)}, u32[]{:S(2)}, u32[]{:S(2)}) collective-permute-start(bf16[64,768]{1,0:T(8,128)(2,1)S(1)} %middle.2.refs_0_), channel_id=1, source_target_pairs={{0,2},{1,3},{2,4},{3,5},{4,6},{5,7},{6,0},{7,1},{8,10},{9,11},{10,... | collective-permute-start | bytes 294920 | tf_op jit(solution)/shard_map/ppermute | solution.py:44
  77.3 6.4 %collective-permute-start.22 = (bf16[64,768]{1,0:T(8,128)(2,1)S(1)}, bf16[64,768]{1,0:T(8,128)(2,1)S(1)}, u32[]{:S(2)}, u32[]{:S(2)}) collective-permute-start(bf16[64,768]{1,0:T(8,128)(2,1)S(1)} %middle.3.refs_0_), channel_id=1, source_target_pairs={{0,6},{1,7},{2,0},{3,1},{4,2},{5,3},{6,4},{7,5},{8,14},{9,15},{10,... | collective-permute-start | bytes 294920 | tf_op jit(solution)/shard_map/ppermute | solution.py:44
  78.7 6.2 %collective-permute-start.21 = (bf16[64,768]{1,0:T(8,128)(2,1)S(1)}, bf16[64,768]{1,0:T(8,128)(2,1)S(1)}, u32[]{:S(2)}, u32[]{:S(2)}) collective-permute-start(bf16[64,768]{1,0:T(8,128)(2,1)S(1)} %middle.3.refs_0_), channel_id=1, source_target_pairs={{0,4},{1,5},{2,6},{3,7},{4,0},{5,1},{6,2},{7,3},{8,12},{9,13},{10,... | collective-permute-start | bytes 294920 | tf_op jit(solution)/shard_map/ppermute | solution.py:44
  79.4 6.5 %collective-permute-start.20 = (bf16[64,768]{1,0:T(8,128)(2,1)S(1)}, bf16[64,768]{1,0:T(8,128)(2,1)S(1)}, u32[]{:S(2)}, u32[]{:S(2)}) collective-permute-start(bf16[64,768]{1,0:T(8,128)(2,1)S(1)} %middle.3.refs_0_), channel_id=1, source_target_pairs={{0,2},{1,3},{2,4},{3,5},{4,6},{5,7},{6,0},{7,1},{8,10},{9,11},{10,... | collective-permute-start | bytes 294920 | tf_op jit(solution)/shard_map/ppermute | solution.py:44
  87.1 5.2 %collective-permute-start.23 = (bf16[256,896]{1,0:T(8,128)(2,1)S(1)}, bf16[256,896]{1,0:T(8,128)(2,1)S(1)}, u32[]{:S(2)}, u32[]{:S(2)}) collective-permute-start(bf16[256,896]{1,0:T(8,128)(2,1)S(1)} %get-tuple-element.97), channel_id=1, source_target_pairs={{0,1},{1,0},{2,3},{3,2},{4,5},{5,4},{6,7},{7,6},{8,9},{9,8},{10,11... | collective-permute-start | bytes 1376264 | tf_op jit(solution)/shard_map/ppermute | solution.py:44
  87.2 5.2 %collective-permute-start.24 = (bf16[256,896]{1,0:T(8,128)(2,1)S(1)}, bf16[256,896]{1,0:T(8,128)(2,1)S(1)}, u32[]{:S(2)}, u32[]{:S(2)}) collective-permute-start(bf16[256,896]{1,0:T(8,128)(2,1)S(1)} %get-tuple-element.98), channel_id=1, source_target_pairs={{0,1},{1,0},{2,3},{3,2},{4,5},{5,4},{6,7},{7,6},{8,9},{9,8},{10,11... | collective-permute-start | bytes 1376264 | tf_op jit(solution)/shard_map/ppermute | solution.py:44
  87.7 4.7 %collective-permute-start.25 = (bf16[256,896]{1,0:T(8,128)(2,1)S(1)}, bf16[256,896]{1,0:T(8,128)(2,1)S(1)}, u32[]{:S(2)}, u32[]{:S(2)}) collective-permute-start(bf16[256,896]{1,0:T(8,128)(2,1)S(1)} %get-tuple-element.99), channel_id=1, source_target_pairs={{0,1},{1,0},{2,3},{3,2},{4,5},{5,4},{6,7},{7,6},{8,9},{9,8},{10,11... | collective-permute-start | bytes 1376264 | tf_op jit(solution)/shard_map/ppermute | solution.py:44
  89.0 14.1 %collective-permute-start.27 = (bf16[128,1792]{1,0:T(8,128)(2,1)S(1)}, bf16[128,1792]{1,0:T(8,128)(2,1)S(1)}, u32[]{:S(2)}, u32[]{:S(2)}) collective-permute-start(bf16[128,1792]{1,0:T(8,128)(2,1)S(1)} %get-tuple-element.110), channel_id=1, source_target_pairs={{0,8},{1,9},{2,10},{3,11},{4,12},{5,13},{6,14},{7,15},{8,16},{9,17... | collective-permute-start | bytes 1376264 | tf_op jit(solution)/shard_map/ppermute | solution.py:44
  89.1 14.1 %collective-permute-start.26 = (bf16[128,1792]{1,0:T(8,128)(2,1)S(1)}, bf16[128,1792]{1,0:T(8,128)(2,1)S(1)}, u32[]{:S(2)}, u32[]{:S(2)}) collective-permute-start(bf16[128,1792]{1,0:T(8,128)(2,1)S(1)} %get-tuple-element.101), channel_id=1, source_target_pairs={{0,24},{1,25},{2,26},{3,27},{4,28},{5,29},{6,30},{7,31},{8,0},{9,1... | collective-permute-start | bytes 1376264 | tf_op jit(solution)/shard_map/ppermute | solution.py:44
  93.8 9.3 %copy-start.1 = (f32[192,896]{1,0:T(8,128)}, f32[192,896]{1,0:T(8,128)S(1)}, u32[]{:S(2)}) copy-start(f32[192,896]{1,0:T(8,128)S(1)} %get-tuple-element.104.g0) | copy-start | bytes 2064388
  93.8 20.8 %collective-permute-start.30 = (bf16[192,896]{1,0:T(8,128)(2,1)S(1)}, bf16[192,896]{1,0:T(8,128)(2,1)S(1)}, u32[]{:S(2)}, u32[]{:S(2)}) collective-permute-start(bf16[192,896]{1,0:T(8,128)(2,1)S(1)} %get-tuple-element.117), channel_id=1, source_target_pairs={{0,6},{1,7},{2,0},{3,1},{4,2},{5,3},{6,4},{7,5},{8,14},{9,15},{10,... | collective-permute-start | bytes 1032200 | tf_op jit(solution)/shard_map/ppermute | solution.py:44
  94.7 19.9 %collective-permute-start.31 = (bf16[192,896]{1,0:T(8,128)(2,1)S(1)}, bf16[192,896]{1,0:T(8,128)(2,1)S(1)}, u32[]{:S(2)}, u32[]{:S(2)}) collective-permute-start(bf16[192,896]{1,0:T(8,128)(2,1)S(1)} %get-tuple-element.118), channel_id=1, source_target_pairs={{0,4},{1,5},{2,6},{3,7},{4,0},{5,1},{6,2},{7,3},{8,12},{9,13},{10,... | collective-permute-start | bytes 1032200 | tf_op jit(solution)/shard_map/ppermute | solution.py:44
  95.6 19.0 %collective-permute-start.32 = (bf16[192,896]{1,0:T(8,128)(2,1)S(1)}, bf16[192,896]{1,0:T(8,128)(2,1)S(1)}, u32[]{:S(2)}, u32[]{:S(2)}) collective-permute-start(bf16[192,896]{1,0:T(8,128)(2,1)S(1)} %get-tuple-element.119), channel_id=1, source_target_pairs={{0,2},{1,3},{2,4},{3,5},{4,6},{5,7},{6,0},{7,1},{8,10},{9,11},{10,... | collective-permute-start | bytes 1032200 | tf_op jit(solution)/shard_map/ppermute | solution.py:44
  103.8 7.4 %collective-permute-start.28 = (bf16[64,1792]{1,0:T(8,128)(2,1)S(1)}, bf16[64,1792]{1,0:T(8,128)(2,1)S(1)}, u32[]{:S(2)}, u32[]{:S(2)}) collective-permute-start(bf16[64,1792]{1,0:T(8,128)(2,1)S(1)} %get-tuple-element.115), channel_id=1, source_target_pairs={{0,24},{1,25},{2,26},{3,27},{4,28},{5,29},{6,30},{7,31},{8,0},{9,1... | collective-permute-start | bytes 688136 | tf_op jit(solution)/shard_map/ppermute | solution.py:44
  106.8 7.8 %collective-permute-start.29 = (bf16[64,1792]{1,0:T(8,128)(2,1)S(1)}, bf16[64,1792]{1,0:T(8,128)(2,1)S(1)}, u32[]{:S(2)}, u32[]{:S(2)}) collective-permute-start(bf16[64,1792]{1,0:T(8,128)(2,1)S(1)} %get-tuple-element.116), channel_id=1, source_target_pairs={{0,8},{1,9},{2,10},{3,11},{4,12},{5,13},{6,14},{7,15},{8,16},{9,17... | collective-permute-start | bytes 688136 | tf_op jit(solution)/shard_map/ppermute | solution.py:44
  114.6 5.1 %copy-start.6 = (bf16[192,896]{1,0:T(8,128)(2,1)}, bf16[192,896]{1,0:T(8,128)(2,1)S(1)}, u32[]{:S(2)}) copy-start(bf16[192,896]{1,0:T(8,128)(2,1)S(1)} %collective-permute-done.30.g1) | copy-start | bytes 1032196
  114.6 5.1 %copy-start.7 = (bf16[192,896]{1,0:T(8,128)(2,1)}, bf16[192,896]{1,0:T(8,128)(2,1)S(1)}, u32[]{:S(2)}) copy-start(bf16[192,896]{1,0:T(8,128)(2,1)S(1)} %collective-permute-done.31.g2) | copy-start | bytes 1032196
  114.6 5.1 %copy-start.8 = (bf16[192,896]{1,0:T(8,128)(2,1)}, bf16[192,896]{1,0:T(8,128)(2,1)S(1)}, u32[]{:S(2)}) copy-start(bf16[192,896]{1,0:T(8,128)(2,1)S(1)} %collective-permute-done.32.g3) | copy-start | bytes 1032196
  116.1 13.3 %all-to-all-start.1 = ((bf16[16,8,1792]{2,1,0:T(8,128)(2,1)}), bf16[16,8,1792]{2,1,0:T(8,128)(2,1)S(1)}, u32[]{:S(2)}, u32[]{:S(2)}) async-start(bf16[16,8,1792]{2,1,0:T(8,128)(2,1)} %sum_back.1), calls=%async_computation.1 | async-start | bytes 917504 | tf_op jit(solution)/shard_map/all_to_all | solution.py:385
  119.7 9.7 %copy-start.3 = (s32[4]{0:T(128)S(1)}, s32[4]{0:T(128)}, u32[]{:S(2)}) copy-start(s32[4]{0:T(128)} %copy-done.2) | copy-start | bytes 52
  119.7 9.7 %copy-start.4 = (bf16[32,128]{1,0:T(8,128)(2,1)S(1)}, bf16[32,128]{1,0:T(8,128)(2,1)}, u32[]{:S(2)}) copy-start(bf16[32,128]{1,0:T(8,128)(2,1)} %get-tuple-element.66.pick) | copy-start | bytes 24580

commit v6 on v5

--- a/solution.py
+++ b/solution.py
@@ -291,20 +291,16 @@
 
 
 def their_grad_kernel(place, *refs):
-    before, plus, minus, held, o0, o1, o2 = refs[N:]
+    before, plus, minus, held, out = refs[N:]
     assemble(place[2], refs[:N], held)
 
     def add(rows, value):
-        total = (value + before[rows]).astype(BF)
-        for i, o in enumerate((o0, o1, o2)):
-            at = i * N * HID - rows.start
-            if 0 <= at < total.shape[0]:
-                o[...] = total[at : at + N * HID]
+        out[rows] = (value + before[rows]).astype(BF)
 
     weight_grad(1 - place[3], held, (plus, minus), add)
 
 
-def my_grad_kernel(place, got0, got1, got2, held, before, plus, minus, o0, o1, o2, o3, mine):
+def my_grad_kernel(place, got, held, before, plus, minus, o0, o1, o2, o3, mine):
     y = place[2]
 
     def add(rows, value):
@@ -313,9 +309,9 @@
     weight_grad(place[3], held, (plus, minus), add)
     for k, o in enumerate((o0, o1, o2, o3)):
         block = pl.multiple_of(wrap(y - k) * HID, HID)
-        for part, got in enumerate((got0, got1, got2)):
-            own = mine[pl.ds(pl.multiple_of(part * N * HID + block, HID), HID), :]
-            total = own + got[pl.ds(block, HID), :].astype(F32)
+        for part in range(3):
+            rows = pl.ds(pl.multiple_of(part * N * HID + block, HID), HID)
+            total = mine[rows, :] + got[rows, :].astype(F32)
             o[part * HID : (part + 1) * HID] = total.astype(o.dtype)
 
 
@@ -491,10 +487,10 @@
         *first,
         flops=flops,
     )
-    held_two, *theirs = call(
+    held_two, theirs = call(
         their_grad_kernel,
         "their_grad",
-        [((CHUNK, 3 * width), BF)] + [((width, EIGHTH), BF)] * 3,
+        [((CHUNK, 3 * width), BF), ((3 * width, EIGHTH), BF)],
         place,
         *held_two,
         first_theirs,
@@ -503,13 +499,13 @@
     )
     minus, plus = back_part(place, held_two, w_own, w_other, 1)
     got_minus, got_plus = turn(minus, "z", -1), turn(plus, "z", 1)
-    got = [turn(v, "c", 1) for v in theirs]
+    got = turn(theirs, "c", 1)
     blocks = call(
         my_grad_kernel,
         "my_grad",
         [((block_rows, EIGHTH), F32)] + [((block_rows, EIGHTH), BF)] * 3,
         place,
-        *got,
+        got,
         after(held_two, minus),
         first_mine,
         *second,

time: 132 us -> 132 us (level)
    ppermute x33 -> x31, starting transfers between devices: 35.3 us -> 34.7 us  [turn(): return lax.ppermute(value, ('expert', 'dp'), rotation(axis, step))]
    ppermute x33 -> x31, waiting for transfers between devices: 38 us -> 38.1 us  [turn(): return lax.ppermute(value, ('expert', 'dp'), rotation(axis, step))]
  transfers between devices with their start and end apart: 35 -> 33, of which waited for: 20 -> 20; matrix products, arithmetic and copies ran while one was open for 0% -> 0% of each run, Pallas kernels for 15% -> 15%
where the time goes in v6:
time: 132 us; the launch traced here: 131 us
  waiting for transfers between devices  55.4 us (42%)
  starting transfers between devices  45.5 us (34%)
  Pallas kernels  28.4 us (22%)
    ppermute x31, waiting for transfers between devices, turn(): return lax.ppermute(value, ('expert', 'dp'), rotation(axis, step))  38.1 us
    ppermute x31, starting transfers between devices, turn(): return lax.ppermute(value, ('expert', 'dp'), rotation(axis, step))  34.7 us
    pallas_call x16, Pallas kernels, call(): pl.pallas_call(kernel, name=name, out_shape=outs, in_specs=[pl.BlockSpec(...  18 us
    all_to_all x2, waiting for transfers between devices, exchange(): lax.all_to_all(value, 'expert', 0, 0, axis_index_groups=list(groups.value...  17.3 us
    all_to_all x2, starting transfers between devices, exchange(): lax.all_to_all(value, 'expert', 0, 0, axis_index_groups=list(groups.value...  10.8 us
    pallas_call x1, Pallas kernels, moments(): pl.pallas_call(moments_kernel, name='moments', grid_spec=pltpu.PrefetchSc...  6.9 us
    pallas_call x1, Pallas kernels, route(): pl.pallas_call(route_kernel, name='route', in_specs=[hbm] * 4, out_specs=...  3.5 us
  transfers between devices with their start and end apart: 33, of which 20 were waited for; matrix products, arithmetic and copies ran while one was open for 0% of the time, Pallas kernels for 15%

profile of v6, /device:TPU:0, one launch (start us, length us, event | category | flops | bytes accessed | tf_op | source)
XLA Modules:
  0.0 131.3 jit_solution(7655999295779109598)
XLA Ops:
  0.6 3.5 %route.1 = (bf16[16,16,1792]{2,1,0:T(8,128)(2,1)}, bf16[32,128]{1,0:T(8,128)(2,1)}) custom-call(s32[8,128]{1,0:T(8,128)} %bitcast.6, f32[8,128]{1,0:T(8,128)} %bitcast.7, bf16[128,7168]{1,0:T(8,128)(2,1)} %tokens.1, bf16[128,7168]{1,0:T(8,128)(2,1)} %grads.1), custom_call_target="tpu_custom_call" | custom-call | flops 117440512 | bytes 5505024 | tf_op jit(solution)/shard_map/route/pallas_call | solution.py:143
  4.2 7.3 %all-to-all-start = ((bf16[16,16,1792]{2,1,0:T(8,128)(2,1)}), bf16[16,16,1792]{2,1,0:T(8,128)(2,1)S(1)}, u32[]{:S(2)}, u32[]{:S(2)}) async-start(bf16[16,16,1792]{2,1,0:T(8,128)(2,1)} %get-tuple-element.65), calls=%async_computation | async-start | bytes 1835008 | tf_op jit(solution)/shard_map/all_to_all | solution.py:381
  12.2 0.7 copy-done.5
  12.9 14.5 %all-to-all-done.got = bf16[16,16,1792]{2,1,0:T(8,128)(2,1)S(1)} async-done(((bf16[16,16,1792]{2,1,0:T(8,128)(2,1)}), bf16[16,16,1792]{2,1,0:T(8,128)(2,1)S(1)}, u32[]{:S(2)}, u32[]{:S(2)}) %all-to-all-start) | async-done | bytes 917536 | tf_op jit(solution)/shard_map/all_to_all | solution.py:381
  28.1 2.0 %collective-permute-start = (bf16[128,1792]{1,0:T(8,128)(2,1)S(1)}, bf16[128,1792]{1,0:T(8,128)(2,1)S(1)}, u32[]{:S(2)}, u32[]{:S(2)}) collective-permute-start(bf16[128,1792]{1,0:T(8,128)(2,1)S(1)} %get-tuple-element.68.a0.refs_0_.refs_4_), channel_id=1, source_target_pairs={{0,8},{1,9},{2,10},{3,11},{4,12},{5,13},{6,14},{7,15},{8,16},{9,17... | collective-permute-start | bytes 1376264 | tf_op jit(solution)/shard_map/ppermute | solution.py:44
  30.0 2.2 %collective-permute-start.1 = (bf16[128,1792]{1,0:T(8,128)(2,1)S(1)}, bf16[128,1792]{1,0:T(8,128)(2,1)S(1)}, u32[]{:S(2)}, u32[]{:S(2)}) collective-permute-start(bf16[128,1792]{1,0:T(8,128)(2,1)S(1)} %get-tuple-element.69.b0.refs_1_.refs_5_), channel_id=1, source_target_pairs={{0,24},{1,25},{2,26},{3,27},{4,28},{5,29},{6,30},{7,31},{8,0},{9,1... | collective-permute-start | bytes 1376264 | tf_op jit(solution)/shard_map/ppermute | solution.py:44
  32.2 0.9 collective-permute-start.3
  33.1 2.4 %collective-permute-start.4 = (bf16[192,896]{1,0:T(8,128)(2,1)S(1)}, bf16[192,896]{1,0:T(8,128)(2,1)S(1)}, u32[]{:S(2)}, u32[]{:S(2)}) collective-permute-start(bf16[192,896]{1,0:T(8,128)(2,1)S(1)} %get-tuple-element.72), channel_id=1, source_target_pairs={{0,6},{1,7},{2,0},{3,1},{4,2},{5,3},{6,4},{7,5},{8,14},{9,15},{10,... | collective-permute-start | bytes 1032200 | tf_op jit(solution)/shard_map/ppermute | solution.py:44
  35.5 4.9 %collective-permute-done.a1.refs_2_.refs_6_ = bf16[128,1792]{1,0:T(8,128)(2,1)S(1)} collective-permute-done((bf16[128,1792]{1,0:T(8,128)(2,1)S(1)}, bf16[128,1792]{1,0:T(8,128)(2,1)S(1)}, u32[]{:S(2)}, u32[]{:S(2)}) %collective-permute-start) | collective-permute-done | bytes 458784 | tf_op jit(solution)/shard_map/ppermute | solution.py:44
  41.1 3.1 %collective-permute-start.13 = (bf16[256,1792]{1,0:T(8,128)(2,1)S(1)}, bf16[256,1792]{1,0:T(8,128)(2,1)S(1)}, u32[]{:S(2)}, u32[]{:S(2)}) collective-permute-start(bf16[256,1792]{1,0:T(8,128)(2,1)S(1)} %get-tuple-element.84), channel_id=1, source_target_pairs={{0,24},{1,25},{2,26},{3,27},{4,28},{5,29},{6,30},{7,31},{8,0},{9,1... | collective-permute-start | bytes 2752520 | tf_op jit(solution)/shard_map/ppermute | solution.py:44
  44.2 0.7 collective-permute-done.3.refs_2_
  44.9 2.9 %collective-permute-done.4.refs_3_ = bf16[192,896]{1,0:T(8,128)(2,1)S(1)} collective-permute-done((bf16[192,896]{1,0:T(8,128)(2,1)S(1)}, bf16[192,896]{1,0:T(8,128)(2,1)S(1)}, u32[]{:S(2)}, u32[]{:S(2)}) %collective-permute-start.4) | collective-permute-done | bytes 344096 | tf_op jit(solution)/shard_map/ppermute | solution.py:44
  47.8 0.8 collective-permute-done.2.refs_1_
  49.1 1.1 collective-permute-done.5.refs_4_
  51.9 0.8 stack_weights.1
  52.7 1.6 %forward.2 = (f32[64,768]{1,0:T(8,128)S(1)}, bf16[64,768]{1,0:T(8,128)(2,1)S(1)}, bf16[64,768]{1,0:T(8,128)(2,1)S(1)}, bf16[64,768]{1,0:T(8,128)(2,1)S(1)}) custom-call(s32[4]{0:T(128)S(1)} %pad_add_fusion.place, bf16[128,1792]{1,0:T(8,128)(2,1)S(1)} %get-tuple-element.68.a0.refs_0_.refs_4_, bf16[128,1792]{1,0:T(8,128)(2,1)S(1)} %get-tuple-element.69.b0.refs_1_.refs_5_, ...), custom_call_target="tpu_custom_call" | custom-call | flops 704643072 | bytes 5079040 | tf_op jit(solution)/shard_map/forward/pallas_call | solution.py:50
  54.3 1.9 %collective-permute-start.9 = (bf16[64,768]{1,0:T(8,128)(2,1)S(1)}, bf16[64,768]{1,0:T(8,128)(2,1)S(1)}, u32[]{:S(2)}, u32[]{:S(2)}) collective-permute-start(bf16[64,768]{1,0:T(8,128)(2,1)S(1)} %get-tuple-element.81), channel_id=1, source_target_pairs={{0,6},{1,7},{2,0},{3,1},{4,2},{5,3},{6,4},{7,5},{8,14},{9,15},{10,... | collective-permute-start | bytes 294920 | tf_op jit(solution)/shard_map/ppermute | solution.py:44
  56.2 0.8 collective-permute-start.10
  57.6 3.0 %collective-permute-done.13.refs_1_.refs_6_.minus = bf16[256,1792]{1,0:T(8,128)(2,1)S(1)} collective-permute-done((bf16[256,1792]{1,0:T(8,128)(2,1)S(1)}, bf16[256,1792]{1,0:T(8,128)(2,1)S(1)}, u32[]{:S(2)}, u32[]{:S(2)}) %collective-permute-start.13) | collective-permute-done | bytes 917536 | tf_op jit(solution)/shard_map/ppermute | solution.py:44
  60.6 3.4 %collective-permute-done.12.refs_0_.refs_5_.plus = bf16[256,1792]{1,0:T(8,128)(2,1)S(1)} collective-permute-done((bf16[256,1792]{1,0:T(8,128)(2,1)S(1)}, bf16[256,1792]{1,0:T(8,128)(2,1)S(1)}, u32[]{:S(2)}, u32[]{:S(2)}) %collective-permute-start.12) | collective-permute-done | bytes 917536 | tf_op jit(solution)/shard_map/ppermute | solution.py:44
  64.0 1.6 %forward.3 = (f32[64,768]{1,0:T(8,128)S(1)}, bf16[64,768]{1,0:T(8,128)(2,1)S(1)}, bf16[64,768]{1,0:T(8,128)(2,1)S(1)}, bf16[64,768]{1,0:T(8,128)(2,1)S(1)}) custom-call(s32[4]{0:T(128)S(1)} %pad_add_fusion.place, bf16[256,1792]{1,0:T(8,128)(2,1)S(1)} %collective-permute-done.12.refs_0_.refs_5_.plus, ...), custom_call_target="tpu_custom_call" | custom-call | flops 704643072 | bytes 5079040 | tf_op jit(solution)/shard_map/forward/pallas_call | solution.py:50
  65.6 2.9 %collective-permute-start.18 = (bf16[64,768]{1,0:T(8,128)(2,1)S(1)}, bf16[64,768]{1,0:T(8,128)(2,1)S(1)}, u32[]{:S(2)}, u32[]{:S(2)}) collective-permute-start(bf16[64,768]{1,0:T(8,128)(2,1)S(1)} %get-tuple-element.92), channel_id=1, source_target_pairs={{0,4},{1,5},{2,6},{3,7},{4,0},{5,1},{6,2},{7,3},{8,12},{9,13},{10,... | collective-permute-start | bytes 294920 | tf_op jit(solution)/shard_map/ppermute | solution.py:44
  69.2 1.5 %collective-permute-start.19 = (bf16[64,768]{1,0:T(8,128)(2,1)S(1)}, bf16[64,768]{1,0:T(8,128)(2,1)S(1)}, u32[]{:S(2)}, u32[]{:S(2)}) collective-permute-start(bf16[64,768]{1,0:T(8,128)(2,1)S(1)} %get-tuple-element.93), channel_id=1, source_target_pairs={{0,2},{1,3},{2,4},{3,5},{4,6},{5,7},{6,0},{7,1},{8,10},{9,11},{10,... | collective-permute-start | bytes 294920 | tf_op jit(solution)/shard_map/ppermute | solution.py:44
  71.3 1.9 %collective-permute-start.16 = (bf16[64,768]{1,0:T(8,128)(2,1)S(1)}, bf16[64,768]{1,0:T(8,128)(2,1)S(1)}, u32[]{:S(2)}, u32[]{:S(2)}) collective-permute-start(bf16[64,768]{1,0:T(8,128)(2,1)S(1)} %middle.2.refs_0_), channel_id=1, source_target_pairs={{0,6},{1,7},{2,0},{3,1},{4,2},{5,3},{6,4},{7,5},{8,14},{9,15},{10,... | collective-permute-start | bytes 294920 | tf_op jit(solution)/shard_map/ppermute | solution.py:44
  73.2 1.6 %collective-permute-start.15 = (bf16[64,768]{1,0:T(8,128)(2,1)S(1)}, bf16[64,768]{1,0:T(8,128)(2,1)S(1)}, u32[]{:S(2)}, u32[]{:S(2)}) collective-permute-start(bf16[64,768]{1,0:T(8,128)(2,1)S(1)} %middle.2.refs_0_), channel_id=1, source_target_pairs={{0,4},{1,5},{2,6},{3,7},{4,0},{5,1},{6,2},{7,3},{8,12},{9,13},{10,... | collective-permute-start | bytes 294920 | tf_op jit(solution)/shard_map/ppermute | solution.py:44
  74.8 1.9 %collective-permute-done.19.p3 = bf16[64,768]{1,0:T(8,128)(2,1)S(1)} collective-permute-done((bf16[64,768]{1,0:T(8,128)(2,1)S(1)}, bf16[64,768]{1,0:T(8,128)(2,1)S(1)}, u32[]{:S(2)}, u32[]{:S(2)}) %collective-permute-start.19) | collective-permute-done | bytes 98336 | tf_op jit(solution)/shard_map/ppermute | solution.py:44
  77.3 1.4 %collective-permute-start.22 = (bf16[64,768]{1,0:T(8,128)(2,1)S(1)}, bf16[64,768]{1,0:T(8,128)(2,1)S(1)}, u32[]{:S(2)}, u32[]{:S(2)}) collective-permute-start(bf16[64,768]{1,0:T(8,128)(2,1)S(1)} %middle.3.refs_0_), channel_id=1, source_target_pairs={{0,6},{1,7},{2,0},{3,1},{4,2},{5,3},{6,4},{7,5},{8,14},{9,15},{10,... | collective-permute-start | bytes 294920 | tf_op jit(solution)/shard_map/ppermute | solution.py:44
  78.8 0.7 collective-permute-start.21
  80.4 1.8 %collective-permute-done.14.refs_1_ = bf16[64,768]{1,0:T(8,128)(2,1)S(1)} collective-permute-done((bf16[64,768]{1,0:T(8,128)(2,1)S(1)}, bf16[64,768]{1,0:T(8,128)(2,1)S(1)}, u32[]{:S(2)}, u32[]{:S(2)}) %collective-permute-start.14) | collective-permute-done | bytes 98336 | tf_op jit(solution)/shard_map/ppermute | solution.py:44
  82.1 1.6 %first_grad.1 = (bf16[256,768]{1,0:T(8,128)(2,1)S(1)}, f32[768,896]{1,0:T(8,128)S(1)}, f32[768,896]{1,0:T(8,128)S(1)}) custom-call(s32[4]{0:T(128)S(1)} %pad_add_fusion.place, bf16[64,768]{1,0:T(8,128)(2,1)S(1)} %middle.2.refs_0_, bf16[64,768]{1,0:T(8,128)(2,1)S(1)} %collective-permute-done.14.refs_1_, bf16[64,768]{1,0:T(8,128)(2,1)S(1)} %collective-permute-done.15.refs_2_, ...), custom_call_target="tpu_custom_call" | custom-call | flops 704643072 | bytes 8126464 | tf_op jit(solution)/shard_map/first_grad/pallas_call | solution.py:50
  83.7 1.2 collective-permute-done.21.refs_2_
  84.9 1.0 collective-permute-done.20.refs_1_
  85.9 1.2 their_grad.1
  87.2 1.2 back.2
  88.6 3.2 %collective-permute-start.24 = (bf16[128,1792]{1,0:T(8,128)(2,1)S(1)}, bf16[128,1792]{1,0:T(8,128)(2,1)S(1)}, u32[]{:S(2)}, u32[]{:S(2)}) collective-permute-start(bf16[128,1792]{1,0:T(8,128)(2,1)S(1)} %get-tuple-element.97), channel_id=1, source_target_pairs={{0,24},{1,25},{2,26},{3,27},{4,28},{5,29},{6,30},{7,31},{8,0},{9,1... | collective-permute-start | bytes 1376264 | tf_op jit(solution)/shard_map/ppermute | solution.py:44
  91.8 1.5 %my_grad.1 = (f32[192,896]{1,0:T(8,128)S(1)}, bf16[192,896]{1,0:T(8,128)(2,1)S(1)}, bf16[192,896]{1,0:T(8,128)(2,1)S(1)}, bf16[192,896]{1,0:T(8,128)(2,1)S(1)}) custom-call(s32[4]{0:T(128)S(1)} %pad_add_fusion.place, bf16[768,896]{1,0:T(8,128)(2,1)S(1)} %collective-permute-done.23.got, bf16[256,768]{1,0:T(8,128)(2,1)S(1)} %get-tuple-element.98.held, ...), custom_call_target="tpu_custom_call" | custom-call | flops 352321536 | bytes 8077312 | tf_op jit(solution)/shard_map/my_grad/pallas_call | solution.py:50
  93.3 0.9 collective-permute-start.28
  94.2 0.9 collective-permute-start.29
  95.7 1.2 back.3
  97.0 5.7 %collective-permute-done.25.got_b.got_plus = bf16[128,1792]{1,0:T(8,128)(2,1)S(1)} collective-permute-done((bf16[128,1792]{1,0:T(8,128)(2,1)S(1)}, bf16[128,1792]{1,0:T(8,128)(2,1)S(1)}, u32[]{:S(2)}, u32[]{:S(2)}) %collective-permute-start.25) | collective-permute-done | bytes 458784 | tf_op jit(solution)/shard_map/ppermute | solution.py:44
  103.3 3.0 %collective-permute-start.26 = (bf16[64,1792]{1,0:T(8,128)(2,1)S(1)}, bf16[64,1792]{1,0:T(8,128)(2,1)S(1)}, u32[]{:S(2)}, u32[]{:S(2)}) collective-permute-start(bf16[64,1792]{1,0:T(8,128)(2,1)S(1)} %get-tuple-element.111), channel_id=1, source_target_pairs={{0,24},{1,25},{2,26},{3,27},{4,28},{5,29},{6,30},{7,31},{8,0},{9,1... | collective-permute-start | bytes 688136 | tf_op jit(solution)/shard_map/ppermute | solution.py:44
  106.4 4.4 %collective-permute-done.26.a1 = bf16[64,1792]{1,0:T(8,128)(2,1)S(1)} collective-permute-done((bf16[64,1792]{1,0:T(8,128)(2,1)S(1)}, bf16[64,1792]{1,0:T(8,128)(2,1)S(1)}, u32[]{:S(2)}, u32[]{:S(2)}) %collective-permute-start.26) | collective-permute-done | bytes 229408 | tf_op jit(solution)/shard_map/ppermute | solution.py:44
  110.8 3.4 %collective-permute-done.27.b3 = bf16[64,1792]{1,0:T(8,128)(2,1)S(1)} collective-permute-done((bf16[64,1792]{1,0:T(8,128)(2,1)S(1)}, bf16[64,1792]{1,0:T(8,128)(2,1)S(1)}, u32[]{:S(2)}, u32[]{:S(2)}) %collective-permute-start.27) | collective-permute-done | bytes 229408 | tf_op jit(solution)/shard_map/ppermute | solution.py:44
  114.2 1.5 %sum_back.1 = bf16[16,8,1792]{2,1,0:T(8,128)(2,1)} custom-call(s32[4]{0:T(128)S(1)} %pad_add_fusion.place, bf16[64,1792]{1,0:T(8,128)(2,1)S(1)} %get-tuple-element.116.a0, bf16[64,1792]{1,0:T(8,128)(2,1)S(1)} %get-tuple-element.117.b0, bf16[64,1792]{1,0:T(8,128)(2,1)S(1)} %collective-permute-done.26.a1, bf16[64,1792]{1,0:T(8,128)(2,1)S(1)} %collective-permute-done.27.b3, ...), custom_call_target="tpu_custom_call" | custom-call | bytes 2293760 | tf_op jit(solution)/shard_map/sum_back/pallas_call | solution.py:50
  115.7 3.6 %all-to-all-start.1 = ((bf16[16,8,1792]{2,1,0:T(8,128)(2,1)}), bf16[16,8,1792]{2,1,0:T(8,128)(2,1)S(1)}, u32[]{:S(2)}, u32[]{:S(2)}) async-start(bf16[16,8,1792]{2,1,0:T(8,128)(2,1)} %sum_back.1), calls=%async_computation.1 | async-start | bytes 917504 | tf_op jit(solution)/shard_map/all_to_all | solution.py:381
  119.3 6.9 %moments.1 = (f32[1,192,3584]{2,1,0:T(8,128)}, f32[1,192,3584]{2,1,0:T(8,128)}) custom-call(s32[4]{0:T(128)} %copy-done.2, f32[192,896]{1,0:T(8,128)} %copy-done.1, bf16[192,896]{1,0:T(8,128)(2,1)} %copy-done.6, bf16[192,896]{1,0:T(8,128)(2,1)} %copy-done.7, bf16[192,896]{1,0:T(8,128)(2,1)} %copy-done.8, f32[1,192,3584]{2,1,0:T(8,128)} %one.1, ...), custom_call_target="tpu_custom_call" | custom-call | flops 4128768 | bytes 11698176 | tf_op jit(solution)/shard_map/moments/pallas_call | solution.py:359
  126.2 2.8 %all-to-all-done.1.got = bf16[16,8,1792]{2,1,0:T(8,128)(2,1)S(1)} async-done(((bf16[16,8,1792]{2,1,0:T(8,128)(2,1)}), bf16[16,8,1792]{2,1,0:T(8,128)(2,1)S(1)}, u32[]{:S(2)}, u32[]{:S(2)}) %all-to-all-start.1) | async-done | bytes 458784 | tf_op jit(solution)/shard_map/all_to_all | solution.py:381
  129.0 2.1 %combine.1 = bf16[128,7168]{1,0:T(8,128)(2,1)} custom-call(s32[4]{0:T(128)S(1)} %copy-done.3, bf16[32,128]{1,0:T(8,128)(2,1)S(1)} %copy-done.4, bf16[16,8,1792]{2,1,0:T(8,128)(2,1)S(1)} %all-to-all-done.1.got), custom_call_target="tpu_custom_call" | custom-call | flops 58720256 | bytes 2301952 | tf_op jit(solution)/shard_map/combine/pallas_call | solution.py:50
  (55 shorter events, 9.2 us)
Async XLA Ops:
  4.1 7.4 %copy-start = (bf16[1,192,3584]{2,1,0:T(8,128)(2,1)S(1)}, bf16[1,192,3584]{2,1,0:T(8,128)(2,1)}, u32[]{:S(2)}) copy-start(bf16[1,192,3584]{2,1,0:T(8,128)(2,1)} %w.1) | copy-start | bytes 4128772
  4.2 23.3 %all-to-all-start = ((bf16[16,16,1792]{2,1,0:T(8,128)(2,1)}), bf16[16,16,1792]{2,1,0:T(8,128)(2,1)S(1)}, u32[]{:S(2)}, u32[]{:S(2)}) async-start(bf16[16,16,1792]{2,1,0:T(8,128)(2,1)} %get-tuple-element.65), calls=%async_computation | async-start | bytes 1835008 | tf_op jit(solution)/shard_map/all_to_all | solution.py:381
  11.5 102.7 %copy-start.2 = (s32[4]{0:T(128)}, s32[4]{0:T(128)S(1)}, u32[]{:S(2)}) copy-start(s32[4]{0:T(128)S(1)} %pad_add_fusion.place) | copy-start | bytes 52
  12.2 0.7 copy-start.5
  28.1 12.4 %collective-permute-start = (bf16[128,1792]{1,0:T(8,128)(2,1)S(1)}, bf16[128,1792]{1,0:T(8,128)(2,1)S(1)}, u32[]{:S(2)}, u32[]{:S(2)}) collective-permute-start(bf16[128,1792]{1,0:T(8,128)(2,1)S(1)} %get-tuple-element.68.a0.refs_0_.refs_4_), channel_id=1, source_target_pairs={{0,8},{1,9},{2,10},{3,11},{4,12},{5,13},{6,14},{7,15},{8,16},{9,17... | collective-permute-start | bytes 1376264 | tf_op jit(solution)/shard_map/ppermute | solution.py:44
  30.0 10.4 %collective-permute-start.1 = (bf16[128,1792]{1,0:T(8,128)(2,1)S(1)}, bf16[128,1792]{1,0:T(8,128)(2,1)S(1)}, u32[]{:S(2)}, u32[]{:S(2)}) collective-permute-start(bf16[128,1792]{1,0:T(8,128)(2,1)S(1)} %get-tuple-element.69.b0.refs_1_.refs_5_), channel_id=1, source_target_pairs={{0,24},{1,25},{2,26},{3,27},{4,28},{5,29},{6,30},{7,31},{8,0},{9,1... | collective-permute-start | bytes 1376264 | tf_op jit(solution)/shard_map/ppermute | solution.py:44
  32.2 12.7 %collective-permute-start.3 = (bf16[192,896]{1,0:T(8,128)(2,1)}, bf16[192,896]{1,0:T(8,128)(2,1)S(1)}, u32[]{:S(2)}, u32[]{:S(2)}) collective-permute-start(bf16[192,896]{1,0:T(8,128)(2,1)} %copy-done.5), channel_id=1, source_target_pairs={{0,4},{1,5},{2,6},{3,7},{4,0},{5,1},{6,2},{7,3},{8,12},{9,13},{10,... | collective-permute-start | bytes 1032200 | tf_op jit(solution)/shard_map/ppermute | solution.py:44
  33.1 14.7 %collective-permute-start.4 = (bf16[192,896]{1,0:T(8,128)(2,1)S(1)}, bf16[192,896]{1,0:T(8,128)(2,1)S(1)}, u32[]{:S(2)}, u32[]{:S(2)}) collective-permute-start(bf16[192,896]{1,0:T(8,128)(2,1)S(1)} %get-tuple-element.72), channel_id=1, source_target_pairs={{0,6},{1,7},{2,0},{3,1},{4,2},{5,3},{6,4},{7,5},{8,14},{9,15},{10,... | collective-permute-start | bytes 1032200 | tf_op jit(solution)/shard_map/ppermute | solution.py:44
  35.5 13.1 %collective-permute-start.2 = (bf16[192,896]{1,0:T(8,128)(2,1)S(1)}, bf16[192,896]{1,0:T(8,128)(2,1)S(1)}, u32[]{:S(2)}, u32[]{:S(2)}) collective-permute-start(bf16[192,896]{1,0:T(8,128)(2,1)S(1)} %get-tuple-element.66), channel_id=1, source_target_pairs={{0,2},{1,3},{2,4},{3,5},{4,6},{5,7},{6,0},{7,1},{8,10},{9,11},{10,... | collective-permute-start | bytes 1032200 | tf_op jit(solution)/shard_map/ppermute | solution.py:44
  41.1 19.5 %collective-permute-start.13 = (bf16[256,1792]{1,0:T(8,128)(2,1)S(1)}, bf16[256,1792]{1,0:T(8,128)(2,1)S(1)}, u32[]{:S(2)}, u32[]{:S(2)}) collective-permute-start(bf16[256,1792]{1,0:T(8,128)(2,1)S(1)} %get-tuple-element.84), channel_id=1, source_target_pairs={{0,24},{1,25},{2,26},{3,27},{4,28},{5,29},{6,30},{7,31},{8,0},{9,1... | collective-permute-start | bytes 2752520 | tf_op jit(solution)/shard_map/ppermute | solution.py:44
  44.2 19.8 %collective-permute-start.12 = (bf16[256,1792]{1,0:T(8,128)(2,1)S(1)}, bf16[256,1792]{1,0:T(8,128)(2,1)S(1)}, u32[]{:S(2)}, u32[]{:S(2)}) collective-permute-start(bf16[256,1792]{1,0:T(8,128)(2,1)S(1)} %get-tuple-element.73), channel_id=1, source_target_pairs={{0,8},{1,9},{2,10},{3,11},{4,12},{5,13},{6,14},{7,15},{8,16},{9,17... | collective-permute-start | bytes 2752520 | tf_op jit(solution)/shard_map/ppermute | solution.py:44
  48.6 1.7 %collective-permute-start.5 = (bf16[192,896]{1,0:T(8,128)(2,1)S(1)}, bf16[192,896]{1,0:T(8,128)(2,1)S(1)}, u32[]{:S(2)}, u32[]{:S(2)}) collective-permute-start(bf16[192,896]{1,0:T(8,128)(2,1)S(1)} %get-tuple-element.74.refs_0_), channel_id=1, source_target_pairs={{0,1},{1,0},{2,3},{3,2},{4,5},{5,4},{6,7},{7,6},{8,9},{9,8},{10,11... | collective-permute-start | bytes 1032200 | tf_op jit(solution)/shard_map/ppermute | solution.py:44
  48.6 2.1 %collective-permute-start.6 = (bf16[192,896]{1,0:T(8,128)(2,1)S(1)}, bf16[192,896]{1,0:T(8,128)(2,1)S(1)}, u32[]{:S(2)}, u32[]{:S(2)}) collective-permute-start(bf16[192,896]{1,0:T(8,128)(2,1)S(1)} %collective-permute-done.2.refs_1_), channel_id=1, source_target_pairs={{0,1},{1,0},{2,3},{3,2},{4,5},{5,4},{6,7},{7,6},{8,9},{9,8},{10,11... | collective-permute-start | bytes 1032200 | tf_op jit(solution)/shard_map/ppermute | solution.py:44
  49.1 2.1 %collective-permute-start.7 = (bf16[192,896]{1,0:T(8,128)(2,1)S(1)}, bf16[192,896]{1,0:T(8,128)(2,1)S(1)}, u32[]{:S(2)}, u32[]{:S(2)}) collective-permute-start(bf16[192,896]{1,0:T(8,128)(2,1)S(1)} %collective-permute-done.3.refs_2_), channel_id=1, source_target_pairs={{0,1},{1,0},{2,3},{3,2},{4,5},{5,4},{6,7},{7,6},{8,9},{9,8},{10,11... | collective-permute-start | bytes 1032200 | tf_op jit(solution)/shard_map/ppermute | solution.py:44
  50.3 1.7 %collective-permute-start.8 = (bf16[192,896]{1,0:T(8,128)(2,1)S(1)}, bf16[192,896]{1,0:T(8,128)(2,1)S(1)}, u32[]{:S(2)}, u32[]{:S(2)}) collective-permute-start(bf16[192,896]{1,0:T(8,128)(2,1)S(1)} %collective-permute-done.4.refs_3_), channel_id=1, source_target_pairs={{0,1},{1,0},{2,3},{3,2},{4,5},{5,4},{6,7},{7,6},{8,9},{9,8},{10,11... | collective-permute-start | bytes 1032200 | tf_op jit(solution)/shard_map/ppermute | solution.py:44
  54.3 14.9 %collective-permute-start.9 = (bf16[64,768]{1,0:T(8,128)(2,1)S(1)}, bf16[64,768]{1,0:T(8,128)(2,1)S(1)}, u32[]{:S(2)}, u32[]{:S(2)}) collective-permute-start(bf16[64,768]{1,0:T(8,128)(2,1)S(1)} %get-tuple-element.81), channel_id=1, source_target_pairs={{0,6},{1,7},{2,0},{3,1},{4,2},{5,3},{6,4},{7,5},{8,14},{9,15},{10,... | collective-permute-start | bytes 294920 | tf_op jit(solution)/shard_map/ppermute | solution.py:44
  56.2 13.0 %collective-permute-start.10 = (bf16[64,768]{1,0:T(8,128)(2,1)S(1)}, bf16[64,768]{1,0:T(8,128)(2,1)S(1)}, u32[]{:S(2)}, u32[]{:S(2)}) collective-permute-start(bf16[64,768]{1,0:T(8,128)(2,1)S(1)} %get-tuple-element.82), channel_id=1, source_target_pairs={{0,4},{1,5},{2,6},{3,7},{4,0},{5,1},{6,2},{7,3},{8,12},{9,13},{10,... | collective-permute-start | bytes 294920 | tf_op jit(solution)/shard_map/ppermute | solution.py:44
  56.9 12.3 %collective-permute-start.11 = (bf16[64,768]{1,0:T(8,128)(2,1)S(1)}, bf16[64,768]{1,0:T(8,128)(2,1)S(1)}, u32[]{:S(2)}, u32[]{:S(2)}) collective-permute-start(bf16[64,768]{1,0:T(8,128)(2,1)S(1)} %get-tuple-element.83), channel_id=1, source_target_pairs={{0,2},{1,3},{2,4},{3,5},{4,6},{5,7},{6,0},{7,1},{8,10},{9,11},{10,... | collective-permute-start | bytes 294920 | tf_op jit(solution)/shard_map/ppermute | solution.py:44
  65.6 9.2 %collective-permute-start.18 = (bf16[64,768]{1,0:T(8,128)(2,1)S(1)}, bf16[64,768]{1,0:T(8,128)(2,1)S(1)}, u32[]{:S(2)}, u32[]{:S(2)}) collective-permute-start(bf16[64,768]{1,0:T(8,128)(2,1)S(1)} %get-tuple-element.92), channel_id=1, source_target_pairs={{0,4},{1,5},{2,6},{3,7},{4,0},{5,1},{6,2},{7,3},{8,12},{9,13},{10,... | collective-permute-start | bytes 294920 | tf_op jit(solution)/shard_map/ppermute | solution.py:44
  68.5 8.2 %collective-permute-start.17 = (bf16[64,768]{1,0:T(8,128)(2,1)S(1)}, bf16[64,768]{1,0:T(8,128)(2,1)S(1)}, u32[]{:S(2)}, u32[]{:S(2)}) collective-permute-start(bf16[64,768]{1,0:T(8,128)(2,1)S(1)} %get-tuple-element.85), channel_id=1, source_target_pairs={{0,6},{1,7},{2,0},{3,1},{4,2},{5,3},{6,4},{7,5},{8,14},{9,15},{10,... | collective-permute-start | bytes 294920 | tf_op jit(solution)/shard_map/ppermute | solution.py:44
  69.2 7.5 %collective-permute-start.19 = (bf16[64,768]{1,0:T(8,128)(2,1)S(1)}, bf16[64,768]{1,0:T(8,128)(2,1)S(1)}, u32[]{:S(2)}, u32[]{:S(2)}) collective-permute-start(bf16[64,768]{1,0:T(8,128)(2,1)S(1)} %get-tuple-element.93), channel_id=1, source_target_pairs={{0,2},{1,3},{2,4},{3,5},{4,6},{5,7},{6,0},{7,1},{8,10},{9,11},{10,... | collective-permute-start | bytes 294920 | tf_op jit(solution)/shard_map/ppermute | solution.py:44
  71.3 8.2 %collective-permute-start.16 = (bf16[64,768]{1,0:T(8,128)(2,1)S(1)}, bf16[64,768]{1,0:T(8,128)(2,1)S(1)}, u32[]{:S(2)}, u32[]{:S(2)}) collective-permute-start(bf16[64,768]{1,0:T(8,128)(2,1)S(1)} %middle.2.refs_0_), channel_id=1, source_target_pairs={{0,6},{1,7},{2,0},{3,1},{4,2},{5,3},{6,4},{7,5},{8,14},{9,15},{10,... | collective-permute-start | bytes 294920 | tf_op jit(solution)/shard_map/ppermute | solution.py:44
  73.2 7.2 %collective-permute-start.15 = (bf16[64,768]{1,0:T(8,128)(2,1)S(1)}, bf16[64,768]{1,0:T(8,128)(2,1)S(1)}, u32[]{:S(2)}, u32[]{:S(2)}) collective-permute-start(bf16[64,768]{1,0:T(8,128)(2,1)S(1)} %middle.2.refs_0_), channel_id=1, source_target_pairs={{0,4},{1,5},{2,6},{3,7},{4,0},{5,1},{6,2},{7,3},{8,12},{9,13},{10,... | collective-permute-start | bytes 294920 | tf_op jit(solution)/shard_map/ppermute | solution.py:44
  74.8 7.3 %collective-permute-start.14 = (bf16[64,768]{1,0:T(8,128)(2,1)S(1)}, bf16[64,768]{1,0:T(8,128)(2,1)S(1)}, u32[]{:S(2)}, u32[]{:S(2)}) collective-permute-start(bf16[64,768]{1,0:T(8,128)(2,1)S(1)} %middle.2.refs_0_), channel_id=1, source_target_pairs={{0,2},{1,3},{2,4},{3,5},{4,6},{5,7},{6,0},{7,1},{8,10},{9,11},{10,... | collective-permute-start | bytes 294920 | tf_op jit(solution)/shard_map/ppermute | solution.py:44
  77.3 6.4 %collective-permute-start.22 = (bf16[64,768]{1,0:T(8,128)(2,1)S(1)}, bf16[64,768]{1,0:T(8,128)(2,1)S(1)}, u32[]{:S(2)}, u32[]{:S(2)}) collective-permute-start(bf16[64,768]{1,0:T(8,128)(2,1)S(1)} %middle.3.refs_0_), channel_id=1, source_target_pairs={{0,6},{1,7},{2,0},{3,1},{4,2},{5,3},{6,4},{7,5},{8,14},{9,15},{10,... | collective-permute-start | bytes 294920 | tf_op jit(solution)/shard_map/ppermute | solution.py:44
  78.8 6.2 %collective-permute-start.21 = (bf16[64,768]{1,0:T(8,128)(2,1)S(1)}, bf16[64,768]{1,0:T(8,128)(2,1)S(1)}, u32[]{:S(2)}, u32[]{:S(2)}) collective-permute-start(bf16[64,768]{1,0:T(8,128)(2,1)S(1)} %middle.3.refs_0_), channel_id=1, source_target_pairs={{0,4},{1,5},{2,6},{3,7},{4,0},{5,1},{6,2},{7,3},{8,12},{9,13},{10,... | collective-permute-start | bytes 294920 | tf_op jit(solution)/shard_map/ppermute | solution.py:44
  79.5 6.5 %collective-permute-start.20 = (bf16[64,768]{1,0:T(8,128)(2,1)S(1)}, bf16[64,768]{1,0:T(8,128)(2,1)S(1)}, u32[]{:S(2)}, u32[]{:S(2)}) collective-permute-start(bf16[64,768]{1,0:T(8,128)(2,1)S(1)} %middle.3.refs_0_), channel_id=1, source_target_pairs={{0,2},{1,3},{2,4},{3,5},{4,6},{5,7},{6,0},{7,1},{8,10},{9,11},{10,... | collective-permute-start | bytes 294920 | tf_op jit(solution)/shard_map/ppermute | solution.py:44
  87.1 4.7 %collective-permute-start.23 = (bf16[768,896]{1,0:T(8,128)(2,1)S(1)}, bf16[768,896]{1,0:T(8,128)(2,1)S(1)}, u32[]{:S(2)}, u32[]{:S(2)}) collective-permute-start(bf16[768,896]{1,0:T(8,128)(2,1)S(1)} %get-tuple-element.95), channel_id=1, source_target_pairs={{0,1},{1,0},{2,3},{3,2},{4,5},{5,4},{6,7},{7,6},{8,9},{9,8},{10,11... | collective-permute-start | bytes 4128776 | tf_op jit(solution)/shard_map/ppermute | solution.py:44
  88.5 14.2 %collective-permute-start.25 = (bf16[128,1792]{1,0:T(8,128)(2,1)S(1)}, bf16[128,1792]{1,0:T(8,128)(2,1)S(1)}, u32[]{:S(2)}, u32[]{:S(2)}) collective-permute-start(bf16[128,1792]{1,0:T(8,128)(2,1)S(1)} %get-tuple-element.106), channel_id=1, source_target_pairs={{0,8},{1,9},{2,10},{3,11},{4,12},{5,13},{6,14},{7,15},{8,16},{9,17... | collective-permute-start | bytes 1376264 | tf_op jit(solution)/shard_map/ppermute | solution.py:44
  88.6 14.1 %collective-permute-start.24 = (bf16[128,1792]{1,0:T(8,128)(2,1)S(1)}, bf16[128,1792]{1,0:T(8,128)(2,1)S(1)}, u32[]{:S(2)}, u32[]{:S(2)}) collective-permute-start(bf16[128,1792]{1,0:T(8,128)(2,1)S(1)} %get-tuple-element.97), channel_id=1, source_target_pairs={{0,24},{1,25},{2,26},{3,27},{4,28},{5,29},{6,30},{7,31},{8,0},{9,1... | collective-permute-start | bytes 1376264 | tf_op jit(solution)/shard_map/ppermute | solution.py:44
  93.3 9.4 %copy-start.1 = (f32[192,896]{1,0:T(8,128)}, f32[192,896]{1,0:T(8,128)S(1)}, u32[]{:S(2)}) copy-start(f32[192,896]{1,0:T(8,128)S(1)} %get-tuple-element.100.g0) | copy-start | bytes 2064388
  93.3 20.9 %collective-permute-start.28 = (bf16[192,896]{1,0:T(8,128)(2,1)S(1)}, bf16[192,896]{1,0:T(8,128)(2,1)S(1)}, u32[]{:S(2)}, u32[]{:S(2)}) collective-permute-start(bf16[192,896]{1,0:T(8,128)(2,1)S(1)} %get-tuple-element.113), channel_id=1, source_target_pairs={{0,6},{1,7},{2,0},{3,1},{4,2},{5,3},{6,4},{7,5},{8,14},{9,15},{10,... | collective-permute-start | bytes 1032200 | tf_op jit(solution)/shard_map/ppermute | solution.py:44
  94.2 20.0 %collective-permute-start.29 = (bf16[192,896]{1,0:T(8,128)(2,1)S(1)}, bf16[192,896]{1,0:T(8,128)(2,1)S(1)}, u32[]{:S(2)}, u32[]{:S(2)}) collective-permute-start(bf16[192,896]{1,0:T(8,128)(2,1)S(1)} %get-tuple-element.114), channel_id=1, source_target_pairs={{0,4},{1,5},{2,6},{3,7},{4,0},{5,1},{6,2},{7,3},{8,12},{9,13},{10,... | collective-permute-start | bytes 1032200 | tf_op jit(solution)/shard_map/ppermute | solution.py:44
  95.0 19.2 %collective-permute-start.30 = (bf16[192,896]{1,0:T(8,128)(2,1)S(1)}, bf16[192,896]{1,0:T(8,128)(2,1)S(1)}, u32[]{:S(2)}, u32[]{:S(2)}) collective-permute-start(bf16[192,896]{1,0:T(8,128)(2,1)S(1)} %get-tuple-element.115), channel_id=1, source_target_pairs={{0,2},{1,3},{2,4},{3,5},{4,6},{5,7},{6,0},{7,1},{8,10},{9,11},{10,... | collective-permute-start | bytes 1032200 | tf_op jit(solution)/shard_map/ppermute | solution.py:44
  103.3 7.4 %collective-permute-start.26 = (bf16[64,1792]{1,0:T(8,128)(2,1)S(1)}, bf16[64,1792]{1,0:T(8,128)(2,1)S(1)}, u32[]{:S(2)}, u32[]{:S(2)}) collective-permute-start(bf16[64,1792]{1,0:T(8,128)(2,1)S(1)} %get-tuple-element.111), channel_id=1, source_target_pairs={{0,24},{1,25},{2,26},{3,27},{4,28},{5,29},{6,30},{7,31},{8,0},{9,1... | collective-permute-start | bytes 688136 | tf_op jit(solution)/shard_map/ppermute | solution.py:44
  106.3 7.8 %collective-permute-start.27 = (bf16[64,1792]{1,0:T(8,128)(2,1)S(1)}, bf16[64,1792]{1,0:T(8,128)(2,1)S(1)}, u32[]{:S(2)}, u32[]{:S(2)}) collective-permute-start(bf16[64,1792]{1,0:T(8,128)(2,1)S(1)} %get-tuple-element.112), channel_id=1, source_target_pairs={{0,8},{1,9},{2,10},{3,11},{4,12},{5,13},{6,14},{7,15},{8,16},{9,17... | collective-permute-start | bytes 688136 | tf_op jit(solution)/shard_map/ppermute | solution.py:44
  114.2 5.1 %copy-start.6 = (bf16[192,896]{1,0:T(8,128)(2,1)}, bf16[192,896]{1,0:T(8,128)(2,1)S(1)}, u32[]{:S(2)}) copy-start(bf16[192,896]{1,0:T(8,128)(2,1)S(1)} %collective-permute-done.28.g1) | copy-start | bytes 1032196
  114.2 5.1 %copy-start.7 = (bf16[192,896]{1,0:T(8,128)(2,1)}, bf16[192,896]{1,0:T(8,128)(2,1)S(1)}, u32[]{:S(2)}) copy-start(bf16[192,896]{1,0:T(8,128)(2,1)S(1)} %collective-permute-done.29.g2) | copy-start | bytes 1032196
  114.2 5.1 %copy-start.8 = (bf16[192,896]{1,0:T(8,128)(2,1)}, bf16[192,896]{1,0:T(8,128)(2,1)S(1)}, u32[]{:S(2)}) copy-start(bf16[192,896]{1,0:T(8,128)(2,1)S(1)} %collective-permute-done.30.g3) | copy-start | bytes 1032196
  115.7 13.3 %all-to-all-start.1 = ((bf16[16,8,1792]{2,1,0:T(8,128)(2,1)}), bf16[16,8,1792]{2,1,0:T(8,128)(2,1)S(1)}, u32[]{:S(2)}, u32[]{:S(2)}) async-start(bf16[16,8,1792]{2,1,0:T(8,128)(2,1)} %sum_back.1), calls=%async_computation.1 | async-start | bytes 917504 | tf_op jit(solution)/shard_map/all_to_all | solution.py:381
  119.3 9.7 %copy-start.3 = (s32[4]{0:T(128)S(1)}, s32[4]{0:T(128)}, u32[]{:S(2)}) copy-start(s32[4]{0:T(128)} %copy-done.2) | copy-start | bytes 52
  119.3 9.7 %copy-start.4 = (bf16[32,128]{1,0:T(8,128)(2,1)S(1)}, bf16[32,128]{1,0:T(8,128)(2,1)}, u32[]{:S(2)}) copy-start(bf16[32,128]{1,0:T(8,128)(2,1)} %get-tuple-element.64.pick) | copy-start | bytes 24580

commit v7 on v6

--- a/solution.py
+++ b/solution.py
@@ -487,6 +487,8 @@
         *first,
         flops=flops,
     )
+    a0, b0, a1, b3 = back_part(place, held_one, w_own, w_other, 0)
+    held_two = after(held_two, a0)
     held_two, theirs = call(
         their_grad_kernel,
         "their_grad",
@@ -512,7 +514,6 @@
         flops=flops // 2,
         scratch=[pltpu.VMEM((3 * width, EIGHTH), F32)],
     )
-    a0, b0, a1, b3 = back_part(place, after(held_one, blocks[0]), w_own, w_other, 0)
     a1, b3 = pass_on(place, *after((a1, b3, got_minus, got_plus), blocks[0]))
     a1, b3 = turn(a1, "z", -1), turn(b3, "z", 1)
     blocks = spread(blocks, "y", -1)

time: 132 us -> 132 us (level)
  transfers between devices with their start and end apart: 33 -> 33, of which waited for: 20 -> 19; matrix products, arithmetic and copies ran while one was open for 0% -> 0% of each run, Pallas kernels for 15% -> 15%
where the time goes in v7:
time: 132 us
  waiting for transfers between devices  55.3 us (42%)
  starting transfers between devices  45.5 us (34%)
  Pallas kernels  28.4 us (22%)
  local copies, waits for them, and re-layouts  1.6 us (1%)
    ppermute x31, waiting for transfers between devices, turn(): return lax.ppermute(value, ('expert', 'dp'), rotation(axis, step))  37.3 us
    ppermute x31, starting transfers between devices, turn(): return lax.ppermute(value, ('expert', 'dp'), rotation(axis, step))  34.6 us
    pallas_call x16, Pallas kernels, call(): pl.pallas_call(kernel, name=name, out_shape=outs, in_specs=[pl.BlockSpec(...  18 us
    all_to_all x2, waiting for transfers between devices, exchange(): lax.all_to_all(value, 'expert', 0, 0, axis_index_groups=list(groups.value...  18 us
    all_to_all x2, starting transfers between devices, exchange(): lax.all_to_all(value, 'expert', 0, 0, axis_index_groups=list(groups.value...  10.8 us
    pallas_call x1, Pallas kernels, moments(): pl.pallas_call(moments_kernel, name='moments', grid_spec=pltpu.PrefetchSc...  6.9 us
    pallas_call x1, Pallas kernels, route(): pl.pallas_call(route_kernel, name='route', in_specs=[hbm] * 4, out_specs=...  3.5 us
  transfers between devices with their start and end apart: 33, of which 19 were waited for; matrix products, arithmetic and copies ran while one was open for 0% of the time, Pallas kernels for 15%

profile of v7, /device:TPU:0, one launch (start us, length us, event | category | flops | bytes accessed | tf_op | source)
XLA Modules:
  0.0 132.0 jit_solution(1370064547435903568)
XLA Ops:
  0.6 3.5 %route.1 = (bf16[16,16,1792]{2,1,0:T(8,128)(2,1)}, bf16[32,128]{1,0:T(8,128)(2,1)}) custom-call(s32[8,128]{1,0:T(8,128)} %bitcast.6, f32[8,128]{1,0:T(8,128)} %bitcast.7, bf16[128,7168]{1,0:T(8,128)(2,1)} %tokens.1, bf16[128,7168]{1,0:T(8,128)(2,1)} %grads.1), custom_call_target="tpu_custom_call" | custom-call | flops 117440512 | bytes 5505024 | tf_op jit(solution)/shard_map/route/pallas_call | solution.py:143
  4.2 7.3 %all-to-all-start = ((bf16[16,16,1792]{2,1,0:T(8,128)(2,1)}), bf16[16,16,1792]{2,1,0:T(8,128)(2,1)S(1)}, u32[]{:S(2)}, u32[]{:S(2)}) async-start(bf16[16,16,1792]{2,1,0:T(8,128)(2,1)} %get-tuple-element.68), calls=%async_computation | async-start | bytes 1835008 | tf_op jit(solution)/shard_map/all_to_all | solution.py:381
  12.2 0.7 copy-done.5
  12.9 14.5 %all-to-all-done.got = bf16[16,16,1792]{2,1,0:T(8,128)(2,1)S(1)} async-done(((bf16[16,16,1792]{2,1,0:T(8,128)(2,1)}), bf16[16,16,1792]{2,1,0:T(8,128)(2,1)S(1)}, u32[]{:S(2)}, u32[]{:S(2)}) %all-to-all-start) | async-done | bytes 917536 | tf_op jit(solution)/shard_map/all_to_all | solution.py:381
  28.1 2.0 %collective-permute-start = (bf16[128,1792]{1,0:T(8,128)(2,1)S(1)}, bf16[128,1792]{1,0:T(8,128)(2,1)S(1)}, u32[]{:S(2)}, u32[]{:S(2)}) collective-permute-start(bf16[128,1792]{1,0:T(8,128)(2,1)S(1)} %get-tuple-element.71.a0.refs_0_.refs_4_), channel_id=1, source_target_pairs={{0,8},{1,9},{2,10},{3,11},{4,12},{5,13},{6,14},{7,15},{8,16},{9,17... | collective-permute-start | bytes 1376264 | tf_op jit(solution)/shard_map/ppermute | solution.py:44
  30.0 2.2 %collective-permute-start.1 = (bf16[128,1792]{1,0:T(8,128)(2,1)S(1)}, bf16[128,1792]{1,0:T(8,128)(2,1)S(1)}, u32[]{:S(2)}, u32[]{:S(2)}) collective-permute-start(bf16[128,1792]{1,0:T(8,128)(2,1)S(1)} %get-tuple-element.72.b0.refs_1_.refs_5_), channel_id=1, source_target_pairs={{0,24},{1,25},{2,26},{3,27},{4,28},{5,29},{6,30},{7,31},{8,0},{9,1... | collective-permute-start | bytes 1376264 | tf_op jit(solution)/shard_map/ppermute | solution.py:44
  32.2 0.9 collective-permute-start.3
  33.1 2.4 %collective-permute-start.4 = (bf16[192,896]{1,0:T(8,128)(2,1)S(1)}, bf16[192,896]{1,0:T(8,128)(2,1)S(1)}, u32[]{:S(2)}, u32[]{:S(2)}) collective-permute-start(bf16[192,896]{1,0:T(8,128)(2,1)S(1)} %get-tuple-element.75), channel_id=1, source_target_pairs={{0,6},{1,7},{2,0},{3,1},{4,2},{5,3},{6,4},{7,5},{8,14},{9,15},{10,... | collective-permute-start | bytes 1032200 | tf_op jit(solution)/shard_map/ppermute | solution.py:44
  35.5 4.9 %collective-permute-done.a1.refs_2_.refs_6_ = bf16[128,1792]{1,0:T(8,128)(2,1)S(1)} collective-permute-done((bf16[128,1792]{1,0:T(8,128)(2,1)S(1)}, bf16[128,1792]{1,0:T(8,128)(2,1)S(1)}, u32[]{:S(2)}, u32[]{:S(2)}) %collective-permute-start) | collective-permute-done | bytes 458784 | tf_op jit(solution)/shard_map/ppermute | solution.py:44
  41.1 3.1 %collective-permute-start.13 = (bf16[256,1792]{1,0:T(8,128)(2,1)S(1)}, bf16[256,1792]{1,0:T(8,128)(2,1)S(1)}, u32[]{:S(2)}, u32[]{:S(2)}) collective-permute-start(bf16[256,1792]{1,0:T(8,128)(2,1)S(1)} %get-tuple-element.87), channel_id=1, source_target_pairs={{0,24},{1,25},{2,26},{3,27},{4,28},{5,29},{6,30},{7,31},{8,0},{9,1... | collective-permute-start | bytes 2752520 | tf_op jit(solution)/shard_map/ppermute | solution.py:44
  44.2 0.7 collective-permute-done.3.refs_2_
  44.9 2.9 %collective-permute-done.4.refs_3_ = bf16[192,896]{1,0:T(8,128)(2,1)S(1)} collective-permute-done((bf16[192,896]{1,0:T(8,128)(2,1)S(1)}, bf16[192,896]{1,0:T(8,128)(2,1)S(1)}, u32[]{:S(2)}, u32[]{:S(2)}) %collective-permute-start.4) | collective-permute-done | bytes 344096 | tf_op jit(solution)/shard_map/ppermute | solution.py:44
  47.8 0.8 collective-permute-done.2.refs_1_
  49.1 1.1 collective-permute-done.5.refs_4_
  51.9 0.8 stack_weights.1
  52.7 1.6 %forward.2 = (f32[64,768]{1,0:T(8,128)S(1)}, bf16[64,768]{1,0:T(8,128)(2,1)S(1)}, bf16[64,768]{1,0:T(8,128)(2,1)S(1)}, bf16[64,768]{1,0:T(8,128)(2,1)S(1)}) custom-call(s32[4]{0:T(128)S(1)} %pad_add_fusion.place, bf16[128,1792]{1,0:T(8,128)(2,1)S(1)} %get-tuple-element.71.a0.refs_0_.refs_4_, bf16[128,1792]{1,0:T(8,128)(2,1)S(1)} %get-tuple-element.72.b0.refs_1_.refs_5_, ...), custom_call_target="tpu_custom_call" | custom-call | flops 704643072 | bytes 5079040 | tf_op jit(solution)/shard_map/forward/pallas_call | solution.py:50
  54.3 1.9 %collective-permute-start.9 = (bf16[64,768]{1,0:T(8,128)(2,1)S(1)}, bf16[64,768]{1,0:T(8,128)(2,1)S(1)}, u32[]{:S(2)}, u32[]{:S(2)}) collective-permute-start(bf16[64,768]{1,0:T(8,128)(2,1)S(1)} %get-tuple-element.84), channel_id=1, source_target_pairs={{0,6},{1,7},{2,0},{3,1},{4,2},{5,3},{6,4},{7,5},{8,14},{9,15},{10,... | collective-permute-start | bytes 294920 | tf_op jit(solution)/shard_map/ppermute | solution.py:44
  56.2 0.8 collective-permute-start.10
  57.6 3.0 %collective-permute-done.13.refs_1_.refs_6_.minus = bf16[256,1792]{1,0:T(8,128)(2,1)S(1)} collective-permute-done((bf16[256,1792]{1,0:T(8,128)(2,1)S(1)}, bf16[256,1792]{1,0:T(8,128)(2,1)S(1)}, u32[]{:S(2)}, u32[]{:S(2)}) %collective-permute-start.13) | collective-permute-done | bytes 917536 | tf_op jit(solution)/shard_map/ppermute | solution.py:44
  60.6 3.4 %collective-permute-done.12.refs_0_.refs_5_.plus = bf16[256,1792]{1,0:T(8,128)(2,1)S(1)} collective-permute-done((bf16[256,1792]{1,0:T(8,128)(2,1)S(1)}, bf16[256,1792]{1,0:T(8,128)(2,1)S(1)}, u32[]{:S(2)}, u32[]{:S(2)}) %collective-permute-start.12) | collective-permute-done | bytes 917536 | tf_op jit(solution)/shard_map/ppermute | solution.py:44
  64.0 1.6 %forward.3 = (f32[64,768]{1,0:T(8,128)S(1)}, bf16[64,768]{1,0:T(8,128)(2,1)S(1)}, bf16[64,768]{1,0:T(8,128)(2,1)S(1)}, bf16[64,768]{1,0:T(8,128)(2,1)S(1)}) custom-call(s32[4]{0:T(128)S(1)} %pad_add_fusion.place, bf16[256,1792]{1,0:T(8,128)(2,1)S(1)} %collective-permute-done.12.refs_0_.refs_5_.plus, ...), custom_call_target="tpu_custom_call" | custom-call | flops 704643072 | bytes 5079040 | tf_op jit(solution)/shard_map/forward/pallas_call | solution.py:50
  65.6 2.9 %collective-permute-start.18 = (bf16[64,768]{1,0:T(8,128)(2,1)S(1)}, bf16[64,768]{1,0:T(8,128)(2,1)S(1)}, u32[]{:S(2)}, u32[]{:S(2)}) collective-permute-start(bf16[64,768]{1,0:T(8,128)(2,1)S(1)} %get-tuple-element.99), channel_id=1, source_target_pairs={{0,4},{1,5},{2,6},{3,7},{4,0},{5,1},{6,2},{7,3},{8,12},{9,13},{10,... | collective-permute-start | bytes 294920 | tf_op jit(solution)/shard_map/ppermute | solution.py:44
  69.2 1.5 %collective-permute-start.19 = (bf16[64,768]{1,0:T(8,128)(2,1)S(1)}, bf16[64,768]{1,0:T(8,128)(2,1)S(1)}, u32[]{:S(2)}, u32[]{:S(2)}) collective-permute-start(bf16[64,768]{1,0:T(8,128)(2,1)S(1)} %get-tuple-element.100), channel_id=1, source_target_pairs={{0,2},{1,3},{2,4},{3,5},{4,6},{5,7},{6,0},{7,1},{8,10},{9,11},{10,... | collective-permute-start | bytes 294920 | tf_op jit(solution)/shard_map/ppermute | solution.py:44
  71.3 1.9 %collective-permute-start.16 = (bf16[64,768]{1,0:T(8,128)(2,1)S(1)}, bf16[64,768]{1,0:T(8,128)(2,1)S(1)}, u32[]{:S(2)}, u32[]{:S(2)}) collective-permute-start(bf16[64,768]{1,0:T(8,128)(2,1)S(1)} %middle.2.refs_0_), channel_id=1, source_target_pairs={{0,6},{1,7},{2,0},{3,1},{4,2},{5,3},{6,4},{7,5},{8,14},{9,15},{10,... | collective-permute-start | bytes 294920 | tf_op jit(solution)/shard_map/ppermute | solution.py:44
  73.2 1.6 %collective-permute-start.15 = (bf16[64,768]{1,0:T(8,128)(2,1)S(1)}, bf16[64,768]{1,0:T(8,128)(2,1)S(1)}, u32[]{:S(2)}, u32[]{:S(2)}) collective-permute-start(bf16[64,768]{1,0:T(8,128)(2,1)S(1)} %middle.2.refs_0_), channel_id=1, source_target_pairs={{0,4},{1,5},{2,6},{3,7},{4,0},{5,1},{6,2},{7,3},{8,12},{9,13},{10,... | collective-permute-start | bytes 294920 | tf_op jit(solution)/shard_map/ppermute | solution.py:44
  74.8 1.9 %collective-permute-done.19.p3 = bf16[64,768]{1,0:T(8,128)(2,1)S(1)} collective-permute-done((bf16[64,768]{1,0:T(8,128)(2,1)S(1)}, bf16[64,768]{1,0:T(8,128)(2,1)S(1)}, u32[]{:S(2)}, u32[]{:S(2)}) %collective-permute-start.19) | collective-permute-done | bytes 98336 | tf_op jit(solution)/shard_map/ppermute | solution.py:44
  77.3 1.4 %collective-permute-start.22 = (bf16[64,768]{1,0:T(8,128)(2,1)S(1)}, bf16[64,768]{1,0:T(8,128)(2,1)S(1)}, u32[]{:S(2)}, u32[]{:S(2)}) collective-permute-start(bf16[64,768]{1,0:T(8,128)(2,1)S(1)} %middle.3.refs_0_), channel_id=1, source_target_pairs={{0,6},{1,7},{2,0},{3,1},{4,2},{5,3},{6,4},{7,5},{8,14},{9,15},{10,... | collective-permute-start | bytes 294920 | tf_op jit(solution)/shard_map/ppermute | solution.py:44
  78.8 0.7 collective-permute-start.21
  80.4 1.8 %collective-permute-done.14.refs_1_ = bf16[64,768]{1,0:T(8,128)(2,1)S(1)} collective-permute-done((bf16[64,768]{1,0:T(8,128)(2,1)S(1)}, bf16[64,768]{1,0:T(8,128)(2,1)S(1)}, u32[]{:S(2)}, u32[]{:S(2)}) %collective-permute-start.14) | collective-permute-done | bytes 98336 | tf_op jit(solution)/shard_map/ppermute | solution.py:44
  82.1 1.6 %first_grad.1 = (bf16[256,768]{1,0:T(8,128)(2,1)S(1)}, f32[768,896]{1,0:T(8,128)S(1)}, f32[768,896]{1,0:T(8,128)S(1)}) custom-call(s32[4]{0:T(128)S(1)} %pad_add_fusion.place, bf16[64,768]{1,0:T(8,128)(2,1)S(1)} %middle.2.refs_0_, bf16[64,768]{1,0:T(8,128)(2,1)S(1)} %collective-permute-done.14.refs_1_, bf16[64,768]{1,0:T(8,128)(2,1)S(1)} %collective-permute-done.15.refs_2_, ...), custom_call_target="tpu_custom_call" | custom-call | flops 704643072 | bytes 8126464 | tf_op jit(solution)/shard_map/first_grad/pallas_call | solution.py:50
  83.7 1.2 back.2
  85.0 0.9 collective-permute-done.20.refs_1_
  85.9 1.2 their_grad.1
  87.2 1.2 back.3
  88.6 3.2 %collective-permute-start.23 = (bf16[128,1792]{1,0:T(8,128)(2,1)S(1)}, bf16[128,1792]{1,0:T(8,128)(2,1)S(1)}, u32[]{:S(2)}, u32[]{:S(2)}) collective-permute-start(bf16[128,1792]{1,0:T(8,128)(2,1)S(1)} %get-tuple-element.107), channel_id=1, source_target_pairs={{0,24},{1,25},{2,26},{3,27},{4,28},{5,29},{6,30},{7,31},{8,0},{9,1... | collective-permute-start | bytes 1376264 | tf_op jit(solution)/shard_map/ppermute | solution.py:44
  91.8 1.5 %my_grad.1 = (f32[192,896]{1,0:T(8,128)S(1)}, bf16[192,896]{1,0:T(8,128)(2,1)S(1)}, bf16[192,896]{1,0:T(8,128)(2,1)S(1)}, bf16[192,896]{1,0:T(8,128)(2,1)S(1)}) custom-call(s32[4]{0:T(128)S(1)} %pad_add_fusion.place, bf16[768,896]{1,0:T(8,128)(2,1)S(1)} %collective-permute-done.25.got, bf16[256,768]{1,0:T(8,128)(2,1)S(1)} %get-tuple-element.110.held, ...), custom_call_target="tpu_custom_call" | custom-call | flops 352321536 | bytes 8077312 | tf_op jit(solution)/shard_map/my_grad/pallas_call | solution.py:50
  93.3 0.8 copy-done.1
  94.1 0.8 collective-permute-start.28
  94.9 0.9 collective-permute-start.29
  96.5 6.2 %collective-permute-done.24.got_b.got_plus = bf16[128,1792]{1,0:T(8,128)(2,1)S(1)} collective-permute-done((bf16[128,1792]{1,0:T(8,128)(2,1)S(1)}, bf16[128,1792]{1,0:T(8,128)(2,1)S(1)}, u32[]{:S(2)}, u32[]{:S(2)}) %collective-permute-start.24) | collective-permute-done | bytes 458784 | tf_op jit(solution)/shard_map/ppermute | solution.py:44
  103.3 3.0 %collective-permute-start.26 = (bf16[64,1792]{1,0:T(8,128)(2,1)S(1)}, bf16[64,1792]{1,0:T(8,128)(2,1)S(1)}, u32[]{:S(2)}, u32[]{:S(2)}) collective-permute-start(bf16[64,1792]{1,0:T(8,128)(2,1)S(1)} %get-tuple-element.117), channel_id=1, source_target_pairs={{0,24},{1,25},{2,26},{3,27},{4,28},{5,29},{6,30},{7,31},{8,0},{9,1... | collective-permute-start | bytes 688136 | tf_op jit(solution)/shard_map/ppermute | solution.py:44
  106.3 4.4 %collective-permute-done.26.a1 = bf16[64,1792]{1,0:T(8,128)(2,1)S(1)} collective-permute-done((bf16[64,1792]{1,0:T(8,128)(2,1)S(1)}, bf16[64,1792]{1,0:T(8,128)(2,1)S(1)}, u32[]{:S(2)}, u32[]{:S(2)}) %collective-permute-start.26) | collective-permute-done | bytes 229408 | tf_op jit(solution)/shard_map/ppermute | solution.py:44
  110.8 3.4 %collective-permute-done.27.b3 = bf16[64,1792]{1,0:T(8,128)(2,1)S(1)} collective-permute-done((bf16[64,1792]{1,0:T(8,128)(2,1)S(1)}, bf16[64,1792]{1,0:T(8,128)(2,1)S(1)}, u32[]{:S(2)}, u32[]{:S(2)}) %collective-permute-start.27) | collective-permute-done | bytes 229408 | tf_op jit(solution)/shard_map/ppermute | solution.py:44
  114.2 1.5 %sum_back.1 = bf16[16,8,1792]{2,1,0:T(8,128)(2,1)} custom-call(s32[4]{0:T(128)S(1)} %pad_add_fusion.place, bf16[64,1792]{1,0:T(8,128)(2,1)S(1)} %get-tuple-element.122.a0, bf16[64,1792]{1,0:T(8,128)(2,1)S(1)} %get-tuple-element.123.b0, bf16[64,1792]{1,0:T(8,128)(2,1)S(1)} %collective-permute-done.26.a1, bf16[64,1792]{1,0:T(8,128)(2,1)S(1)} %collective-permute-done.27.b3, ...), custom_call_target="tpu_custom_call" | custom-call | bytes 2293760 | tf_op jit(solution)/shard_map/sum_back/pallas_call | solution.py:50
  115.7 3.6 %all-to-all-start.1 = ((bf16[16,8,1792]{2,1,0:T(8,128)(2,1)}), bf16[16,8,1792]{2,1,0:T(8,128)(2,1)S(1)}, u32[]{:S(2)}, u32[]{:S(2)}) async-start(bf16[16,8,1792]{2,1,0:T(8,128)(2,1)} %sum_back.1), calls=%async_computation.1 | async-start | bytes 917504 | tf_op jit(solution)/shard_map/all_to_all | solution.py:381
  119.3 6.9 %moments.1 = (f32[1,192,3584]{2,1,0:T(8,128)}, f32[1,192,3584]{2,1,0:T(8,128)}) custom-call(s32[4]{0:T(128)} %copy-done.2, f32[192,896]{1,0:T(8,128)} %copy-done.1, bf16[192,896]{1,0:T(8,128)(2,1)} %copy-done.6, bf16[192,896]{1,0:T(8,128)(2,1)} %copy-done.7, bf16[192,896]{1,0:T(8,128)(2,1)} %copy-done.8, f32[1,192,3584]{2,1,0:T(8,128)} %one.1, ...), custom_call_target="tpu_custom_call" | custom-call | flops 4128768 | bytes 11698176 | tf_op jit(solution)/shard_map/moments/pallas_call | solution.py:359
  126.2 3.5 %all-to-all-done.1.got = bf16[16,8,1792]{2,1,0:T(8,128)(2,1)S(1)} async-done(((bf16[16,8,1792]{2,1,0:T(8,128)(2,1)}), bf16[16,8,1792]{2,1,0:T(8,128)(2,1)S(1)}, u32[]{:S(2)}, u32[]{:S(2)}) %all-to-all-start.1) | async-done | bytes 458784 | tf_op jit(solution)/shard_map/all_to_all | solution.py:381
  129.7 2.1 %combine.1 = bf16[128,7168]{1,0:T(8,128)(2,1)} custom-call(s32[4]{0:T(128)S(1)} %copy-done.3, bf16[32,128]{1,0:T(8,128)(2,1)S(1)} %copy-done.4, bf16[16,8,1792]{2,1,0:T(8,128)(2,1)S(1)} %all-to-all-done.1.got), custom_call_target="tpu_custom_call" | custom-call | flops 58720256 | bytes 2301952 | tf_op jit(solution)/shard_map/combine/pallas_call | solution.py:50
  (55 shorter events, 9.2 us)
Async XLA Ops:
  4.1 7.4 %copy-start = (bf16[1,192,3584]{2,1,0:T(8,128)(2,1)S(1)}, bf16[1,192,3584]{2,1,0:T(8,128)(2,1)}, u32[]{:S(2)}) copy-start(bf16[1,192,3584]{2,1,0:T(8,128)(2,1)} %w.1) | copy-start | bytes 4128772
  4.2 23.3 %all-to-all-start = ((bf16[16,16,1792]{2,1,0:T(8,128)(2,1)}), bf16[16,16,1792]{2,1,0:T(8,128)(2,1)S(1)}, u32[]{:S(2)}, u32[]{:S(2)}) async-start(bf16[16,16,1792]{2,1,0:T(8,128)(2,1)} %get-tuple-element.68), calls=%async_computation | async-start | bytes 1835008 | tf_op jit(solution)/shard_map/all_to_all | solution.py:381
  11.5 102.7 %copy-start.2 = (s32[4]{0:T(128)}, s32[4]{0:T(128)S(1)}, u32[]{:S(2)}) copy-start(s32[4]{0:T(128)S(1)} %pad_add_fusion.place) | copy-start | bytes 52
  12.2 0.7 copy-start.5
  28.1 12.4 %collective-permute-start = (bf16[128,1792]{1,0:T(8,128)(2,1)S(1)}, bf16[128,1792]{1,0:T(8,128)(2,1)S(1)}, u32[]{:S(2)}, u32[]{:S(2)}) collective-permute-start(bf16[128,1792]{1,0:T(8,128)(2,1)S(1)} %get-tuple-element.71.a0.refs_0_.refs_4_), channel_id=1, source_target_pairs={{0,8},{1,9},{2,10},{3,11},{4,12},{5,13},{6,14},{7,15},{8,16},{9,17... | collective-permute-start | bytes 1376264 | tf_op jit(solution)/shard_map/ppermute | solution.py:44
  30.0 10.4 %collective-permute-start.1 = (bf16[128,1792]{1,0:T(8,128)(2,1)S(1)}, bf16[128,1792]{1,0:T(8,128)(2,1)S(1)}, u32[]{:S(2)}, u32[]{:S(2)}) collective-permute-start(bf16[128,1792]{1,0:T(8,128)(2,1)S(1)} %get-tuple-element.72.b0.refs_1_.refs_5_), channel_id=1, source_target_pairs={{0,24},{1,25},{2,26},{3,27},{4,28},{5,29},{6,30},{7,31},{8,0},{9,1... | collective-permute-start | bytes 1376264 | tf_op jit(solution)/shard_map/ppermute | solution.py:44
  32.2 12.7 %collective-permute-start.3 = (bf16[192,896]{1,0:T(8,128)(2,1)}, bf16[192,896]{1,0:T(8,128)(2,1)S(1)}, u32[]{:S(2)}, u32[]{:S(2)}) collective-permute-start(bf16[192,896]{1,0:T(8,128)(2,1)} %copy-done.5), channel_id=1, source_target_pairs={{0,4},{1,5},{2,6},{3,7},{4,0},{5,1},{6,2},{7,3},{8,12},{9,13},{10,... | collective-permute-start | bytes 1032200 | tf_op jit(solution)/shard_map/ppermute | solution.py:44
  33.1 14.7 %collective-permute-start.4 = (bf16[192,896]{1,0:T(8,128)(2,1)S(1)}, bf16[192,896]{1,0:T(8,128)(2,1)S(1)}, u32[]{:S(2)}, u32[]{:S(2)}) collective-permute-start(bf16[192,896]{1,0:T(8,128)(2,1)S(1)} %get-tuple-element.75), channel_id=1, source_target_pairs={{0,6},{1,7},{2,0},{3,1},{4,2},{5,3},{6,4},{7,5},{8,14},{9,15},{10,... | collective-permute-start | bytes 1032200 | tf_op jit(solution)/shard_map/ppermute | solution.py:44
  35.5 13.1 %collective-permute-start.2 = (bf16[192,896]{1,0:T(8,128)(2,1)S(1)}, bf16[192,896]{1,0:T(8,128)(2,1)S(1)}, u32[]{:S(2)}, u32[]{:S(2)}) collective-permute-start(bf16[192,896]{1,0:T(8,128)(2,1)S(1)} %get-tuple-element.69), channel_id=1, source_target_pairs={{0,2},{1,3},{2,4},{3,5},{4,6},{5,7},{6,0},{7,1},{8,10},{9,11},{10,... | collective-permute-start | bytes 1032200 | tf_op jit(solution)/shard_map/ppermute | solution.py:44
  41.1 19.5 %collective-permute-start.13 = (bf16[256,1792]{1,0:T(8,128)(2,1)S(1)}, bf16[256,1792]{1,0:T(8,128)(2,1)S(1)}, u32[]{:S(2)}, u32[]{:S(2)}) collective-permute-start(bf16[256,1792]{1,0:T(8,128)(2,1)S(1)} %get-tuple-element.87), channel_id=1, source_target_pairs={{0,24},{1,25},{2,26},{3,27},{4,28},{5,29},{6,30},{7,31},{8,0},{9,1... | collective-permute-start | bytes 2752520 | tf_op jit(solution)/shard_map/ppermute | solution.py:44
  44.2 19.8 %collective-permute-start.12 = (bf16[256,1792]{1,0:T(8,128)(2,1)S(1)}, bf16[256,1792]{1,0:T(8,128)(2,1)S(1)}, u32[]{:S(2)}, u32[]{:S(2)}) collective-permute-start(bf16[256,1792]{1,0:T(8,128)(2,1)S(1)} %get-tuple-element.76), channel_id=1, source_target_pairs={{0,8},{1,9},{2,10},{3,11},{4,12},{5,13},{6,14},{7,15},{8,16},{9,17... | collective-permute-start | bytes 2752520 | tf_op jit(solution)/shard_map/ppermute | solution.py:44
  48.6 1.7 %collective-permute-start.5 = (bf16[192,896]{1,0:T(8,128)(2,1)S(1)}, bf16[192,896]{1,0:T(8,128)(2,1)S(1)}, u32[]{:S(2)}, u32[]{:S(2)}) collective-permute-start(bf16[192,896]{1,0:T(8,128)(2,1)S(1)} %get-tuple-element.77.refs_0_), channel_id=1, source_target_pairs={{0,1},{1,0},{2,3},{3,2},{4,5},{5,4},{6,7},{7,6},{8,9},{9,8},{10,11... | collective-permute-start | bytes 1032200 | tf_op jit(solution)/shard_map/ppermute | solution.py:44
  48.6 2.1 %collective-permute-start.6 = (bf16[192,896]{1,0:T(8,128)(2,1)S(1)}, bf16[192,896]{1,0:T(8,128)(2,1)S(1)}, u32[]{:S(2)}, u32[]{:S(2)}) collective-permute-start(bf16[192,896]{1,0:T(8,128)(2,1)S(1)} %collective-permute-done.2.refs_1_), channel_id=1, source_target_pairs={{0,1},{1,0},{2,3},{3,2},{4,5},{5,4},{6,7},{7,6},{8,9},{9,8},{10,11... | collective-permute-start | bytes 1032200 | tf_op jit(solution)/shard_map/ppermute | solution.py:44
  49.1 2.1 %collective-permute-start.7 = (bf16[192,896]{1,0:T(8,128)(2,1)S(1)}, bf16[192,896]{1,0:T(8,128)(2,1)S(1)}, u32[]{:S(2)}, u32[]{:S(2)}) collective-permute-start(bf16[192,896]{1,0:T(8,128)(2,1)S(1)} %collective-permute-done.3.refs_2_), channel_id=1, source_target_pairs={{0,1},{1,0},{2,3},{3,2},{4,5},{5,4},{6,7},{7,6},{8,9},{9,8},{10,11... | collective-permute-start | bytes 1032200 | tf_op jit(solution)/shard_map/ppermute | solution.py:44
  50.3 1.7 %collective-permute-start.8 = (bf16[192,896]{1,0:T(8,128)(2,1)S(1)}, bf16[192,896]{1,0:T(8,128)(2,1)S(1)}, u32[]{:S(2)}, u32[]{:S(2)}) collective-permute-start(bf16[192,896]{1,0:T(8,128)(2,1)S(1)} %collective-permute-done.4.refs_3_), channel_id=1, source_target_pairs={{0,1},{1,0},{2,3},{3,2},{4,5},{5,4},{6,7},{7,6},{8,9},{9,8},{10,11... | collective-permute-start | bytes 1032200 | tf_op jit(solution)/shard_map/ppermute | solution.py:44
  54.3 14.9 %collective-permute-start.9 = (bf16[64,768]{1,0:T(8,128)(2,1)S(1)}, bf16[64,768]{1,0:T(8,128)(2,1)S(1)}, u32[]{:S(2)}, u32[]{:S(2)}) collective-permute-start(bf16[64,768]{1,0:T(8,128)(2,1)S(1)} %get-tuple-element.84), channel_id=1, source_target_pairs={{0,6},{1,7},{2,0},{3,1},{4,2},{5,3},{6,4},{7,5},{8,14},{9,15},{10,... | collective-permute-start | bytes 294920 | tf_op jit(solution)/shard_map/ppermute | solution.py:44
  56.2 13.0 %collective-permute-start.10 = (bf16[64,768]{1,0:T(8,128)(2,1)S(1)}, bf16[64,768]{1,0:T(8,128)(2,1)S(1)}, u32[]{:S(2)}, u32[]{:S(2)}) collective-permute-start(bf16[64,768]{1,0:T(8,128)(2,1)S(1)} %get-tuple-element.85), channel_id=1, source_target_pairs={{0,4},{1,5},{2,6},{3,7},{4,0},{5,1},{6,2},{7,3},{8,12},{9,13},{10,... | collective-permute-start | bytes 294920 | tf_op jit(solution)/shard_map/ppermute | solution.py:44
  56.9 12.3 %collective-permute-start.11 = (bf16[64,768]{1,0:T(8,128)(2,1)S(1)}, bf16[64,768]{1,0:T(8,128)(2,1)S(1)}, u32[]{:S(2)}, u32[]{:S(2)}) collective-permute-start(bf16[64,768]{1,0:T(8,128)(2,1)S(1)} %get-tuple-element.86), channel_id=1, source_target_pairs={{0,2},{1,3},{2,4},{3,5},{4,6},{5,7},{6,0},{7,1},{8,10},{9,11},{10,... | collective-permute-start | bytes 294920 | tf_op jit(solution)/shard_map/ppermute | solution.py:44
  65.6 9.2 %collective-permute-start.18 = (bf16[64,768]{1,0:T(8,128)(2,1)S(1)}, bf16[64,768]{1,0:T(8,128)(2,1)S(1)}, u32[]{:S(2)}, u32[]{:S(2)}) collective-permute-start(bf16[64,768]{1,0:T(8,128)(2,1)S(1)} %get-tuple-element.99), channel_id=1, source_target_pairs={{0,4},{1,5},{2,6},{3,7},{4,0},{5,1},{6,2},{7,3},{8,12},{9,13},{10,... | collective-permute-start | bytes 294920 | tf_op jit(solution)/shard_map/ppermute | solution.py:44
  68.5 8.2 %collective-permute-start.17 = (bf16[64,768]{1,0:T(8,128)(2,1)S(1)}, bf16[64,768]{1,0:T(8,128)(2,1)S(1)}, u32[]{:S(2)}, u32[]{:S(2)}) collective-permute-start(bf16[64,768]{1,0:T(8,128)(2,1)S(1)} %get-tuple-element.88), channel_id=1, source_target_pairs={{0,6},{1,7},{2,0},{3,1},{4,2},{5,3},{6,4},{7,5},{8,14},{9,15},{10,... | collective-permute-start | bytes 294920 | tf_op jit(solution)/shard_map/ppermute | solution.py:44
  69.2 7.5 %collective-permute-start.19 = (bf16[64,768]{1,0:T(8,128)(2,1)S(1)}, bf16[64,768]{1,0:T(8,128)(2,1)S(1)}, u32[]{:S(2)}, u32[]{:S(2)}) collective-permute-start(bf16[64,768]{1,0:T(8,128)(2,1)S(1)} %get-tuple-element.100), channel_id=1, source_target_pairs={{0,2},{1,3},{2,4},{3,5},{4,6},{5,7},{6,0},{7,1},{8,10},{9,11},{10,... | collective-permute-start | bytes 294920 | tf_op jit(solution)/shard_map/ppermute | solution.py:44
  71.3 8.2 %collective-permute-start.16 = (bf16[64,768]{1,0:T(8,128)(2,1)S(1)}, bf16[64,768]{1,0:T(8,128)(2,1)S(1)}, u32[]{:S(2)}, u32[]{:S(2)}) collective-permute-start(bf16[64,768]{1,0:T(8,128)(2,1)S(1)} %middle.2.refs_0_), channel_id=1, source_target_pairs={{0,6},{1,7},{2,0},{3,1},{4,2},{5,3},{6,4},{7,5},{8,14},{9,15},{10,... | collective-permute-start | bytes 294920 | tf_op jit(solution)/shard_map/ppermute | solution.py:44
  73.2 7.2 %collective-permute-start.15 = (bf16[64,768]{1,0:T(8,128)(2,1)S(1)}, bf16[64,768]{1,0:T(8,128)(2,1)S(1)}, u32[]{:S(2)}, u32[]{:S(2)}) collective-permute-start(bf16[64,768]{1,0:T(8,128)(2,1)S(1)} %middle.2.refs_0_), channel_id=1, source_target_pairs={{0,4},{1,5},{2,6},{3,7},{4,0},{5,1},{6,2},{7,3},{8,12},{9,13},{10,... | collective-permute-start | bytes 294920 | tf_op jit(solution)/shard_map/ppermute | solution.py:44
  74.8 7.3 %collective-permute-start.14 = (bf16[64,768]{1,0:T(8,128)(2,1)S(1)}, bf16[64,768]{1,0:T(8,128)(2,1)S(1)}, u32[]{:S(2)}, u32[]{:S(2)}) collective-permute-start(bf16[64,768]{1,0:T(8,128)(2,1)S(1)} %middle.2.refs_0_), channel_id=1, source_target_pairs={{0,2},{1,3},{2,4},{3,5},{4,6},{5,7},{6,0},{7,1},{8,10},{9,11},{10,... | collective-permute-start | bytes 294920 | tf_op jit(solution)/shard_map/ppermute | solution.py:44
  77.3 7.6 %collective-permute-start.22 = (bf16[64,768]{1,0:T(8,128)(2,1)S(1)}, bf16[64,768]{1,0:T(8,128)(2,1)S(1)}, u32[]{:S(2)}, u32[]{:S(2)}) collective-permute-start(bf16[64,768]{1,0:T(8,128)(2,1)S(1)} %middle.3.refs_0_), channel_id=1, source_target_pairs={{0,6},{1,7},{2,0},{3,1},{4,2},{5,3},{6,4},{7,5},{8,14},{9,15},{10,... | collective-permute-start | bytes 294920 | tf_op jit(solution)/shard_map/ppermute | solution.py:44
  78.8 6.2 %collective-permute-start.21 = (bf16[64,768]{1,0:T(8,128)(2,1)S(1)}, bf16[64,768]{1,0:T(8,128)(2,1)S(1)}, u32[]{:S(2)}, u32[]{:S(2)}) collective-permute-start(bf16[64,768]{1,0:T(8,128)(2,1)S(1)} %middle.3.refs_0_), channel_id=1, source_target_pairs={{0,4},{1,5},{2,6},{3,7},{4,0},{5,1},{6,2},{7,3},{8,12},{9,13},{10,... | collective-permute-start | bytes 294920 | tf_op jit(solution)/shard_map/ppermute | solution.py:44
  79.5 6.5 %collective-permute-start.20 = (bf16[64,768]{1,0:T(8,128)(2,1)S(1)}, bf16[64,768]{1,0:T(8,128)(2,1)S(1)}, u32[]{:S(2)}, u32[]{:S(2)}) collective-permute-start(bf16[64,768]{1,0:T(8,128)(2,1)S(1)} %middle.3.refs_0_), channel_id=1, source_target_pairs={{0,2},{1,3},{2,4},{3,5},{4,6},{5,7},{6,0},{7,1},{8,10},{9,11},{10,... | collective-permute-start | bytes 294920 | tf_op jit(solution)/shard_map/ppermute | solution.py:44
  87.1 4.7 %collective-permute-start.25 = (bf16[768,896]{1,0:T(8,128)(2,1)S(1)}, bf16[768,896]{1,0:T(8,128)(2,1)S(1)}, u32[]{:S(2)}, u32[]{:S(2)}) collective-permute-start(bf16[768,896]{1,0:T(8,128)(2,1)S(1)} %get-tuple-element.109), channel_id=1, source_target_pairs={{0,1},{1,0},{2,3},{3,2},{4,5},{5,4},{6,7},{7,6},{8,9},{9,8},{10,11... | collective-permute-start | bytes 4128776 | tf_op jit(solution)/shard_map/ppermute | solution.py:44
  88.5 14.2 %collective-permute-start.24 = (bf16[128,1792]{1,0:T(8,128)(2,1)S(1)}, bf16[128,1792]{1,0:T(8,128)(2,1)S(1)}, u32[]{:S(2)}, u32[]{:S(2)}) collective-permute-start(bf16[128,1792]{1,0:T(8,128)(2,1)S(1)} %get-tuple-element.108), channel_id=1, source_target_pairs={{0,8},{1,9},{2,10},{3,11},{4,12},{5,13},{6,14},{7,15},{8,16},{9,17... | collective-permute-start | bytes 1376264 | tf_op jit(solution)/shard_map/ppermute | solution.py:44
  88.6 14.1 %collective-permute-start.23 = (bf16[128,1792]{1,0:T(8,128)(2,1)S(1)}, bf16[128,1792]{1,0:T(8,128)(2,1)S(1)}, u32[]{:S(2)}, u32[]{:S(2)}) collective-permute-start(bf16[128,1792]{1,0:T(8,128)(2,1)S(1)} %get-tuple-element.107), channel_id=1, source_target_pairs={{0,24},{1,25},{2,26},{3,27},{4,28},{5,29},{6,30},{7,31},{8,0},{9,1... | collective-permute-start | bytes 1376264 | tf_op jit(solution)/shard_map/ppermute | solution.py:44
  93.3 0.8 copy-start.1
  94.1 20.1 %collective-permute-start.28 = (bf16[192,896]{1,0:T(8,128)(2,1)S(1)}, bf16[192,896]{1,0:T(8,128)(2,1)S(1)}, u32[]{:S(2)}, u32[]{:S(2)}) collective-permute-start(bf16[192,896]{1,0:T(8,128)(2,1)S(1)} %get-tuple-element.119), channel_id=1, source_target_pairs={{0,6},{1,7},{2,0},{3,1},{4,2},{5,3},{6,4},{7,5},{8,14},{9,15},{10,... | collective-permute-start | bytes 1032200 | tf_op jit(solution)/shard_map/ppermute | solution.py:44
  94.9 19.3 %collective-permute-start.29 = (bf16[192,896]{1,0:T(8,128)(2,1)S(1)}, bf16[192,896]{1,0:T(8,128)(2,1)S(1)}, u32[]{:S(2)}, u32[]{:S(2)}) collective-permute-start(bf16[192,896]{1,0:T(8,128)(2,1)S(1)} %get-tuple-element.120), channel_id=1, source_target_pairs={{0,4},{1,5},{2,6},{3,7},{4,0},{5,1},{6,2},{7,3},{8,12},{9,13},{10,... | collective-permute-start | bytes 1032200 | tf_op jit(solution)/shard_map/ppermute | solution.py:44
  95.8 18.4 %collective-permute-start.30 = (bf16[192,896]{1,0:T(8,128)(2,1)S(1)}, bf16[192,896]{1,0:T(8,128)(2,1)S(1)}, u32[]{:S(2)}, u32[]{:S(2)}) collective-permute-start(bf16[192,896]{1,0:T(8,128)(2,1)S(1)} %get-tuple-element.121), channel_id=1, source_target_pairs={{0,2},{1,3},{2,4},{3,5},{4,6},{5,7},{6,0},{7,1},{8,10},{9,11},{10,... | collective-permute-start | bytes 1032200 | tf_op jit(solution)/shard_map/ppermute | solution.py:44
  103.3 7.4 %collective-permute-start.26 = (bf16[64,1792]{1,0:T(8,128)(2,1)S(1)}, bf16[64,1792]{1,0:T(8,128)(2,1)S(1)}, u32[]{:S(2)}, u32[]{:S(2)}) collective-permute-start(bf16[64,1792]{1,0:T(8,128)(2,1)S(1)} %get-tuple-element.117), channel_id=1, source_target_pairs={{0,24},{1,25},{2,26},{3,27},{4,28},{5,29},{6,30},{7,31},{8,0},{9,1... | collective-permute-start | bytes 688136 | tf_op jit(solution)/shard_map/ppermute | solution.py:44
  106.3 7.8 %collective-permute-start.27 = (bf16[64,1792]{1,0:T(8,128)(2,1)S(1)}, bf16[64,1792]{1,0:T(8,128)(2,1)S(1)}, u32[]{:S(2)}, u32[]{:S(2)}) collective-permute-start(bf16[64,1792]{1,0:T(8,128)(2,1)S(1)} %get-tuple-element.118), channel_id=1, source_target_pairs={{0,8},{1,9},{2,10},{3,11},{4,12},{5,13},{6,14},{7,15},{8,16},{9,17... | collective-permute-start | bytes 688136 | tf_op jit(solution)/shard_map/ppermute | solution.py:44
  114.2 5.1 %copy-start.6 = (bf16[192,896]{1,0:T(8,128)(2,1)}, bf16[192,896]{1,0:T(8,128)(2,1)S(1)}, u32[]{:S(2)}) copy-start(bf16[192,896]{1,0:T(8,128)(2,1)S(1)} %collective-permute-done.28.g1) | copy-start | bytes 1032196
  114.2 5.1 %copy-start.7 = (bf16[192,896]{1,0:T(8,128)(2,1)}, bf16[192,896]{1,0:T(8,128)(2,1)S(1)}, u32[]{:S(2)}) copy-start(bf16[192,896]{1,0:T(8,128)(2,1)S(1)} %collective-permute-done.29.g2) | copy-start | bytes 1032196
  114.2 5.1 %copy-start.8 = (bf16[192,896]{1,0:T(8,128)(2,1)}, bf16[192,896]{1,0:T(8,128)(2,1)S(1)}, u32[]{:S(2)}) copy-start(bf16[192,896]{1,0:T(8,128)(2,1)S(1)} %collective-permute-done.30.g3) | copy-start | bytes 1032196
  115.7 14.0 %all-to-all-start.1 = ((bf16[16,8,1792]{2,1,0:T(8,128)(2,1)}), bf16[16,8,1792]{2,1,0:T(8,128)(2,1)S(1)}, u32[]{:S(2)}, u32[]{:S(2)}) async-start(bf16[16,8,1792]{2,1,0:T(8,128)(2,1)} %sum_back.1), calls=%async_computation.1 | async-start | bytes 917504 | tf_op jit(solution)/shard_map/all_to_all | solution.py:381
  119.3 10.4 %copy-start.3 = (s32[4]{0:T(128)S(1)}, s32[4]{0:T(128)}, u32[]{:S(2)}) copy-start(s32[4]{0:T(128)} %copy-done.2) | copy-start | bytes 52
  119.3 10.4 %copy-start.4 = (bf16[32,128]{1,0:T(8,128)(2,1)S(1)}, bf16[32,128]{1,0:T(8,128)(2,1)}, u32[]{:S(2)}) copy-start(bf16[32,128]{1,0:T(8,128)(2,1)} %get-tuple-element.67.pick) | copy-start | bytes 24580
